TPU v7x, 32 devices: a whole 2x2x4 slice. The times are simulated.
32 devices in a mesh: px: 8 (over z, x), vx: 4 (over y, core).
Axes of the slice: x: 2, y: 2, z: 4, core: 2. Of those that a mesh axis runs over, the one named last changes fastest.
Arguments:
- value_field: float32 [16, 96, 64, 384], P('px', 'vx'), may hold values from -6 to 6
- cost_field: float32 [16, 96, 64, 384], P('px', 'vx'), may hold values from -6 to 6
- accel_first: float32 [16, 96], P('px', 'vx'), may hold values from -3 to 3
- accel_second: float32 [64, 384], replicated, may hold values from -1 to 1
Outputs:
- final_value: float32 [16, 96, 64, 384], P('px', 'vx')
- funnel_slice: float32 [16, 384], P('px')
All inputs are finite; a program needn't handle non-finite values.
Results may differ from a plain program's by a relative error of at most 0.00002.
Values sent between devices are 32-bit elements; how exact they have to be, the bound alone decides.
No kernel may reach another device: no remote copies, remote signals or barrier semaphores. Data moves between devices by JAX's collectives and lax.ppermute only.
A program may use at most 128 MiB of HBM per device.

v0:
```python
import jax
import jax.numpy as jnp
from jax import lax
from jax.sharding import PartitionSpec as P

VELOCITY_LIMIT = 1.0
PLANNER_SPEED = 0.3
DISTURBANCE = 0.2
CONTROL_COST = 1.0
COURANT = 0.5


def padded_2(cells, sides, width):
    for axis, dim in sides:
        count = lax.axis_size(axis)
        ends = count - 1
        head = lax.slice_in_dim(cells, 0, width, axis=dim)
        tail = lax.slice_in_dim(cells, cells.shape[dim] - width, cells.shape[dim], axis=dim)
        cells = jnp.concatenate(
            [
                lax.ppermute(tail, axis, [(i, (i + 1) % count) for i in range(ends)]),
                cells,
                lax.ppermute(head, axis, [((i + 1) % count, i) for i in range(ends)]),
            ],
            axis=dim,
        )
    return cells


def interior(padded, dimension, offset):
    index_list = []
    for axis_number in range(4):
        size_here = padded.shape[axis_number]
        if axis_number == dimension:
            index_list.append(slice(1 + offset, size_here - 1 + offset))
        else:
            index_list.append(slice(1, size_here - 1))
    return padded[tuple(index_list)]


def slopes(padded, spacings):
    center = interior(padded, 0, 0)
    gradients = []
    curvatures = []
    for dimension in range(4):
        upper = interior(padded, dimension, 1)
        lower = interior(padded, dimension, -1)
        gradients.append((upper - lower) / (2.0 * spacings[dimension]))
        curvatures.append((upper - 2.0 * center + lower) / spacings[dimension])
    return (center, gradients, curvatures)


def hamiltonian(gradients, curvatures, speed_first, speed_second, push_first, push_second, rates):
    total = gradients[0] * speed_first + gradients[3] * speed_second
    total = total + PLANNER_SPEED * (jnp.abs(gradients[0]) + jnp.abs(gradients[3]))
    total = total + gradients[1] * push_first + gradients[2] * push_second
    total = total + DISTURBANCE * (jnp.abs(gradients[1]) + jnp.abs(gradients[2]))
    total = total - (gradients[1] * gradients[1] + gradients[2] * gradients[2]) / (
        2.0 * CONTROL_COST
    )
    damping = (
        rates[0] * curvatures[0]
        + rates[1] * curvatures[1]
        + rates[2] * curvatures[2]
        + rates[3] * curvatures[3]
    )
    return total - 0.5 * damping


def fill_edges(padded, width):
    edge_flags = (
        (0, lax.axis_index("px") == 0, lax.axis_index("px") == lax.axis_size("px") - 1),
        (1, lax.axis_index("vx") == 0, lax.axis_index("vx") == lax.axis_size("vx") - 1),
    )
    for dimension, is_first, is_last in edge_flags:
        count = padded.shape[dimension]
        low_edge = lax.slice_in_dim(padded, width, width + 1, axis=dimension)
        high_edge = lax.slice_in_dim(padded, count - width - 1, count - width, axis=dimension)
        shape_small = [1, 1, 1, 1]
        shape_small[dimension] = count
        position = lax.broadcasted_iota(jnp.int32, tuple(shape_small), dimension)
        padded = jnp.where(jnp.logical_and(is_first, position < width), low_edge, padded)
        padded = jnp.where(jnp.logical_and(is_last, position >= count - width), high_edge, padded)
    return padded


def pad_local(padded):
    return jnp.pad(padded, ((0, 0), (0, 0), (1, 1), (1, 1)), mode="edge")


def halo_once(field):
    return padded_2(field, (("px", 0), ("vx", 1)), 1)


def bound_speeds(gradient_vx, gradient_vy):
    return lax.pmax((jnp.max(jnp.abs(gradient_vx)), jnp.max(jnp.abs(gradient_vy))), ("px", "vx"))


def per_device(value_field, cost_field, accel_first, accel_second):
    cells_x = value_field.shape[0]
    cells_v = value_field.shape[1]
    total_vx = cells_v * lax.axis_size("vx")
    total_vy = value_field.shape[2]
    velocity_step_x = 2.0 * VELOCITY_LIMIT / total_vx
    velocity_step_y = 2.0 * VELOCITY_LIMIT / total_vy
    position_step = velocity_step_x * velocity_step_y
    spacings = (position_step, velocity_step_x, velocity_step_y, position_step)
    first_global = lax.axis_index("vx") * cells_v
    speed_second = (
        (2.0 * jnp.arange(total_vy, dtype=jnp.float32) + 1.0 - total_vy)
        * (VELOCITY_LIMIT / total_vy)
    ).reshape(total_vy, 1)
    push_limit = lax.pmax(jnp.max(jnp.abs(accel_first)), ("px", "vx"))
    push_second_limit = jnp.max(jnp.abs(accel_second))
    rate_first = VELOCITY_LIMIT * (total_vx - 1) / total_vx + PLANNER_SPEED
    rate_last = VELOCITY_LIMIT * (total_vy - 1) / total_vy + PLANNER_SPEED

    def make_rates(maxima):
        return (
            rate_first,
            push_limit + DISTURBANCE + maxima[0] / CONTROL_COST,
            push_second_limit + DISTURBANCE + maxima[1] / CONTROL_COST,
            rate_last,
        )

    positions = (first_global + jnp.arange(cells_v, dtype=jnp.int32)).astype(jnp.float32)
    speed_own = ((2.0 * positions + 1.0 - total_vx) * (VELOCITY_LIMIT / total_vx)).reshape(
        cells_v, 1, 1
    )
    push_own = accel_first.reshape(cells_x, cells_v, 1, 1)
    current = value_field
    for repeat in range(2):
        padded = pad_local(fill_edges(halo_once(current), 1))
        center, gradients, curvatures = slopes(padded, spacings)
        rates = make_rates(bound_speeds(gradients[1], gradients[2]))
        step_size = COURANT / (
            rates[0] / spacings[0]
            + rates[1] / spacings[1]
            + rates[2] / spacings[2]
            + rates[3] / spacings[3]
        )
        change = hamiltonian(
            gradients, curvatures, speed_own, speed_second, push_own, accel_second, rates
        )
        middle = jnp.maximum(cost_field, center + step_size * change)
        padded = pad_local(fill_edges(halo_once(middle), 1))
        center, gradients, curvatures = slopes(padded, spacings)
        rates = make_rates(bound_speeds(gradients[1], gradients[2]))
        change = hamiltonian(
            gradients, curvatures, speed_own, speed_second, push_own, accel_second, rates
        )
        current = jnp.maximum(cost_field, 0.5 * current + 0.5 * (center + step_size * change))
    funnel_local = jnp.min(current, axis=(1, 2))
    funnel_slice = lax.pmin(funnel_local, "vx")
    return (current, funnel_slice)


def solution(mesh):
    placed = (P("px", "vx", None, None), P("px", "vx", None, None), P("px", "vx"), P())
    return jax.shard_map(
        per_device,
        mesh=mesh,
        in_specs=placed,
        out_specs=(P("px", "vx", None, None), P("px", None)),
        check_vma=False,
    )
```

profile of v0, /device:TPU:0, one launch (start us, length us, event | category | flops | bytes accessed | tf_op | source)
XLA Modules:
  0.0 812.5 jit_solution(15296024993012722608)
XLA Ops:
  0.6 5.1 fusion.55
  5.8 6.3 collective-permute-start
  12.0 1.3 collective-permute-start.1
  13.3 0.6 broadcast_multiply_fusion
  14.6 97.3 %collective-permute-done = f32[1,24,64,384]{3,2,1,0:T(8,128)} collective-permute-done((f32[1,24,64,384]{3,2,1,0:T(8,128)}, f32[1,24,64,384]{3,2,1,0:T(8,128)}, u32[]{:S(2)}, u32[]{:S(2)}) %collective-permute-start) | collective-permute-done | bytes 2359328 | tf_op jit(solution)/shard_map/ppermute | solution.py:21
  112.0 1.8 constant_dynamic-update-slice_fusion.2
  113.8 0.3 constant_dynamic-update-slice_fusion.1
  114.2 0.2 constant_dynamic-update-slice_fusion
  114.5 1.3 collective-permute-start.2
  115.8 1.3 collective-permute-start.3
  117.1 0.6 broadcast_multiply_fusion.1
  117.8 3.4 collective-permute-done.3
  121.1 4.6 pad_maximum_fusion
  125.8 2.8 slice_bitcast_fusion.7
  128.6 2.0 select_select_fusion.7
  130.7 4.9 select_select_fusion.6
  135.6 0.2 fusion.50
  135.9 4.7 abs_reduce_fusion.7
  140.5 46.4 %all-reduce.3 = (f32[]{:T(128)}, f32[]{:T(128)}, f32[]{:T(128)}) all-reduce(f32[]{:T(128)} %get-tuple-element.9, f32[]{:T(128)} %get-tuple-element.64, f32[]{:T(128)} %get-tuple-element.8), channel_id=1, replica_groups=mesh['px'=8,'vx'=4] {'px','vx'}, use_global_device_ids=true, to_apply=%region_6.7 | all-reduce | flops 3 | bytes 24 | tf_op jit(solution)/shard_map/pmax | solution.py:96
  188.8 24.4 %add_maximum_fusion.1 = f32[2,24,64,384]{3,2,1,0:T(8,128)S(1)} fusion(f32[2,24,64,384]{3,2,1,0:T(8,128)} %param.5, f32[4,26,64,384]{3,2,1,0:T(8,128)} %copy-done.1, f32[4,26,1,384]{3,2,1,0:T(1,128)S(1)} %get-tuple-element.40, f32[4,26,1,384]{3,2,1,0:T(1,128)S(1)} %get-tuple-element.39, f32[]{:T(128)S(6)} %div.105, f32[]{:T(128)S(6)} %div.103, ...), kind=kLoop, calls=%fused_computation.104 | loop fusion | flops 86114304 | bytes 43672108 | tf_op jit(solution)/shard_map/max | solution.py:145
  213.2 0.5 fusion.54
  213.7 4.3 collective-permute-start.4
  218.1 1.3 collective-permute-start.5
  219.4 97.5 %collective-permute-done.4 = f32[1,24,64,384]{3,2,1,0:T(8,128)S(1)} collective-permute-done((f32[1,24,64,384]{3,2,1,0:T(8,128)S(1)}, f32[1,24,64,384]{3,2,1,0:T(8,128)S(1)}, u32[]{:S(2)}, u32[]{:S(2)}) %collective-permute-start.4) | collective-permute-done | bytes 2359328 | tf_op jit(solution)/shard_map/ppermute | solution.py:21
  317.0 1.3 collective-permute-start.6
  318.3 1.3 collective-permute-start.7
  319.6 4.5 collective-permute-done.7
  324.1 0.8 pad_maximum_fusion.1
  324.9 0.3 slice_bitcast_fusion.5
  325.3 3.1 select_select_fusion.5
  328.4 4.5 select_select_fusion.4
  332.9 0.2 fusion.49
  333.2 4.7 abs_reduce_fusion.5
  337.8 45.0 %all-reduce.2 = (f32[]{:T(128)}, f32[]{:T(128)}) all-reduce(f32[]{:T(128)} %get-tuple-element.7, f32[]{:T(128)} %get-tuple-element.6), channel_id=1, replica_groups=mesh['px'=8,'vx'=4] {'px','vx'}, use_global_device_ids=true, to_apply=%region_10.11 | all-reduce | flops 2 | bytes 16 | tf_op jit(solution)/shard_map/pmax | solution.py:96
  384.1 25.3 %multiply_maximum_fusion.1 = f32[2,24,64,384]{3,2,1,0:T(8,128)S(1)} fusion(f32[2,24,64,384]{3,2,1,0:T(8,128)} %param.5, f32[2,24,64,384]{3,2,1,0:T(8,128)} %param.4, f32[4,26,64,384]{3,2,1,0:T(8,128)} %copy-done.3, f32[4,26,1,384]{3,2,1,0:T(1,128)S(1)} %get-tuple-element.34, f32[4,26,1,384]{3,2,1,0:T(1,128)S(1)} %get-tuple-element.33, f32[]{:T(128)S(6)} %mul.414, ...), kind=kLoop, calls=%fused_computation.96 | loop fusion | flops 88473600 | bytes 48390700 | tf_op jit(solution)/shard_map/max | solution.py:152
  409.4 0.5 fusion.53
  409.9 4.3 collective-permute-start.8
  414.3 1.3 collective-permute-start.9
  415.6 98.9 %collective-permute-done.8 = f32[1,24,64,384]{3,2,1,0:T(8,128)S(1)} collective-permute-done((f32[1,24,64,384]{3,2,1,0:T(8,128)S(1)}, f32[1,24,64,384]{3,2,1,0:T(8,128)S(1)}, u32[]{:S(2)}, u32[]{:S(2)}) %collective-permute-start.8) | collective-permute-done | bytes 2359328 | tf_op jit(solution)/shard_map/ppermute | solution.py:21
  514.6 1.3 collective-permute-start.10
  515.9 1.3 collective-permute-start.11
  517.2 3.1 collective-permute-done.11
  520.3 0.8 pad_maximum_fusion.2
  521.1 0.3 slice_bitcast_fusion.3
  521.4 3.1 select_select_fusion.3
  524.6 4.5 select_select_fusion.2
  529.4 4.7 abs_reduce_fusion.3
  534.0 46.5 %all-reduce.1 = (f32[]{:T(128)}, f32[]{:T(128)}) all-reduce(f32[]{:T(128)} %get-tuple-element.5, f32[]{:T(128)} %get-tuple-element.4), channel_id=1, replica_groups=mesh['px'=8,'vx'=4] {'px','vx'}, use_global_device_ids=true, to_apply=%region_14.15 | all-reduce | flops 2 | bytes 16 | tf_op jit(solution)/shard_map/pmax | solution.py:96
  581.8 24.4 %add_maximum_fusion = f32[2,24,64,384]{3,2,1,0:T(8,128)S(1)} fusion(f32[2,24,64,384]{3,2,1,0:T(8,128)} %param.5, f32[4,26,64,384]{3,2,1,0:T(8,128)} %copy-done.2, f32[4,26,1,384]{3,2,1,0:T(1,128)S(1)} %get-tuple-element.28, f32[4,26,1,384]{3,2,1,0:T(1,128)S(1)} %get-tuple-element.27, f32[]{:T(128)S(6)} %div.118, f32[]{:T(128)S(6)} %div.116, f32[]{:T(128)S(6)} %div.119, ...), kind=kLoop, calls=%fused_computation.88 | loop fusion | flops 86114304 | bytes 43672108 | tf_op jit(solution)/shard_map/max | solution.py:145
  606.2 0.5 fusion.52
  606.7 4.3 collective-permute-start.12
  611.1 1.3 collective-permute-start.13
  612.4 99.3 %collective-permute-done.12 = f32[1,24,64,384]{3,2,1,0:T(8,128)S(1)} collective-permute-done((f32[1,24,64,384]{3,2,1,0:T(8,128)S(1)}, f32[1,24,64,384]{3,2,1,0:T(8,128)S(1)}, u32[]{:S(2)}, u32[]{:S(2)}) %collective-permute-start.12) | collective-permute-done | bytes 2359328 | tf_op jit(solution)/shard_map/ppermute | solution.py:21
  711.8 1.3 collective-permute-start.14
  713.1 1.3 collective-permute-start.15
  714.4 2.7 collective-permute-done.15
  717.1 0.8 pad_maximum_fusion.3
  717.9 0.3 slice_bitcast_fusion.1
  718.2 3.1 select_select_fusion.1
  721.4 4.5 select_select_fusion
  726.2 4.7 abs_reduce_fusion.1
  730.8 46.0 %all-reduce = (f32[]{:T(128)}, f32[]{:T(128)}) all-reduce(f32[]{:T(128)} %get-tuple-element.3, f32[]{:T(128)} %get-tuple-element.2), channel_id=1, replica_groups=mesh['px'=8,'vx'=4] {'px','vx'}, use_global_device_ids=true, to_apply=%region_18.19 | all-reduce | flops 2 | bytes 16 | tf_op jit(solution)/shard_map/pmax | solution.py:96
  778.0 26.4 %fusion.46 = (f32[2,384]{1,0:T(2,128)S(1)}, f32[2,24,64,384]{3,2,1,0:T(8,128)}) fusion(f32[2,24,64,384]{3,2,1,0:T(8,128)} %param.5, f32[2,24,64,384]{3,2,1,0:T(8,128)} %copy-done.4, f32[]{:T(128)S(6)} %mul.452, f32[]{:T(128)S(6)} %mul.449, f32[64,384]{1,0:T(8,128)S(1)} %get-tuple-element.61, f32[4,26,64,384]{3,2,1,0:T(8,128)} %copy-done, ...), kind=kLoop, calls=%fused_computation.162 | loop fusion | flops 89652480 | bytes 48393772 | tf_op jit(solution)/shard_map/reduce_min | solution.py:153
  804.4 7.9 pmin.7
  (38 shorter events, 1.0 us)
Async XLA Ops:
  0.6 12.7 %copy-start.6 = (f32[64,384]{1,0:T(8,128)S(1)}, f32[64,384]{1,0:T(8,128)}, u32[]{:S(2)}) copy-start(f32[64,384]{1,0:T(8,128)} %param.7) | copy-start | bytes 294916
  5.8 106.2 %collective-permute-start = (f32[1,24,64,384]{3,2,1,0:T(8,128)}, f32[1,24,64,384]{3,2,1,0:T(8,128)}, u32[]{:S(2)}, u32[]{:S(2)}) collective-permute-start(f32[1,24,64,384]{3,2,1,0:T(8,128)} %get-tuple-element.60), channel_id=1, source_target_pairs={{0,4},{4,8},{8,12},{12,16},{16,20},{20,24},{24,28},{1,5},{5,9},{9,... | collective-permute-start | bytes 7077896 | tf_op jit(solution)/shard_map/ppermute | solution.py:21
  12.0 102.1 %collective-permute-start.1 = (f32[1,24,64,384]{3,2,1,0:T(8,128)}, f32[1,24,64,384]{3,2,1,0:T(8,128)S(1)}, u32[]{:S(2)}, u32[]{:S(2)}) collective-permute-start(f32[1,24,64,384]{3,2,1,0:T(8,128)} %get-tuple-element.59), channel_id=1, source_target_pairs={{4,0},{8,4},{12,8},{16,12},{20,16},{24,20},{28,24},{5,1},{9,5},{13... | collective-permute-start | bytes 7077896 | tf_op jit(solution)/shard_map/ppermute | solution.py:23
  14.6 99.2 %copy-start.5 = (f32[2,24,64,384]{3,2,1,0:T(8,128)S(1)}, f32[2,24,64,384]{3,2,1,0:T(8,128)}, u32[]{:S(2)}) copy-start(f32[2,24,64,384]{3,2,1,0:T(8,128)} %param.4) | copy-start | bytes 14155780
  114.1 3.0 copy-start.7
  114.5 3.3 collective-permute-start.2
  115.8 5.3 collective-permute-start.3
  135.6 4.9 copy-start.1
  213.7 103.2 %collective-permute-start.4 = (f32[1,24,64,384]{3,2,1,0:T(8,128)S(1)}, f32[1,24,64,384]{3,2,1,0:T(8,128)S(1)}, u32[]{:S(2)}, u32[]{:S(2)}) collective-permute-start(f32[1,24,64,384]{3,2,1,0:T(8,128)S(1)} %get-tuple-element.57), channel_id=1, source_target_pairs={{0,4},{4,8},{8,12},{12,16},{16,20},{20,24},{24,28},{1,5},{5,9},{9,... | collective-permute-start | bytes 7077896 | tf_op jit(solution)/shard_map/ppermute | solution.py:21
  218.1 98.8 %collective-permute-start.5 = (f32[1,24,64,384]{3,2,1,0:T(8,128)S(1)}, f32[1,24,64,384]{3,2,1,0:T(8,128)S(1)}, u32[]{:S(2)}, u32[]{:S(2)}) collective-permute-start(f32[1,24,64,384]{3,2,1,0:T(8,128)S(1)} %get-tuple-element.58), channel_id=1, source_target_pairs={{4,0},{8,4},{12,8},{16,12},{20,16},{24,20},{28,24},{5,1},{9,5},{13... | collective-permute-start | bytes 7077896 | tf_op jit(solution)/shard_map/ppermute | solution.py:23
  317.0 2.6 collective-permute-start.6
  318.3 5.8 collective-permute-start.7
  332.9 4.9 copy-start.3
  409.4 115.2 %copy-start.4 = (f32[2,24,64,384]{3,2,1,0:T(8,128)}, f32[2,24,64,384]{3,2,1,0:T(8,128)S(1)}, u32[]{:S(2)}) copy-start(f32[2,24,64,384]{3,2,1,0:T(8,128)S(1)} %multiply_maximum_fusion.1) | copy-start | bytes 14155780
  409.9 104.6 %collective-permute-start.8 = (f32[1,24,64,384]{3,2,1,0:T(8,128)S(1)}, f32[1,24,64,384]{3,2,1,0:T(8,128)S(1)}, u32[]{:S(2)}, u32[]{:S(2)}) collective-permute-start(f32[1,24,64,384]{3,2,1,0:T(8,128)S(1)} %get-tuple-element.55), channel_id=1, source_target_pairs={{0,4},{4,8},{8,12},{12,16},{16,20},{20,24},{24,28},{1,5},{5,9},{9,... | collective-permute-start | bytes 7077896 | tf_op jit(solution)/shard_map/ppermute | solution.py:21
  414.3 100.2 %collective-permute-start.9 = (f32[1,24,64,384]{3,2,1,0:T(8,128)S(1)}, f32[1,24,64,384]{3,2,1,0:T(8,128)S(1)}, u32[]{:S(2)}, u32[]{:S(2)}) collective-permute-start(f32[1,24,64,384]{3,2,1,0:T(8,128)S(1)} %get-tuple-element.56), channel_id=1, source_target_pairs={{4,0},{8,4},{12,8},{16,12},{20,16},{24,20},{28,24},{5,1},{9,5},{13... | collective-permute-start | bytes 7077896 | tf_op jit(solution)/shard_map/ppermute | solution.py:23
  514.6 2.6 collective-permute-start.10
  515.9 4.4 collective-permute-start.11
  529.1 4.9 copy-start.2
  606.7 105.0 %collective-permute-start.12 = (f32[1,24,64,384]{3,2,1,0:T(8,128)S(1)}, f32[1,24,64,384]{3,2,1,0:T(8,128)S(1)}, u32[]{:S(2)}, u32[]{:S(2)}) collective-permute-start(f32[1,24,64,384]{3,2,1,0:T(8,128)S(1)} %get-tuple-element.53), channel_id=1, source_target_pairs={{0,4},{4,8},{8,12},{12,16},{16,20},{20,24},{24,28},{1,5},{5,9},{9,... | collective-permute-start | bytes 7077896 | tf_op jit(solution)/shard_map/ppermute | solution.py:21
  611.1 100.6 %collective-permute-start.13 = (f32[1,24,64,384]{3,2,1,0:T(8,128)S(1)}, f32[1,24,64,384]{3,2,1,0:T(8,128)S(1)}, u32[]{:S(2)}, u32[]{:S(2)}) collective-permute-start(f32[1,24,64,384]{3,2,1,0:T(8,128)S(1)} %get-tuple-element.54), channel_id=1, source_target_pairs={{4,0},{8,4},{12,8},{16,12},{20,16},{24,20},{28,24},{5,1},{9,5},{13... | collective-permute-start | bytes 7077896 | tf_op jit(solution)/shard_map/ppermute | solution.py:23
  711.8 2.6 collective-permute-start.14
  713.1 4.0 collective-permute-start.15
  725.9 4.9 copy-start
where the time goes:
time: 820 us; the launch traced here: 812 us
  waiting for transfers between devices  407 us (50%)
  blocking collectives  192 us (23%)
  other arithmetic  157 us (19%)
  starting transfers between devices  34.8 us (4%)
  local copies, waits for them, and re-layouts  14.1 us (2%)
    ppermute x8, waiting for transfers between devices, padded_2(): lax.ppermute(tail, axis, [(i, (i + 1) % count) for i in range(ends)])  393 us
    pmax x4, blocking collectives, bound_speeds(): lax.pmax((jnp.max(jnp.abs(gradient_vx)), jnp.max(jnp.abs(gradient_vy))),...  184 us
    max x2, other arithmetic, per_device(): middle = jnp.maximum(cost_field, center + step_size * change)  48.8 us
    select_n x8, other arithmetic, fill_edges(): jnp.where(jnp.logical_and(is_last, position >= count - width), high_edge,...  29.7 us
    reduce_min x1, other arithmetic, per_device(): funnel_local = jnp.min(current, axis=(1, 2))  26.4 us
    max x1, other arithmetic, per_device(): jnp.maximum(cost_field, 0.5 * current + 0.5 * (center + step_size * change))  25.3 us
    ppermute x8, starting transfers between devices, padded_2(): lax.ppermute(tail, axis, [(i, (i + 1) % count) for i in range(ends)])  24.5 us
    reduce_max x4, other arithmetic, bound_speeds(): jnp.max(jnp.abs(gradient_vx))  18.6 us
  transfers between devices with their start and end apart: 16, of which 8 were waited for; matrix products, arithmetic and copies ran while one was open for 0% of the time, Pallas kernels for 0%

commit v1 on v0

v1 whole, which is shorter than its diff:
```python
import functools

import jax
import jax.numpy as jnp
from jax import lax
from jax.experimental import pallas as pl
from jax.experimental.pallas import tpu as pltpu
from jax.sharding import PartitionSpec as P

VELOCITY_LIMIT = 1.0
PLANNER_SPEED = 0.3
DISTURBANCE = 0.2
CONTROL_COST = 1.0
COURANT = 0.5

LANES = 128


def compiler_params():
    return pltpu.CompilerParams(vmem_limit_bytes=56 * 1024 * 1024)


def whole():
    return pl.BlockSpec(memory_space=pltpu.VMEM)


def scalars():
    return pl.BlockSpec(memory_space=pltpu.SMEM)


def fold(tile):
    rows = tile.shape[0]
    out = tile[0:8]
    for start in range(8, rows, 8):
        out = jnp.maximum(out, tile[start : start + 8])
    return out


def fold_min(tile):
    rows = tile.shape[0]
    out = tile[0:8]
    for start in range(8, rows, 8):
        out = jnp.minimum(out, tile[start : start + 8])
    return out


def lane_max(ref, lane):
    values = ref[...]
    position = lax.broadcasted_iota(jnp.int32, values.shape, 1)
    return jnp.max(jnp.where(position == lane, values, 0.0))


class Own:
    def __init__(self, array, outer):
        self.array, self.outer = array, outer

    def reader(self, ref, parity, half):
        row = parity if self.outer else 1 - parity
        start = pl.multiple_of(parity * half, half)
        return lambda j: ref[row, j, pl.ds(start, half), :]


class Row:
    def __init__(self, array):
        self.array = array

    def reader(self, ref, parity, half):
        return lambda j: ref[j]


def sweep(sizes, targets, rows, costs, bases, halo_rows, vx_low, vx_high, vy_next, maxima, accel_second, flags, push, speed, with_min=False):
    cells_v, half, width, total_vx, total_vy = sizes
    step_2 = 2.0 * VELOCITY_LIMIT / total_vx
    step_3 = 2.0 * VELOCITY_LIMIT / total_vy
    step_1 = step_2 * step_3
    rate_1 = VELOCITY_LIMIT * (total_vx - 1) / total_vx + PLANNER_SPEED
    rate_4 = VELOCITY_LIMIT * (total_vy - 1) / total_vy + PLANNER_SPEED
    count = len(targets)
    heun = bases is not None

    arrays = []

    def add(array):
        for position, known in enumerate(arrays):
            if known is array:
                return position
        arrays.append(array)
        return len(arrays) - 1

    needed = sorted({k for t in targets for k in (t - 1, t, t + 1) if 0 <= k <= 3})
    row_at = {k: add(rows[k].array) for k in needed}
    halo_at = {k: add(halo_rows[i]) for i, k in enumerate((-1, 4)) if any(abs(t - k) == 1 for t in targets)}
    cost_at = [add(c.array) for c in costs]
    base_at = [add(b.array) for b in bases] if heun else []
    low_at, high_at, vy_at, accel_at = add(vx_low), add(vx_high), add(vy_next), add(accel_second)
    maxima_at = [add(m) for m in maxima]
    n_in = len(arrays)

    def body(flags_ref, push_ref, speed_ref, *refs):
        ins = refs[:n_in]
        outs = refs[n_in:]
        out_rows = outs[:count]
        first_ref, second_ref, before_ref, last_ref, edge_ref, inner_ref, part_ref = outs[count : count + 7]
        min_ref = outs[count + 7] if with_min else None
        adv_up, adv_down, acc_up, acc_down = outs[-4:]
        parity, edge_low, edge_high, vx_first, vx_last = (flags_ref[i] for i in range(5))
        is_even = parity == 0

        limit_1 = lane_max(ins[maxima_at[0]], 2)
        limit_2 = lane_max(ins[maxima_at[0]], 3)

        def rates(ref):
            return (
                limit_1 + DISTURBANCE + lane_max(ref, 0) * (1.0 / (2.0 * step_2 * CONTROL_COST)),
                limit_2 + DISTURBANCE + lane_max(ref, 1) * (1.0 / (2.0 * step_3 * CONTROL_COST)),
            )

        old_2, old_3 = rates(ins[maxima_at[1]])
        rate_2, rate_3 = (old_2, old_3) if maxima_at[2] == maxima_at[1] else rates(ins[maxima_at[2]])
        total_rate = rate_1 / step_1 + old_2 / step_2 + old_3 / step_3 + rate_4 / step_1
        time_step = jnp.max(COURANT / jnp.full((8, LANES), total_rate, jnp.float32))
        scale = 0.5 * time_step if heun else time_step

        damp_1 = scale * (0.5 * rate_1 / step_1)
        damp_2 = scale * (0.5 / step_2) * rate_2
        damp_3 = scale * (0.5 / step_3) * rate_3
        damp_4 = scale * (0.5 * rate_4 / step_1)
        keep = (0.5 if heun else 1.0) + 2.0 * (damp_1 + damp_2 + damp_3 + damp_4)
        planner = scale * (PLANNER_SPEED / (2.0 * step_1))
        disturb_2 = scale * (DISTURBANCE / (2.0 * step_2))
        disturb_3 = scale * (DISTURBANCE / (2.0 * step_3))
        control_2 = scale * (1.0 / (8.0 * CONTROL_COST * step_2 * step_2))
        control_3 = scale * (1.0 / (8.0 * CONTROL_COST * step_3 * step_3))
        to_1 = scale / (2.0 * step_1)
        to_2 = scale / (2.0 * step_2)
        to_3 = scale / (2.0 * step_3)

        start = pl.multiple_of(parity * half, half)
        vy = (parity * half + lax.broadcasted_iota(jnp.int32, (half, width), 0)).astype(jnp.float32)
        speed_y = (2.0 * vy + (1.0 - total_vy)) * (VELOCITY_LIMIT / total_vy) * to_1
        adv_up[...] = speed_y + planner
        adv_down[...] = speed_y - planner
        accel = ins[accel_at][pl.ds(start, half), :] * to_3
        acc_up[...] = accel + disturb_3
        acc_down[...] = accel - disturb_3

        readers = {k: rows[k].reader(ins[row_at[k]], parity, half) for k in needed}
        cost_readers = [c.reader(ins[a], parity, half) for c, a in zip(costs, cost_at)]
        base_readers = [b.reader(ins[a], parity, half) for b, a in zip(bases, base_at)] if heun else None
        vy_row = lax.broadcasted_iota(jnp.int32, (half, width), 0)
        y_lane = lax.broadcasted_iota(jnp.int32, (half, width), 1)
        send_at = jnp.where(is_even, half - 1, 0)
        inner_at = jnp.where(is_even, half - 2, 1)
        wall_at = jnp.where(is_even, 0, half - 1)
        next_at = jnp.where(is_even, 1, half - 2)

        def neighbour(k, j, center):
            if k == -1:
                return jnp.where(edge_low == 1, center, ins[halo_at[-1]][j])
            if k == 4:
                return jnp.where(edge_high == 1, center, ins[halo_at[4]][j])
            return readers[k](j)

        def tile(i, j, low_2, high_2):
            t = targets[i]
            w = readers[t](j)
            low_1 = neighbour(t - 1, j, w)
            high_1 = neighbour(t + 1, j, w)
            if low_2 is None:
                low_2 = jnp.where(vx_first == 1, w, ins[low_at][t])
            else:
                low_2 = readers[t](low_2)
            if high_2 is None:
                high_2 = jnp.where(vx_last == 1, w, ins[high_at][t])
            else:
                high_2 = readers[t](high_2)
            beyond = ins[vy_at][3 - t, pl.ds(j, 1), :]
            below = jnp.where(is_even, w[0:1], beyond)
            above = jnp.where(is_even, beyond, w[half - 1 : half])
            low_3 = jnp.where(vy_row == 0, below, pltpu.roll(w, 1, 0))
            high_3 = jnp.where(vy_row == half - 1, above, pltpu.roll(w, half - 1, 0))
            low_4 = jnp.where(y_lane == 0, w, pltpu.roll(w, 1, 1))
            high_4 = jnp.where(y_lane == width - 1, w, pltpu.roll(w, width - 1, 1))

            flow = speed_ref[j] * to_1
            drift = push_ref[t, j] * to_2
            total = keep * w - damp_1 * (low_1 + high_1) - damp_4 * (low_4 + high_4)
            total = total - damp_2 * (low_2 + high_2) - damp_3 * (low_3 + high_3)
            slope = high_1 - low_1
            total = total + jnp.maximum((flow + planner) * slope, (flow - planner) * slope)
            slope = high_4 - low_4
            total = total + jnp.maximum(adv_up[...] * slope, adv_down[...] * slope)
            slope = high_2 - low_2
            bent = control_2 * slope
            total = total + jnp.maximum((drift + disturb_2 - bent) * slope, (drift - disturb_2 - bent) * slope)
            slope = high_3 - low_3
            bent = control_3 * slope
            total = total + jnp.maximum((acc_up[...] - bent) * slope, (acc_down[...] - bent) * slope)
            if heun:
                total = total + 0.5 * base_readers[i](j)
            y = jnp.maximum(cost_readers[i](j), total)
            out_rows[i][j] = y
            return y

        def finish(i, j, y, most_3):
            edge_ref[i, pl.ds(j, 1), :] = out_rows[i][j, pl.ds(send_at, 1), :]
            inner_ref[i, pl.ds(j, 1), :] = out_rows[i][j, pl.ds(inner_at, 1), :]
            wall = jnp.abs(out_rows[i][j, pl.ds(next_at, 1), :] - out_rows[i][j, pl.ds(wall_at, 1), :])
            bend = jnp.where(vy_row >= 2, jnp.abs(y - pltpu.roll(y, 2, 0)), 0.0)
            return jnp.maximum(most_3, jnp.maximum(fold(bend), wall))

        zero = jnp.zeros((8, width), jnp.float32)
        most_2, most_3 = zero, zero
        least = [jnp.full((8, width), jnp.inf, jnp.float32) for _ in targets]
        for i in range(count):
            y = tile(i, 0, None, 1)
            first_ref[i] = y
            most_3 = finish(i, 0, y, most_3)
            least[i] = jnp.minimum(least[i], fold_min(y))
            y = tile(i, 1, 0, 2)
            second_ref[i] = y
            most_3 = finish(i, 1, y, most_3)
            least[i] = jnp.minimum(least[i], fold_min(y))

        def step(j, carry):
            most_2, most_3, least = carry
            least = list(least)
            for i in range(count):
                y = tile(i, j, j - 1, j + 1)
                most_3 = finish(i, j, y, most_3)
                most_2 = jnp.maximum(most_2, fold(jnp.abs(y - out_rows[i][j - 2])))
                if with_min:
                    least[i] = jnp.minimum(least[i], fold_min(y))
            return most_2, most_3, tuple(least)

        most_2, most_3, least = lax.fori_loop(2, cells_v - 1, step, (most_2, most_3, tuple(least)))
        least = list(least)
        for i in range(count):
            before_ref[i] = out_rows[i][cells_v - 2]
            y = tile(i, cells_v - 1, cells_v - 2, None)
            last_ref[i] = y
            most_3 = finish(i, cells_v - 1, y, most_3)
            most_2 = jnp.maximum(most_2, fold(jnp.abs(y - out_rows[i][cells_v - 3])))
            least[i] = jnp.minimum(least[i], fold_min(y))
        part_ref[0] = most_2
        part_ref[1] = most_3
        if with_min:
            for i in range(count):
                min_ref[pl.ds(i, 1), :] = jnp.min(least[i], axis=0, keepdims=True)

    def f32(*shape):
        return jax.ShapeDtypeStruct(shape, jnp.float32)

    shapes = [f32(cells_v, half, width)] * count + [f32(count, half, width)] * 4 + [f32(count, cells_v, width)] * 2 + [f32(2, 8, width)]
    if with_min:
        shapes.append(f32(count, width))
    cells = count * cells_v * half * width
    result = pl.pallas_call(
        body,
        out_shape=shapes,
        in_specs=[scalars()] * 3 + [whole()] * n_in,
        out_specs=[whole()] * len(shapes),
        scratch_shapes=[pltpu.VMEM((half, width), jnp.float32)] * 4,
        compiler_params=compiler_params(),
        cost_estimate=pl.CostEstimate(flops=60 * cells, bytes_accessed=16 * cells, transcendentals=0),
        name="sweep_" + "".join(str(t) for t in targets),
    )(flags, push, speed, *arrays)
    return result


def spread(shape, lanes):
    position = lax.broadcasted_iota(jnp.int32, shape, 1)
    out = jnp.zeros(shape, jnp.float32)
    for lane, value in enumerate(lanes):
        out = jnp.where(position == lane, value, out)
    return out


def first_maxima(devices, value, vx_low, vx_high, accel_first, accel_second, flags):
    rows, cells_v, total_vy, width = value.shape

    def body(flags_ref, v_ref, low_ref, high_ref, first_ref, second_ref, out_ref):
        vx_first, vx_last = flags_ref[3], flags_ref[4]
        vy_row = lax.broadcasted_iota(jnp.int32, (total_vy, width), 0)

        def of_vy(x):
            inner = jnp.where(vy_row >= 2, jnp.abs(x - pltpu.roll(x, 2, 0)), 0.0)
            wall = jnp.maximum(jnp.abs(x[1:2] - x[0:1]), jnp.abs(x[total_vy - 1 : total_vy] - x[total_vy - 2 : total_vy - 1]))
            return jnp.maximum(fold(inner), wall)

        most_2 = jnp.zeros((8, width), jnp.float32)
        most_3 = jnp.zeros((8, width), jnp.float32)
        for r in range(rows):
            x = v_ref[r, 0]
            most_3 = jnp.maximum(most_3, of_vy(x))
            most_2 = jnp.maximum(most_2, fold(jnp.abs(v_ref[r, 1] - jnp.where(vx_first == 1, x, low_ref[r]))))
            x = v_ref[r, cells_v - 1]
            most_3 = jnp.maximum(most_3, of_vy(x))
            most_2 = jnp.maximum(most_2, fold(jnp.abs(v_ref[r, cells_v - 2] - jnp.where(vx_last == 1, x, high_ref[r]))))

            def step(j, carry, r=r):
                most_2, most_3 = carry
                most_3 = jnp.maximum(most_3, of_vy(v_ref[r, j]))
                most_2 = jnp.maximum(most_2, fold(jnp.abs(v_ref[r, j + 1] - v_ref[r, j - 1])))
                return most_2, most_3

            most_2, most_3 = lax.fori_loop(1, cells_v - 1, step, (most_2, most_3))
        values = (jnp.max(most_2), jnp.max(most_3), jnp.max(jnp.abs(first_ref[...])), jnp.max(jnp.abs(second_ref[...])))
        out_ref[...] = spread((devices, LANES), values)

    return pl.pallas_call(
        body,
        out_shape=jax.ShapeDtypeStruct((devices, LANES), jnp.float32),
        in_specs=[scalars()] + [whole()] * 5,
        out_specs=whole(),
        compiler_params=compiler_params(),
        name="first_maxima",
    )(flags, value, vx_low, vx_high, accel_first, accel_second)


def edge_maxima(devices, parts, edges, vx_low, vx_high, inner, vy_next, flags):
    first, second, before, last = edges
    n_parts = len(parts)

    def body(flags_ref, first_ref, second_ref, before_ref, last_ref, low_ref, high_ref, inner_ref, next_ref, *rest):
        part_refs, out_ref = rest[:n_parts], rest[n_parts]
        vx_first, vx_last = flags_ref[3], flags_ref[4]
        most_2 = functools.reduce(jnp.maximum, [p[0] for p in part_refs])
        most_3 = functools.reduce(jnp.maximum, [p[1] for p in part_refs])
        for t in range(4):
            low = jnp.where(vx_first == 1, first_ref[t], low_ref[t])
            high = jnp.where(vx_last == 1, last_ref[t], high_ref[t])
            most_2 = jnp.maximum(most_2, fold(jnp.abs(second_ref[t] - low)))
            most_2 = jnp.maximum(most_2, fold(jnp.abs(high - before_ref[t])))
            most_3 = jnp.maximum(most_3, fold(jnp.abs(inner_ref[t] - next_ref[3 - t])))
        out_ref[...] = spread((devices, LANES), (jnp.max(most_2), jnp.max(most_3)))

    return pl.pallas_call(
        body,
        out_shape=jax.ShapeDtypeStruct((devices, LANES), jnp.float32),
        in_specs=[scalars()] + [whole()] * (8 + n_parts),
        out_specs=whole(),
        compiler_params=compiler_params(),
        name="edge_maxima",
    )(flags, first, second, before, last, vx_low, vx_high, inner, vy_next, *parts)


def assemble(parity, own, received, shape):
    rows, cells_v, total_vy, width = shape
    half = total_vy // 2
    block = 8 if cells_v % 8 == 0 else cells_v

    def body(parity_ref, own_outer, own_inner, got_outer, got_inner, out_ref):
        parity = parity_ref[0]
        mine = pl.multiple_of(parity * half, half)
        other = pl.multiple_of((1 - parity) * half, half)
        out_ref[parity, :, pl.ds(mine, half), :] = own_outer[...]
        out_ref[1 - parity, :, pl.ds(mine, half), :] = own_inner[...]
        out_ref[parity, :, pl.ds(other, half), :] = got_outer[...]
        out_ref[1 - parity, :, pl.ds(other, half), :] = got_inner[...]

    part = pl.BlockSpec((block, half, width), lambda j: (j, 0, 0))
    return pl.pallas_call(
        body,
        grid=(cells_v // block,),
        out_shape=jax.ShapeDtypeStruct(shape, jnp.float32),
        in_specs=[scalars()] + [part] * 4,
        out_specs=pl.BlockSpec((rows, block, total_vy, width), lambda j: (0, j, 0, 0)),
        compiler_params=compiler_params(),
        name="assemble",
    )(parity, *own, *received)


def per_device(value, cost, accel_first, accel_second):
    n_px, n_vx = lax.axis_size("px"), lax.axis_size("vx")
    devices = n_px * n_vx
    rows, cells_v, total_vy, width = value.shape
    half = total_vy // 2
    total_vx = cells_v * n_vx
    sizes = (cells_v, half, width, total_vx, total_vy)
    px, vx = lax.axis_index("px"), lax.axis_index("vx")
    parity = px % 2
    flags = jnp.stack(
        [
            parity,
            ((px == 0) | (px == n_px - 1)).astype(jnp.int32),
            ((px == 1) | (px == n_px - 2)).astype(jnp.int32),
            (vx == 0).astype(jnp.int32),
            (vx == n_vx - 1).astype(jnp.int32),
        ]
    ).astype(jnp.int32)

    def partner(x):
        return lax.ppermute(x, "px", [(i, i ^ 1) for i in range(n_px)])

    def from_low_vx(x):
        return lax.ppermute(x, "vx", [(i, i + 1) for i in range(n_vx - 1)])

    def from_high_vx(x):
        return lax.ppermute(x, "vx", [(i + 1, i) for i in range(n_vx - 1)])

    def halo_before(outermost):
        moves = [(i, i + 2) for i in range(0, n_px - 2, 2)] + [(i, i - 2) for i in range(3, n_px, 2)]
        return lax.ppermute(outermost, "px", moves)

    def halo_after(outer):
        moves = [(i, i - 2) for i in range(2, n_px, 2)] + [(i, i + 2) for i in range(1, n_px - 2, 2)]
        return lax.ppermute(outer, "px", moves)

    def share(maxima):
        return lax.all_to_all(maxima, ("px", "vx"), 0, 0, tiled=True)

    def half_of(array, row, which):
        return lax.dynamic_slice(array, (row, 0, which * half, 0), (1, cells_v, half, width))[0]

    value_outer_got = partner(half_of(value, parity, 1 - parity))
    value_inner_got = partner(half_of(value, 1 - parity, 1 - parity))
    cost_send = (half_of(cost, parity, 1 - parity), half_of(cost, 1 - parity, 1 - parity))

    low_own = from_low_vx(value[:, cells_v - 1])
    high_own = from_high_vx(value[:, 0])
    shared_first = share(first_maxima(devices, value, low_own, high_own, accel_first, accel_second, flags))

    def chain_halo(own):
        given = lax.dynamic_slice(own, (0, (1 - parity) * half, 0), (rows, half, width))
        mine = lax.dynamic_slice(own, (0, parity * half, 0), (rows, half, width))
        return mine, given

    low_mine, low_given = chain_halo(low_own)
    high_mine, high_given = chain_halo(high_own)
    got = partner(jnp.concatenate([low_given, high_given], axis=0))
    row_given = lax.dynamic_slice(value, (0, 0, half - parity, 0), (rows, cells_v, 1, width))[:, :, 0]
    row_needed = lax.dynamic_slice(value, (0, 0, half - parity, 0), (rows, cells_v, 1, width))[:, :, 0]
    row_given = lax.dynamic_slice(value, (0, 0, half - 1 + parity, 0), (rows, cells_v, 1, width))[:, :, 0]
    row_got = partner(row_given)
    push_got = partner(accel_first)

    def pick(x, which):
        return lax.dynamic_index_in_dim(x, which, 0, keepdims=True)

    def in_chain(mine, others):
        return jnp.concatenate([pick(mine, parity), pick(mine, 1 - parity), pick(others, parity), pick(others, 1 - parity)], axis=0)

    vx_low = in_chain(low_mine, got[:rows])
    vx_high = in_chain(high_mine, got[rows:])
    vy_next = jnp.concatenate([pick(row_got, 1 - parity), pick(row_got, parity), pick(row_needed, 1 - parity), pick(row_needed, parity)], axis=0)
    push = in_chain(accel_first, push_got)
    positions = (vx * cells_v + jnp.arange(cells_v, dtype=jnp.int32)).astype(jnp.float32)
    speed = (2.0 * positions + 1.0 - total_vx) * (VELOCITY_LIMIT / total_vx)
    speed = jnp.where(parity == 0, speed, -speed)

    chain = [Own(value, True), Own(value, False), Row(value_inner_got), Row(value_outer_got)]
    halo_rows = (halo_before(value_outer_got), halo_after(half_of(value, parity, parity)))
    cost_send, _ = lax.optimization_barrier((cost_send, (value_outer_got, value_inner_got)))
    cost_outer_got = partner(cost_send[0])
    cost_inner_got = partner(cost_send[1])
    costs = [Own(cost, True), Own(cost, False), Row(cost_inner_got), Row(cost_outer_got)]

    run = functools.partial(sweep, sizes, accel_second=accel_second, flags=flags, push=push, speed=speed)

    def exchange(outs):
        fields, (first, second, before, last, edge, inner, part) = outs[:4], outs[4:11]
        new_halo = (halo_before(fields[3]), halo_after(fields[0]))
        low, high, row = from_low_vx(last), from_high_vx(first), partner(edge)
        shared = share(edge_maxima(devices, [part], (first, second, before, last), low, high, inner, row, flags))
        return [Row(f) for f in fields], new_halo, low, high, row, shared

    def sub(targets, **kw):
        return run(targets, chain, [costs[t] for t in targets], None, halo_rows, vx_low, vx_high, vy_next, (shared_first,) * 3)

    own_out = sub((0, 1))
    outer_out = sub((3,))
    inner_out = sub((2,))
    joined = [jnp.concatenate([a, b, c], axis=0) for a, b, c in zip(own_out[2:8], inner_out[1:7], outer_out[1:7])]
    first, second, before, last, edge, inner = joined
    fields = [own_out[0], own_out[1], inner_out[0], outer_out[0]]
    halo_rows = (halo_before(fields[3]), halo_after(fields[0]))
    vx_low, vx_high, vy_next = from_low_vx(last), from_high_vx(first), partner(edge)
    shared = share(
        edge_maxima(devices, [own_out[8], inner_out[7], outer_out[7]], (first, second, before, last), vx_low, vx_high, inner, vy_next, flags)
    )
    middle = [Row(f) for f in fields]

    every = (0, 1, 2, 3)
    outs = run(every, middle, costs, chain, halo_rows, vx_low, vx_high, vy_next, (shared_first, shared_first, shared))
    chain, halo_rows, vx_low, vx_high, vy_next, shared_second = exchange(outs)
    outs = run(every, chain, costs, None, halo_rows, vx_low, vx_high, vy_next, (shared_first, shared_second, shared_second))
    middle, halo_rows, vx_low, vx_high, vy_next, shared = exchange(outs)
    outs = run(every, middle, costs, chain, halo_rows, vx_low, vx_high, vy_next, (shared_first, shared_second, shared), with_min=True)

    fields, least = outs[:4], outs[-1]
    least_got = partner(least[2:])
    outer_got = partner(fields[3])
    inner_got = partner(fields[2])
    final = assemble(flags[:1], (fields[0], fields[1]), (outer_got, inner_got), value.shape)
    funnel = jnp.minimum(least[:2], least_got[::-1])
    funnel = jnp.concatenate([pick(funnel, parity), pick(funnel, 1 - parity)], axis=0)
    return final, lax.pmin(funnel, "vx")


def solution(mesh):
    placed = (P("px", "vx", None, None), P("px", "vx", None, None), P("px", "vx"), P())
    return jax.shard_map(
        per_device,
        mesh=mesh,
        in_specs=placed,
        out_specs=(P("px", "vx", None, None), P("px", None)),
        check_vma=False,
    )
```

time: 820 us -> 380 us (0.46)
  waiting for transfers between devices: 407 us -> 134 us
  other arithmetic: 157 us -> 15.4 us
  blocking collectives: 192 us -> 56.3 us
  Pallas kernels: 0 us -> 91.9 us
  starting transfers between devices: 34.8 us -> 53 us
  local copies, waits for them, and re-layouts: 14.1 us -> 26.9 us
    ppermute x16 -> x29, waiting for transfers between devices: 407 us -> 134 us  [the longest x13 133 us: partner(): return lax.ppermute(x, 'px', [(i, i ^ 1) for i in range(n_px)])]
    pmax x4 -> x0, blocking collectives: 184 us -> none  [bound_speeds(): lax.pmax((jnp.max(jnp.abs(gradient_vx)), jnp.max(jnp.abs(gradient_vy))),...]
    pallas_call x0 -> x10, Pallas kernels: none -> 91.9 us  [the longest x5 75.2 us: sweep(): pl.pallas_call(body, out_shape=shapes, in_specs=[scalars()] * 3 + [whole(...]
    max x3 -> x0, other arithmetic: 74.1 us -> none  [the longest x2 48.8 us: per_device(): middle = jnp.maximum(cost_field, center + step_size * change)]
    all_to_all x0 -> x3, blocking collectives: none -> 49.8 us  [share(): return lax.all_to_all(maxima, ('px', 'vx'), 0, 0, tiled=True)]
    select_n x8 -> x1, other arithmetic: 29.7 us -> 0.49 us  [per_device(): speed = jnp.where(parity == 0, speed, -speed)]
    reduce_min x1 -> x0, other arithmetic: 26.4 us -> none  [per_device(): funnel_local = jnp.min(current, axis=(1, 2))]
    reduce_max x4 -> x0, other arithmetic: 18.6 us -> none  [bound_speeds(): jnp.max(jnp.abs(gradient_vx))]
  transfers between devices with their start and end apart: 16 -> 30, of which waited for: 8 -> 7; matrix products, arithmetic and copies ran while one was open for 0% -> 9% of each run, Pallas kernels for 0% -> 8%
where the time goes in v1:
time: 380 us; the launch traced here: 379 us
  waiting for transfers between devices  134 us (35%)
  Pallas kernels  91.9 us (24%)
  blocking collectives  56.3 us (15%)
  starting transfers between devices  53 us (14%)
  local copies, waits for them, and re-layouts  26.9 us (7%)
  other arithmetic  15.4 us (4%)
    ppermute x13, waiting for transfers between devices, partner(): return lax.ppermute(x, 'px', [(i, i ^ 1) for i in range(n_px)])  133 us
    pallas_call x5, Pallas kernels, sweep(): pl.pallas_call(body, out_shape=shapes, in_specs=[scalars()] * 3 + [whole(...  75.2 us
    all_to_all x3, blocking collectives, share(): return lax.all_to_all(maxima, ('px', 'vx'), 0, 0, tiled=True)  49.8 us
    ppermute x4, starting transfers between devices, halo_before(): return lax.ppermute(outermost, 'px', moves)  18.5 us
    ppermute x13, starting transfers between devices, partner(): return lax.ppermute(x, 'px', [(i, i ^ 1) for i in range(n_px)])  14.4 us
    unnamed x84, local copies, waits for them, and re-layouts  9.04 us
  transfers between devices with their start and end apart: 30, of which 7 were waited for; matrix products, arithmetic and copies ran while one was open for 9% of the time, Pallas kernels for 8%

profile of v1, /device:TPU:0, one launch (start us, length us, event | category | flops | bytes accessed | tf_op | source)
XLA Modules:
  0.0 378.9 jit_solution(2261807924240727446)
XLA Ops:
  0.6 3.0 collective-permute-start
  3.6 1.1 constant_dynamic-slice_fusion.6
  5.4 3.3 dynamic-slice_bitcast_fusion
  8.7 2.0 collective-permute-start.2
  10.7 1.8 slice_bitcast_fusion.1
  12.6 2.0 collective-permute-start.4
  15.0 1.1 constant_dynamic-slice_fusion.3
  16.1 3.2 dynamic-slice_bitcast_fusion.1
  20.7 1.3 collective-permute-start.5
  22.6 15.1 %collective-permute-done.2.refs_1_.refs_11_ = f32[24,32,384]{2,1,0:T(8,128)} collective-permute-done((f32[24,32,384]{2,1,0:T(8,128)S(1)}, f32[24,32,384]{2,1,0:T(8,128)}, u32[]{:S(2)}, u32[]{:S(2)}) %collective-permute-start.2) | collective-permute-done | bytes 1179680 | tf_op jit(solution)/shard_map/ppermute | solution.py:394
  37.7 1.3 collective-permute-start.9
  39.0 22.4 %collective-permute-done.1.refs_1_.refs_0_.refs_10_ = f32[24,32,384]{2,1,0:T(8,128)S(1)} collective-permute-done((f32[24,32,384]{2,1,0:T(8,128)S(1)}, f32[24,32,384]{2,1,0:T(8,128)S(1)}, u32[]{:S(2)}, u32[]{:S(2)}) %collective-permute-start.1) | collective-permute-done | bytes 1179680 | tf_op jit(solution)/shard_map/ppermute | solution.py:394
  61.4 1.7 collective-permute-start.10
  63.1 4.5 %collective-permute-start.3 = (f32[24,32,384]{2,1,0:T(8,128)}, f32[24,32,384]{2,1,0:T(8,128)}, u32[]{:S(2)}, u32[]{:S(2)}) collective-permute-start(f32[24,32,384]{2,1,0:T(8,128)} %collective-permute-done.2.refs_1_.refs_11_), channel_id=1, source_target_pairs={{0,8},{8,16},{16,24},{12,4},{20,12},{28,20},{1,9},{9,17},{17,25},{... | collective-permute-start | bytes 3538952 | tf_op jit(solution)/shard_map/ppermute | solution.py:404
  67.6 0.8 constant_dynamic-slice_fusion.5
  68.4 0.9 constant_dynamic-slice_fusion.14
  69.4 0.7 pad_maximum_fusion
  70.1 2.0 collective-permute-start.6
  72.1 1.5 pad_maximum_fusion.5.refs_6_
  73.6 4.8 %first_maxima.1 = f32[32,128]{1,0:T(8,128)} custom-call(s32[5]{0:T(128)} %stack.39.flags_ref, f32[2,24,64,384]{3,2,1,0:T(8,128)} %refs_9_.1, f32[2,64,384]{2,1,0:T(8,128)} %collective-permute-done.4.low_ref, f32[2,64,384]{2,1,0:T(8,128)} %copy-done.20, f32[2,24]{1,0:T(2,128)} %first_ref.1, f32[64,384]{1,0:T(8,128)} %refs_16_.1), custom_call_target="tpu_custom_call" | custom-call | tf_op jit(solution)/shard_map/first_maxima/pallas_call | solution.py:311
  78.3 3.8 all-to-all-start
  82.1 1.0 constant_dynamic-slice_fusion.10
  83.1 34.9 %collective-permute-done.6 = f32[4,32,384]{2,1,0:T(8,128)} collective-permute-done((f32[4,32,384]{2,1,0:T(8,128)}, f32[4,32,384]{2,1,0:T(8,128)}, u32[]{:S(2)}, u32[]{:S(2)}) %collective-permute-start.6) | collective-permute-done | bytes 196640 | tf_op jit(solution)/shard_map/ppermute | solution.py:394
  118.0 1.0 fusion.9
  121.4 6.9 %sweep_3.1 = (f32[24,32,384]{2,1,0:T(8,128)}, f32[1,32,384]{2,1,0:T(8,128)}, f32[1,32,384]{2,1,0:T(8,128)}, f32[1,32,384]{2,1,0:T(8,128)}, f32[1,32,384]{2,1,0:T...) custom-call(s32[5]{0:T(128)} %stack.39.flags_ref, ...), custom_call_target="tpu_custom_call" | custom-call | flops 17694720 | bytes 4718592 | tf_op jit(solution)/shard_map/sweep_3/pallas_call | solution.py:258
  128.4 4.7 %collective-permute-start.11 = (f32[24,32,384]{2,1,0:T(8,128)}, f32[24,32,384]{2,1,0:T(8,128)}, u32[]{:S(2)}, u32[]{:S(2)}) collective-permute-start(f32[24,32,384]{2,1,0:T(8,128)} %get-tuple-element.61.refs_3_), channel_id=1, source_target_pairs={{0,8},{8,16},{16,24},{12,4},{20,12},{28,20},{1,9},{9,17},{17,25},{... | collective-permute-start | bytes 3538952 | tf_op jit(solution)/shard_map/ppermute | solution.py:404
  133.2 11.4 %sweep_01.1 = (f32[24,32,384]{2,1,0:T(8,128)}, f32[24,32,384]{2,1,0:T(8,128)}, f32[2,32,384]{2,1,0:T(8,128)}, f32[2,32,384]{2,1,0:T(8,128)}, f32[2,32,384]{2,1,0...) custom-call(s32[5]{0:T(128)} %stack.39.flags_ref, ...), custom_call_target="tpu_custom_call" | custom-call | flops 35389440 | bytes 9437184 | tf_op jit(solution)/shard_map/sweep_01/pallas_call | solution.py:258
  144.6 1.3 collective-permute-start.12
  145.9 0.9 constant_dynamic-update-slice_fusion.2
  147.0 6.2 %sweep_2.1 = (f32[4,32,384]{2,1,0:T(8,128)S(1)}, f32[24,32,384]{2,1,0:T(8,128)}, f32[1,32,384]{2,1,0:T(8,128)S(1)}, f32[1,24,384]{2,1,0:T(8,128)S(1)}, f32[1,32,...) fusion(f32[4,32,384]{2,1,0:T(8,128)S(1)} %constant_dynamic-update-slice_fus, ...), kind=kCustom, calls=%fused_computation.19 | custom fusion | flops 17694720 | bytes 10390528 | tf_op jit(solution)/shard_map/sweep_2/pallas_call | solution.py:258
  153.2 0.9 pad_maximum_fusion.6
  154.1 2.5 collective-permute-start.15
  156.6 0.8 constant_dynamic-update-slice_fusion.last_ref
  157.4 1.3 collective-permute-start.13
  158.7 0.8 constant_dynamic-update-slice_fusion.3.first_ref
  159.5 1.3 collective-permute-start.14
  160.8 1.6 pad_maximum_fusion.3.second_ref
  163.8 0.8 collective-permute-done.14.high_ref.refs_13_
  165.3 2.2 edge_maxima.3
  167.5 15.2 %all_to_all.44 = f32[32,1,128]{2,1,0:T(1,128)} all-to-all(f32[32,1,128]{2,1,0:T(1,128)} %bitcast.58), channel_id=1, replica_groups=mesh['px'=8,'vx'=4] {'px','vx'}, dimensions={0} | all-to-all | bytes 32768 | tf_op jit(solution)/shard_map/all_to_all | solution.py:411
  182.7 19.8 %sweep_0123.3 = (f32[24,32,384]{2,1,0:T(8,128)}, f32[24,32,384]{2,1,0:T(8,128)}, f32[24,32,384]{2,1,0:T(8,128)}, f32[24,32,384]{2,1,0:T(8,128)}, f32[4,32,384]{2...) custom-call(s32[5]{0:T(128)} %stack.39.flags_ref, ...), custom_call_target="tpu_custom_call" | custom-call | flops 70778880 | bytes 18874368 | tf_op jit(solution)/shard_map/sweep_0123/pallas_call | solution.py:258
  202.5 1.3 collective-permute-start.17
  203.8 4.6 %collective-permute-start.16 = (f32[24,32,384]{2,1,0:T(8,128)}, f32[24,32,384]{2,1,0:T(8,128)S(1)}, u32[]{:S(2)}, u32[]{:S(2)}) collective-permute-start(f32[24,32,384]{2,1,0:T(8,128)} %get-tuple-element.86.refs_3_.refs_12_), channel_id=1, source_target_pairs={{0,8},{8,16},{16,24},{12,4},{20,12},{28,20},{1,9},{9,17},{17,25},{... | collective-permute-start | bytes 3538952 | tf_op jit(solution)/shard_map/ppermute | solution.py:404
  208.5 1.4 collective-permute-start.18
  209.9 1.3 collective-permute-start.19
  211.2 6.0 %collective-permute-done.20.next_ref.refs_11_ = f32[4,24,384]{2,1,0:T(8,128)S(1)} collective-permute-done((f32[4,24,384]{2,1,0:T(8,128)}, f32[4,24,384]{2,1,0:T(8,128)S(1)}, u32[]{:S(2)}, u32[]{:S(2)}) %collective-permute-start.20) | collective-permute-done | bytes 147488 | tf_op jit(solution)/shard_map/ppermute | solution.py:394
  218.1 2.2 edge_maxima.4
  220.3 14.8 %all_to_all.45 = f32[32,1,128]{2,1,0:T(1,128)} all-to-all(f32[32,1,128]{2,1,0:T(1,128)} %bitcast.59), channel_id=1, replica_groups=mesh['px'=8,'vx'=4] {'px','vx'}, dimensions={0} | all-to-all | bytes 32768 | tf_op jit(solution)/shard_map/all_to_all | solution.py:411
  235.1 1.0 copy-done.8
  236.5 17.7 %sweep_0123.4 = (f32[24,32,384]{2,1,0:T(8,128)}, f32[24,32,384]{2,1,0:T(8,128)}, f32[24,32,384]{2,1,0:T(8,128)}, f32[24,32,384]{2,1,0:T(8,128)}, f32[4,32,384]{2...) custom-call(s32[5]{0:T(128)} %stack.39.flags_ref, ...), custom_call_target="tpu_custom_call" | custom-call | flops 70778880 | bytes 18874368 | tf_op jit(solution)/shard_map/sweep_0123/pallas_call | solution.py:258
  254.2 1.3 collective-permute-start.22
  255.5 4.6 %collective-permute-start.21 = (f32[24,32,384]{2,1,0:T(8,128)}, f32[24,32,384]{2,1,0:T(8,128)S(1)}, u32[]{:S(2)}, u32[]{:S(2)}) collective-permute-start(f32[24,32,384]{2,1,0:T(8,128)} %get-tuple-element.97.refs_3_), channel_id=1, source_target_pairs={{0,8},{8,16},{16,24},{12,4},{20,12},{28,20},{1,9},{9,17},{17,25},{... | collective-permute-start | bytes 3538952 | tf_op jit(solution)/shard_map/ppermute | solution.py:404
  260.1 1.3 collective-permute-start.23
  261.4 1.3 collective-permute-start.24
  263.2 4.9 %collective-permute-done.25.next_ref.refs_15_ = f32[4,24,384]{2,1,0:T(8,128)S(1)} collective-permute-done((f32[4,24,384]{2,1,0:T(8,128)}, f32[4,24,384]{2,1,0:T(8,128)S(1)}, u32[]{:S(2)}, u32[]{:S(2)}) %collective-permute-start.25) | collective-permute-done | bytes 147488 | tf_op jit(solution)/shard_map/ppermute | solution.py:394
  268.9 2.2 edge_maxima.5
  271.2 19.8 %all_to_all.46 = f32[32,1,128]{2,1,0:T(1,128)} all-to-all(f32[32,1,128]{2,1,0:T(1,128)} %bitcast.60), channel_id=1, replica_groups=mesh['px'=8,'vx'=4] {'px','vx'}, dimensions={0} | all-to-all | bytes 32768 | tf_op jit(solution)/shard_map/all_to_all | solution.py:411
  291.0 1.0 copy-done.12
  292.4 19.3 %sweep_0123.5 = (f32[24,32,384]{2,1,0:T(8,128)}, f32[24,32,384]{2,1,0:T(8,128)}, f32[24,32,384]{2,1,0:T(8,128)}, f32[24,32,384]{2,1,0:T(8,128)}, f32[4,32,384]{2...) custom-call(s32[5]{0:T(128)} %stack.39.flags_ref, ...), custom_call_target="tpu_custom_call" | custom-call | flops 70778880 | bytes 18874368 | tf_op jit(solution)/shard_map/sweep_0123/pallas_call | solution.py:258
  312.2 1.6 collective-permute-start.27
  315.0 50.0 %collective-permute-done.28 = f32[2,384]{1,0:T(2,128)S(1)} collective-permute-done((f32[2,384]{1,0:T(2,128)S(1)}, f32[2,384]{1,0:T(2,128)S(1)}, u32[]{:S(2)}, u32[]{:S(2)}) %collective-permute-start.28) | collective-permute-done | bytes 3104 | tf_op jit(solution)/shard_map/ppermute | solution.py:394
  365.7 6.5 %pmin.7 = f32[2,384]{1,0:T(2,128)} all-reduce(f32[2,384]{1,0:T(2,128)S(1)} %pad_maximum_fusion.8), channel_id=1, replica_groups=mesh['px'=8,'vx'=4] {'vx'}, use_global_device_ids=true, to_apply=%region_0.1 | all-reduce | flops 768 | bytes 6144 | tf_op jit(solution)/shard_map/pmin | solution.py:498
  372.3 1.0 copy-done.10
  373.6 5.3 %assemble.1 = f32[2,24,64,384]{3,2,1,0:T(8,128)} custom-call(s32[1]{0:T(128)} %bitcast.parity_ref, f32[24,32,384]{2,1,0:T(8,128)} %get-tuple-element.105.own_outer, f32[24,32,384]{2,1,0:T(8,128)} %get-tuple-element.106.own_inner, f32[24,32,384]{2,1,0:T(8,128)} %copy-done.10, f32[24,32,384]{2,1,0:T(8,128)} %copy-done.11), custom_call_target="tpu_custom_call" | custom-call | tf_op jit(solution)/shard_map/assemble/pallas_call | solution.py:363
  (128 shorter events, 13.5 us)
Async XLA Ops:
  0.6 20.0 %collective-permute-start = (f32[2,24]{1,0:T(2,128)}, f32[2,24]{1,0:T(2,128)S(1)}, u32[]{:S(2)}, u32[]{:S(2)}) collective-permute-start(f32[2,24]{1,0:T(2,128)} %first_ref.1), channel_id=1, source_target_pairs={{0,4},{4,0},{8,12},{12,8},{16,20},{20,16},{24,28},{28,24},{1,5},{5... | collective-permute-start | bytes 584 | tf_op jit(solution)/shard_map/ppermute | solution.py:394
  5.4 57.7 %collective-permute-start.7 = (f32[2,24,384]{2,1,0:T(8,128)}, f32[2,24,384]{2,1,0:T(8,128)}, u32[]{:S(2)}, u32[]{:S(2)}) collective-permute-start(f32[2,24,384]{2,1,0:T(8,128)} %bitcast.45), channel_id=1, source_target_pairs={{0,4},{4,0},{8,12},{12,8},{16,20},{20,16},{24,28},{28,24},{1,5},{5... | collective-permute-start | bytes 221192 | tf_op jit(solution)/shard_map/ppermute | solution.py:394
  5.4 9.6 %copy-start.37 = (f32[2,24]{1,0:T(2,128)S(1)}, f32[2,24]{1,0:T(2,128)}, u32[]{:S(2)}) copy-start(f32[2,24]{1,0:T(2,128)} %first_ref.1) | copy-start | bytes 580
  8.7 29.0 %collective-permute-start.2 = (f32[24,32,384]{2,1,0:T(8,128)S(1)}, f32[24,32,384]{2,1,0:T(8,128)}, u32[]{:S(2)}, u32[]{:S(2)}) collective-permute-start(f32[24,32,384]{2,1,0:T(8,128)S(1)} %get-tuple-element.127), channel_id=1, source_target_pairs={{0,4},{4,0},{8,12},{12,8},{16,20},{20,16},{24,28},{28,24},{1,5},{5... | collective-permute-start | bytes 3538952 | tf_op jit(solution)/shard_map/ppermute | solution.py:394
  10.7 50.7 %collective-permute-start.1 = (f32[24,32,384]{2,1,0:T(8,128)S(1)}, f32[24,32,384]{2,1,0:T(8,128)S(1)}, u32[]{:S(2)}, u32[]{:S(2)}) collective-permute-start(f32[24,32,384]{2,1,0:T(8,128)S(1)} %get-tuple-element.128), channel_id=1, source_target_pairs={{0,4},{4,0},{8,12},{12,8},{16,20},{20,16},{24,28},{28,24},{1,5},{5... | collective-permute-start | bytes 3538952 | tf_op jit(solution)/shard_map/ppermute | solution.py:394
  12.6 55.9 %collective-permute-start.4 = (f32[2,64,384]{2,1,0:T(8,128)}, f32[2,64,384]{2,1,0:T(8,128)}, u32[]{:S(2)}, u32[]{:S(2)}) collective-permute-start(f32[2,64,384]{2,1,0:T(8,128)} %get-tuple-element.133), channel_id=1, source_target_pairs={{0,1},{1,2},{2,3},{4,5},{5,6},{6,7},{8,9},{9,10},{10,11},{12,13},{... | collective-permute-start | bytes 589832 | tf_op jit(solution)/shard_map/ppermute | solution.py:397
  20.7 48.7 %collective-permute-start.5 = (f32[2,64,384]{2,1,0:T(8,128)}, f32[2,64,384]{2,1,0:T(8,128)S(1)}, u32[]{:S(2)}, u32[]{:S(2)}) collective-permute-start(f32[2,64,384]{2,1,0:T(8,128)} %get-tuple-element.134), channel_id=1, source_target_pairs={{1,0},{2,1},{3,2},{5,4},{6,5},{7,6},{9,8},{10,9},{11,10},{13,12},{... | collective-permute-start | bytes 589832 | tf_op jit(solution)/shard_map/ppermute | solution.py:400
  37.7 82.7 %collective-permute-start.9 = (f32[24,32,384]{2,1,0:T(8,128)}, f32[24,32,384]{2,1,0:T(8,128)}, u32[]{:S(2)}, u32[]{:S(2)}) collective-permute-start(f32[24,32,384]{2,1,0:T(8,128)} %get-tuple-element.126), channel_id=1, source_target_pairs={{8,0},{16,8},{24,16},{4,12},{12,20},{20,28},{9,1},{17,9},{25,17},{... | collective-permute-start | bytes 3538952 | tf_op jit(solution)/shard_map/ppermute | solution.py:408
  61.4 17.0 %copy-start = (f32[24,32,384]{2,1,0:T(8,128)}, f32[24,32,384]{2,1,0:T(8,128)S(1)}, u32[]{:S(2)}) copy-start(f32[24,32,384]{2,1,0:T(8,128)S(1)} %collective-permute-done.1.refs_1_.refs_0_.refs_10_) | copy-start | bytes 3538948
  61.4 59.0 %collective-permute-start.10 = (f32[24,32,384]{2,1,0:T(8,128)}, f32[24,32,384]{2,1,0:T(8,128)S(1)}, u32[]{:S(2)}, u32[]{:S(2)}) collective-permute-start(f32[24,32,384]{2,1,0:T(8,128)} %get-tuple-element.60), channel_id=1, source_target_pairs={{0,4},{4,0},{8,12},{12,8},{16,20},{20,16},{24,28},{28,24},{1,5},{5... | collective-permute-start | bytes 3538952 | tf_op jit(solution)/shard_map/ppermute | solution.py:394
  63.1 70.1 %collective-permute-start.3 = (f32[24,32,384]{2,1,0:T(8,128)}, f32[24,32,384]{2,1,0:T(8,128)}, u32[]{:S(2)}, u32[]{:S(2)}) collective-permute-start(f32[24,32,384]{2,1,0:T(8,128)} %collective-permute-done.2.refs_1_.refs_11_), channel_id=1, source_target_pairs={{0,8},{8,16},{16,24},{12,4},{20,12},{28,20},{1,9},{9,17},{17,25},{... | collective-permute-start | bytes 3538952 | tf_op jit(solution)/shard_map/ppermute | solution.py:404
  69.3 77.5 %collective-permute-start.8 = (f32[24,32,384]{2,1,0:T(8,128)}, f32[24,32,384]{2,1,0:T(8,128)S(1)}, u32[]{:S(2)}, u32[]{:S(2)}) collective-permute-start(f32[24,32,384]{2,1,0:T(8,128)} %get-tuple-element.58), channel_id=1, source_target_pairs={{0,4},{4,0},{8,12},{12,8},{16,20},{20,16},{24,28},{28,24},{1,5},{5... | collective-permute-start | bytes 3538952 | tf_op jit(solution)/shard_map/ppermute | solution.py:394
  69.4 4.2 %copy-start.20 = (f32[2,64,384]{2,1,0:T(8,128)}, f32[2,64,384]{2,1,0:T(8,128)S(1)}, u32[]{:S(2)}) copy-start(f32[2,64,384]{2,1,0:T(8,128)S(1)} %collective-permute-done.5.high_ref) | copy-start | bytes 589828
  70.1 47.9 %collective-permute-start.6 = (f32[4,32,384]{2,1,0:T(8,128)}, f32[4,32,384]{2,1,0:T(8,128)}, u32[]{:S(2)}, u32[]{:S(2)}) collective-permute-start(f32[4,32,384]{2,1,0:T(8,128)} %pad_maximum_fusion), channel_id=1, source_target_pairs={{0,4},{4,0},{8,12},{12,8},{16,20},{20,16},{24,28},{28,24},{1,5},{5... | collective-permute-start | bytes 589832 | tf_op jit(solution)/shard_map/ppermute | solution.py:394
  78.3 42.0 %all-to-all-start = ((f32[32,1,128]{2,1,0:T(1,128)}), f32[32,1,128]{2,1,0:T(1,128)S(1)}, u32[]{:S(2)}, u32[]{:S(2)}) async-start(f32[32,1,128]{2,1,0:T(1,128)} %bitcast.56), calls=%async_computation | async-start | bytes 32768 | tf_op jit(solution)/shard_map/all_to_all | solution.py:411
  120.4 1.0 copy-start.3
  128.3 18.5 %slice-start = ((s8[4718592]{0:T(1024)(128)(4,1)}), s8[4194304]{0:T(1024)(128)(4,1)S(1)}, s32[]{:S(2)}) async-start(s8[4718592]{0:T(1024)(128)(4,1)} %bitcast.46), calls=%async_computation.4 | async-start | bytes 8388608
  128.3 18.5 %slice-start.1 = ((s8[4718592]{0:T(1024)(128)(4,1)}), s8[524288]{0:T(1024)(128)(4,1)S(1)}, s32[]{:S(2)}) async-start(s8[4718592]{0:T(1024)(128)(4,1)} %bitcast.46), calls=%async_computation.5 | async-start | bytes 1048576
  128.3 18.5 %copy-start.1 = (f32[24,32,384]{2,1,0:T(8,128)S(1)}, f32[24,32,384]{2,1,0:T(8,128)}, u32[]{:S(2)}) copy-start(f32[24,32,384]{2,1,0:T(8,128)} %copy-done) | copy-start | bytes 3538948
  128.4 18.5 %copy-start.4 = (f32[64,384]{1,0:T(8,128)S(1)}, f32[64,384]{1,0:T(8,128)}, u32[]{:S(2)}) copy-start(f32[64,384]{1,0:T(8,128)} %refs_16_.1) | copy-start | bytes 294916
  128.4 18.5 %copy-start.5 = (f32[4,32,384]{2,1,0:T(8,128)S(1)}, f32[4,32,384]{2,1,0:T(8,128)}, u32[]{:S(2)}) copy-start(f32[4,32,384]{2,1,0:T(8,128)} %pad_maximum_fusion.2.refs_5_) | copy-start | bytes 589828
  128.4 18.5 %copy-start.6 = (f32[4,32,384]{2,1,0:T(8,128)S(1)}, f32[4,32,384]{2,1,0:T(8,128)}, u32[]{:S(2)}) copy-start(f32[4,32,384]{2,1,0:T(8,128)} %pad_maximum_fusion.1.refs_4_) | copy-start | bytes 589828
  128.4 18.5 %copy-start.7 = (f32[4,24,384]{2,1,0:T(8,128)S(1)}, f32[4,24,384]{2,1,0:T(8,128)}, u32[]{:S(2)}) copy-start(f32[4,24,384]{2,1,0:T(8,128)} %pad_maximum_fusion.5.refs_6_) | copy-start | bytes 442372
  128.4 18.5 %copy-start.15 = (f32[32,1,128]{2,1,0:T(1,128)S(1)}, f32[32,1,128]{2,1,0:T(1,128)}, u32[]{:S(2)}) copy-start(f32[32,1,128]{2,1,0:T(1,128)} %copy-done.14) | copy-start | bytes 49156
  128.4 18.5 %copy-start.28 = (f32[4,24]{1,0:T(4,128)S(1)}, f32[4,24]{1,0:T(4,128)}, u32[]{:S(2)}) copy-start(f32[4,24]{1,0:T(4,128)} %pad_maximum_fusion.9.push_ref) | copy-start | bytes 1156
  128.4 18.5 %copy-start.32 = (s32[5]{0:T(128)S(1)}, s32[5]{0:T(128)}, u32[]{:S(2)}) copy-start(s32[5]{0:T(128)} %stack.39.flags_ref) | copy-start | bytes 64
  128.4 18.5 %copy-start.36 = (f32[24]{0:T(128)S(1)}, f32[24]{0:T(128)}, u32[]{:S(2)}) copy-start(f32[24]{0:T(128)} %broadcast_select_fusion.speed_ref) | copy-start | bytes 292
  128.4 54.3 %collective-permute-start.11 = (f32[24,32,384]{2,1,0:T(8,128)}, f32[24,32,384]{2,1,0:T(8,128)}, u32[]{:S(2)}, u32[]{:S(2)}) collective-permute-start(f32[24,32,384]{2,1,0:T(8,128)} %get-tuple-element.61.refs_3_), channel_id=1, source_target_pairs={{0,8},{8,16},{16,24},{12,4},{20,12},{28,20},{1,9},{9,17},{17,25},{... | collective-permute-start | bytes 3538952 | tf_op jit(solution)/shard_map/ppermute | solution.py:404
  144.6 38.1 %collective-permute-start.12 = (f32[24,32,384]{2,1,0:T(8,128)}, f32[24,32,384]{2,1,0:T(8,128)}, u32[]{:S(2)}, u32[]{:S(2)}) collective-permute-start(f32[24,32,384]{2,1,0:T(8,128)} %get-tuple-element.56.refs_0_), channel_id=1, source_target_pairs={{8,0},{16,8},{24,16},{4,12},{12,20},{20,28},{9,1},{17,9},{25,17},{... | collective-permute-start | bytes 3538952 | tf_op jit(solution)/shard_map/ppermute | solution.py:408
  146.8 6.3 %copy-start.35 = (f32[1,24,384]{2,1,0:T(8,128)S(1)}, f32[1,24,384]{2,1,0:T(8,128)}, u32[]{:S(2)}) copy-start(f32[1,24,384]{2,1,0:T(8,128)} %get-tuple-element.70) | copy-start | bytes 110596
  146.8 11.9 %copy-start.29 = (f32[2,32,384]{2,1,0:T(8,128)S(1)}, f32[2,32,384]{2,1,0:T(8,128)}, u32[]{:S(2)}) copy-start(f32[2,32,384]{2,1,0:T(8,128)} %get-tuple-element.65) | copy-start | bytes 294916
  147.0 6.2 %copy-start.2 = (f32[24,32,384]{2,1,0:T(8,128)}, f32[24,32,384]{2,1,0:T(8,128)S(1)}, u32[]{:S(2)}) copy-start(f32[24,32,384]{2,1,0:T(8,128)S(1)} %collective-permute-done.8.refs_7_) | copy-start | bytes 3538948
  153.1 9.3 %copy-start.31 = (f32[2,24,384]{2,1,0:T(8,128)S(1)}, f32[2,24,384]{2,1,0:T(8,128)}, u32[]{:S(2)}) copy-start(f32[2,24,384]{2,1,0:T(8,128)} %get-tuple-element.77) | copy-start | bytes 221188
  153.1 9.3 %copy-start.34 = (f32[1,24,384]{2,1,0:T(8,128)S(1)}, f32[1,24,384]{2,1,0:T(8,128)}, u32[]{:S(2)}) copy-start(f32[1,24,384]{2,1,0:T(8,128)} %get-tuple-element.79) | copy-start | bytes 110596
  153.1 10.0 %copy-start.30 = (f32[2,32,384]{2,1,0:T(8,128)S(1)}, f32[2,32,384]{2,1,0:T(8,128)}, u32[]{:S(2)}) copy-start(f32[2,32,384]{2,1,0:T(8,128)} %get-tuple-element.74) | copy-start | bytes 294916
  153.1 10.0 %copy-start.33 = (f32[1,32,384]{2,1,0:T(8,128)S(1)}, f32[1,32,384]{2,1,0:T(8,128)}, u32[]{:S(2)}) copy-start(f32[1,32,384]{2,1,0:T(8,128)} %get-tuple-element.76) | copy-start | bytes 147460
  154.1 9.7 %collective-permute-start.15 = (f32[4,24,384]{2,1,0:T(8,128)S(1)}, f32[4,24,384]{2,1,0:T(8,128)S(1)}, u32[]{:S(2)}, u32[]{:S(2)}) collective-permute-start(f32[4,24,384]{2,1,0:T(8,128)S(1)} %pad_maximum_fusion.6), channel_id=1, source_target_pairs={{0,4},{4,0},{8,12},{12,8},{16,20},{20,16},{24,28},{28,24},{1,5},{5... | collective-permute-start | bytes 442376 | tf_op jit(solution)/shard_map/ppermute | solution.py:394
  157.4 7.2 %copy-start.26 = (f32[4,32,384]{2,1,0:T(8,128)}, f32[4,32,384]{2,1,0:T(8,128)S(1)}, u32[]{:S(2)}) copy-start(f32[4,32,384]{2,1,0:T(8,128)S(1)} %constant_dynamic-update-slice_fusion.last_ref) | copy-start | bytes 589828
  157.4 6.4 %collective-permute-start.13 = (f32[4,32,384]{2,1,0:T(8,128)S(1)}, f32[4,32,384]{2,1,0:T(8,128)S(1)}, u32[]{:S(2)}, u32[]{:S(2)}) collective-permute-start(f32[4,32,384]{2,1,0:T(8,128)S(1)} %constant_dynamic-update-slice_fusion.last_ref), channel_id=1, source_target_pairs={{0,1},{1,2},{2,3},{4,5},{5,6},{6,7},{8,9},{9,10},{10,11},{12,13},{... | collective-permute-start | bytes 589832 | tf_op jit(solution)/shard_map/ppermute | solution.py:397
  159.5 5.1 %copy-start.27 = (f32[4,32,384]{2,1,0:T(8,128)}, f32[4,32,384]{2,1,0:T(8,128)S(1)}, u32[]{:S(2)}) copy-start(f32[4,32,384]{2,1,0:T(8,128)S(1)} %constant_dynamic-update-slice_fusion.3.first_ref) | copy-start | bytes 589828
  159.5 5.1 %collective-permute-start.14 = (f32[4,32,384]{2,1,0:T(8,128)S(1)}, f32[4,32,384]{2,1,0:T(8,128)S(1)}, u32[]{:S(2)}, u32[]{:S(2)}) collective-permute-start(f32[4,32,384]{2,1,0:T(8,128)S(1)} %constant_dynamic-update-slice_fusion.3.first_ref), channel_id=1, source_target_pairs={{1,0},{2,1},{3,2},{5,4},{6,5},{7,6},{9,8},{10,9},{11,10},{13,12},{... | collective-permute-start | bytes 589832 | tf_op jit(solution)/shard_map/ppermute | solution.py:400
  163.8 0.8 copy-start.23
  163.8 0.8 copy-start.16
  202.5 32.6 %collective-permute-start.17 = (f32[24,32,384]{2,1,0:T(8,128)}, f32[24,32,384]{2,1,0:T(8,128)S(1)}, u32[]{:S(2)}, u32[]{:S(2)}) collective-permute-start(f32[24,32,384]{2,1,0:T(8,128)} %get-tuple-element.83.refs_0_.refs_9_), channel_id=1, source_target_pairs={{8,0},{16,8},{24,16},{4,12},{12,20},{20,28},{9,1},{17,9},{25,17},{... | collective-permute-start | bytes 3538952 | tf_op jit(solution)/shard_map/ppermute | solution.py:408
  203.8 31.3 %collective-permute-start.16 = (f32[24,32,384]{2,1,0:T(8,128)}, f32[24,32,384]{2,1,0:T(8,128)S(1)}, u32[]{:S(2)}, u32[]{:S(2)}) collective-permute-start(f32[24,32,384]{2,1,0:T(8,128)} %get-tuple-element.86.refs_3_.refs_12_), channel_id=1, source_target_pairs={{0,8},{8,16},{16,24},{12,4},{20,12},{28,20},{1,9},{9,17},{17,25},{... | collective-permute-start | bytes 3538952 | tf_op jit(solution)/shard_map/ppermute | solution.py:404
  208.5 8.8 %collective-permute-start.18 = (f32[4,32,384]{2,1,0:T(8,128)}, f32[4,32,384]{2,1,0:T(8,128)S(1)}, u32[]{:S(2)}, u32[]{:S(2)}) collective-permute-start(f32[4,32,384]{2,1,0:T(8,128)} %get-tuple-element.87.last_ref), channel_id=1, source_target_pairs={{0,1},{1,2},{2,3},{4,5},{5,6},{6,7},{8,9},{9,10},{10,11},{12,13},{... | collective-permute-start | bytes 589832 | tf_op jit(solution)/shard_map/ppermute | solution.py:397
  209.9 7.4 %collective-permute-start.19 = (f32[4,32,384]{2,1,0:T(8,128)}, f32[4,32,384]{2,1,0:T(8,128)S(1)}, u32[]{:S(2)}, u32[]{:S(2)}) collective-permute-start(f32[4,32,384]{2,1,0:T(8,128)} %get-tuple-element.88.first_ref), channel_id=1, source_target_pairs={{1,0},{2,1},{3,2},{5,4},{6,5},{7,6},{9,8},{10,9},{11,10},{13,12},{... | collective-permute-start | bytes 589832 | tf_op jit(solution)/shard_map/ppermute | solution.py:400
  211.2 6.1 %collective-permute-start.20 = (f32[4,24,384]{2,1,0:T(8,128)}, f32[4,24,384]{2,1,0:T(8,128)S(1)}, u32[]{:S(2)}, u32[]{:S(2)}) collective-permute-start(f32[4,24,384]{2,1,0:T(8,128)} %get-tuple-element.89), channel_id=1, source_target_pairs={{0,4},{4,0},{8,12},{12,8},{16,20},{20,16},{24,28},{28,24},{1,5},{5... | collective-permute-start | bytes 442376 | tf_op jit(solution)/shard_map/ppermute | solution.py:394
  217.3 0.8 copy-start.19
  235.1 1.0 copy-start.8
  235.1 1.4 copy-start.9
  254.2 36.8 %collective-permute-start.22 = (f32[24,32,384]{2,1,0:T(8,128)}, f32[24,32,384]{2,1,0:T(8,128)S(1)}, u32[]{:S(2)}, u32[]{:S(2)}) collective-permute-start(f32[24,32,384]{2,1,0:T(8,128)} %get-tuple-element.94.refs_0_), channel_id=1, source_target_pairs={{8,0},{16,8},{24,16},{4,12},{12,20},{20,28},{9,1},{17,9},{25,17},{... | collective-permute-start | bytes 3538952 | tf_op jit(solution)/shard_map/ppermute | solution.py:408
  255.5 35.5 %collective-permute-start.21 = (f32[24,32,384]{2,1,0:T(8,128)}, f32[24,32,384]{2,1,0:T(8,128)S(1)}, u32[]{:S(2)}, u32[]{:S(2)}) collective-permute-start(f32[24,32,384]{2,1,0:T(8,128)} %get-tuple-element.97.refs_3_), channel_id=1, source_target_pairs={{0,8},{8,16},{16,24},{12,4},{20,12},{28,20},{1,9},{9,17},{17,25},{... | collective-permute-start | bytes 3538952 | tf_op jit(solution)/shard_map/ppermute | solution.py:404
  260.1 8.0 %collective-permute-start.23 = (f32[4,32,384]{2,1,0:T(8,128)}, f32[4,32,384]{2,1,0:T(8,128)S(1)}, u32[]{:S(2)}, u32[]{:S(2)}) collective-permute-start(f32[4,32,384]{2,1,0:T(8,128)} %get-tuple-element.98.last_ref), channel_id=1, source_target_pairs={{0,1},{1,2},{2,3},{4,5},{5,6},{6,7},{8,9},{9,10},{10,11},{12,13},{... | collective-permute-start | bytes 589832 | tf_op jit(solution)/shard_map/ppermute | solution.py:397
  261.4 6.7 %collective-permute-start.24 = (f32[4,32,384]{2,1,0:T(8,128)}, f32[4,32,384]{2,1,0:T(8,128)S(1)}, u32[]{:S(2)}, u32[]{:S(2)}) collective-permute-start(f32[4,32,384]{2,1,0:T(8,128)} %get-tuple-element.99.first_ref), channel_id=1, source_target_pairs={{1,0},{2,1},{3,2},{5,4},{6,5},{7,6},{9,8},{10,9},{11,10},{13,12},{... | collective-permute-start | bytes 589832 | tf_op jit(solution)/shard_map/ppermute | solution.py:400
  262.7 5.4 %collective-permute-start.25 = (f32[4,24,384]{2,1,0:T(8,128)}, f32[4,24,384]{2,1,0:T(8,128)S(1)}, u32[]{:S(2)}, u32[]{:S(2)}) collective-permute-start(f32[4,24,384]{2,1,0:T(8,128)} %get-tuple-element.100), channel_id=1, source_target_pairs={{0,4},{4,0},{8,12},{12,8},{16,20},{20,16},{24,28},{28,24},{1,5},{5... | collective-permute-start | bytes 442376 | tf_op jit(solution)/shard_map/ppermute | solution.py:394
  268.1 0.8 copy-start.22
  291.0 1.0 copy-start.12
  291.0 1.4 copy-start.13
  311.7 60.5 %collective-permute-start.26 = (f32[24,32,384]{2,1,0:T(8,128)}, f32[24,32,384]{2,1,0:T(8,128)S(1)}, u32[]{:S(2)}, u32[]{:S(2)}) collective-permute-start(f32[24,32,384]{2,1,0:T(8,128)} %get-tuple-element.107), channel_id=1, source_target_pairs={{0,4},{4,0},{8,12},{12,8},{16,20},{20,16},{24,28},{28,24},{1,5},{5... | collective-permute-start | bytes 3538952 | tf_op jit(solution)/shard_map/ppermute | solution.py:394
  312.2 60.0 %collective-permute-start.27 = (f32[24,32,384]{2,1,0:T(8,128)}, f32[24,32,384]{2,1,0:T(8,128)S(1)}, u32[]{:S(2)}, u32[]{:S(2)}) collective-permute-start(f32[24,32,384]{2,1,0:T(8,128)} %get-tuple-element.108), channel_id=1, source_target_pairs={{0,4},{4,0},{8,12},{12,8},{16,20},{20,16},{24,28},{28,24},{1,5},{5... | collective-permute-start | bytes 3538952 | tf_op jit(solution)/shard_map/ppermute | solution.py:394
  314.5 50.4 %collective-permute-start.28 = (f32[2,384]{1,0:T(2,128)S(1)}, f32[2,384]{1,0:T(2,128)S(1)}, u32[]{:S(2)}, u32[]{:S(2)}) collective-permute-start(f32[2,384]{1,0:T(2,128)S(1)} %slice.23), channel_id=1, source_target_pairs={{0,4},{4,0},{8,12},{12,8},{16,20},{20,16},{24,28},{28,24},{1,5},{5... | collective-permute-start | bytes 9224 | tf_op jit(solution)/shard_map/ppermute | solution.py:394
  372.2 1.0 copy-start.10
  372.3 1.4 copy-start.11
  (6 other events, 4.1 us)

commit v2 on v1

v2 whole, which is shorter than its diff:
```python
import functools

import jax
import jax.numpy as jnp
from jax import lax
from jax.experimental import pallas as pl
from jax.experimental.pallas import tpu as pltpu
from jax.sharding import PartitionSpec as P

VELOCITY_LIMIT = 1.0
PLANNER_SPEED = 0.3
DISTURBANCE = 0.2
CONTROL_COST = 1.0
COURANT = 0.5

LANES = 128


def compiler_params():
    return pltpu.CompilerParams(vmem_limit_bytes=8 * 1024 * 1024)


def whole():
    return pl.BlockSpec(memory_space=pltpu.VMEM)


def scalars():
    return pl.BlockSpec(memory_space=pltpu.SMEM)


def fold(tile):
    rows = tile.shape[0]
    out = tile[0:8]
    for start in range(8, rows, 8):
        out = jnp.maximum(out, tile[start : start + 8])
    return out


def fold_min(tile):
    rows = tile.shape[0]
    out = tile[0:8]
    for start in range(8, rows, 8):
        out = jnp.minimum(out, tile[start : start + 8])
    return out


def lane_max(ref, lane):
    values = ref[...]
    position = lax.broadcasted_iota(jnp.int32, values.shape, 1)
    return jnp.max(jnp.where(position == lane, values, 0.0))


class Own:
    def __init__(self, array, outer):
        self.array, self.outer = array, outer

    def reader(self, ref, parity, half):
        row = parity if self.outer else 1 - parity
        start = pl.multiple_of(parity * half, half)
        return lambda j, g: ref[row, j, pl.ds(pl.multiple_of(start + 8 * g, 8), 8), :]


class Row:
    def __init__(self, array):
        self.array = array

    def reader(self, ref, parity, half):
        return lambda j, g: ref[j, pl.ds(8 * g, 8), :]


class Scalars:
    def __init__(self, sizes):
        cells_v, half, width, total_vx, total_vy = sizes
        self.step_2 = 2.0 * VELOCITY_LIMIT / total_vx
        self.step_3 = 2.0 * VELOCITY_LIMIT / total_vy
        self.step_1 = self.step_2 * self.step_3
        self.rate_1 = VELOCITY_LIMIT * (total_vx - 1) / total_vx + PLANNER_SPEED
        self.rate_4 = VELOCITY_LIMIT * (total_vy - 1) / total_vy + PLANNER_SPEED

    def rates(self, limits, maxima):
        rate_2 = lane_max(limits, 2) + DISTURBANCE + lane_max(maxima, 0) * (0.5 / (self.step_2 * CONTROL_COST))
        rate_3 = lane_max(limits, 3) + DISTURBANCE + lane_max(maxima, 1) * (0.5 / (self.step_3 * CONTROL_COST))
        return rate_2 * (1.0 / self.step_2), rate_3 * (1.0 / self.step_3)

    def time_step(self, rates):
        total = rates[0] + rates[1] + (self.rate_1 + self.rate_4) / self.step_1
        return jnp.max(COURANT / jnp.full((8, LANES), total, jnp.float32))


class Operands:
    def __init__(self):
        self.arrays = []

    def add(self, array):
        for position, known in enumerate(self.arrays):
            if known is array:
                return position
        self.arrays.append(array)
        return len(self.arrays) - 1


def f32(*shape):
    return jax.ShapeDtypeStruct(shape, jnp.float32)


def estimate(cells, flops):
    return pl.CostEstimate(flops=flops * cells, bytes_accessed=4 * cells, transcendentals=0)


def slabs(tile):
    return [tile[start : start + 8] for start in range(0, tile.shape[0], 8)]


def advance(sizes, targets, rows, bases, halo_rows, vx_low, vx_high, vy_next, maxima, stepper, accel_second, flags, push, speed):
    cells_v, half, width, total_vx, total_vy = sizes
    count = len(targets)
    heun = bases is not None
    late = stepper is None
    full = not heun and not late
    ops = Operands()
    needed = sorted({k for t in targets for k in (t - 1, t, t + 1) if 0 <= k <= 3})
    row_at = {k: ops.add(rows[k].array) for k in needed}
    halo_at = {k: ops.add(halo_rows[i]) for i, k in enumerate((-1, 4)) if any(abs(t - k) == 1 for t in targets)}
    base_at = [ops.add(b.array) for b in bases] if heun else []
    low_at, high_at, vy_at, accel_at = ops.add(vx_low), ops.add(vx_high), ops.add(vy_next), ops.add(accel_second)
    maxima_at = [] if late else [ops.add(maxima), ops.add(stepper)]
    n_in = len(ops.arrays)
    n_out = count * (1 if full else 3)
    groups = half // 8

    def body(flags_ref, push_ref, speed_ref, *refs):
        ins, outs = refs[:n_in], refs[n_in : n_in + n_out]
        adv_up, adv_down, acc_up, acc_down = refs[n_in + n_out :]
        parity, edge_low, edge_high, vx_first, vx_last = (flags_ref[i] for i in range(5))
        is_even = parity == 0
        known = Scalars(sizes)
        step_1, step_2, step_3 = known.step_1, known.step_2, known.step_3
        if late:
            scale = jnp.float32(1.0)
        else:
            rates = known.rates(ins[maxima_at[0]], ins[maxima_at[1]])
            scale = known.time_step(rates) * (0.5 if heun else 1.0)
        damp_1 = scale * (0.5 * known.rate_1 / step_1)
        damp_4 = scale * (0.5 * known.rate_4 / step_1)
        keep = 2.0 * (damp_1 + damp_4)
        if not late:
            keep = keep + (0.5 if heun else 1.0)
        if full:
            damp_2, damp_3 = scale * 0.5 * rates[0], scale * 0.5 * rates[1]
        planner = scale * (PLANNER_SPEED / (2.0 * step_1))
        disturb_2 = scale * (DISTURBANCE / (2.0 * step_2))
        disturb_3 = scale * (DISTURBANCE / (2.0 * step_3))
        control_2 = scale * (1.0 / (8.0 * CONTROL_COST * step_2 * step_2))
        control_3 = scale * (1.0 / (8.0 * CONTROL_COST * step_3 * step_3))
        to_1, to_2, to_3 = scale / (2.0 * step_1), scale / (2.0 * step_2), scale / (2.0 * step_3)

        start = pl.multiple_of(parity * half, half)
        vy = (parity * half + lax.broadcasted_iota(jnp.int32, (half, LANES), 0)).astype(jnp.float32)
        speed_y = (2.0 * vy + (1.0 - total_vy)) * (VELOCITY_LIMIT / total_vy) * to_1
        adv_up[...] = speed_y + planner
        adv_down[...] = speed_y - planner
        accel = ins[accel_at][pl.ds(start, half), :] * to_3
        acc_up[...] = accel + disturb_3
        acc_down[...] = accel - disturb_3

        readers = {k: rows[k].reader(ins[row_at[k]], parity, half) for k in needed}
        base_readers = [b.reader(ins[a], parity, half) for b, a in zip(bases, base_at)] if heun else None
        sublane = lax.broadcasted_iota(jnp.int32, (8, width), 0)
        lane = lax.broadcasted_iota(jnp.int32, (8, LANES), 1)

        def neighbour(k, j, g, center):
            if k == -1:
                return jnp.where(edge_low == 1, center, ins[halo_at[-1]][j, pl.ds(8 * g, 8), :])
            if k == 4:
                return jnp.where(edge_high == 1, center, ins[halo_at[4]][j, pl.ds(8 * g, 8), :])
            return readers[k](j, g)

        def lane_pieces(x):
            return [x[:, start : start + LANES] for start in range(0, width, LANES)]

        def upwind(up, down, slope):
            return jnp.maximum(up * slope, down * slope)

        def tile(i, j, low_j, high_j):
            t = targets[i]
            flow = speed_ref[j] * to_1
            drift = push_ref[t, j] * to_2
            flow_up, flow_down = flow + planner, flow - planner
            drift_up, drift_down = drift + disturb_2, drift - disturb_2
            beyond = ins[vy_at][3 - t, pl.ds(j, 1), :]
            first = readers[t](j, 0)
            last = readers[t](j, groups - 1)
            below = jnp.broadcast_to(jnp.where(is_even, first[0:1], beyond), (8, width))
            above = jnp.broadcast_to(jnp.where(is_even, beyond, last[7:8]), (8, width))
            ups = [below] + [pltpu.roll(readers[t](j, g), 1, 0) for g in range(groups)]
            downs = [pltpu.roll(readers[t](j, g), 7, 0) for g in range(groups)] + [above]
            for g in range(groups):
                w = readers[t](j, g)
                here = pl.ds(8 * g, 8)
                low_1, high_1 = neighbour(t - 1, j, g, w), neighbour(t + 1, j, g, w)
                total = keep * w - damp_1 * (low_1 + high_1)
                total = total + upwind(flow_up, flow_down, high_1 - low_1)

                pieces = lane_pieces(w)
                right = [pltpu.roll(p, 1, 1) for p in pieces]
                left = [pltpu.roll(p, LANES - 1, 1) for p in pieces]
                parts = []
                for p in range(len(pieces)):
                    low_4 = jnp.where(lane == 0, right[p - 1] if p > 0 else pieces[0], right[p])
                    high_4 = jnp.where(lane == LANES - 1, left[p + 1] if p + 1 < len(pieces) else pieces[p], left[p])
                    parts.append(upwind(adv_up[here, :], adv_down[here, :], high_4 - low_4) - damp_4 * (low_4 + high_4))
                total = total + jnp.concatenate(parts, axis=1)

                if low_j is None:
                    low_2 = jnp.where(vx_first == 1, w, ins[low_at][t, here, :])
                else:
                    low_2 = readers[t](low_j, g)
                if high_j is None:
                    high_2 = jnp.where(vx_last == 1, w, ins[high_at][t, here, :])
                else:
                    high_2 = readers[t](high_j, g)
                slope = high_2 - low_2
                bent = control_2 * slope
                total = total + jnp.maximum((drift_up - bent) * slope, (drift_down - bent) * slope)

                low_3 = jnp.where(sublane == 0, ups[g], ups[g + 1])
                high_3 = jnp.where(sublane == 7, downs[g + 1], downs[g])
                slope = high_3 - low_3
                bent = control_3 * slope
                total = total + jnp.maximum((acc_up[here, :] - bent) * slope, (acc_down[here, :] - bent) * slope)

                twice = w + w
                bend_2 = low_2 + high_2 - twice
                bend_3 = low_3 + high_3 - twice
                if heun:
                    total = total + 0.5 * base_readers[i](j, g)
                if full:
                    total = total - damp_2 * bend_2 - damp_3 * bend_3
                    outs[i][j, here, :] = total
                else:
                    outs[3 * i][j, here, :] = total
                    outs[3 * i + 1][j, here, :] = bend_2
                    outs[3 * i + 2][j, here, :] = bend_3

        for i in range(count):
            tile(i, 0, None, 1)

        @pl.loop(1, cells_v - 1)
        def _(j):
            for i in range(count):
                tile(i, j, j - 1, j + 1)

        for i in range(count):
            tile(i, cells_v - 1, cells_v - 2, None)

    return pl.pallas_call(
        body,
        out_shape=[f32(cells_v, half, width)] * n_out,
        in_specs=[scalars()] * 3 + [whole()] * n_in,
        out_specs=[whole()] * n_out,
        scratch_shapes=[pltpu.VMEM((half, LANES), jnp.float32)] * 2 + [pltpu.VMEM((half, width), jnp.float32)] * 2,
        compiler_params=compiler_params(),
        cost_estimate=estimate(count * cells_v * half * width, 45),
        name="advance_" + "".join(str(t) for t in targets),
    )(flags, push, speed, *ops.arrays)


def settle(sizes, targets, updates, costs, flags, damping=None, fields=None, prior=None, with_edges=True):
    cells_v, half, width, total_vx, total_vy = sizes
    count = len(targets)
    ops = Operands()
    update_at = [[ops.add(a) for a in u] for u in updates]
    cost_at = [ops.add(c.array) for c in costs]
    field_at = [ops.add(f.array) for f in fields] if fields is not None else []
    maxima_at = [ops.add(m) for m in damping[:3]] if damping is not None else []
    before_targets, before_outs = prior if prior is not None else ((), ())
    prior_at = [ops.add(a) for a in before_outs]
    n_in = len(ops.arrays)
    every = sorted(tuple(before_targets) + tuple(targets))
    groups = half // 8

    def body(flags_ref, *refs):
        ins, outs = refs[:n_in], refs[n_in:]
        fields_out = outs[:count]
        parity = flags_ref[0]
        is_even = parity == 0
        if damping is not None:
            known = Scalars(sizes)
            step_rates = known.rates(ins[maxima_at[0]], ins[maxima_at[1]])
            rates = step_rates if maxima_at[1] == maxima_at[2] else known.rates(ins[maxima_at[0]], ins[maxima_at[2]])
            scale = known.time_step(step_rates) * damping[3]
            if fields is None:
                damp_2, damp_3 = scale * 0.5 * rates[0], scale * 0.5 * rates[1]
            else:
                damp_2, damp_3 = 0.5 * rates[0], 0.5 * rates[1]
        cost_readers = [c.reader(ins[a], parity, half) for c, a in zip(costs, cost_at)]
        field_readers = [f.reader(ins[a], parity, half) for f, a in zip(fields or (), field_at)]
        sublane = lax.broadcasted_iota(jnp.int32, (8, width), 0)

        def tile(i, j):
            out = []
            for g in range(groups):
                here = pl.ds(8 * g, 8)
                total = ins[update_at[i][0]][j, here, :]
                if damping is not None:
                    total = total - damp_2 * ins[update_at[i][1]][j, here, :] - damp_3 * ins[update_at[i][2]][j, here, :]
                    if fields is not None:
                        total = field_readers[i](j, g) + scale * total
                y = jnp.maximum(cost_readers[i](j, g), total)
                fields_out[i][j, here, :] = y
                out.append(y)
            return out

        if not with_edges:
            least_ref = outs[count]
            for i in range(count):

                def step(j, least, i=i):
                    return functools.reduce(jnp.minimum, tile(i, j), least)

                least = lax.fori_loop(0, cells_v, step, jnp.full((8, width), jnp.inf, jnp.float32))
                least_ref[pl.ds(i, 1), :] = jnp.min(least, axis=0, keepdims=True)
            return

        first_ref, second_ref, before_ref, last_ref, edge_ref, inner_ref, part_ref = outs[count : count + 7]
        send_at = jnp.where(is_even, half - 1, 0)
        inner_at = jnp.where(is_even, half - 2, 1)
        wall_at = jnp.where(is_even, 0, half - 1)
        next_at = jnp.where(is_even, 1, half - 2)
        for position, t in enumerate(sorted(before_targets)):
            slot = every.index(t)
            for ref, at in zip((first_ref, second_ref, before_ref, last_ref, edge_ref, inner_ref), prior_at):
                ref[slot] = ins[at][position]

        def one(i, j, most_3):
            slot = every.index(targets[i])
            out = tile(i, j)
            edge_ref[slot, pl.ds(j, 1), :] = fields_out[i][j, pl.ds(send_at, 1), :]
            inner_ref[slot, pl.ds(j, 1), :] = fields_out[i][j, pl.ds(inner_at, 1), :]
            wall = jnp.abs(fields_out[i][j, pl.ds(next_at, 1), :] - fields_out[i][j, pl.ds(wall_at, 1), :])
            most_3 = jnp.maximum(most_3, wall)
            rolled = [pltpu.roll(y, 2, 0) for y in out]
            for g in range(groups):
                apart = jnp.where(sublane < 2, rolled[g - 1] if g > 0 else out[0], rolled[g])
                most_3 = jnp.maximum(most_3, jnp.abs(out[g] - apart))
            return out, most_3

        most_2 = jnp.zeros((8, width), jnp.float32)
        most_3 = most_2
        if prior is not None:
            most_2, most_3 = ins[prior_at[6]][0], ins[prior_at[6]][1]
        for i in range(count):
            for j in (0, 1):
                _, most_3 = one(i, j, most_3)

            def step(j, carry, i=i):
                most_2, most_3 = carry
                out, most_3 = one(i, j, most_3)
                for g in range(groups):
                    most_2 = jnp.maximum(most_2, jnp.abs(out[g] - fields_out[i][j - 2, pl.ds(8 * g, 8), :]))
                return most_2, most_3

            most_2, most_3 = lax.fori_loop(2, cells_v, step, (most_2, most_3))
            slot = every.index(targets[i])
            first_ref[slot] = fields_out[i][0]
            second_ref[slot] = fields_out[i][1]
            before_ref[slot] = fields_out[i][cells_v - 2]
            last_ref[slot] = fields_out[i][cells_v - 1]
        part_ref[0] = most_2
        part_ref[1] = most_3

    n = len(every)
    shapes = [f32(cells_v, half, width)] * count
    if with_edges:
        shapes += [f32(n, half, width)] * 4 + [f32(n, cells_v, width)] * 2 + [f32(2, 8, width)]
    else:
        shapes.append(f32(count, width))
    outs = pl.pallas_call(
        body,
        out_shape=shapes,
        in_specs=[scalars()] + [whole()] * n_in,
        out_specs=[whole()] * len(shapes),
        compiler_params=compiler_params(),
        cost_estimate=estimate(count * cells_v * half * width, 15),
        name="settle_" + "".join(str(t) for t in targets),
    )(flags, *ops.arrays)
    return outs[:count], outs[count:]


def spread(shape, lanes):
    position = lax.broadcasted_iota(jnp.int32, shape, 1)
    out = jnp.zeros(shape, jnp.float32)
    for lane, value in enumerate(lanes):
        out = jnp.where(position == lane, value, out)
    return out


def first_maxima(value, vx_low, vx_high, accel_first, accel_second, flags):
    rows, cells_v, total_vy, width = value.shape

    def body(flags_ref, v_ref, low_ref, high_ref, first_ref, second_ref, out_ref):
        vx_first, vx_last = flags_ref[3], flags_ref[4]
        vy_row = lax.broadcasted_iota(jnp.int32, (total_vy, width), 0)

        def of_vy(x):
            inner = jnp.where(vy_row >= 2, jnp.abs(x - pltpu.roll(x, 2, 0)), 0.0)
            wall = jnp.maximum(jnp.abs(x[1:2] - x[0:1]), jnp.abs(x[total_vy - 1 : total_vy] - x[total_vy - 2 : total_vy - 1]))
            return jnp.maximum(fold(inner), wall)

        most_2 = jnp.zeros((8, width), jnp.float32)
        most_3 = jnp.zeros((8, width), jnp.float32)
        for r in range(rows):
            x = v_ref[r, 0]
            most_3 = jnp.maximum(most_3, of_vy(x))
            most_2 = jnp.maximum(most_2, fold(jnp.abs(v_ref[r, 1] - jnp.where(vx_first == 1, x, low_ref[r]))))
            x = v_ref[r, cells_v - 1]
            most_3 = jnp.maximum(most_3, of_vy(x))
            most_2 = jnp.maximum(most_2, fold(jnp.abs(v_ref[r, cells_v - 2] - jnp.where(vx_last == 1, x, high_ref[r]))))

            def step(j, carry, r=r):
                most_2, most_3 = carry
                most_3 = jnp.maximum(most_3, of_vy(v_ref[r, j]))
                most_2 = jnp.maximum(most_2, fold(jnp.abs(v_ref[r, j + 1] - v_ref[r, j - 1])))
                return most_2, most_3

            most_2, most_3 = lax.fori_loop(1, cells_v - 1, step, (most_2, most_3))
        values = (jnp.max(most_2), jnp.max(most_3), jnp.max(jnp.abs(first_ref[...])), jnp.max(jnp.abs(second_ref[...])))
        out_ref[...] = spread((8, LANES), values)

    return pl.pallas_call(
        body,
        out_shape=f32(8, LANES),
        in_specs=[scalars()] + [whole()] * 5,
        out_specs=whole(),
        compiler_params=compiler_params(),
        name="first_maxima",
    )(flags, value, vx_low, vx_high, accel_first, accel_second)


def edge_maxima(edges, vx_low, vx_high, vy_next, flags):
    first, second, before, last, _, inner, part = edges

    def body(flags_ref, first_ref, second_ref, before_ref, last_ref, low_ref, high_ref, inner_ref, next_ref, part_ref, out_ref):
        vx_first, vx_last = flags_ref[3], flags_ref[4]
        most_2, most_3 = part_ref[0], part_ref[1]
        for t in range(4):
            low = jnp.where(vx_first == 1, first_ref[t], low_ref[t])
            high = jnp.where(vx_last == 1, last_ref[t], high_ref[t])
            most_2 = jnp.maximum(most_2, fold(jnp.abs(second_ref[t] - low)))
            most_2 = jnp.maximum(most_2, fold(jnp.abs(high - before_ref[t])))
            most_3 = jnp.maximum(most_3, fold(jnp.abs(inner_ref[t] - next_ref[3 - t])))
        out_ref[...] = spread((8, LANES), (jnp.max(most_2), jnp.max(most_3)))

    return pl.pallas_call(
        body,
        out_shape=f32(8, LANES),
        in_specs=[scalars()] + [whole()] * 9,
        out_specs=whole(),
        compiler_params=compiler_params(),
        name="edge_maxima",
    )(flags, first, second, before, last, vx_low, vx_high, inner, vy_next, part)


def place(flags, pieces, which, result, shape):
    rows, cells_v, total_vy, width = shape
    half = total_vy // 2
    block = 8 if cells_v % 8 == 0 else cells_v
    count = len(pieces)

    def body(flags_ref, *refs):
        out_ref = refs[-1]
        piece = pl.program_id(0)
        for i in range(count):

            @pl.when(piece == i)
            def _(i=i):
                out_ref[0] = refs[i][...]

    def target(i, j, flags_ref):
        outer = functools.reduce(lambda a, b: a + b, [(i == k) * int(p[0]) for k, p in enumerate(pieces)])
        parity = flags_ref[0]
        return (jnp.where(outer == 1, parity, 1 - parity), j, parity if which == 0 else 1 - parity, 0)

    def source(k):
        return lambda i, j, flags_ref: (jnp.where(i == k, j, jnp.where(i < k, 0, cells_v // block - 1)), 0, 0)

    in_specs = [pl.BlockSpec((block, half, width), source(k)) for k in range(count)]
    extra = []
    if result is not None:
        in_specs.append(pl.BlockSpec(memory_space=pl.ANY))
        extra = [result]
    return pl.pallas_call(
        body,
        grid_spec=pltpu.PrefetchScalarGridSpec(
            num_scalar_prefetch=1,
            grid=(count, cells_v // block),
            in_specs=in_specs,
            out_specs=pl.BlockSpec((1, block, half, width), target),
        ),
        out_shape=jax.ShapeDtypeStruct(shape, jnp.float32),
        input_output_aliases={1 + count: 0} if result is not None else {},
        compiler_params=compiler_params(),
        name="place",
    )(flags, *[p[1] for p in pieces], *extra)


def per_device(value, cost, accel_first, accel_second):
    n_px, n_vx = lax.axis_size("px"), lax.axis_size("vx")
    rows, cells_v, total_vy, width = value.shape
    half = total_vy // 2
    total_vx = cells_v * n_vx
    sizes = (cells_v, half, width, total_vx, total_vy)
    px, vx = lax.axis_index("px"), lax.axis_index("vx")
    parity = px % 2
    flags = jnp.stack(
        [
            parity,
            ((px == 0) | (px == n_px - 1)).astype(jnp.int32),
            ((px == 1) | (px == n_px - 2)).astype(jnp.int32),
            (vx == 0).astype(jnp.int32),
            (vx == n_vx - 1).astype(jnp.int32),
        ]
    ).astype(jnp.int32)

    def partner(x):
        return lax.ppermute(x, "px", [(i, i ^ 1) for i in range(n_px)])

    def from_low_vx(x):
        return lax.ppermute(x, "vx", [(i, i + 1) for i in range(n_vx - 1)])

    def from_high_vx(x):
        return lax.ppermute(x, "vx", [(i + 1, i) for i in range(n_vx - 1)])

    def halo_before(outermost):
        moves = [(i, i + 2) for i in range(0, n_px - 2, 2)] + [(i, i - 2) for i in range(3, n_px, 2)]
        return lax.ppermute(outermost, "px", moves)

    def halo_after(outer):
        moves = [(i, i - 2) for i in range(2, n_px, 2)] + [(i, i + 2) for i in range(1, n_px - 2, 2)]
        return lax.ppermute(outer, "px", moves)

    def share(maxima):
        for axis, count in (("vx", n_vx), ("px", n_px)):
            apart = 1
            while apart < count:
                other = lax.ppermute(maxima, axis, [(i, i ^ apart) for i in range(count)])
                maxima = jnp.maximum(maxima, other)
                apart *= 2
        return maxima

    def half_of(array, row, which):
        return lax.dynamic_slice(array, (row, 0, which * half, 0), (1, cells_v, half, width))[0]

    value_outer_got = partner(half_of(value, parity, 1 - parity))
    value_inner_got = partner(half_of(value, 1 - parity, 1 - parity))
    cost_outer, value_outer_got = lax.optimization_barrier((half_of(cost, parity, 1 - parity), value_outer_got))
    cost_inner, value_inner_got = lax.optimization_barrier((half_of(cost, 1 - parity, 1 - parity), value_inner_got))
    cost_outer_got = partner(cost_outer)
    cost_inner_got = partner(cost_inner)

    low_own = from_low_vx(value[:, cells_v - 1])
    high_own = from_high_vx(value[:, 0])
    shared_first = share(first_maxima(value, low_own, high_own, accel_first, accel_second, flags))

    def chain_halo(own):
        given = lax.dynamic_slice(own, (0, (1 - parity) * half, 0), (rows, half, width))
        mine = lax.dynamic_slice(own, (0, parity * half, 0), (rows, half, width))
        return mine, given

    low_mine, low_given = chain_halo(low_own)
    high_mine, high_given = chain_halo(high_own)
    got = partner(jnp.concatenate([low_given, high_given], axis=0))
    row_given = lax.dynamic_slice(value, (0, 0, half - parity, 0), (rows, cells_v, 1, width))[:, :, 0]
    row_needed = lax.dynamic_slice(value, (0, 0, half - parity, 0), (rows, cells_v, 1, width))[:, :, 0]
    row_given = lax.dynamic_slice(value, (0, 0, half - 1 + parity, 0), (rows, cells_v, 1, width))[:, :, 0]
    row_got = partner(row_given)
    push_got = partner(accel_first)

    def pick(x, which):
        return lax.dynamic_index_in_dim(x, which, 0, keepdims=True)

    def in_chain(mine, others):
        return jnp.concatenate([pick(mine, parity), pick(mine, 1 - parity), pick(others, parity), pick(others, 1 - parity)], axis=0)

    vx_low = in_chain(low_mine, got[:rows])
    vx_high = in_chain(high_mine, got[rows:])
    vy_next = jnp.concatenate([pick(row_got, 1 - parity), pick(row_got, parity), pick(row_needed, 1 - parity), pick(row_needed, parity)], axis=0)
    push = in_chain(accel_first, push_got)
    positions = (vx * cells_v + jnp.arange(cells_v, dtype=jnp.int32)).astype(jnp.float32)
    speed = (2.0 * positions + 1.0 - total_vx) * (VELOCITY_LIMIT / total_vx)
    speed = jnp.where(parity == 0, speed, -speed)

    chain = [Own(value, True), Own(value, False), Row(value_inner_got), Row(value_outer_got)]
    costs = [Own(cost, True), Own(cost, False), Row(cost_inner_got), Row(cost_outer_got)]
    halo_rows = (halo_before(value_outer_got), halo_after(half_of(value, parity, parity)))

    def advanced(field, bases, stepper):
        out = {}
        for targets in ((1, 2), (0, 3)):
            some = None if bases is None else [bases[t] for t in targets]
            got = advance(
                sizes, targets, field, some, halo_rows, vx_low, vx_high, vy_next, shared_first, stepper, accel_second, flags, push, speed
            )
            each = len(got) // 2
            out.update({t: got[each * i : each * (i + 1)] for i, t in enumerate(targets)})
        return out

    def settled(targets, updates, **kw):
        return settle(sizes, targets, [updates[t] for t in targets], [costs[t] for t in targets], flags, **kw)

    def exchange(edges):
        first, _, _, last, edge, _, _ = edges
        low, high, row = from_low_vx(last), from_high_vx(first), partner(edge)
        return low, high, row, share(edge_maxima(edges, low, high, row, flags))

    every = (0, 1, 2, 3)

    updates = advanced(chain, None, shared_first)
    (outer, inner), edges = settled((0, 1), updates)
    after = halo_after(outer)
    (far,), edges = settled((3,), updates, prior=((0, 1), edges))
    before = halo_before(far)
    (near,), edges = settled((2,), updates, prior=((0, 1, 3), edges))
    halo_rows = (before, after)
    middle = [Row(f) for f in (outer, inner, near, far)]
    vx_low, vx_high, vy_next, shared = exchange(edges)

    updates = advanced(middle, chain, shared_first)
    fields, edges = settled(every, updates, damping=(shared_first, shared_first, shared, 0.5))
    halo_rows = (halo_before(fields[3]), halo_after(fields[0]))
    chain = [Row(f) for f in fields]
    vx_low, vx_high, vy_next, shared_second = exchange(edges)

    updates = advanced(chain, None, None)
    fields, edges = settled(every, updates, damping=(shared_first, shared_second, shared_second, 1.0), fields=chain)
    halo_rows = (halo_before(fields[3]), halo_after(fields[0]))
    middle = [Row(f) for f in fields]
    vx_low, vx_high, vy_next, shared = exchange(edges)

    updates = advanced(middle, chain, shared_second)
    damping = (shared_first, shared_second, shared, 0.5)
    (inner, near), (least_inner,) = settled((1, 2), updates, damping=damping, with_edges=False)
    inner_got = partner(near)
    (outer, far), (least_outer,) = settled((0, 3), updates, damping=damping, with_edges=False)
    outer_got = partner(far)
    least = lax.pmin(jnp.concatenate([least_outer, least_inner], axis=0), "vx")
    least_got = partner(least[1::2][::-1])
    final = place(flags, [(True, outer), (False, inner)], 0, None, value.shape)
    final = place(flags, [(False, inner_got)], 1, final, value.shape)
    final = place(flags, [(True, outer_got)], 1, final, value.shape)
    funnel = jnp.minimum(least[0::2], least_got[::-1])
    return final, jnp.concatenate([pick(funnel, parity), pick(funnel, 1 - parity)], axis=0)


def solution(mesh):
    placed = (P("px", "vx", None, None), P("px", "vx", None, None), P("px", "vx"), P())
    return jax.shard_map(
        per_device,
        mesh=mesh,
        in_specs=placed,
        out_specs=(P("px", "vx", None, None), P("px", None)),
        check_vma=False,
    )
```

time: 380 us -> 309 us (0.81)
  blocking collectives: 56.3 us -> 6.16 us
  starting transfers between devices: 53 us -> 85.7 us
  Pallas kernels: 91.9 us -> 68.7 us
  other arithmetic: 15.4 us -> 1.34 us
  local copies, waits for them, and re-layouts: 26.9 us -> 15.4 us
  waiting for transfers between devices: 134 us -> 129 us
    ppermute x13, waiting for transfers between devices: 133 us -> 57.8 us  [partner(): return lax.ppermute(x, 'px', [(i, i ^ 1) for i in range(n_px)])]
    ppermute x0 -> x20, waiting for transfers between devices: none -> 71.4 us  [share(): other = lax.ppermute(maxima, axis, [(i, i ^ apart) for i in range(count)])]
    all_to_all x3 -> x0, blocking collectives: 49.8 us -> none  [share(): return lax.all_to_all(maxima, ('px', 'vx'), 0, 0, tiled=True)]
    ppermute x0 -> x20, starting transfers between devices: none -> 36.4 us  [share(): other = lax.ppermute(maxima, axis, [(i, i ^ apart) for i in range(count)])]
    pallas_call x10 -> x22, Pallas kernels: 91.9 us -> 68.7 us  [the longest x8 38.3 us: advance(): pl.pallas_call(body, out_shape=[f32(cells_v, half, width)] * n_out, in_sp...]
    unnamed x84 -> x15, local copies, waits for them, and re-layouts: 9.04 us -> 2.37 us
    pallas_call x1 -> x0, other arithmetic: 6.15 us -> none  [sweep(): pl.pallas_call(body, out_shape=shapes, in_specs=[scalars()] * 3 + [whole(...]
  transfers between devices with their start and end apart: 30 -> 49, of which waited for: 7 -> 23; matrix products, arithmetic and copies ran while one was open for 9% -> 5% of each run, Pallas kernels for 8% -> 15%
where the time goes in v2:
time: 309 us; the launch traced here: 308 us
  waiting for transfers between devices  129 us (42%)
  starting transfers between devices  85.7 us (28%)
  Pallas kernels  68.7 us (22%)
  local copies, waits for them, and re-layouts  15.4 us (5%)
  blocking collectives  6.16 us (2%)
    ppermute x20, waiting for transfers between devices, share(): other = lax.ppermute(maxima, axis, [(i, i ^ apart) for i in range(count)])  71.4 us
    ppermute x13, waiting for transfers between devices, partner(): return lax.ppermute(x, 'px', [(i, i ^ 1) for i in range(n_px)])  57.8 us
    pallas_call x8, Pallas kernels, advance(): pl.pallas_call(body, out_shape=[f32(cells_v, half, width)] * n_out, in_sp...  38.3 us
    ppermute x20, starting transfers between devices, share(): other = lax.ppermute(maxima, axis, [(i, i ^ apart) for i in range(count)])  36.4 us
    pallas_call x7, Pallas kernels, settle(): pl.pallas_call(body, out_shape=shapes, in_specs=[scalars()] + [whole()] *...  17.3 us
    ppermute x13, starting transfers between devices, partner(): return lax.ppermute(x, 'px', [(i, i ^ 1) for i in range(n_px)])  17.2 us
    ppermute x4, starting transfers between devices, halo_before(): return lax.ppermute(outermost, 'px', moves)  16.3 us
    pallas_call x3, Pallas kernels, place(): pl.pallas_call(body, grid_spec=pltpu.PrefetchScalarGridSpec(num_scalar_pr...  8.83 us
  transfers between devices with their start and end apart: 49, of which 23 were waited for; matrix products, arithmetic and copies ran while one was open for 5% of the time, Pallas kernels for 15%

profile of v2, /device:TPU:0, one launch (start us, length us, event | category | flops | bytes accessed | tf_op | source)
XLA Modules:
  0.0 307.9 jit_solution(5334188611026354485)
XLA Ops:
  0.6 3.0 collective-permute-start
  4.9 3.7 %dynamic-slice_bitcast_fusion = (f32[24,32,384]{2,1,0:T(8,128)S(1)}, f32[24,32,384]{2,1,0:T(8,128)}, f32[24,32,384]{2,1,0:T(8,128)}) fusion(f32[2,24,64,384]{3,2,1,0:T(8,128)} %refs_4_.1, s32[]{:T(128)S(6)} %select_n.74, s32[]{:T(128)S(6)} %select_n.79, s32[]{:T(128)S(6)} %select_n.78, s32[]{:T(128)S(6)} %select_n.75), kind=kLoop, calls=%fused_computation | loop fusion | bytes 7077904 | tf_op jit(solution)/shard_map/squeeze | solution.py:552
  8.5 2.0 collective-permute-start.2
  15.4 3.2 %dynamic-slice_bitcast_fusion.2 = (f32[24,32,384]{2,1,0:T(8,128)}, f32[24,32,384]{2,1,0:T(8,128)}) fusion(f32[2,24,64,384]{3,2,1,0:T(8,128)} %refs_6_.7, s32[]{:T(128)S(6)} %select_n.74, s32[]{:T(128)S(6)} %select_n.78, s32[]{:T(128)S(6)} %select_n.75), kind=kLoop, calls=%fused_computation.2 | loop fusion | bytes 4718604 | tf_op jit(solution)/shard_map/squeeze | solution.py:552
  20.1 2.3 copy-done
  22.5 2.2 first_maxima.1
  24.7 3.1 %collective-permute-start.9 = (f32[8,128]{1,0:T(8,128)S(1)}, f32[8,128]{1,0:T(8,128)S(1)}, u32[]{:S(2)}, u32[]{:S(2)}) collective-permute-start(f32[8,128]{1,0:T(8,128)S(1)} %first_maxima.1), channel_id=1, source_target_pairs={{0,1},{1,0},{2,3},{3,2},{4,5},{5,4},{6,7},{7,6},{8,9},{9,8},{10,11... | collective-permute-start | bytes 12296 | tf_op jit(solution)/shard_map/ppermute | solution.py:546
  28.6 2.2 collective-permute-start.10
  30.9 6.8 %collective-permute-done.2.refs_2_.refs_7_ = f32[24,32,384]{2,1,0:T(8,128)S(1)} collective-permute-done((f32[24,32,384]{2,1,0:T(8,128)}, f32[24,32,384]{2,1,0:T(8,128)S(1)}, u32[]{:S(2)}, u32[]{:S(2)}) %collective-permute-start.2) | collective-permute-done | bytes 1179680 | tf_op jit(solution)/shard_map/ppermute | solution.py:526
  37.7 2.0 collective-permute-start.15
  39.6 3.5 %collective-permute-start.3 = (f32[24,32,384]{2,1,0:T(8,128)S(1)}, f32[24,32,384]{2,1,0:T(8,128)S(1)}, u32[]{:S(2)}, u32[]{:S(2)}) collective-permute-start(f32[24,32,384]{2,1,0:T(8,128)S(1)} %collective-permute-done.2.refs_2_.refs_7_), channel_id=1, source_target_pairs={{0,8},{8,16},{16,24},{12,4},{20,12},{28,20},{1,9},{9,17},{17,25},{... | collective-permute-start | bytes 3538952 | tf_op jit(solution)/shard_map/ppermute | solution.py:536
  43.4 43.5 %collective-permute-done.11 = f32[8,128]{1,0:T(8,128)S(1)} collective-permute-done((f32[8,128]{1,0:T(8,128)S(1)}, f32[8,128]{1,0:T(8,128)S(1)}, u32[]{:S(2)}, u32[]{:S(2)}) %collective-permute-start.11) | collective-permute-done | bytes 4128 | tf_op jit(solution)/shard_map/ppermute | solution.py:546
  86.8 1.8 collective-permute-start.12
  88.6 1.8 collective-permute-done.12
  90.5 2.8 collective-permute-start.13
  93.3 1.7 collective-permute-done.13
  95.0 1.7 collective-permute-start.7
  96.7 6.0 %collective-permute-done.7 = f32[4,32,384]{2,1,0:T(8,128)S(1)} collective-permute-done((f32[4,32,384]{2,1,0:T(8,128)S(1)}, f32[4,32,384]{2,1,0:T(8,128)S(1)}, u32[]{:S(2)}, u32[]{:S(2)}) %collective-permute-start.7) | collective-permute-done | bytes 196640 | tf_op jit(solution)/shard_map/ppermute | solution.py:526
  102.8 1.8 collective-permute-start.14
  104.6 4.9 %advance_12.4 = (f32[24,32,384]{2,1,0:T(8,128)S(1)}, f32[24,32,384]{2,1,0:T(8,128)S(1)}) custom-call(s32[5]{0:T(128)S(1)} %stack.39.flags_ref, f32[4,24]{1,0:T(4,128)S(1)} %pad_maximum_fusion.6.push_ref, f32[24]{0:T(128)S(1)} %broadcast_select_fusion.speed_ref, f32[2,24,64,384]{3,2,1,0:T(8,128)S(1)} %copy-done.1, ...), custom_call_target="tpu_custom_call" | custom-call | flops 26542080 | bytes 2359296 | tf_op jit(solution)/shard_map/advance_12/pallas_call | solution.py:256
  109.6 5.1 %advance_03.4 = (f32[24,32,384]{2,1,0:T(8,128)S(1)}, f32[24,32,384]{2,1,0:T(8,128)S(1)}) custom-call(s32[5]{0:T(128)S(1)} %stack.39.flags_ref, f32[4,24]{1,0:T(4,128)S(1)} %pad_maximum_fusion.6.push_ref, f32[24]{0:T(128)S(1)} %broadcast_select_fusion.speed_ref, f32[2,24,64,384]{3,2,1,0:T(8,128)S(1)} %copy-done.1, ...), custom_call_target="tpu_custom_call" | custom-call | flops 26542080 | bytes 2359296 | tf_op jit(solution)/shard_map/advance_03/pallas_call | solution.py:256
  114.7 1.8 settle_01.1
  117.6 3.6 %collective-permute-start.16 = (f32[24,32,384]{2,1,0:T(8,128)S(1)}, f32[24,32,384]{2,1,0:T(8,128)S(1)}, u32[]{:S(2)}, u32[]{:S(2)}) collective-permute-start(f32[24,32,384]{2,1,0:T(8,128)S(1)} %get-tuple-element.124.refs_3_), channel_id=1, source_target_pairs={{0,8},{8,16},{16,24},{12,4},{20,12},{28,20},{1,9},{9,17},{17,25},{... | collective-permute-start | bytes 3538952 | tf_op jit(solution)/shard_map/ppermute | solution.py:536
  122.5 3.4 %collective-permute-done.14.refs_1_.refs_13_.refs_7_ = f32[24,32,384]{2,1,0:T(8,128)S(1)} collective-permute-done((f32[24,32,384]{2,1,0:T(8,128)S(1)}, f32[24,32,384]{2,1,0:T(8,128)S(1)}, u32[]{:S(2)}, u32[]{:S(2)}) %collective-permute-start.14) | collective-permute-done | bytes 1179680 | tf_op jit(solution)/shard_map/ppermute | solution.py:526
  131.2 3.7 %collective-permute-done.20.refs_10_.refs_8_.next_ref = f32[4,24,384]{2,1,0:T(8,128)S(1)} collective-permute-done((f32[4,24,384]{2,1,0:T(8,128)S(1)}, f32[4,24,384]{2,1,0:T(8,128)S(1)}, u32[]{:S(2)}, u32[]{:S(2)}) %collective-permute-start.20) | collective-permute-done | bytes 147488 | tf_op jit(solution)/shard_map/ppermute | solution.py:526
  135.6 3.0 collective-permute-start.21
  139.5 1.8 collective-permute-start.22
  141.3 1.8 collective-permute-done.22
  144.6 2.1 collective-permute-done.23
  146.7 1.6 collective-permute-start.24
  148.3 2.0 collective-permute-done.24
  150.3 2.6 collective-permute-start.25
  152.9 4.8 %advance_12.5 = (f32[24,32,384]{2,1,0:T(8,128)S(1)}, f32[24,32,384]{2,1,0:T(8,128)S(1)}, f32[24,32,384]{2,1,0:T(8,128)S(1)}, f32[24,32,384]{2,1,0:T(8,128)S(1)},...) custom-call(s32[5]{0:T(128)S(1)} %stack.39.flags_ref, f32[4,24]{1,0:T(4,128)S(1)} %pad_maximum_fusion.6.push_ref, ...), custom_call_target="tpu_custom_call" | custom-call | flops 26542080 | bytes 2359296 | tf_op jit(solution)/shard_map/advance_12/pallas_call | solution.py:256
  157.7 5.0 %advance_03.5 = (f32[24,32,384]{2,1,0:T(8,128)S(1)}, f32[24,32,384]{2,1,0:T(8,128)S(1)}, f32[24,32,384]{2,1,0:T(8,128)S(1)}, f32[24,32,384]{2,1,0:T(8,128)S(1)},...) custom-call(s32[5]{0:T(128)S(1)} %stack.39.flags_ref, f32[4,24]{1,0:T(4,128)S(1)} %pad_maximum_fusion.6.push_ref, ...), custom_call_target="tpu_custom_call" | custom-call | flops 26542080 | bytes 2359296 | tf_op jit(solution)/shard_map/advance_03/pallas_call | solution.py:256
  162.7 3.8 %settle_0123.2 = (f32[24,32,384]{2,1,0:T(8,128)S(1)}, f32[24,32,384]{2,1,0:T(8,128)S(1)}, f32[24,32,384]{2,1,0:T(8,128)S(1)}, f32[24,32,384]{2,1,0:T(8,128)S(1)}...) custom-call(s32[5]{0:T(128)S(1)} %stack.39.flags_ref, ...), custom_call_target="tpu_custom_call" | custom-call | flops 17694720 | bytes 4718592 | tf_op jit(solution)/shard_map/settle_0123/pallas_call | solution.py:378
  167.8 4.6 %collective-permute-start.26 = (f32[24,32,384]{2,1,0:T(8,128)S(1)}, f32[24,32,384]{2,1,0:T(8,128)S(1)}, u32[]{:S(2)}, u32[]{:S(2)}) collective-permute-start(f32[24,32,384]{2,1,0:T(8,128)S(1)} %get-tuple-element.147.refs_3_.refs_18_.refs_7_), channel_id=1, source_target_pairs={{0,8},{8,16},{16,24},{12,4},{20,12},{28,20},{1,9},{9,17},{17,25},{... | collective-permute-start | bytes 3538952 | tf_op jit(solution)/shard_map/ppermute | solution.py:536
  175.5 4.7 %collective-permute-done.30.refs_8_.refs_6_.next_ref = f32[4,24,384]{2,1,0:T(8,128)S(1)} collective-permute-done((f32[4,24,384]{2,1,0:T(8,128)S(1)}, f32[4,24,384]{2,1,0:T(8,128)S(1)}, u32[]{:S(2)}, u32[]{:S(2)}) %collective-permute-start.30) | collective-permute-done | bytes 147488 | tf_op jit(solution)/shard_map/ppermute | solution.py:526
  181.0 3.4 %collective-permute-start.31 = (f32[8,128]{1,0:T(8,128)S(1)}, f32[8,128]{1,0:T(8,128)S(1)}, u32[]{:S(2)}, u32[]{:S(2)}) collective-permute-start(f32[8,128]{1,0:T(8,128)S(1)} %edge_maxima.4), channel_id=1, source_target_pairs={{0,1},{1,0},{2,3},{3,2},{4,5},{5,4},{6,7},{7,6},{8,9},{9,8},{10,11... | collective-permute-start | bytes 12296 | tf_op jit(solution)/shard_map/ppermute | solution.py:546
  185.2 1.8 collective-permute-start.32
  187.0 1.8 collective-permute-done.32
  189.2 3.2 %collective-permute-done.33 = f32[8,128]{1,0:T(8,128)S(1)} collective-permute-done((f32[8,128]{1,0:T(8,128)S(1)}, f32[8,128]{1,0:T(8,128)S(1)}, u32[]{:S(2)}, u32[]{:S(2)}) %collective-permute-start.33) | collective-permute-done | bytes 4128 | tf_op jit(solution)/shard_map/ppermute | solution.py:546
  193.9 2.1 collective-permute-done.34
  197.0 4.4 %advance_12.6 = (f32[24,32,384]{2,1,0:T(8,128)S(1)}, f32[24,32,384]{2,1,0:T(8,128)S(1)}, f32[24,32,384]{2,1,0:T(8,128)S(1)}, f32[24,32,384]{2,1,0:T(8,128)S(1)},...) custom-call(s32[5]{0:T(128)S(1)} %stack.39.flags_ref, f32[4,24]{1,0:T(4,128)S(1)} %pad_maximum_fusion.6.push_ref, ...), custom_call_target="tpu_custom_call" | custom-call | flops 26542080 | bytes 2359296 | tf_op jit(solution)/shard_map/advance_12/pallas_call | solution.py:256
  201.4 4.6 %advance_03.6 = (f32[24,32,384]{2,1,0:T(8,128)S(1)}, f32[24,32,384]{2,1,0:T(8,128)S(1)}, f32[24,32,384]{2,1,0:T(8,128)S(1)}, f32[24,32,384]{2,1,0:T(8,128)S(1)},...) custom-call(s32[5]{0:T(128)S(1)} %stack.39.flags_ref, f32[4,24]{1,0:T(4,128)S(1)} %pad_maximum_fusion.6.push_ref, ...), custom_call_target="tpu_custom_call" | custom-call | flops 26542080 | bytes 2359296 | tf_op jit(solution)/shard_map/advance_03/pallas_call | solution.py:256
  206.0 4.2 %settle_0123.3 = (f32[24,32,384]{2,1,0:T(8,128)S(1)}, f32[24,32,384]{2,1,0:T(8,128)S(1)}, f32[24,32,384]{2,1,0:T(8,128)S(1)}, f32[24,32,384]{2,1,0:T(8,128)S(1)}...) custom-call(s32[5]{0:T(128)S(1)} %stack.39.flags_ref, ...), custom_call_target="tpu_custom_call" | custom-call | flops 17694720 | bytes 4718592 | tf_op jit(solution)/shard_map/settle_0123/pallas_call | solution.py:378
  211.5 4.6 %collective-permute-start.36 = (f32[24,32,384]{2,1,0:T(8,128)S(1)}, f32[24,32,384]{2,1,0:T(8,128)S(1)}, u32[]{:S(2)}, u32[]{:S(2)}) collective-permute-start(f32[24,32,384]{2,1,0:T(8,128)S(1)} %get-tuple-element.170.refs_3_), channel_id=1, source_target_pairs={{0,8},{8,16},{16,24},{12,4},{20,12},{28,20},{1,9},{9,17},{17,25},{... | collective-permute-start | bytes 3538952 | tf_op jit(solution)/shard_map/ppermute | solution.py:536
  219.0 5.1 %collective-permute-done.40.refs_10_.next_ref.refs_8_ = f32[4,24,384]{2,1,0:T(8,128)S(1)} collective-permute-done((f32[4,24,384]{2,1,0:T(8,128)S(1)}, f32[4,24,384]{2,1,0:T(8,128)S(1)}, u32[]{:S(2)}, u32[]{:S(2)}) %collective-permute-start.40) | collective-permute-done | bytes 147488 | tf_op jit(solution)/shard_map/ppermute | solution.py:526
  224.9 3.2 %collective-permute-start.41 = (f32[8,128]{1,0:T(8,128)S(1)}, f32[8,128]{1,0:T(8,128)S(1)}, u32[]{:S(2)}, u32[]{:S(2)}) collective-permute-start(f32[8,128]{1,0:T(8,128)S(1)} %edge_maxima.5), channel_id=1, source_target_pairs={{0,1},{1,0},{2,3},{3,2},{4,5},{5,4},{6,7},{7,6},{8,9},{9,8},{10,11... | collective-permute-start | bytes 12296 | tf_op jit(solution)/shard_map/ppermute | solution.py:546
  228.9 2.0 collective-permute-start.42
  230.9 1.6 collective-permute-done.42
  232.5 3.6 %collective-permute-done.43 = f32[8,128]{1,0:T(8,128)S(1)} collective-permute-done((f32[8,128]{1,0:T(8,128)S(1)}, f32[8,128]{1,0:T(8,128)S(1)}, u32[]{:S(2)}, u32[]{:S(2)}) %collective-permute-start.43) | collective-permute-done | bytes 4128 | tf_op jit(solution)/shard_map/ppermute | solution.py:546
  236.8 2.9 collective-permute-done.44
  239.7 2.0 collective-permute-start.45
  241.7 4.7 %advance_12.7 = (f32[24,32,384]{2,1,0:T(8,128)S(1)}, f32[24,32,384]{2,1,0:T(8,128)S(1)}, f32[24,32,384]{2,1,0:T(8,128)S(1)}, f32[24,32,384]{2,1,0:T(8,128)S(1)},...) custom-call(s32[5]{0:T(128)S(1)} %stack.39.flags_ref, f32[4,24]{1,0:T(4,128)S(1)} %pad_maximum_fusion.6.push_ref, ...), custom_call_target="tpu_custom_call" | custom-call | flops 26542080 | bytes 2359296 | tf_op jit(solution)/shard_map/advance_12/pallas_call | solution.py:256
  246.4 2.6 settle_12.1
  249.0 2.5 collective-permute-start.47
  251.5 4.9 %advance_03.7 = (f32[24,32,384]{2,1,0:T(8,128)S(1)}, f32[24,32,384]{2,1,0:T(8,128)S(1)}, f32[24,32,384]{2,1,0:T(8,128)S(1)}, f32[24,32,384]{2,1,0:T(8,128)S(1)},...) custom-call(s32[5]{0:T(128)S(1)} %stack.39.flags_ref, f32[4,24]{1,0:T(4,128)S(1)} %pad_maximum_fusion.6.push_ref, ...), custom_call_target="tpu_custom_call" | custom-call | flops 26542080 | bytes 2359296 | tf_op jit(solution)/shard_map/advance_03/pallas_call | solution.py:256
  256.4 2.6 settle_03.1
  259.6 6.2 %pmin.7 = f32[4,384]{1,0:T(4,128)S(1)} all-reduce(f32[4,384]{1,0:T(4,128)} %pad_maximum_fusion.4), channel_id=1, replica_groups=mesh['px'=8,'vx'=4] {'vx'}, use_global_device_ids=true, to_apply=%region_0.1 | all-reduce | flops 1536 | bytes 12288 | tf_op jit(solution)/shard_map/pmin | solution.py:646
  267.0 2.0 collective-permute-start.48
  269.0 3.0 place.3.refs_1_
  272.1 28.0 %collective-permute-done.48 = f32[2,384]{1,0:T(2,128)} collective-permute-done((f32[2,384]{1,0:T(2,128)}, f32[2,384]{1,0:T(2,128)}, u32[]{:S(2)}, u32[]{:S(2)}) %collective-permute-start.48) | collective-permute-done | bytes 3104 | tf_op jit(solution)/shard_map/ppermute | solution.py:526
  302.1 2.1 place.4.refs_1_
  304.2 3.7 %place.5 = f32[2,24,64,384]{3,2,1,0:T(8,128)} custom-call(s32[5]{0:T(128)S(1)} %stack.39.flags_ref, f32[24,32,384]{2,1,0:T(8,128)} %collective-permute-done.46.refs_0_, f32[2,24,64,384]{3,2,1,0:T(8,128)} %place.4.refs_1_), custom_call_target="tpu_custom_call", output_to_operand_aliasing={{}: (2, {})} | custom-call | tf_op jit(solution)/shard_map/place/pallas_call | solution.py:492
  (122 shorter events, 38.4 us)
Async XLA Ops:
  0.6 18.1 %collective-permute-start = (f32[2,24]{1,0:T(2,128)}, f32[2,24]{1,0:T(2,128)S(1)}, u32[]{:S(2)}, u32[]{:S(2)}) collective-permute-start(f32[2,24]{1,0:T(2,128)} %first_ref.1), channel_id=1, source_target_pairs={{0,4},{4,0},{8,12},{12,8},{16,20},{20,16},{24,28},{28,24},{1,5},{5... | collective-permute-start | bytes 584 | tf_op jit(solution)/shard_map/ppermute | solution.py:526
  4.8 34.9 %collective-permute-start.8 = (f32[2,24,384]{2,1,0:T(8,128)S(1)}, f32[2,24,384]{2,1,0:T(8,128)S(1)}, u32[]{:S(2)}, u32[]{:S(2)}) collective-permute-start(f32[2,24,384]{2,1,0:T(8,128)S(1)} %bitcast.32), channel_id=1, source_target_pairs={{0,4},{4,0},{8,12},{12,8},{16,20},{20,16},{24,28},{28,24},{1,5},{5... | collective-permute-start | bytes 221192 | tf_op jit(solution)/shard_map/ppermute | solution.py:526
  4.9 9.4 %copy-start.3 = (f32[2,24]{1,0:T(2,128)S(1)}, f32[2,24]{1,0:T(2,128)}, u32[]{:S(2)}) copy-start(f32[2,24]{1,0:T(2,128)} %first_ref.1) | copy-start | bytes 580
  8.5 29.1 %collective-permute-start.2 = (f32[24,32,384]{2,1,0:T(8,128)}, f32[24,32,384]{2,1,0:T(8,128)S(1)}, u32[]{:S(2)}, u32[]{:S(2)}) collective-permute-start(f32[24,32,384]{2,1,0:T(8,128)} %get-tuple-element.201), channel_id=1, source_target_pairs={{0,4},{4,0},{8,12},{12,8},{16,20},{20,16},{24,28},{28,24},{1,5},{5... | collective-permute-start | bytes 3538952 | tf_op jit(solution)/shard_map/ppermute | solution.py:526
  11.6 7.2 %collective-permute-start.5 = (f32[2,64,384]{2,1,0:T(8,128)S(1)}, f32[2,64,384]{2,1,0:T(8,128)S(1)}, u32[]{:S(2)}, u32[]{:S(2)}) collective-permute-start(f32[2,64,384]{2,1,0:T(8,128)S(1)} %get-tuple-element.198), channel_id=1, source_target_pairs={{0,1},{1,2},{2,3},{4,5},{5,6},{6,7},{8,9},{9,10},{10,11},{12,13},{... | collective-permute-start | bytes 589832 | tf_op jit(solution)/shard_map/ppermute | solution.py:529
  12.9 7.2 %collective-permute-start.6 = (f32[2,64,384]{2,1,0:T(8,128)S(1)}, f32[2,64,384]{2,1,0:T(8,128)S(1)}, u32[]{:S(2)}, u32[]{:S(2)}) collective-permute-start(f32[2,64,384]{2,1,0:T(8,128)S(1)} %get-tuple-element.199), channel_id=1, source_target_pairs={{1,0},{2,1},{3,2},{5,4},{6,5},{7,6},{9,8},{10,9},{11,10},{13,12},{... | collective-permute-start | bytes 589832 | tf_op jit(solution)/shard_map/ppermute | solution.py:532
  15.4 4.7 %copy-start.2 = (f32[64,384]{1,0:T(8,128)S(1)}, f32[64,384]{1,0:T(8,128)}, u32[]{:S(2)}) copy-start(f32[64,384]{1,0:T(8,128)} %refs_9_.5) | copy-start | bytes 294916
  18.7 84.0 %collective-permute-start.1 = (f32[24,32,384]{2,1,0:T(8,128)}, f32[24,32,384]{2,1,0:T(8,128)S(1)}, u32[]{:S(2)}, u32[]{:S(2)}) collective-permute-start(f32[24,32,384]{2,1,0:T(8,128)} %get-tuple-element.202), channel_id=1, source_target_pairs={{0,4},{4,0},{8,12},{12,8},{16,20},{20,16},{24,28},{28,24},{1,5},{5... | collective-permute-start | bytes 3538952 | tf_op jit(solution)/shard_map/ppermute | solution.py:526
  18.8 90.8 %collective-permute-start.4 = (f32[24,32,384]{2,1,0:T(8,128)S(1)}, f32[24,32,384]{2,1,0:T(8,128)S(1)}, u32[]{:S(2)}, u32[]{:S(2)}) collective-permute-start(f32[24,32,384]{2,1,0:T(8,128)S(1)} %get-tuple-element.200), channel_id=1, source_target_pairs={{8,0},{16,8},{24,16},{4,12},{12,20},{20,28},{9,1},{17,9},{25,17},{... | collective-permute-start | bytes 3538952 | tf_op jit(solution)/shard_map/ppermute | solution.py:540
  20.1 2.3 copy-start
  22.5 82.1 %copy-start.1 = (f32[2,24,64,384]{3,2,1,0:T(8,128)S(1)}, f32[2,24,64,384]{3,2,1,0:T(8,128)}, u32[]{:S(2)}) copy-start(f32[2,24,64,384]{3,2,1,0:T(8,128)} %refs_4_.1) | copy-start | bytes 14155780
  24.7 4.0 %collective-permute-start.9 = (f32[8,128]{1,0:T(8,128)S(1)}, f32[8,128]{1,0:T(8,128)S(1)}, u32[]{:S(2)}, u32[]{:S(2)}) collective-permute-start(f32[8,128]{1,0:T(8,128)S(1)} %first_maxima.1), channel_id=1, source_target_pairs={{0,1},{1,0},{2,3},{3,2},{4,5},{5,4},{6,7},{7,6},{8,9},{9,8},{10,11... | collective-permute-start | bytes 12296 | tf_op jit(solution)/shard_map/ppermute | solution.py:546
  28.6 14.6 %collective-permute-start.10 = (f32[8,128]{1,0:T(8,128)S(1)}, f32[8,128]{1,0:T(8,128)S(1)}, u32[]{:S(2)}, u32[]{:S(2)}) collective-permute-start(f32[8,128]{1,0:T(8,128)S(1)} %max.60), channel_id=1, source_target_pairs={{0,2},{1,3},{2,0},{3,1},{4,6},{5,7},{6,4},{7,5},{8,10},{9,11},{10,... | collective-permute-start | bytes 12296 | tf_op jit(solution)/shard_map/ppermute | solution.py:546
  37.7 78.8 %collective-permute-start.15 = (f32[24,32,384]{2,1,0:T(8,128)}, f32[24,32,384]{2,1,0:T(8,128)S(1)}, u32[]{:S(2)}, u32[]{:S(2)}) collective-permute-start(f32[24,32,384]{2,1,0:T(8,128)} %get-tuple-element.108), channel_id=1, source_target_pairs={{0,4},{4,0},{8,12},{12,8},{16,20},{20,16},{24,28},{28,24},{1,5},{5... | collective-permute-start | bytes 3538952 | tf_op jit(solution)/shard_map/ppermute | solution.py:526
  39.6 69.9 %collective-permute-start.3 = (f32[24,32,384]{2,1,0:T(8,128)S(1)}, f32[24,32,384]{2,1,0:T(8,128)S(1)}, u32[]{:S(2)}, u32[]{:S(2)}) collective-permute-start(f32[24,32,384]{2,1,0:T(8,128)S(1)} %collective-permute-done.2.refs_2_.refs_7_), channel_id=1, source_target_pairs={{0,8},{8,16},{16,24},{12,4},{20,12},{28,20},{1,9},{9,17},{17,25},{... | collective-permute-start | bytes 3538952 | tf_op jit(solution)/shard_map/ppermute | solution.py:536
  43.2 59.5 %copy-start.4 = (f32[24,32,384]{2,1,0:T(8,128)S(1)}, f32[24,32,384]{2,1,0:T(8,128)}, u32[]{:S(2)}) copy-start(f32[24,32,384]{2,1,0:T(8,128)} %get-tuple-element.106) | copy-start | bytes 3538948
  43.3 43.6 %collective-permute-start.11 = (f32[8,128]{1,0:T(8,128)S(1)}, f32[8,128]{1,0:T(8,128)S(1)}, u32[]{:S(2)}, u32[]{:S(2)}) collective-permute-start(f32[8,128]{1,0:T(8,128)S(1)} %max.61), channel_id=1, source_target_pairs={{0,4},{4,0},{8,12},{12,8},{16,20},{20,16},{24,28},{28,24},{1,5},{5... | collective-permute-start | bytes 12296 | tf_op jit(solution)/shard_map/ppermute | solution.py:546
  86.8 3.6 %collective-permute-start.12 = (f32[8,128]{1,0:T(8,128)S(1)}, f32[8,128]{1,0:T(8,128)S(1)}, u32[]{:S(2)}, u32[]{:S(2)}) collective-permute-start(f32[8,128]{1,0:T(8,128)S(1)} %max.62), channel_id=1, source_target_pairs={{0,8},{4,12},{8,0},{12,4},{16,24},{20,28},{24,16},{28,20},{1,9},{5... | collective-permute-start | bytes 12296 | tf_op jit(solution)/shard_map/ppermute | solution.py:546
  90.5 4.5 %collective-permute-start.13 = (f32[8,128]{1,0:T(8,128)S(1)}, f32[8,128]{1,0:T(8,128)S(1)}, u32[]{:S(2)}, u32[]{:S(2)}) collective-permute-start(f32[8,128]{1,0:T(8,128)S(1)} %max.63), channel_id=1, source_target_pairs={{0,16},{4,20},{8,24},{12,28},{16,0},{20,4},{24,8},{28,12},{1,17},{... | collective-permute-start | bytes 12296 | tf_op jit(solution)/shard_map/ppermute | solution.py:546
  95.0 7.7 %collective-permute-start.7 = (f32[4,32,384]{2,1,0:T(8,128)S(1)}, f32[4,32,384]{2,1,0:T(8,128)S(1)}, u32[]{:S(2)}, u32[]{:S(2)}) collective-permute-start(f32[4,32,384]{2,1,0:T(8,128)S(1)} %pad_maximum_fusion), channel_id=1, source_target_pairs={{0,4},{4,0},{8,12},{12,8},{16,20},{20,16},{24,28},{28,24},{1,5},{5... | collective-permute-start | bytes 589832 | tf_op jit(solution)/shard_map/ppermute | solution.py:526
  102.8 23.1 %collective-permute-start.14 = (f32[24,32,384]{2,1,0:T(8,128)S(1)}, f32[24,32,384]{2,1,0:T(8,128)S(1)}, u32[]{:S(2)}, u32[]{:S(2)}) collective-permute-start(f32[24,32,384]{2,1,0:T(8,128)S(1)} %copy-done.4), channel_id=1, source_target_pairs={{0,4},{4,0},{8,12},{12,8},{16,20},{20,16},{24,28},{28,24},{1,5},{5... | collective-permute-start | bytes 3538952 | tf_op jit(solution)/shard_map/ppermute | solution.py:526
  104.6 10.0 %slice-start = ((s8[4718592]{0:T(1024)(128)(4,1)}), s8[4194304]{0:T(1024)(128)(4,1)S(1)}, s32[]{:S(2)}) async-start(s8[4718592]{0:T(1024)(128)(4,1)} %bitcast.30), calls=%async_computation | async-start | bytes 8388608
  109.6 5.1 %slice-start.1 = ((s8[4718592]{0:T(1024)(128)(4,1)}), s8[524288]{0:T(1024)(128)(4,1)S(1)}, s32[]{:S(2)}) async-start(s8[4718592]{0:T(1024)(128)(4,1)} %bitcast.30), calls=%async_computation.1 | async-start | bytes 1048576
  117.6 40.1 %collective-permute-start.16 = (f32[24,32,384]{2,1,0:T(8,128)S(1)}, f32[24,32,384]{2,1,0:T(8,128)S(1)}, u32[]{:S(2)}, u32[]{:S(2)}) collective-permute-start(f32[24,32,384]{2,1,0:T(8,128)S(1)} %get-tuple-element.124.refs_3_), channel_id=1, source_target_pairs={{0,8},{8,16},{16,24},{12,4},{20,12},{28,20},{1,9},{9,17},{17,25},{... | collective-permute-start | bytes 3538952 | tf_op jit(solution)/shard_map/ppermute | solution.py:536
  121.2 36.5 %collective-permute-start.17 = (f32[24,32,384]{2,1,0:T(8,128)S(1)}, f32[24,32,384]{2,1,0:T(8,128)S(1)}, u32[]{:S(2)}, u32[]{:S(2)}) collective-permute-start(f32[24,32,384]{2,1,0:T(8,128)S(1)} %get-tuple-element.103.refs_0_), channel_id=1, source_target_pairs={{8,0},{16,8},{24,16},{4,12},{12,20},{20,28},{9,1},{17,9},{25,17},{... | collective-permute-start | bytes 3538952 | tf_op jit(solution)/shard_map/ppermute | solution.py:540
  127.1 7.8 %collective-permute-start.18 = (f32[4,32,384]{2,1,0:T(8,128)S(1)}, f32[4,32,384]{2,1,0:T(8,128)S(1)}, u32[]{:S(2)}, u32[]{:S(2)}) collective-permute-start(f32[4,32,384]{2,1,0:T(8,128)S(1)} %get-tuple-element.125.last_ref), channel_id=1, source_target_pairs={{0,1},{1,2},{2,3},{4,5},{5,6},{6,7},{8,9},{9,10},{10,11},{12,13},{... | collective-permute-start | bytes 589832 | tf_op jit(solution)/shard_map/ppermute | solution.py:529
  128.4 6.5 %collective-permute-start.19 = (f32[4,32,384]{2,1,0:T(8,128)S(1)}, f32[4,32,384]{2,1,0:T(8,128)S(1)}, u32[]{:S(2)}, u32[]{:S(2)}) collective-permute-start(f32[4,32,384]{2,1,0:T(8,128)S(1)} %get-tuple-element.126.first_ref), channel_id=1, source_target_pairs={{1,0},{2,1},{3,2},{5,4},{6,5},{7,6},{9,8},{10,9},{11,10},{13,12},{... | collective-permute-start | bytes 589832 | tf_op jit(solution)/shard_map/ppermute | solution.py:532
  129.7 5.2 %collective-permute-start.20 = (f32[4,24,384]{2,1,0:T(8,128)S(1)}, f32[4,24,384]{2,1,0:T(8,128)S(1)}, u32[]{:S(2)}, u32[]{:S(2)}) collective-permute-start(f32[4,24,384]{2,1,0:T(8,128)S(1)} %get-tuple-element.127), channel_id=1, source_target_pairs={{0,4},{4,0},{8,12},{12,8},{16,20},{20,16},{24,28},{28,24},{1,5},{5... | collective-permute-start | bytes 442376 | tf_op jit(solution)/shard_map/ppermute | solution.py:526
  135.6 3.8 %collective-permute-start.21 = (f32[8,128]{1,0:T(8,128)S(1)}, f32[8,128]{1,0:T(8,128)S(1)}, u32[]{:S(2)}, u32[]{:S(2)}) collective-permute-start(f32[8,128]{1,0:T(8,128)S(1)} %edge_maxima.3), channel_id=1, source_target_pairs={{0,1},{1,0},{2,3},{3,2},{4,5},{5,4},{6,7},{7,6},{8,9},{9,8},{10,11... | collective-permute-start | bytes 12296 | tf_op jit(solution)/shard_map/ppermute | solution.py:546
  139.5 3.6 %collective-permute-start.22 = (f32[8,128]{1,0:T(8,128)S(1)}, f32[8,128]{1,0:T(8,128)S(1)}, u32[]{:S(2)}, u32[]{:S(2)}) collective-permute-start(f32[8,128]{1,0:T(8,128)S(1)} %max.65), channel_id=1, source_target_pairs={{0,2},{1,3},{2,0},{3,1},{4,6},{5,7},{6,4},{7,5},{8,10},{9,11},{10,... | collective-permute-start | bytes 12296 | tf_op jit(solution)/shard_map/ppermute | solution.py:546
  143.1 3.6 %collective-permute-start.23 = (f32[8,128]{1,0:T(8,128)S(1)}, f32[8,128]{1,0:T(8,128)S(1)}, u32[]{:S(2)}, u32[]{:S(2)}) collective-permute-start(f32[8,128]{1,0:T(8,128)S(1)} %max.66), channel_id=1, source_target_pairs={{0,4},{4,0},{8,12},{12,8},{16,20},{20,16},{24,28},{28,24},{1,5},{5... | collective-permute-start | bytes 12296 | tf_op jit(solution)/shard_map/ppermute | solution.py:546
  146.7 3.6 %collective-permute-start.24 = (f32[8,128]{1,0:T(8,128)S(1)}, f32[8,128]{1,0:T(8,128)S(1)}, u32[]{:S(2)}, u32[]{:S(2)}) collective-permute-start(f32[8,128]{1,0:T(8,128)S(1)} %max.67), channel_id=1, source_target_pairs={{0,8},{4,12},{8,0},{12,4},{16,24},{20,28},{24,16},{28,20},{1,9},{5... | collective-permute-start | bytes 12296 | tf_op jit(solution)/shard_map/ppermute | solution.py:546
  150.3 7.4 %collective-permute-start.25 = (f32[8,128]{1,0:T(8,128)S(1)}, f32[8,128]{1,0:T(8,128)S(1)}, u32[]{:S(2)}, u32[]{:S(2)}) collective-permute-start(f32[8,128]{1,0:T(8,128)S(1)} %max.68), channel_id=1, source_target_pairs={{0,16},{4,20},{8,24},{12,28},{16,0},{20,4},{24,8},{28,12},{1,17},{... | collective-permute-start | bytes 12296 | tf_op jit(solution)/shard_map/ppermute | solution.py:546
  166.5 34.9 %collective-permute-start.27 = (f32[24,32,384]{2,1,0:T(8,128)S(1)}, f32[24,32,384]{2,1,0:T(8,128)S(1)}, u32[]{:S(2)}, u32[]{:S(2)}) collective-permute-start(f32[24,32,384]{2,1,0:T(8,128)S(1)} %get-tuple-element.144.refs_0_.refs_15_.refs_6_), channel_id=1, source_target_pairs={{8,0},{16,8},{24,16},{4,12},{12,20},{20,28},{9,1},{17,9},{25,17},{... | collective-permute-start | bytes 3538952 | tf_op jit(solution)/shard_map/ppermute | solution.py:540
  167.8 33.6 %collective-permute-start.26 = (f32[24,32,384]{2,1,0:T(8,128)S(1)}, f32[24,32,384]{2,1,0:T(8,128)S(1)}, u32[]{:S(2)}, u32[]{:S(2)}) collective-permute-start(f32[24,32,384]{2,1,0:T(8,128)S(1)} %get-tuple-element.147.refs_3_.refs_18_.refs_7_), channel_id=1, source_target_pairs={{0,8},{8,16},{16,24},{12,4},{20,12},{28,20},{1,9},{9,17},{17,25},{... | collective-permute-start | bytes 3538952 | tf_op jit(solution)/shard_map/ppermute | solution.py:536
  172.4 7.8 %collective-permute-start.28 = (f32[4,32,384]{2,1,0:T(8,128)S(1)}, f32[4,32,384]{2,1,0:T(8,128)S(1)}, u32[]{:S(2)}, u32[]{:S(2)}) collective-permute-start(f32[4,32,384]{2,1,0:T(8,128)S(1)} %get-tuple-element.148.last_ref), channel_id=1, source_target_pairs={{0,1},{1,2},{2,3},{4,5},{5,6},{6,7},{8,9},{9,10},{10,11},{12,13},{... | collective-permute-start | bytes 589832 | tf_op jit(solution)/shard_map/ppermute | solution.py:529
  173.7 6.5 %collective-permute-start.29 = (f32[4,32,384]{2,1,0:T(8,128)S(1)}, f32[4,32,384]{2,1,0:T(8,128)S(1)}, u32[]{:S(2)}, u32[]{:S(2)}) collective-permute-start(f32[4,32,384]{2,1,0:T(8,128)S(1)} %get-tuple-element.149.first_ref), channel_id=1, source_target_pairs={{1,0},{2,1},{3,2},{5,4},{6,5},{7,6},{9,8},{10,9},{11,10},{13,12},{... | collective-permute-start | bytes 589832 | tf_op jit(solution)/shard_map/ppermute | solution.py:532
  175.0 5.2 %collective-permute-start.30 = (f32[4,24,384]{2,1,0:T(8,128)S(1)}, f32[4,24,384]{2,1,0:T(8,128)S(1)}, u32[]{:S(2)}, u32[]{:S(2)}) collective-permute-start(f32[4,24,384]{2,1,0:T(8,128)S(1)} %get-tuple-element.150), channel_id=1, source_target_pairs={{0,4},{4,0},{8,12},{12,8},{16,20},{20,16},{24,28},{28,24},{1,5},{5... | collective-permute-start | bytes 442376 | tf_op jit(solution)/shard_map/ppermute | solution.py:526
  181.0 4.2 %collective-permute-start.31 = (f32[8,128]{1,0:T(8,128)S(1)}, f32[8,128]{1,0:T(8,128)S(1)}, u32[]{:S(2)}, u32[]{:S(2)}) collective-permute-start(f32[8,128]{1,0:T(8,128)S(1)} %edge_maxima.4), channel_id=1, source_target_pairs={{0,1},{1,0},{2,3},{3,2},{4,5},{5,4},{6,7},{7,6},{8,9},{9,8},{10,11... | collective-permute-start | bytes 12296 | tf_op jit(solution)/shard_map/ppermute | solution.py:546
  185.2 3.6 %collective-permute-start.32 = (f32[8,128]{1,0:T(8,128)S(1)}, f32[8,128]{1,0:T(8,128)S(1)}, u32[]{:S(2)}, u32[]{:S(2)}) collective-permute-start(f32[8,128]{1,0:T(8,128)S(1)} %max.70), channel_id=1, source_target_pairs={{0,2},{1,3},{2,0},{3,1},{4,6},{5,7},{6,4},{7,5},{8,10},{9,11},{10,... | collective-permute-start | bytes 12296 | tf_op jit(solution)/shard_map/ppermute | solution.py:546
  188.8 3.6 %collective-permute-start.33 = (f32[8,128]{1,0:T(8,128)S(1)}, f32[8,128]{1,0:T(8,128)S(1)}, u32[]{:S(2)}, u32[]{:S(2)}) collective-permute-start(f32[8,128]{1,0:T(8,128)S(1)} %max.71), channel_id=1, source_target_pairs={{0,4},{4,0},{8,12},{12,8},{16,20},{20,16},{24,28},{28,24},{1,5},{5... | collective-permute-start | bytes 12296 | tf_op jit(solution)/shard_map/ppermute | solution.py:546
  192.4 3.6 %collective-permute-start.34 = (f32[8,128]{1,0:T(8,128)S(1)}, f32[8,128]{1,0:T(8,128)S(1)}, u32[]{:S(2)}, u32[]{:S(2)}) collective-permute-start(f32[8,128]{1,0:T(8,128)S(1)} %max.72), channel_id=1, source_target_pairs={{0,8},{4,12},{8,0},{12,4},{16,24},{20,28},{24,16},{28,20},{1,9},{5... | collective-permute-start | bytes 12296 | tf_op jit(solution)/shard_map/ppermute | solution.py:546
  196.0 5.4 %collective-permute-start.35 = (f32[8,128]{1,0:T(8,128)S(1)}, f32[8,128]{1,0:T(8,128)S(1)}, u32[]{:S(2)}, u32[]{:S(2)}) collective-permute-start(f32[8,128]{1,0:T(8,128)S(1)} %max.73), channel_id=1, source_target_pairs={{0,16},{4,20},{8,24},{12,28},{16,0},{20,4},{24,8},{28,12},{1,17},{... | collective-permute-start | bytes 12296 | tf_op jit(solution)/shard_map/ppermute | solution.py:546
  210.2 41.3 %collective-permute-start.37 = (f32[24,32,384]{2,1,0:T(8,128)S(1)}, f32[24,32,384]{2,1,0:T(8,128)S(1)}, u32[]{:S(2)}, u32[]{:S(2)}) collective-permute-start(f32[24,32,384]{2,1,0:T(8,128)S(1)} %get-tuple-element.167.refs_0_), channel_id=1, source_target_pairs={{8,0},{16,8},{24,16},{4,12},{12,20},{20,28},{9,1},{17,9},{25,17},{... | collective-permute-start | bytes 3538952 | tf_op jit(solution)/shard_map/ppermute | solution.py:540
  211.5 40.0 %collective-permute-start.36 = (f32[24,32,384]{2,1,0:T(8,128)S(1)}, f32[24,32,384]{2,1,0:T(8,128)S(1)}, u32[]{:S(2)}, u32[]{:S(2)}) collective-permute-start(f32[24,32,384]{2,1,0:T(8,128)S(1)} %get-tuple-element.170.refs_3_), channel_id=1, source_target_pairs={{0,8},{8,16},{16,24},{12,4},{20,12},{28,20},{1,9},{9,17},{17,25},{... | collective-permute-start | bytes 3538952 | tf_op jit(solution)/shard_map/ppermute | solution.py:536
  216.1 8.0 %collective-permute-start.38 = (f32[4,32,384]{2,1,0:T(8,128)S(1)}, f32[4,32,384]{2,1,0:T(8,128)S(1)}, u32[]{:S(2)}, u32[]{:S(2)}) collective-permute-start(f32[4,32,384]{2,1,0:T(8,128)S(1)} %get-tuple-element.171.last_ref), channel_id=1, source_target_pairs={{0,1},{1,2},{2,3},{4,5},{5,6},{6,7},{8,9},{9,10},{10,11},{12,13},{... | collective-permute-start | bytes 589832 | tf_op jit(solution)/shard_map/ppermute | solution.py:529
  217.4 6.7 %collective-permute-start.39 = (f32[4,32,384]{2,1,0:T(8,128)S(1)}, f32[4,32,384]{2,1,0:T(8,128)S(1)}, u32[]{:S(2)}, u32[]{:S(2)}) collective-permute-start(f32[4,32,384]{2,1,0:T(8,128)S(1)} %get-tuple-element.172.first_ref), channel_id=1, source_target_pairs={{1,0},{2,1},{3,2},{5,4},{6,5},{7,6},{9,8},{10,9},{11,10},{13,12},{... | collective-permute-start | bytes 589832 | tf_op jit(solution)/shard_map/ppermute | solution.py:532
  218.9 5.2 %collective-permute-start.40 = (f32[4,24,384]{2,1,0:T(8,128)S(1)}, f32[4,24,384]{2,1,0:T(8,128)S(1)}, u32[]{:S(2)}, u32[]{:S(2)}) collective-permute-start(f32[4,24,384]{2,1,0:T(8,128)S(1)} %get-tuple-element.173), channel_id=1, source_target_pairs={{0,4},{4,0},{8,12},{12,8},{16,20},{20,16},{24,28},{28,24},{1,5},{5... | collective-permute-start | bytes 442376 | tf_op jit(solution)/shard_map/ppermute | solution.py:526
  224.9 4.0 %collective-permute-start.41 = (f32[8,128]{1,0:T(8,128)S(1)}, f32[8,128]{1,0:T(8,128)S(1)}, u32[]{:S(2)}, u32[]{:S(2)}) collective-permute-start(f32[8,128]{1,0:T(8,128)S(1)} %edge_maxima.5), channel_id=1, source_target_pairs={{0,1},{1,0},{2,3},{3,2},{4,5},{5,4},{6,7},{7,6},{8,9},{9,8},{10,11... | collective-permute-start | bytes 12296 | tf_op jit(solution)/shard_map/ppermute | solution.py:546
  228.9 3.6 %collective-permute-start.42 = (f32[8,128]{1,0:T(8,128)S(1)}, f32[8,128]{1,0:T(8,128)S(1)}, u32[]{:S(2)}, u32[]{:S(2)}) collective-permute-start(f32[8,128]{1,0:T(8,128)S(1)} %max.75), channel_id=1, source_target_pairs={{0,2},{1,3},{2,0},{3,1},{4,6},{5,7},{6,4},{7,5},{8,10},{9,11},{10,... | collective-permute-start | bytes 12296 | tf_op jit(solution)/shard_map/ppermute | solution.py:546
  232.5 3.6 %collective-permute-start.43 = (f32[8,128]{1,0:T(8,128)S(1)}, f32[8,128]{1,0:T(8,128)S(1)}, u32[]{:S(2)}, u32[]{:S(2)}) collective-permute-start(f32[8,128]{1,0:T(8,128)S(1)} %max.76), channel_id=1, source_target_pairs={{0,4},{4,0},{8,12},{12,8},{16,20},{20,16},{24,28},{28,24},{1,5},{5... | collective-permute-start | bytes 12296 | tf_op jit(solution)/shard_map/ppermute | solution.py:546
  236.1 3.6 %collective-permute-start.44 = (f32[8,128]{1,0:T(8,128)S(1)}, f32[8,128]{1,0:T(8,128)S(1)}, u32[]{:S(2)}, u32[]{:S(2)}) collective-permute-start(f32[8,128]{1,0:T(8,128)S(1)} %max.77), channel_id=1, source_target_pairs={{0,8},{4,12},{8,0},{12,4},{16,24},{20,28},{24,16},{28,20},{1,9},{5... | collective-permute-start | bytes 12296 | tf_op jit(solution)/shard_map/ppermute | solution.py:546
  239.7 6.7 %collective-permute-start.45 = (f32[8,128]{1,0:T(8,128)S(1)}, f32[8,128]{1,0:T(8,128)S(1)}, u32[]{:S(2)}, u32[]{:S(2)}) collective-permute-start(f32[8,128]{1,0:T(8,128)S(1)} %max.78), channel_id=1, source_target_pairs={{0,16},{4,20},{8,24},{12,28},{16,0},{20,4},{24,8},{28,12},{1,17},{... | collective-permute-start | bytes 12296 | tf_op jit(solution)/shard_map/ppermute | solution.py:546
  249.0 53.1 %collective-permute-start.47 = (f32[24,32,384]{2,1,0:T(8,128)}, f32[24,32,384]{2,1,0:T(8,128)S(1)}, u32[]{:S(2)}, u32[]{:S(2)}) collective-permute-start(f32[24,32,384]{2,1,0:T(8,128)} %get-tuple-element.191), channel_id=1, source_target_pairs={{0,4},{4,0},{8,12},{12,8},{16,20},{20,16},{24,28},{28,24},{1,5},{5... | collective-permute-start | bytes 3538952 | tf_op jit(solution)/shard_map/ppermute | solution.py:526
  259.0 45.2 %collective-permute-start.46 = (f32[24,32,384]{2,1,0:T(8,128)}, f32[24,32,384]{2,1,0:T(8,128)}, u32[]{:S(2)}, u32[]{:S(2)}) collective-permute-start(f32[24,32,384]{2,1,0:T(8,128)} %get-tuple-element.184), channel_id=1, source_target_pairs={{0,4},{4,0},{8,12},{12,8},{16,20},{20,16},{24,28},{28,24},{1,5},{5... | collective-permute-start | bytes 3538952 | tf_op jit(solution)/shard_map/ppermute | solution.py:526
  267.0 33.1 %collective-permute-start.48 = (f32[2,384]{1,0:T(2,128)}, f32[2,384]{1,0:T(2,128)}, u32[]{:S(2)}, u32[]{:S(2)}) collective-permute-start(f32[2,384]{1,0:T(2,128)} %rev.6), channel_id=1, source_target_pairs={{0,4},{4,0},{8,12},{12,8},{16,20},{20,16},{24,28},{28,24},{1,5},{5... | collective-permute-start | bytes 9224 | tf_op jit(solution)/shard_map/ppermute | solution.py:526

commit v3 on v2

--- a/solution.py
+++ b/solution.py
@@ -44,10 +44,8 @@
     return out
 
 
-def lane_max(ref, lane):
-    values = ref[...]
-    position = lax.broadcasted_iota(jnp.int32, values.shape, 1)
-    return jnp.max(jnp.where(position == lane, values, 0.0))
+def maximum_row(ref, row):
+    return jnp.broadcast_to(ref[pl.ds(row, 1), :], (8, LANES))
 
 
 class Own:
@@ -68,7 +66,7 @@
         return lambda j, g: ref[j, pl.ds(8 * g, 8), :]
 
 
-class Scalars:
+class Rates:
     def __init__(self, sizes):
         cells_v, half, width, total_vx, total_vy = sizes
         self.step_2 = 2.0 * VELOCITY_LIMIT / total_vx
@@ -78,13 +76,13 @@
         self.rate_4 = VELOCITY_LIMIT * (total_vy - 1) / total_vy + PLANNER_SPEED
 
     def rates(self, limits, maxima):
-        rate_2 = lane_max(limits, 2) + DISTURBANCE + lane_max(maxima, 0) * (0.5 / (self.step_2 * CONTROL_COST))
-        rate_3 = lane_max(limits, 3) + DISTURBANCE + lane_max(maxima, 1) * (0.5 / (self.step_3 * CONTROL_COST))
+        rate_2 = maximum_row(limits, 2) + DISTURBANCE + maximum_row(maxima, 0) * (0.5 / (self.step_2 * CONTROL_COST))
+        rate_3 = maximum_row(limits, 3) + DISTURBANCE + maximum_row(maxima, 1) * (0.5 / (self.step_3 * CONTROL_COST))
         return rate_2 * (1.0 / self.step_2), rate_3 * (1.0 / self.step_3)
 
     def time_step(self, rates):
         total = rates[0] + rates[1] + (self.rate_1 + self.rate_4) / self.step_1
-        return jnp.max(COURANT / jnp.full((8, LANES), total, jnp.float32))
+        return COURANT / total
 
 
 class Operands:
@@ -111,7 +109,7 @@
     return [tile[start : start + 8] for start in range(0, tile.shape[0], 8)]
 
 
-def advance(sizes, targets, rows, bases, halo_rows, vx_low, vx_high, vy_next, maxima, stepper, accel_second, flags, push, speed):
+def advance(sizes, targets, rows, bases, halo_rows, vx_low, vx_high, vy_next, maxima, stepper, accel_second, table):
     cells_v, half, width, total_vx, total_vy = sizes
     count = len(targets)
     heun = bases is not None
@@ -128,15 +126,16 @@
     n_out = count * (1 if full else 3)
     groups = half // 8
 
-    def body(flags_ref, push_ref, speed_ref, *refs):
+    def body(table_ref, *refs):
         ins, outs = refs[:n_in], refs[n_in : n_in + n_out]
         adv_up, adv_down, acc_up, acc_down = refs[n_in + n_out :]
-        parity, edge_low, edge_high, vx_first, vx_last = (flags_ref[i] for i in range(5))
-        is_even = parity == 0
-        known = Scalars(sizes)
+        is_odd, edge_low, edge_high, vx_first, vx_last = (table_ref[5, i] > 0.5 for i in range(5))
+        is_even = jnp.logical_not(is_odd)
+        parity = jnp.where(is_odd, 1, 0)
+        known = Rates(sizes)
         step_1, step_2, step_3 = known.step_1, known.step_2, known.step_3
         if late:
-            scale = jnp.float32(1.0)
+            scale = jnp.ones((8, LANES), jnp.float32)
         else:
             rates = known.rates(ins[maxima_at[0]], ins[maxima_at[1]])
             scale = known.time_step(rates) * (0.5 if heun else 1.0)
@@ -154,14 +153,22 @@
         control_3 = scale * (1.0 / (8.0 * CONTROL_COST * step_3 * step_3))
         to_1, to_2, to_3 = scale / (2.0 * step_1), scale / (2.0 * step_2), scale / (2.0 * step_3)
 
+        def wide(x):
+            return jnp.concatenate([x] * (width // LANES), axis=1)
+
         start = pl.multiple_of(parity * half, half)
-        vy = (parity * half + lax.broadcasted_iota(jnp.int32, (half, LANES), 0)).astype(jnp.float32)
-        speed_y = (2.0 * vy + (1.0 - total_vy)) * (VELOCITY_LIMIT / total_vy) * to_1
-        adv_up[...] = speed_y + planner
-        adv_down[...] = speed_y - planner
-        accel = ins[accel_at][pl.ds(start, half), :] * to_3
-        acc_up[...] = accel + disturb_3
-        acc_down[...] = accel - disturb_3
+        for g in range(groups):
+            here = pl.ds(8 * g, 8)
+            vy = (parity * half + 8 * g + lax.broadcasted_iota(jnp.int32, (8, LANES), 0)).astype(jnp.float32)
+            speed_y = (2.0 * vy + (1.0 - total_vy)) * (VELOCITY_LIMIT / total_vy) * to_1
+            adv_up[here, :] = speed_y + planner
+            adv_down[here, :] = speed_y - planner
+            accel = ins[accel_at][pl.ds(pl.multiple_of(start + 8 * g, 8), 8), :] * wide(to_3)
+            acc_up[here, :] = accel + wide(disturb_3)
+            acc_down[here, :] = accel - wide(disturb_3)
+        keep, damp_1, control_2, control_3 = wide(keep), wide(damp_1), wide(control_2), wide(control_3)
+        if full:
+            damp_2, damp_3 = wide(damp_2), wide(damp_3)
 
         readers = {k: rows[k].reader(ins[row_at[k]], parity, half) for k in needed}
         base_readers = [b.reader(ins[a], parity, half) for b, a in zip(bases, base_at)] if heun else None
@@ -170,9 +177,9 @@
 
         def neighbour(k, j, g, center):
             if k == -1:
-                return jnp.where(edge_low == 1, center, ins[halo_at[-1]][j, pl.ds(8 * g, 8), :])
+                return jnp.where(edge_low, center, ins[halo_at[-1]][j, pl.ds(8 * g, 8), :])
             if k == 4:
-                return jnp.where(edge_high == 1, center, ins[halo_at[4]][j, pl.ds(8 * g, 8), :])
+                return jnp.where(edge_high, center, ins[halo_at[4]][j, pl.ds(8 * g, 8), :])
             return readers[k](j, g)
 
         def lane_pieces(x):
@@ -183,10 +190,10 @@
 
         def tile(i, j, low_j, high_j):
             t = targets[i]
-            flow = speed_ref[j] * to_1
-            drift = push_ref[t, j] * to_2
-            flow_up, flow_down = flow + planner, flow - planner
-            drift_up, drift_down = drift + disturb_2, drift - disturb_2
+            flow = table_ref[4, j] * to_1
+            drift = table_ref[t, j] * to_2
+            flow_up, flow_down = wide(flow + planner), wide(flow - planner)
+            drift_up, drift_down = wide(drift + disturb_2), wide(drift - disturb_2)
             beyond = ins[vy_at][3 - t, pl.ds(j, 1), :]
             first = readers[t](j, 0)
             last = readers[t](j, groups - 1)
@@ -212,22 +219,22 @@
                 total = total + jnp.concatenate(parts, axis=1)
 
                 if low_j is None:
-                    low_2 = jnp.where(vx_first == 1, w, ins[low_at][t, here, :])
+                    low_2 = jnp.where(vx_first, w, ins[low_at][t, here, :])
                 else:
                     low_2 = readers[t](low_j, g)
                 if high_j is None:
-                    high_2 = jnp.where(vx_last == 1, w, ins[high_at][t, here, :])
+                    high_2 = jnp.where(vx_last, w, ins[high_at][t, here, :])
                 else:
                     high_2 = readers[t](high_j, g)
                 slope = high_2 - low_2
                 bent = control_2 * slope
-                total = total + jnp.maximum((drift_up - bent) * slope, (drift_down - bent) * slope)
+                total = total + (jnp.where(slope > 0.0, drift_up, drift_down) - bent) * slope
 
                 low_3 = jnp.where(sublane == 0, ups[g], ups[g + 1])
                 high_3 = jnp.where(sublane == 7, downs[g + 1], downs[g])
                 slope = high_3 - low_3
                 bent = control_3 * slope
-                total = total + jnp.maximum((acc_up[here, :] - bent) * slope, (acc_down[here, :] - bent) * slope)
+                total = total + (jnp.where(slope > 0.0, acc_up[here, :], acc_down[here, :]) - bent) * slope
 
                 twice = w + w
                 bend_2 = low_2 + high_2 - twice
@@ -245,10 +252,13 @@
         for i in range(count):
             tile(i, 0, None, 1)
 
-        @pl.loop(1, cells_v - 1)
+        together = 2 if count == 1 and cells_v % 2 == 0 else 1
+
+        @pl.loop(1, cells_v - 1, step=together)
         def _(j):
-            for i in range(count):
-                tile(i, j, j - 1, j + 1)
+            for ahead in range(together):
+                for i in range(count):
+                    tile(i, j + ahead, j + ahead - 1, j + ahead + 1)
 
         for i in range(count):
             tile(i, cells_v - 1, cells_v - 2, None)
@@ -256,13 +266,13 @@
     return pl.pallas_call(
         body,
         out_shape=[f32(cells_v, half, width)] * n_out,
-        in_specs=[scalars()] * 3 + [whole()] * n_in,
+        in_specs=[scalars()] + [whole()] * n_in,
         out_specs=[whole()] * n_out,
         scratch_shapes=[pltpu.VMEM((half, LANES), jnp.float32)] * 2 + [pltpu.VMEM((half, width), jnp.float32)] * 2,
         compiler_params=compiler_params(),
         cost_estimate=estimate(count * cells_v * half * width, 45),
         name="advance_" + "".join(str(t) for t in targets),
-    )(flags, push, speed, *ops.arrays)
+    )(table, *ops.arrays)
 
 
 def settle(sizes, targets, updates, costs, flags, damping=None, fields=None, prior=None, with_edges=True):
@@ -285,7 +295,7 @@
         parity = flags_ref[0]
         is_even = parity == 0
         if damping is not None:
-            known = Scalars(sizes)
+            known = Rates(sizes)
             step_rates = known.rates(ins[maxima_at[0]], ins[maxima_at[1]])
             rates = step_rates if maxima_at[1] == maxima_at[2] else known.rates(ins[maxima_at[0]], ins[maxima_at[2]])
             scale = known.time_step(step_rates) * damping[3]
@@ -293,6 +303,7 @@
                 damp_2, damp_3 = scale * 0.5 * rates[0], scale * 0.5 * rates[1]
             else:
                 damp_2, damp_3 = 0.5 * rates[0], 0.5 * rates[1]
+            damp_2, damp_3, scale = (jnp.concatenate([x] * (width // LANES), axis=1) for x in (damp_2, damp_3, scale))
         cost_readers = [c.reader(ins[a], parity, half) for c, a in zip(costs, cost_at)]
         field_readers = [f.reader(ins[a], parity, half) for f, a in zip(fields or (), field_at)]
         sublane = lax.broadcasted_iota(jnp.int32, (8, width), 0)
@@ -387,11 +398,11 @@
     return outs[:count], outs[count:]
 
 
-def spread(shape, lanes):
-    position = lax.broadcasted_iota(jnp.int32, shape, 1)
-    out = jnp.zeros(shape, jnp.float32)
-    for lane, value in enumerate(lanes):
-        out = jnp.where(position == lane, value, out)
+def spread(values):
+    position = lax.broadcasted_iota(jnp.int32, (8, LANES), 0)
+    out = jnp.zeros((8, LANES), jnp.float32)
+    for row, value in enumerate(values):
+        out = jnp.where(position == row, value, out)
     return out
 
 
@@ -425,7 +436,7 @@
 
             most_2, most_3 = lax.fori_loop(1, cells_v - 1, step, (most_2, most_3))
         values = (jnp.max(most_2), jnp.max(most_3), jnp.max(jnp.abs(first_ref[...])), jnp.max(jnp.abs(second_ref[...])))
-        out_ref[...] = spread((8, LANES), values)
+        out_ref[...] = spread(values)
 
     return pl.pallas_call(
         body,
@@ -449,7 +460,7 @@
             most_2 = jnp.maximum(most_2, fold(jnp.abs(second_ref[t] - low)))
             most_2 = jnp.maximum(most_2, fold(jnp.abs(high - before_ref[t])))
             most_3 = jnp.maximum(most_3, fold(jnp.abs(inner_ref[t] - next_ref[3 - t])))
-        out_ref[...] = spread((8, LANES), (jnp.max(most_2), jnp.max(most_3)))
+        out_ref[...] = spread((jnp.max(most_2), jnp.max(most_3)))
 
     return pl.pallas_call(
         body,
@@ -461,44 +472,55 @@
     )(flags, first, second, before, last, vx_low, vx_high, inner, vy_next, part)
 
 
-def place(flags, pieces, which, result, shape):
-    rows, cells_v, total_vy, width = shape
+def take(flags, array, outer, which):
+    _, cells_v, total_vy, width = array.shape
     half = total_vy // 2
-    block = 8 if cells_v % 8 == 0 else cells_v
-    count = len(pieces)
-
-    def body(flags_ref, *refs):
-        out_ref = refs[-1]
-        piece = pl.program_id(0)
-        for i in range(count):
-
-            @pl.when(piece == i)
-            def _(i=i):
-                out_ref[0] = refs[i][...]
-
-    def target(i, j, flags_ref):
-        outer = functools.reduce(lambda a, b: a + b, [(i == k) * int(p[0]) for k, p in enumerate(pieces)])
+
+    def body(flags_ref, array_ref, out_ref, sem):
         parity = flags_ref[0]
-        return (jnp.where(outer == 1, parity, 1 - parity), j, parity if which == 0 else 1 - parity, 0)
-
-    def source(k):
-        return lambda i, j, flags_ref: (jnp.where(i == k, j, jnp.where(i < k, 0, cells_v // block - 1)), 0, 0)
-
-    in_specs = [pl.BlockSpec((block, half, width), source(k)) for k in range(count)]
-    extra = []
-    if result is not None:
-        in_specs.append(pl.BlockSpec(memory_space=pl.ANY))
-        extra = [result]
+        start = pl.multiple_of((parity if which == 0 else 1 - parity) * half, half)
+        copy = pltpu.make_async_copy(array_ref.at[parity if outer else 1 - parity, :, pl.ds(start, half), :], out_ref, sem)
+        copy.start()
+        copy.wait()
+
     return pl.pallas_call(
         body,
-        grid_spec=pltpu.PrefetchScalarGridSpec(
-            num_scalar_prefetch=1,
-            grid=(count, cells_v // block),
-            in_specs=in_specs,
-            out_specs=pl.BlockSpec((1, block, half, width), target),
-        ),
+        in_specs=[scalars(), pl.BlockSpec(memory_space=pl.ANY)],
+        out_specs=whole(),
+        out_shape=f32(cells_v, half, width),
+        scratch_shapes=[pltpu.SemaphoreType.DMA],
+        compiler_params=compiler_params(),
+        cost_estimate=estimate(cells_v * half * width, 1),
+        name="take",
+    )(flags, array)
+
+
+def place(flags, pieces, which, result, shape):
+    half = shape[2] // 2
+    count = len(pieces)
+
+    def body(flags_ref, *refs):
+        out_ref, sems = refs[-2:]
+        parity = flags_ref[0]
+        start = pl.multiple_of((parity if which == 0 else 1 - parity) * half, half)
+        copies = []
+        for i in range(count):
+            row = parity if pieces[i][0] else 1 - parity
+            copies.append(pltpu.make_async_copy(refs[i], out_ref.at[row, :, pl.ds(start, half), :], sems.at[i]))
+        for copy in copies:
+            copy.start()
+        for copy in copies:
+            copy.wait()
+
+    anywhere = pl.BlockSpec(memory_space=pl.ANY)
+    extra = [] if result is None else [result]
+    return pl.pallas_call(
+        body,
+        in_specs=[scalars()] + [whole()] * count + [anywhere] * len(extra),
+        out_specs=anywhere,
         out_shape=jax.ShapeDtypeStruct(shape, jnp.float32),
-        input_output_aliases={1 + count: 0} if result is not None else {},
+        input_output_aliases={} if result is None else {1 + count: 0},
+        scratch_shapes=[pltpu.SemaphoreType.DMA((count,))],
         compiler_params=compiler_params(),
         name="place",
     )(flags, *[p[1] for p in pieces], *extra)
@@ -539,28 +561,31 @@
         moves = [(i, i - 2) for i in range(2, n_px, 2)] + [(i, i + 2) for i in range(1, n_px - 2, 2)]
         return lax.ppermute(outer, "px", moves)
 
-    def share(maxima):
-        for axis, count in (("vx", n_vx), ("px", n_px)):
-            apart = 1
-            while apart < count:
-                other = lax.ppermute(maxima, axis, [(i, i ^ apart) for i in range(count)])
-                maxima = jnp.maximum(maxima, other)
-                apart *= 2
+    def after(array, *others):
+        return lax.optimization_barrier((array, *others))[0]
+
+    def share(maxima, beside=None, partner_done=False):
+        steps = [("vx", 1 << k) for k in range((n_vx - 1).bit_length())] + [("px", 1 << k) for k in range((n_px - 1).bit_length())]
+        if partner_done:
+            steps.remove(("px", 1))
+        for place_at, (axis, apart) in enumerate(steps):
+            other = lax.ppermute(maxima, axis, [(i, i ^ apart) for i in range(lax.axis_size(axis))])
+            if beside is not None and place_at in beside:
+                other = after(other, *beside[place_at])
+            maxima = jnp.maximum(maxima, other)
         return maxima
 
-    def half_of(array, row, which):
-        return lax.dynamic_slice(array, (row, 0, which * half, 0), (1, cells_v, half, width))[0]
-
-    value_outer_got = partner(half_of(value, parity, 1 - parity))
-    value_inner_got = partner(half_of(value, 1 - parity, 1 - parity))
-    cost_outer, value_outer_got = lax.optimization_barrier((half_of(cost, parity, 1 - parity), value_outer_got))
-    cost_inner, value_inner_got = lax.optimization_barrier((half_of(cost, 1 - parity, 1 - parity), value_inner_got))
-    cost_outer_got = partner(cost_outer)
-    cost_inner_got = partner(cost_inner)
-
-    low_own = from_low_vx(value[:, cells_v - 1])
-    high_own = from_high_vx(value[:, 0])
-    shared_first = share(first_maxima(value, low_own, high_own, accel_first, accel_second, flags))
+    value_outer = take(flags, value, True, 1)
+    value_outer_got = partner(value_outer)
+    value_inner = after(take(flags, value, False, 1), value_outer)
+    value_inner_got = partner(value_inner)
+    push_got = partner(after(accel_first, value_outer))
+
+    low_own = from_low_vx(after(value[:, cells_v - 1], value_outer))
+    high_own = from_high_vx(after(value[:, 0], value_outer))
+    row_needed = lax.dynamic_slice(value, (0, 0, half - parity, 0), (rows, cells_v, 1, width))[:, :, 0]
+    row_given = lax.dynamic_slice(value, (0, 0, half - 1 + parity, 0), (rows, cells_v, 1, width))[:, :, 0]
+    row_got = partner(after(row_given, value_outer))
 
     def chain_halo(own):
         given = lax.dynamic_slice(own, (0, (1 - parity) * half, 0), (rows, half, width))
@@ -569,12 +594,15 @@
 
     low_mine, low_given = chain_halo(low_own)
     high_mine, high_given = chain_halo(high_own)
-    got = partner(jnp.concatenate([low_given, high_given], axis=0))
-    row_given = lax.dynamic_slice(value, (0, 0, half - parity, 0), (rows, cells_v, 1, width))[:, :, 0]
-    row_needed = lax.dynamic_slice(value, (0, 0, half - parity, 0), (rows, cells_v, 1, width))[:, :, 0]
-    row_given = lax.dynamic_slice(value, (0, 0, half - 1 + parity, 0), (rows, cells_v, 1, width))[:, :, 0]
-    row_got = partner(row_given)
-    push_got = partner(accel_first)
+    halo_given = jnp.concatenate([low_given, high_given], axis=0)
+    got = partner(halo_given)
+    maxima = first_maxima(value, low_own, high_own, accel_first, accel_second, flags)
+    maxima = jnp.maximum(maxima, partner(maxima))
+    ahead = (maxima, got, row_got, push_got)
+    cost_outer = after(take(flags, cost, True, 1), *ahead)
+    cost_outer_got = partner(cost_outer)
+    cost_inner_got = partner(after(take(flags, cost, False, 1), *ahead))
+    shared_first = share(maxima, partner_done=True)
 
     def pick(x, which):
         return lax.dynamic_index_in_dim(x, which, 0, keepdims=True)
@@ -589,66 +617,73 @@
     positions = (vx * cells_v + jnp.arange(cells_v, dtype=jnp.int32)).astype(jnp.float32)
     speed = (2.0 * positions + 1.0 - total_vx) * (VELOCITY_LIMIT / total_vx)
     speed = jnp.where(parity == 0, speed, -speed)
+    table = jnp.concatenate([push, speed[None], jnp.pad(flags.astype(jnp.float32), (0, cells_v - flags.shape[0]))[None]], axis=0)
 
     chain = [Own(value, True), Own(value, False), Row(value_inner_got), Row(value_outer_got)]
     costs = [Own(cost, True), Own(cost, False), Row(cost_inner_got), Row(cost_outer_got)]
-    halo_rows = (halo_before(value_outer_got), halo_after(half_of(value, parity, parity)))
-
-    def advanced(field, bases, stepper):
-        out = {}
-        for targets in ((1, 2), (0, 3)):
-            some = None if bases is None else [bases[t] for t in targets]
-            got = advance(
-                sizes, targets, field, some, halo_rows, vx_low, vx_high, vy_next, shared_first, stepper, accel_second, flags, push, speed
-            )
-            each = len(got) // 2
-            out.update({t: got[each * i : each * (i + 1)] for i, t in enumerate(targets)})
-        return out
+    halo_rows = (halo_before(value_outer_got), halo_after(after(take(flags, value, True, 0), value_inner)))
+
+    def advanced(targets, field, bases, halo_rows, vx_low, vx_high, vy_next, stepper):
+        some = None if bases is None else [bases[t] for t in targets]
+        got = advance(
+            sizes, targets, field, some, halo_rows, vx_low, vx_high, vy_next, shared_first, stepper, accel_second, table
+        )
+        each = len(got) // len(targets)
+        return {t: got[each * i : each * (i + 1)] for i, t in enumerate(targets)}
 
     def settled(targets, updates, **kw):
         return settle(sizes, targets, [updates[t] for t in targets], [costs[t] for t in targets], flags, **kw)
 
-    def exchange(edges):
+    def next_updates(field, edges, bases, stepper, halo_rows, halo_early):
         first, _, _, last, edge, _, _ = edges
         low, high, row = from_low_vx(last), from_high_vx(first), partner(edge)
-        return low, high, row, share(edge_maxima(edges, low, high, row, flags))
-
-    every = (0, 1, 2, 3)
-
-    updates = advanced(chain, None, shared_first)
+        maxima = edge_maxima(edges, low, high, row, flags)
+        updates, beside = {}, {}
+        for place_at, t in enumerate((1, 2, 0, 3) if halo_early else (1, 2)):
+            updates.update(advanced((t,), field, bases, halo_rows, low, high, row, stepper))
+            beside[place_at + 1] = updates[t]
+        if not halo_early:
+            updates.update(advanced((0, 3), field, bases, halo_rows, low, high, row, stepper))
+            beside[4] = updates[0] + updates[3]
+        maxima = share(maxima, beside)
+        return updates, maxima
+
+    def settled_all(updates, **kw):
+        fields = kw.pop("fields", None)
+        some = {} if fields is None else {"fields": [fields[0], fields[3]]}
+        (outer, far), edges = settled((0, 3), updates, **some, **kw)
+        halo_rows = (halo_before(far), halo_after(outer))
+        some = {} if fields is None else {"fields": [fields[1], fields[2]]}
+        (inner, near), edges = settled((1, 2), updates, prior=((0, 3), edges), **some, **kw)
+        return [Row(f) for f in (outer, inner, near, far)], edges, halo_rows
+
+    updates = advanced((1, 2), chain, None, halo_rows, vx_low, vx_high, vy_next, shared_first)
+    updates.update(advanced((0, 3), chain, None, halo_rows, vx_low, vx_high, vy_next, shared_first))
     (outer, inner), edges = settled((0, 1), updates)
-    after = halo_after(outer)
+    beyond = halo_after(outer)
     (far,), edges = settled((3,), updates, prior=((0, 1), edges))
-    before = halo_before(far)
+    halo_rows = (halo_before(far), beyond)
     (near,), edges = settled((2,), updates, prior=((0, 1, 3), edges))
-    halo_rows = (before, after)
     middle = [Row(f) for f in (outer, inner, near, far)]
-    vx_low, vx_high, vy_next, shared = exchange(edges)
-
-    updates = advanced(middle, chain, shared_first)
-    fields, edges = settled(every, updates, damping=(shared_first, shared_first, shared, 0.5))
-    halo_rows = (halo_before(fields[3]), halo_after(fields[0]))
-    chain = [Row(f) for f in fields]
-    vx_low, vx_high, vy_next, shared_second = exchange(edges)
-
-    updates = advanced(chain, None, None)
-    fields, edges = settled(every, updates, damping=(shared_first, shared_second, shared_second, 1.0), fields=chain)
-    halo_rows = (halo_before(fields[3]), halo_after(fields[0]))
-    middle = [Row(f) for f in fields]
-    vx_low, vx_high, vy_next, shared = exchange(edges)
-
-    updates = advanced(middle, chain, shared_second)
+
+    updates, shared = next_updates(middle, edges, chain, shared_first, halo_rows, True)
+    chain, edges, halo_rows = settled_all(updates, damping=(shared_first, shared_first, shared, 0.5))
+
+    updates, shared_second = next_updates(chain, edges, None, None, halo_rows, False)
+    middle, edges, halo_rows = settled_all(updates, damping=(shared_first, shared_second, shared_second, 1.0), fields=chain)
+
+    updates, shared = next_updates(middle, edges, chain, shared_second, halo_rows, False)
     damping = (shared_first, shared_second, shared, 0.5)
     (inner, near), (least_inner,) = settled((1, 2), updates, damping=damping, with_edges=False)
     inner_got = partner(near)
     (outer, far), (least_outer,) = settled((0, 3), updates, damping=damping, with_edges=False)
     outer_got = partner(far)
     least = lax.pmin(jnp.concatenate([least_outer, least_inner], axis=0), "vx")
-    least_got = partner(least[1::2][::-1])
+    least_got = partner(after(least[1::2][::-1], far))
     final = place(flags, [(True, outer), (False, inner)], 0, None, value.shape)
     final = place(flags, [(False, inner_got)], 1, final, value.shape)
     final = place(flags, [(True, outer_got)], 1, final, value.shape)
-    funnel = jnp.minimum(least[0::2], least_got[::-1])
+    funnel = jnp.minimum(least[0::2], after(least_got, final)[::-1])
     return final, jnp.concatenate([pick(funnel, parity), pick(funnel, 1 - parity)], axis=0)
 
 

time: 309 us -> 290 us (0.939)
  waiting for transfers between devices: 129 us -> 105 us
  Pallas kernels: 68.7 us -> 78.1 us
  starting transfers between devices: 85.7 us -> 77.6 us
  local copies, waits for them, and re-layouts: 15.4 us -> 19.9 us
    ppermute x20 -> x19, waiting for transfers between devices: 71.4 us -> 29.2 us  [share(): lax.ppermute(maxima, axis, [(i, i ^ apart) for i in range(lax.axis_size(a...]
    ppermute x13 -> x14, waiting for transfers between devices: 57.8 us -> 73.2 us  [partner(): return lax.ppermute(x, 'px', [(i, i ^ 1) for i in range(n_px)])]
    unnamed x15 -> x31, local copies, waits for them, and re-layouts: 2.37 us -> 13.8 us
    ppermute x20 -> x19, starting transfers between devices: 36.4 us -> 27 us  [share(): lax.ppermute(maxima, axis, [(i, i ^ apart) for i in range(lax.axis_size(a...]
    squeeze x3 -> x1, local copies, waits for them, and re-layouts: 7.95 us -> 1.05 us  [per_device(): low_own = from_low_vx(after(value[:, cells_v - 1], value_outer))]
    pallas_call x8 -> x12, Pallas kernels: 38.3 us -> 43.9 us  [advance(): pl.pallas_call(body, out_shape=[f32(cells_v, half, width)] * n_out, in_sp...]
    pallas_call x3 -> x8, Pallas kernels: 8.83 us -> 12.1 us  [the longest x5 6.27 us: take(): pl.pallas_call(body, in_specs=[scalars(), pl.BlockSpec(memory_space=pl.AN...]
    ppermute x13 -> x14, starting transfers between devices: 17.2 us -> 19.4 us  [partner(): return lax.ppermute(x, 'px', [(i, i ^ 1) for i in range(n_px)])]
  transfers between devices with their start and end apart: 49 -> 49, of which waited for: 23 -> 19; matrix products, arithmetic and copies ran while one was open for 5% -> 2% of each run, Pallas kernels for 15% -> 24%
where the time goes in v3:
time: 290 us; the launch traced here: 289 us
  waiting for transfers between devices  105 us (36%)
  Pallas kernels  78.1 us (27%)
  starting transfers between devices  77.6 us (27%)
  local copies, waits for them, and re-layouts  19.9 us (7%)
  blocking collectives  6.26 us (2%)
    ppermute x14, waiting for transfers between devices, partner(): return lax.ppermute(x, 'px', [(i, i ^ 1) for i in range(n_px)])  73.2 us
    pallas_call x12, Pallas kernels, advance(): pl.pallas_call(body, out_shape=[f32(cells_v, half, width)] * n_out, in_sp...  43.9 us
    ppermute x19, waiting for transfers between devices, share(): lax.ppermute(maxima, axis, [(i, i ^ apart) for i in range(lax.axis_size(a...  29.2 us
    ppermute x19, starting transfers between devices, share(): lax.ppermute(maxima, axis, [(i, i ^ apart) for i in range(lax.axis_size(a...  27 us
    ppermute x14, starting transfers between devices, partner(): return lax.ppermute(x, 'px', [(i, i ^ 1) for i in range(n_px)])  19.4 us
    pallas_call x9, Pallas kernels, settle(): pl.pallas_call(body, out_shape=shapes, in_specs=[scalars()] + [whole()] *...  17.7 us
    ppermute x4, starting transfers between devices, halo_before(): return lax.ppermute(outermost, 'px', moves)  15.3 us
    unnamed x31, local copies, waits for them, and re-layouts  13.8 us
  transfers between devices with their start and end apart: 49, of which 19 were waited for; matrix products, arithmetic and copies ran while one was open for 2% of the time, Pallas kernels for 24%

profile of v3, /device:TPU:0, one launch (start us, length us, event | category | flops | bytes accessed | tf_op | source)
XLA Modules:
  0.0 289.4 jit_solution(12657853713241202046)
XLA Ops:
  0.7 2.3 copy-done.1
  3.1 1.7 take.5
  4.8 3.0 %collective-permute-start.2 = (f32[24,32,384]{2,1,0:T(8,128)}, f32[24,32,384]{2,1,0:T(8,128)S(1)}, u32[]{:S(2)}, u32[]{:S(2)}) collective-permute-start(f32[24,32,384]{2,1,0:T(8,128)} %take.5), channel_id=1, source_target_pairs={{0,4},{4,0},{8,12},{12,8},{16,20},{20,16},{24,28},{28,24},{1,5},{5... | collective-permute-start | bytes 3538952 | tf_op jit(solution)/shard_map/ppermute | solution.py:548
  11.5 1.8 collective-permute-start.8
  15.9 2.3 collective-permute-done.6.high_ref
  18.8 2.3 copy-done.2
  21.2 2.2 first_maxima.1
  24.9 2.3 copy-done.3
  27.3 1.7 take.7
  28.9 1.6 take.6
  32.3 7.6 %collective-permute-done.9 = f32[8,128]{1,0:T(8,128)S(1)} collective-permute-done((f32[8,128]{1,0:T(8,128)S(1)}, f32[8,128]{1,0:T(8,128)S(1)}, u32[]{:S(2)}, u32[]{:S(2)}) %collective-permute-start.9) | collective-permute-done | bytes 4128 | tf_op jit(solution)/shard_map/ppermute | solution.py:548
  39.9 1.7 collective-permute-start.1
  42.9 3.8 %collective-permute-start.14 = (f32[24,32,384]{2,1,0:T(8,128)}, f32[24,32,384]{2,1,0:T(8,128)S(1)}, u32[]{:S(2)}, u32[]{:S(2)}) collective-permute-start(f32[24,32,384]{2,1,0:T(8,128)} %copy-done.6), channel_id=1, source_target_pairs={{0,4},{4,0},{8,12},{12,8},{16,20},{20,16},{24,28},{28,24},{1,5},{5... | collective-permute-start | bytes 3538952 | tf_op jit(solution)/shard_map/ppermute | solution.py:548
  46.7 3.6 %collective-permute-start.3 = (f32[24,32,384]{2,1,0:T(8,128)S(1)}, f32[24,32,384]{2,1,0:T(8,128)}, u32[]{:S(2)}, u32[]{:S(2)}) collective-permute-start(f32[24,32,384]{2,1,0:T(8,128)S(1)} %collective-permute-done.2.refs_2_.refs_3_), channel_id=1, source_target_pairs={{0,8},{8,16},{16,24},{12,4},{20,12},{28,20},{1,9},{9,17},{17,25},{... | collective-permute-start | bytes 3538952 | tf_op jit(solution)/shard_map/ppermute | solution.py:558
  50.3 2.3 copy-done
  57.0 2.1 collective-permute-done.11
  59.6 13.2 %collective-permute-done.12 = f32[8,128]{1,0:T(8,128)S(1)} collective-permute-done((f32[8,128]{1,0:T(8,128)S(1)}, f32[8,128]{1,0:T(8,128)S(1)}, u32[]{:S(2)}, u32[]{:S(2)}) %collective-permute-start.12) | collective-permute-done | bytes 4128 | tf_op jit(solution)/shard_map/ppermute | solution.py:572
  72.8 2.1 collective-permute-start.13
  75.0 2.3 collective-permute-done.13
  77.3 2.2 collective-permute-start.16
  79.6 2.3 copy-done.4
  82.0 5.5 %advance_12.1 = (f32[24,32,384]{2,1,0:T(8,128)S(1)}, f32[24,32,384]{2,1,0:T(8,128)S(1)}) custom-call(f32[6,24]{1,0:T(8,128)S(1)} %concatenate.21.table_ref, f32[2,24,64,384]{3,2,1,0:T(8,128)S(1)} %copy-done.4, f32[24,32,384]{2,1,0:T(8,128)} %collective-permute-done.1.refs_1_.refs_3_, f32[24,32,384]{2,1,0:T(8,128)S(1)} %collective-permute-done.2.refs_2_.refs_3_, ...), custom_call_target="tpu_custom_call" | custom-call | flops 26542080 | bytes 2359296 | tf_op jit(solution)/shard_map/advance_12/pallas_call | solution.py:266
  87.5 6.2 %advance_03.3 = (f32[24,32,384]{2,1,0:T(8,128)S(1)}, f32[24,32,384]{2,1,0:T(8,128)S(1)}) custom-call(f32[6,24]{1,0:T(8,128)S(1)} %concatenate.21.table_ref, f32[2,24,64,384]{3,2,1,0:T(8,128)S(1)} %copy-done.4, f32[24,32,384]{2,1,0:T(8,128)} %collective-permute-done.1.refs_1_.refs_3_, f32[24,32,384]{2,1,0:T(8,128)S(1)} %collective-permute-done.2.refs_2_.refs_3_, ...), custom_call_target="tpu_custom_call" | custom-call | flops 26542080 | bytes 2359296 | tf_op jit(solution)/shard_map/advance_03/pallas_call | solution.py:266
  93.8 1.8 settle_01.1
  96.8 2.5 collective-permute-start.15
  100.5 17.3 %collective-permute-done.16.refs_1_.refs_7_ = f32[24,32,384]{2,1,0:T(8,128)S(1)} collective-permute-done((f32[24,32,384]{2,1,0:T(8,128)}, f32[24,32,384]{2,1,0:T(8,128)S(1)}, u32[]{:S(2)}, u32[]{:S(2)}) %collective-permute-start.16) | collective-permute-done | bytes 1179680 | tf_op jit(solution)/shard_map/ppermute | solution.py:548
  123.0 3.7 %collective-permute-done.19.refs_6_.next_ref = f32[4,24,384]{2,1,0:T(8,128)S(1)} collective-permute-done((f32[4,24,384]{2,1,0:T(8,128)S(1)}, f32[4,24,384]{2,1,0:T(8,128)S(1)}, u32[]{:S(2)}, u32[]{:S(2)}) %collective-permute-start.19) | collective-permute-done | bytes 147488 | tf_op jit(solution)/shard_map/ppermute | solution.py:548
  127.5 2.7 collective-permute-start.21
  131.1 2.1 collective-permute-start.22
  133.2 2.8 advance_1.3
  137.6 3.4 %advance_2.3 = (f32[24,32,384]{2,1,0:T(8,128)S(1)}, f32[24,32,384]{2,1,0:T(8,128)S(1)}, f32[24,32,384]{2,1,0:T(8,128)S(1)}) custom-call(f32[6,24]{1,0:T(8,128)S(1)} %concatenate.21.table_ref, f32[24,32,384]{2,1,0:T(8,128)S(1)} %get-tuple-element.138.refs_1_.refs_0_, f32[24,32,384]{2,1,0:T(8,128)S(1)} %get-tuple-element.164.refs_0_.refs_2_.refs_1_, ...), custom_call_target="tpu_custom_call" | custom-call | flops 13271040 | bytes 1179648 | tf_op jit(solution)/shard_map/advance_2/pallas_call | solution.py:266
  141.0 1.6 collective-permute-start.24
  142.7 2.8 advance_0.1
  145.5 2.7 collective-permute-start.25
  148.2 2.8 advance_3.1
  151.0 2.1 settle_03.3
  154.3 4.6 %collective-permute-start.26 = (f32[24,32,384]{2,1,0:T(8,128)S(1)}, f32[24,32,384]{2,1,0:T(8,128)S(1)}, u32[]{:S(2)}, u32[]{:S(2)}) collective-permute-start(f32[24,32,384]{2,1,0:T(8,128)S(1)} %get-tuple-element.192.refs_3_.refs_2_.refs_9_.refs_7_), channel_id=1, source_target_pairs={{0,8},{8,16},{16,24},{12,4},{20,12},{28,20},{1,9},{9,17},{17,25},{... | collective-permute-start | bytes 3538952 | tf_op jit(solution)/shard_map/ppermute | solution.py:558
  159.0 2.1 settle_12.3
  163.8 5.6 %collective-permute-done.30.refs_8_.next_ref.refs_5_ = f32[4,24,384]{2,1,0:T(8,128)S(1)} collective-permute-done((f32[4,24,384]{2,1,0:T(8,128)S(1)}, f32[4,24,384]{2,1,0:T(8,128)S(1)}, u32[]{:S(2)}, u32[]{:S(2)}) %collective-permute-start.30) | collective-permute-done | bytes 147488 | tf_op jit(solution)/shard_map/ppermute | solution.py:548
  170.1 1.8 collective-permute-start.31
  172.8 1.8 collective-permute-start.32
  174.6 2.6 advance_1.4
  177.3 2.6 advance_2.4
  181.5 3.0 %collective-permute-done.34 = f32[8,128]{1,0:T(8,128)S(1)} collective-permute-done((f32[8,128]{1,0:T(8,128)S(1)}, f32[8,128]{1,0:T(8,128)S(1)}, u32[]{:S(2)}, u32[]{:S(2)}) %collective-permute-start.34) | collective-permute-done | bytes 4128 | tf_op jit(solution)/shard_map/ppermute | solution.py:572
  184.5 1.7 collective-permute-start.35
  186.2 4.7 %advance_03.4 = (f32[24,32,384]{2,1,0:T(8,128)S(1)}, f32[24,32,384]{2,1,0:T(8,128)S(1)}, f32[24,32,384]{2,1,0:T(8,128)S(1)}, f32[24,32,384]{2,1,0:T(8,128)S(1)},...) custom-call(f32[6,24]{1,0:T(8,128)S(1)} %concatenate.21.table_ref, ...), custom_call_target="tpu_custom_call" | custom-call | flops 26542080 | bytes 2359296 | tf_op jit(solution)/shard_map/advance_03/pallas_call | solution.py:266
  190.9 2.3 settle_03.4
  194.5 4.6 %collective-permute-start.36 = (f32[24,32,384]{2,1,0:T(8,128)S(1)}, f32[24,32,384]{2,1,0:T(8,128)S(1)}, u32[]{:S(2)}, u32[]{:S(2)}) collective-permute-start(f32[24,32,384]{2,1,0:T(8,128)S(1)} %get-tuple-element.225.refs_3_.refs_2_), channel_id=1, source_target_pairs={{0,8},{8,16},{16,24},{12,4},{20,12},{28,20},{1,9},{9,17},{17,25},{... | collective-permute-start | bytes 3538952 | tf_op jit(solution)/shard_map/ppermute | solution.py:558
  199.1 2.3 settle_12.4
  204.3 5.3 %collective-permute-done.40.refs_10_.next_ref.refs_6_ = f32[4,24,384]{2,1,0:T(8,128)S(1)} collective-permute-done((f32[4,24,384]{2,1,0:T(8,128)S(1)}, f32[4,24,384]{2,1,0:T(8,128)S(1)}, u32[]{:S(2)}, u32[]{:S(2)}) %collective-permute-start.40) | collective-permute-done | bytes 147488 | tf_op jit(solution)/shard_map/ppermute | solution.py:548
  210.4 2.1 collective-permute-start.41
  213.3 2.0 collective-permute-start.42
  215.3 2.7 advance_1.5
  218.2 2.7 advance_2.5
  222.2 3.2 %collective-permute-done.44 = f32[8,128]{1,0:T(8,128)S(1)} collective-permute-done((f32[8,128]{1,0:T(8,128)S(1)}, f32[8,128]{1,0:T(8,128)S(1)}, u32[]{:S(2)}, u32[]{:S(2)}) %collective-permute-start.44) | collective-permute-done | bytes 4128 | tf_op jit(solution)/shard_map/ppermute | solution.py:572
  226.8 5.0 %advance_03.5 = (f32[24,32,384]{2,1,0:T(8,128)S(1)}, f32[24,32,384]{2,1,0:T(8,128)S(1)}, f32[24,32,384]{2,1,0:T(8,128)S(1)}, f32[24,32,384]{2,1,0:T(8,128)S(1)},...) custom-call(f32[6,24]{1,0:T(8,128)S(1)} %concatenate.21.table_ref, ...), custom_call_target="tpu_custom_call" | custom-call | flops 26542080 | bytes 2359296 | tf_op jit(solution)/shard_map/advance_03/pallas_call | solution.py:266
  231.9 2.4 settle_12.5
  235.3 2.4 settle_03.5
  239.3 6.3 %pmin.7 = f32[4,384]{1,0:T(4,128)S(1)} all-reduce(f32[4,384]{1,0:T(4,128)} %pad_maximum_fusion.4), channel_id=1, replica_groups=mesh['px'=8,'vx'=4] {'vx'}, use_global_device_ids=true, to_apply=%region_0.1 | all-reduce | flops 1536 | bytes 12288 | tf_op jit(solution)/shard_map/pmin | solution.py:681
  247.9 2.0 place.3.refs_1_
  249.9 13.7 %collective-permute-done.47.refs_0_ = f32[24,32,384]{2,1,0:T(8,128)} collective-permute-done((f32[24,32,384]{2,1,0:T(8,128)}, f32[24,32,384]{2,1,0:T(8,128)}, u32[]{:S(2)}, u32[]{:S(2)}) %collective-permute-start.47) | collective-permute-done | bytes 1179680 | tf_op jit(solution)/shard_map/ppermute | solution.py:548
  263.5 2.3 place.4.refs_1_
  265.8 20.0 %collective-permute-done.46.refs_0_ = f32[24,32,384]{2,1,0:T(8,128)S(1)} collective-permute-done((f32[24,32,384]{2,1,0:T(8,128)}, f32[24,32,384]{2,1,0:T(8,128)S(1)}, u32[]{:S(2)}, u32[]{:S(2)}) %collective-permute-start.46) | collective-permute-done | bytes 1179680 | tf_op jit(solution)/shard_map/ppermute | solution.py:548
  285.9 1.6 place.5
  (151 shorter events, 50.0 us)
Async XLA Ops:
  0.7 2.3 copy-start.1
  3.1 4.7 %copy-start.8 = (f32[2,24]{1,0:T(2,128)S(1)}, f32[2,24]{1,0:T(2,128)}, u32[]{:S(2)}) copy-start(f32[2,24]{1,0:T(2,128)} %first_ref.1) | copy-start | bytes 580
  4.8 14.1 %copy-start.5 = (f32[64,384]{1,0:T(8,128)S(1)}, f32[64,384]{1,0:T(8,128)}, u32[]{:S(2)}) copy-start(f32[64,384]{1,0:T(8,128)} %refs_7_.11) | copy-start | bytes 294916
  4.8 41.9 %collective-permute-start.2 = (f32[24,32,384]{2,1,0:T(8,128)}, f32[24,32,384]{2,1,0:T(8,128)S(1)}, u32[]{:S(2)}, u32[]{:S(2)}) collective-permute-start(f32[24,32,384]{2,1,0:T(8,128)} %take.5), channel_id=1, source_target_pairs={{0,4},{4,0},{8,12},{12,8},{16,20},{20,16},{24,28},{28,24},{1,5},{5... | collective-permute-start | bytes 3538952 | tf_op jit(solution)/shard_map/ppermute | solution.py:548
  7.8 33.8 %collective-permute-start = (f32[2,24]{1,0:T(2,128)S(1)}, f32[2,24]{1,0:T(2,128)S(1)}, u32[]{:S(2)}, u32[]{:S(2)}) collective-permute-start(f32[2,24]{1,0:T(2,128)S(1)} %copy-done.8), channel_id=1, source_target_pairs={{0,4},{4,0},{8,12},{12,8},{16,20},{20,16},{24,28},{28,24},{1,5},{5... | collective-permute-start | bytes 584 | tf_op jit(solution)/shard_map/ppermute | solution.py:548
  8.9 6.9 %collective-permute-start.5 = (f32[2,64,384]{2,1,0:T(8,128)S(1)}, f32[2,64,384]{2,1,0:T(8,128)S(1)}, u32[]{:S(2)}, u32[]{:S(2)}) collective-permute-start(f32[2,64,384]{2,1,0:T(8,128)S(1)} %get-tuple-element.132), channel_id=1, source_target_pairs={{0,1},{1,2},{2,3},{4,5},{5,6},{6,7},{8,9},{9,10},{10,11},{12,13},{... | collective-permute-start | bytes 589832 | tf_op jit(solution)/shard_map/ppermute | solution.py:551
  11.5 31.4 %collective-permute-start.8 = (f32[2,24,384]{2,1,0:T(8,128)S(1)}, f32[2,24,384]{2,1,0:T(8,128)S(1)}, u32[]{:S(2)}, u32[]{:S(2)}) collective-permute-start(f32[2,24,384]{2,1,0:T(8,128)S(1)} %bitcast.28), channel_id=1, source_target_pairs={{0,4},{4,0},{8,12},{12,8},{16,20},{20,16},{24,28},{28,24},{1,5},{5... | collective-permute-start | bytes 221192 | tf_op jit(solution)/shard_map/ppermute | solution.py:548
  13.4 4.8 %collective-permute-start.6 = (f32[2,64,384]{2,1,0:T(8,128)S(1)}, f32[2,64,384]{2,1,0:T(8,128)S(1)}, u32[]{:S(2)}, u32[]{:S(2)}) collective-permute-start(f32[2,64,384]{2,1,0:T(8,128)S(1)} %get-tuple-element.133), channel_id=1, source_target_pairs={{1,0},{2,1},{3,2},{5,4},{6,5},{7,6},{9,8},{10,9},{11,10},{13,12},{... | collective-permute-start | bytes 589832 | tf_op jit(solution)/shard_map/ppermute | solution.py:554
  18.2 24.7 %collective-permute-start.7 = (f32[4,32,384]{2,1,0:T(8,128)S(1)}, f32[4,32,384]{2,1,0:T(8,128)S(1)}, u32[]{:S(2)}, u32[]{:S(2)}) collective-permute-start(f32[4,32,384]{2,1,0:T(8,128)S(1)} %pad_maximum_fusion), channel_id=1, source_target_pairs={{0,4},{4,0},{8,12},{12,8},{16,20},{20,16},{24,28},{28,24},{1,5},{5... | collective-permute-start | bytes 589832 | tf_op jit(solution)/shard_map/ppermute | solution.py:548
  18.8 2.3 copy-start.2
  21.2 9.4 %slice-start = ((s8[4718592]{0:T(1024)(128)(4,1)}), s8[4194304]{0:T(1024)(128)(4,1)S(1)}, s32[]{:S(2)}) async-start(s8[4718592]{0:T(1024)(128)(4,1)} %bitcast.22), calls=%async_computation | async-start | bytes 8388608
  23.4 16.5 %collective-permute-start.9 = (f32[8,128]{1,0:T(8,128)S(1)}, f32[8,128]{1,0:T(8,128)S(1)}, u32[]{:S(2)}, u32[]{:S(2)}) collective-permute-start(f32[8,128]{1,0:T(8,128)S(1)} %first_maxima.1), channel_id=1, source_target_pairs={{0,4},{4,0},{8,12},{12,8},{16,20},{20,16},{24,28},{28,24},{1,5},{5... | collective-permute-start | bytes 12296 | tf_op jit(solution)/shard_map/ppermute | solution.py:548
  24.9 2.3 copy-start.3
  27.3 3.3 %slice-start.1 = ((s8[4718592]{0:T(1024)(128)(4,1)}), s8[524288]{0:T(1024)(128)(4,1)S(1)}, s32[]{:S(2)}) async-start(s8[4718592]{0:T(1024)(128)(4,1)} %bitcast.22), calls=%async_computation.1 | async-start | bytes 1048576
  31.3 1.0 copy-start.6
  39.9 39.8 %collective-permute-start.1 = (f32[24,32,384]{2,1,0:T(8,128)}, f32[24,32,384]{2,1,0:T(8,128)}, u32[]{:S(2)}, u32[]{:S(2)}) collective-permute-start(f32[24,32,384]{2,1,0:T(8,128)} %take.6), channel_id=1, source_target_pairs={{0,4},{4,0},{8,12},{12,8},{16,20},{20,16},{24,28},{28,24},{1,5},{5... | collective-permute-start | bytes 3538952 | tf_op jit(solution)/shard_map/ppermute | solution.py:548
  41.6 45.9 %collective-permute-start.4 = (f32[24,32,384]{2,1,0:T(8,128)}, f32[24,32,384]{2,1,0:T(8,128)}, u32[]{:S(2)}, u32[]{:S(2)}) collective-permute-start(f32[24,32,384]{2,1,0:T(8,128)} %take.7), channel_id=1, source_target_pairs={{8,0},{16,8},{24,16},{4,12},{12,20},{20,28},{9,1},{17,9},{25,17},{... | collective-permute-start | bytes 3538952 | tf_op jit(solution)/shard_map/ppermute | solution.py:562
  42.9 52.7 %collective-permute-start.14 = (f32[24,32,384]{2,1,0:T(8,128)}, f32[24,32,384]{2,1,0:T(8,128)S(1)}, u32[]{:S(2)}, u32[]{:S(2)}) collective-permute-start(f32[24,32,384]{2,1,0:T(8,128)} %copy-done.6), channel_id=1, source_target_pairs={{0,4},{4,0},{8,12},{12,8},{16,20},{20,16},{24,28},{28,24},{1,5},{5... | collective-permute-start | bytes 3538952 | tf_op jit(solution)/shard_map/ppermute | solution.py:548
  46.7 40.8 %collective-permute-start.3 = (f32[24,32,384]{2,1,0:T(8,128)S(1)}, f32[24,32,384]{2,1,0:T(8,128)}, u32[]{:S(2)}, u32[]{:S(2)}) collective-permute-start(f32[24,32,384]{2,1,0:T(8,128)S(1)} %collective-permute-done.2.refs_2_.refs_3_), channel_id=1, source_target_pairs={{0,8},{8,16},{16,24},{12,4},{20,12},{28,20},{1,9},{9,17},{17,25},{... | collective-permute-start | bytes 3538952 | tf_op jit(solution)/shard_map/ppermute | solution.py:558
  50.3 2.3 copy-start
  53.3 1.0 copy-start.7
  54.3 1.2 collective-permute-start.10
  55.5 3.6 %collective-permute-start.11 = (f32[8,128]{1,0:T(8,128)S(1)}, f32[8,128]{1,0:T(8,128)S(1)}, u32[]{:S(2)}, u32[]{:S(2)}) collective-permute-start(f32[8,128]{1,0:T(8,128)S(1)} %max.61), channel_id=1, source_target_pairs={{0,2},{1,3},{2,0},{3,1},{4,6},{5,7},{6,4},{7,5},{8,10},{9,11},{10,... | collective-permute-start | bytes 12296 | tf_op jit(solution)/shard_map/ppermute | solution.py:572
  59.1 13.7 %collective-permute-start.12 = (f32[8,128]{1,0:T(8,128)S(1)}, f32[8,128]{1,0:T(8,128)S(1)}, u32[]{:S(2)}, u32[]{:S(2)}) collective-permute-start(f32[8,128]{1,0:T(8,128)S(1)} %max.62), channel_id=1, source_target_pairs={{0,8},{4,12},{8,0},{12,4},{16,24},{20,28},{24,16},{28,20},{1,9},{5... | collective-permute-start | bytes 12296 | tf_op jit(solution)/shard_map/ppermute | solution.py:572
  72.8 4.5 %collective-permute-start.13 = (f32[8,128]{1,0:T(8,128)S(1)}, f32[8,128]{1,0:T(8,128)S(1)}, u32[]{:S(2)}, u32[]{:S(2)}) collective-permute-start(f32[8,128]{1,0:T(8,128)S(1)} %max.63), channel_id=1, source_target_pairs={{0,16},{4,20},{8,24},{12,28},{16,0},{20,4},{24,8},{28,12},{1,17},{... | collective-permute-start | bytes 12296 | tf_op jit(solution)/shard_map/ppermute | solution.py:572
  77.3 40.4 %collective-permute-start.16 = (f32[24,32,384]{2,1,0:T(8,128)}, f32[24,32,384]{2,1,0:T(8,128)S(1)}, u32[]{:S(2)}, u32[]{:S(2)}) collective-permute-start(f32[24,32,384]{2,1,0:T(8,128)} %copy-done.7), channel_id=1, source_target_pairs={{0,4},{4,0},{8,12},{12,8},{16,20},{20,16},{24,28},{28,24},{1,5},{5... | collective-permute-start | bytes 3538952 | tf_op jit(solution)/shard_map/ppermute | solution.py:548
  79.6 2.3 copy-start.4
  82.0 11.8 %slice-start.2 = ((s8[4718592]{0:T(1024)(128)(4,1)}), s8[4194304]{0:T(1024)(128)(4,1)S(1)}, s32[]{:S(2)}) async-start(s8[4718592]{0:T(1024)(128)(4,1)} %bitcast.24), calls=%async_computation.2 | async-start | bytes 8388608
  87.5 6.3 %slice-start.3 = ((s8[4718592]{0:T(1024)(128)(4,1)}), s8[524288]{0:T(1024)(128)(4,1)S(1)}, s32[]{:S(2)}) async-start(s8[4718592]{0:T(1024)(128)(4,1)} %bitcast.24), calls=%async_computation.3 | async-start | bytes 1048576
  93.8 39.4 %slice-start.4 = ((s8[4718592]{0:T(1024)(128)(4,1)}), s8[4194304]{0:T(1024)(128)(4,1)S(1)}, s32[]{:S(2)}) async-start(s8[4718592]{0:T(1024)(128)(4,1)} %bitcast.26), calls=%async_computation.4 | async-start | bytes 8388608
  95.6 37.6 %slice-start.5 = ((s8[4718592]{0:T(1024)(128)(4,1)}), s8[524288]{0:T(1024)(128)(4,1)S(1)}, s32[]{:S(2)}) async-start(s8[4718592]{0:T(1024)(128)(4,1)} %bitcast.26), calls=%async_computation.5 | async-start | bytes 1048576
  96.8 45.9 %collective-permute-start.15 = (f32[24,32,384]{2,1,0:T(8,128)S(1)}, f32[24,32,384]{2,1,0:T(8,128)S(1)}, u32[]{:S(2)}, u32[]{:S(2)}) collective-permute-start(f32[24,32,384]{2,1,0:T(8,128)S(1)} %get-tuple-element.148.refs_1_.refs_2_), channel_id=1, source_target_pairs={{0,8},{8,16},{16,24},{12,4},{20,12},{28,20},{1,9},{9,17},{17,25},{... | collective-permute-start | bytes 3538952 | tf_op jit(solution)/shard_map/ppermute | solution.py:558
  99.2 48.9 %collective-permute-start.20 = (f32[24,32,384]{2,1,0:T(8,128)S(1)}, f32[24,32,384]{2,1,0:T(8,128)S(1)}, u32[]{:S(2)}, u32[]{:S(2)}) collective-permute-start(f32[24,32,384]{2,1,0:T(8,128)S(1)} %get-tuple-element.137.refs_0_), channel_id=1, source_target_pairs={{8,0},{16,8},{24,16},{4,12},{12,20},{20,28},{9,1},{17,9},{25,17},{... | collective-permute-start | bytes 3538952 | tf_op jit(solution)/shard_map/ppermute | solution.py:562
  119.0 7.8 %collective-permute-start.17 = (f32[4,32,384]{2,1,0:T(8,128)S(1)}, f32[4,32,384]{2,1,0:T(8,128)S(1)}, u32[]{:S(2)}, u32[]{:S(2)}) collective-permute-start(f32[4,32,384]{2,1,0:T(8,128)S(1)} %get-tuple-element.158.last_ref), channel_id=1, source_target_pairs={{0,1},{1,2},{2,3},{4,5},{5,6},{6,7},{8,9},{9,10},{10,11},{12,13},{... | collective-permute-start | bytes 589832 | tf_op jit(solution)/shard_map/ppermute | solution.py:551
  120.3 6.5 %collective-permute-start.18 = (f32[4,32,384]{2,1,0:T(8,128)S(1)}, f32[4,32,384]{2,1,0:T(8,128)S(1)}, u32[]{:S(2)}, u32[]{:S(2)}) collective-permute-start(f32[4,32,384]{2,1,0:T(8,128)S(1)} %get-tuple-element.159.first_ref), channel_id=1, source_target_pairs={{1,0},{2,1},{3,2},{5,4},{6,5},{7,6},{9,8},{10,9},{11,10},{13,12},{... | collective-permute-start | bytes 589832 | tf_op jit(solution)/shard_map/ppermute | solution.py:554
  121.6 5.2 %collective-permute-start.19 = (f32[4,24,384]{2,1,0:T(8,128)S(1)}, f32[4,24,384]{2,1,0:T(8,128)S(1)}, u32[]{:S(2)}, u32[]{:S(2)}) collective-permute-start(f32[4,24,384]{2,1,0:T(8,128)S(1)} %get-tuple-element.160), channel_id=1, source_target_pairs={{0,4},{4,0},{8,12},{12,8},{16,20},{20,16},{24,28},{28,24},{1,5},{5... | collective-permute-start | bytes 442376 | tf_op jit(solution)/shard_map/ppermute | solution.py:548
  127.5 3.5 %collective-permute-start.21 = (f32[8,128]{1,0:T(8,128)S(1)}, f32[8,128]{1,0:T(8,128)S(1)}, u32[]{:S(2)}, u32[]{:S(2)}) collective-permute-start(f32[8,128]{1,0:T(8,128)S(1)} %edge_maxima.3), channel_id=1, source_target_pairs={{0,1},{1,0},{2,3},{3,2},{4,5},{5,4},{6,7},{7,6},{8,9},{9,8},{10,11... | collective-permute-start | bytes 12296 | tf_op jit(solution)/shard_map/ppermute | solution.py:572
  131.1 4.9 %collective-permute-start.22 = (f32[8,128]{1,0:T(8,128)S(1)}, f32[8,128]{1,0:T(8,128)S(1)}, u32[]{:S(2)}, u32[]{:S(2)}) collective-permute-start(f32[8,128]{1,0:T(8,128)S(1)} %max.65), channel_id=1, source_target_pairs={{0,2},{1,3},{2,0},{3,1},{4,6},{5,7},{6,4},{7,5},{8,10},{9,11},{10,... | collective-permute-start | bytes 12296 | tf_op jit(solution)/shard_map/ppermute | solution.py:572
  136.0 5.0 %collective-permute-start.23 = (f32[8,128]{1,0:T(8,128)S(1)}, f32[8,128]{1,0:T(8,128)S(1)}, u32[]{:S(2)}, u32[]{:S(2)}) collective-permute-start(f32[8,128]{1,0:T(8,128)S(1)} %max.66), channel_id=1, source_target_pairs={{0,4},{4,0},{8,12},{12,8},{16,20},{20,16},{24,28},{28,24},{1,5},{5... | collective-permute-start | bytes 12296 | tf_op jit(solution)/shard_map/ppermute | solution.py:572
  141.0 4.5 %collective-permute-start.24 = (f32[8,128]{1,0:T(8,128)S(1)}, f32[8,128]{1,0:T(8,128)S(1)}, u32[]{:S(2)}, u32[]{:S(2)}) collective-permute-start(f32[8,128]{1,0:T(8,128)S(1)} %max.67), channel_id=1, source_target_pairs={{0,8},{4,12},{8,0},{12,4},{16,24},{20,28},{24,16},{28,20},{1,9},{5... | collective-permute-start | bytes 12296 | tf_op jit(solution)/shard_map/ppermute | solution.py:572
  145.5 5.5 %collective-permute-start.25 = (f32[8,128]{1,0:T(8,128)S(1)}, f32[8,128]{1,0:T(8,128)S(1)}, u32[]{:S(2)}, u32[]{:S(2)}) collective-permute-start(f32[8,128]{1,0:T(8,128)S(1)} %max.68), channel_id=1, source_target_pairs={{0,16},{4,20},{8,24},{12,28},{16,0},{20,4},{24,8},{28,12},{1,17},{... | collective-permute-start | bytes 12296 | tf_op jit(solution)/shard_map/ppermute | solution.py:572
  153.0 33.1 %collective-permute-start.27 = (f32[24,32,384]{2,1,0:T(8,128)S(1)}, f32[24,32,384]{2,1,0:T(8,128)S(1)}, u32[]{:S(2)}, u32[]{:S(2)}) collective-permute-start(f32[24,32,384]{2,1,0:T(8,128)S(1)} %get-tuple-element.182.refs_0_.refs_8_.refs_6_), channel_id=1, source_target_pairs={{8,0},{16,8},{24,16},{4,12},{12,20},{20,28},{9,1},{17,9},{25,17},{... | collective-permute-start | bytes 3538952 | tf_op jit(solution)/shard_map/ppermute | solution.py:562
  154.3 31.8 %collective-permute-start.26 = (f32[24,32,384]{2,1,0:T(8,128)S(1)}, f32[24,32,384]{2,1,0:T(8,128)S(1)}, u32[]{:S(2)}, u32[]{:S(2)}) collective-permute-start(f32[24,32,384]{2,1,0:T(8,128)S(1)} %get-tuple-element.192.refs_3_.refs_2_.refs_9_.refs_7_), channel_id=1, source_target_pairs={{0,8},{8,16},{16,24},{12,4},{20,12},{28,20},{1,9},{9,17},{17,25},{... | collective-permute-start | bytes 3538952 | tf_op jit(solution)/shard_map/ppermute | solution.py:558
  161.1 8.3 %collective-permute-start.28 = (f32[4,32,384]{2,1,0:T(8,128)S(1)}, f32[4,32,384]{2,1,0:T(8,128)S(1)}, u32[]{:S(2)}, u32[]{:S(2)}) collective-permute-start(f32[4,32,384]{2,1,0:T(8,128)S(1)} %get-tuple-element.193.last_ref), channel_id=1, source_target_pairs={{0,1},{1,2},{2,3},{4,5},{5,6},{6,7},{8,9},{9,10},{10,11},{12,13},{... | collective-permute-start | bytes 589832 | tf_op jit(solution)/shard_map/ppermute | solution.py:551
  162.4 7.0 %collective-permute-start.29 = (f32[4,32,384]{2,1,0:T(8,128)S(1)}, f32[4,32,384]{2,1,0:T(8,128)S(1)}, u32[]{:S(2)}, u32[]{:S(2)}) collective-permute-start(f32[4,32,384]{2,1,0:T(8,128)S(1)} %get-tuple-element.194.first_ref), channel_id=1, source_target_pairs={{1,0},{2,1},{3,2},{5,4},{6,5},{7,6},{9,8},{10,9},{11,10},{13,12},{... | collective-permute-start | bytes 589832 | tf_op jit(solution)/shard_map/ppermute | solution.py:554
  163.7 5.7 %collective-permute-start.30 = (f32[4,24,384]{2,1,0:T(8,128)S(1)}, f32[4,24,384]{2,1,0:T(8,128)S(1)}, u32[]{:S(2)}, u32[]{:S(2)}) collective-permute-start(f32[4,24,384]{2,1,0:T(8,128)S(1)} %get-tuple-element.195), channel_id=1, source_target_pairs={{0,4},{4,0},{8,12},{12,8},{16,20},{20,16},{24,28},{28,24},{1,5},{5... | collective-permute-start | bytes 442376 | tf_op jit(solution)/shard_map/ppermute | solution.py:548
  170.1 2.7 collective-permute-start.31
  172.8 4.4 %collective-permute-start.32 = (f32[8,128]{1,0:T(8,128)S(1)}, f32[8,128]{1,0:T(8,128)S(1)}, u32[]{:S(2)}, u32[]{:S(2)}) collective-permute-start(f32[8,128]{1,0:T(8,128)S(1)} %max.70), channel_id=1, source_target_pairs={{0,2},{1,3},{2,0},{3,1},{4,6},{5,7},{6,4},{7,5},{8,10},{9,11},{10,... | collective-permute-start | bytes 12296 | tf_op jit(solution)/shard_map/ppermute | solution.py:572
  177.2 3.7 %collective-permute-start.33 = (f32[8,128]{1,0:T(8,128)S(1)}, f32[8,128]{1,0:T(8,128)S(1)}, u32[]{:S(2)}, u32[]{:S(2)}) collective-permute-start(f32[8,128]{1,0:T(8,128)S(1)} %max.71), channel_id=1, source_target_pairs={{0,4},{4,0},{8,12},{12,8},{16,20},{20,16},{24,28},{28,24},{1,5},{5... | collective-permute-start | bytes 12296 | tf_op jit(solution)/shard_map/ppermute | solution.py:572
  180.9 3.6 %collective-permute-start.34 = (f32[8,128]{1,0:T(8,128)S(1)}, f32[8,128]{1,0:T(8,128)S(1)}, u32[]{:S(2)}, u32[]{:S(2)}) collective-permute-start(f32[8,128]{1,0:T(8,128)S(1)} %max.72), channel_id=1, source_target_pairs={{0,8},{4,12},{8,0},{12,4},{16,24},{20,28},{24,16},{28,20},{1,9},{5... | collective-permute-start | bytes 12296 | tf_op jit(solution)/shard_map/ppermute | solution.py:572
  184.5 6.4 %collective-permute-start.35 = (f32[8,128]{1,0:T(8,128)S(1)}, f32[8,128]{1,0:T(8,128)S(1)}, u32[]{:S(2)}, u32[]{:S(2)}) collective-permute-start(f32[8,128]{1,0:T(8,128)S(1)} %max.73), channel_id=1, source_target_pairs={{0,16},{4,20},{8,24},{12,28},{16,0},{20,4},{24,8},{28,12},{1,17},{... | collective-permute-start | bytes 12296 | tf_op jit(solution)/shard_map/ppermute | solution.py:572
  193.2 33.7 %collective-permute-start.37 = (f32[24,32,384]{2,1,0:T(8,128)S(1)}, f32[24,32,384]{2,1,0:T(8,128)S(1)}, u32[]{:S(2)}, u32[]{:S(2)}) collective-permute-start(f32[24,32,384]{2,1,0:T(8,128)S(1)} %get-tuple-element.215.refs_0_), channel_id=1, source_target_pairs={{8,0},{16,8},{24,16},{4,12},{12,20},{20,28},{9,1},{17,9},{25,17},{... | collective-permute-start | bytes 3538952 | tf_op jit(solution)/shard_map/ppermute | solution.py:562
  194.5 32.4 %collective-permute-start.36 = (f32[24,32,384]{2,1,0:T(8,128)S(1)}, f32[24,32,384]{2,1,0:T(8,128)S(1)}, u32[]{:S(2)}, u32[]{:S(2)}) collective-permute-start(f32[24,32,384]{2,1,0:T(8,128)S(1)} %get-tuple-element.225.refs_3_.refs_2_), channel_id=1, source_target_pairs={{0,8},{8,16},{16,24},{12,4},{20,12},{28,20},{1,9},{9,17},{17,25},{... | collective-permute-start | bytes 3538952 | tf_op jit(solution)/shard_map/ppermute | solution.py:558
  201.4 8.2 %collective-permute-start.38 = (f32[4,32,384]{2,1,0:T(8,128)S(1)}, f32[4,32,384]{2,1,0:T(8,128)S(1)}, u32[]{:S(2)}, u32[]{:S(2)}) collective-permute-start(f32[4,32,384]{2,1,0:T(8,128)S(1)} %get-tuple-element.226.last_ref), channel_id=1, source_target_pairs={{0,1},{1,2},{2,3},{4,5},{5,6},{6,7},{8,9},{9,10},{10,11},{12,13},{... | collective-permute-start | bytes 589832 | tf_op jit(solution)/shard_map/ppermute | solution.py:551
  202.7 6.9 %collective-permute-start.39 = (f32[4,32,384]{2,1,0:T(8,128)S(1)}, f32[4,32,384]{2,1,0:T(8,128)S(1)}, u32[]{:S(2)}, u32[]{:S(2)}) collective-permute-start(f32[4,32,384]{2,1,0:T(8,128)S(1)} %get-tuple-element.227.first_ref), channel_id=1, source_target_pairs={{1,0},{2,1},{3,2},{5,4},{6,5},{7,6},{9,8},{10,9},{11,10},{13,12},{... | collective-permute-start | bytes 589832 | tf_op jit(solution)/shard_map/ppermute | solution.py:554
  204.2 5.4 %collective-permute-start.40 = (f32[4,24,384]{2,1,0:T(8,128)S(1)}, f32[4,24,384]{2,1,0:T(8,128)S(1)}, u32[]{:S(2)}, u32[]{:S(2)}) collective-permute-start(f32[4,24,384]{2,1,0:T(8,128)S(1)} %get-tuple-element.228), channel_id=1, source_target_pairs={{0,4},{4,0},{8,12},{12,8},{16,20},{20,16},{24,28},{28,24},{1,5},{5... | collective-permute-start | bytes 442376 | tf_op jit(solution)/shard_map/ppermute | solution.py:548
  210.4 2.9 %collective-permute-start.41 = (f32[8,128]{1,0:T(8,128)S(1)}, f32[8,128]{1,0:T(8,128)S(1)}, u32[]{:S(2)}, u32[]{:S(2)}) collective-permute-start(f32[8,128]{1,0:T(8,128)S(1)} %edge_maxima.5), channel_id=1, source_target_pairs={{0,1},{1,0},{2,3},{3,2},{4,5},{5,4},{6,7},{7,6},{8,9},{9,8},{10,11... | collective-permute-start | bytes 12296 | tf_op jit(solution)/shard_map/ppermute | solution.py:572
  213.3 4.8 %collective-permute-start.42 = (f32[8,128]{1,0:T(8,128)S(1)}, f32[8,128]{1,0:T(8,128)S(1)}, u32[]{:S(2)}, u32[]{:S(2)}) collective-permute-start(f32[8,128]{1,0:T(8,128)S(1)} %max.75), channel_id=1, source_target_pairs={{0,2},{1,3},{2,0},{3,1},{4,6},{5,7},{6,4},{7,5},{8,10},{9,11},{10,... | collective-permute-start | bytes 12296 | tf_op jit(solution)/shard_map/ppermute | solution.py:572
  218.1 3.7 %collective-permute-start.43 = (f32[8,128]{1,0:T(8,128)S(1)}, f32[8,128]{1,0:T(8,128)S(1)}, u32[]{:S(2)}, u32[]{:S(2)}) collective-permute-start(f32[8,128]{1,0:T(8,128)S(1)} %max.76), channel_id=1, source_target_pairs={{0,4},{4,0},{8,12},{12,8},{16,20},{20,16},{24,28},{28,24},{1,5},{5... | collective-permute-start | bytes 12296 | tf_op jit(solution)/shard_map/ppermute | solution.py:572
  221.8 3.6 %collective-permute-start.44 = (f32[8,128]{1,0:T(8,128)S(1)}, f32[8,128]{1,0:T(8,128)S(1)}, u32[]{:S(2)}, u32[]{:S(2)}) collective-permute-start(f32[8,128]{1,0:T(8,128)S(1)} %max.77), channel_id=1, source_target_pairs={{0,8},{4,12},{8,0},{12,4},{16,24},{20,28},{24,16},{28,20},{1,9},{5... | collective-permute-start | bytes 12296 | tf_op jit(solution)/shard_map/ppermute | solution.py:572
  225.4 6.5 %collective-permute-start.45 = (f32[8,128]{1,0:T(8,128)S(1)}, f32[8,128]{1,0:T(8,128)S(1)}, u32[]{:S(2)}, u32[]{:S(2)}) collective-permute-start(f32[8,128]{1,0:T(8,128)S(1)} %max.78), channel_id=1, source_target_pairs={{0,16},{4,20},{8,24},{12,28},{16,0},{20,4},{24,8},{28,12},{1,17},{... | collective-permute-start | bytes 12296 | tf_op jit(solution)/shard_map/ppermute | solution.py:572
  234.3 29.2 %collective-permute-start.47 = (f32[24,32,384]{2,1,0:T(8,128)}, f32[24,32,384]{2,1,0:T(8,128)}, u32[]{:S(2)}, u32[]{:S(2)}) collective-permute-start(f32[24,32,384]{2,1,0:T(8,128)} %get-tuple-element.249), channel_id=1, source_target_pairs={{0,4},{4,0},{8,12},{12,8},{16,20},{20,16},{24,28},{28,24},{1,5},{5... | collective-permute-start | bytes 3538952 | tf_op jit(solution)/shard_map/ppermute | solution.py:548
  237.8 48.1 %collective-permute-start.46 = (f32[24,32,384]{2,1,0:T(8,128)}, f32[24,32,384]{2,1,0:T(8,128)S(1)}, u32[]{:S(2)}, u32[]{:S(2)}) collective-permute-start(f32[24,32,384]{2,1,0:T(8,128)} %get-tuple-element.248), channel_id=1, source_target_pairs={{0,4},{4,0},{8,12},{12,8},{16,20},{20,16},{24,28},{28,24},{1,5},{5... | collective-permute-start | bytes 3538952 | tf_op jit(solution)/shard_map/ppermute | solution.py:548
  246.8 40.6 %collective-permute-start.48 = (f32[2,384]{1,0:T(2,128)}, f32[2,384]{1,0:T(2,128)}, u32[]{:S(2)}, u32[]{:S(2)}) collective-permute-start(f32[2,384]{1,0:T(2,128)} %rev.6), channel_id=1, source_target_pairs={{0,4},{4,0},{8,12},{12,8},{16,20},{20,16},{24,28},{28,24},{1,5},{5... | collective-permute-start | bytes 9224 | tf_op jit(solution)/shard_map/ppermute | solution.py:548

commit v4 on v3

--- a/solution.py
+++ b/solution.py
@@ -101,12 +101,8 @@
     return jax.ShapeDtypeStruct(shape, jnp.float32)
 
 
-def estimate(cells, flops):
-    return pl.CostEstimate(flops=flops * cells, bytes_accessed=4 * cells, transcendentals=0)
-
-
-def slabs(tile):
-    return [tile[start : start + 8] for start in range(0, tile.shape[0], 8)]
+def estimate():
+    return pl.CostEstimate(flops=0, bytes_accessed=0, transcendentals=0)
 
 
 def advance(sizes, targets, rows, bases, halo_rows, vx_low, vx_high, vy_next, maxima, stepper, accel_second, table):
@@ -270,7 +266,7 @@
         out_specs=[whole()] * n_out,
         scratch_shapes=[pltpu.VMEM((half, LANES), jnp.float32)] * 2 + [pltpu.VMEM((half, width), jnp.float32)] * 2,
         compiler_params=compiler_params(),
-        cost_estimate=estimate(count * cells_v * half * width, 45),
+        cost_estimate=estimate(),
         name="advance_" + "".join(str(t) for t in targets),
     )(table, *ops.arrays)
 
@@ -392,7 +388,7 @@
         in_specs=[scalars()] + [whole()] * n_in,
         out_specs=[whole()] * len(shapes),
         compiler_params=compiler_params(),
-        cost_estimate=estimate(count * cells_v * half * width, 15),
+        cost_estimate=estimate(),
         name="settle_" + "".join(str(t) for t in targets),
     )(flags, *ops.arrays)
     return outs[:count], outs[count:]
@@ -444,6 +440,7 @@
         in_specs=[scalars()] + [whole()] * 5,
         out_specs=whole(),
         compiler_params=compiler_params(),
+        cost_estimate=estimate(),
         name="first_maxima",
     )(flags, value, vx_low, vx_high, accel_first, accel_second)
 
@@ -468,49 +465,30 @@
         in_specs=[scalars()] + [whole()] * 9,
         out_specs=whole(),
         compiler_params=compiler_params(),
+        cost_estimate=estimate(),
         name="edge_maxima",
     )(flags, first, second, before, last, vx_low, vx_high, inner, vy_next, part)
 
 
-def take(flags, array, outer, which):
-    _, cells_v, total_vy, width = array.shape
-    half = total_vy // 2
-
-    def body(flags_ref, array_ref, out_ref, sem):
-        parity = flags_ref[0]
-        start = pl.multiple_of((parity if which == 0 else 1 - parity) * half, half)
-        copy = pltpu.make_async_copy(array_ref.at[parity if outer else 1 - parity, :, pl.ds(start, half), :], out_ref, sem)
-        copy.start()
-        copy.wait()
-
-    return pl.pallas_call(
-        body,
-        in_specs=[scalars(), pl.BlockSpec(memory_space=pl.ANY)],
-        out_specs=whole(),
-        out_shape=f32(cells_v, half, width),
-        scratch_shapes=[pltpu.SemaphoreType.DMA],
-        compiler_params=compiler_params(),
-        cost_estimate=estimate(cells_v * half * width, 1),
-        name="take",
-    )(flags, array)
-
-
-def place(flags, pieces, which, result, shape):
-    half = shape[2] // 2
+def copies(flags_ref, pieces, out_ref, sems, which):
+    parity = flags_ref[0]
+    half = out_ref.shape[2] // 2
+    start = pl.multiple_of((parity if which == 0 else 1 - parity) * half, half)
+    return [
+        pltpu.make_async_copy(ref, out_ref.at[parity if outer else 1 - parity, :, pl.ds(start, half), :], sems.at[i])
+        for i, (outer, ref) in enumerate(pieces)
+    ]
+
+
+def place(flags, pieces, result, shape, which=0):
     count = len(pieces)
 
     def body(flags_ref, *refs):
-        out_ref, sems = refs[-2:]
-        parity = flags_ref[0]
-        start = pl.multiple_of((parity if which == 0 else 1 - parity) * half, half)
-        copies = []
-        for i in range(count):
-            row = parity if pieces[i][0] else 1 - parity
-            copies.append(pltpu.make_async_copy(refs[i], out_ref.at[row, :, pl.ds(start, half), :], sems.at[i]))
-        for copy in copies:
-            copy.start()
-        for copy in copies:
-            copy.wait()
+        moves = copies(flags_ref, [(pieces[i][0], refs[i]) for i in range(count)], refs[-2], refs[-1], which)
+        for move in moves:
+            move.start()
+        for move in moves:
+            move.wait()
 
     anywhere = pl.BlockSpec(memory_space=pl.ANY)
     extra = [] if result is None else [result]
@@ -518,12 +496,36 @@
         body,
         in_specs=[scalars()] + [whole()] * count + [anywhere] * len(extra),
         out_specs=anywhere,
-        out_shape=jax.ShapeDtypeStruct(shape, jnp.float32),
+        out_shape=f32(*shape),
         input_output_aliases={} if result is None else {1 + count: 0},
         scratch_shapes=[pltpu.SemaphoreType.DMA((count,))],
         compiler_params=compiler_params(),
+        cost_estimate=estimate(),
         name="place",
     )(flags, *[p[1] for p in pieces], *extra)
+
+
+def finish(flags, outer, least, least_got, result):
+    def body(flags_ref, outer_ref, least_ref, got_ref, _, out_ref, funnel_ref, sems):
+        parity = flags_ref[0]
+        (move,) = copies(flags_ref, [(True, outer_ref)], out_ref, sems, 1)
+        move.start()
+        funnel_ref[pl.ds(parity, 1), :] = jnp.minimum(least_ref[0:1], got_ref[1:2])
+        funnel_ref[pl.ds(1 - parity, 1), :] = jnp.minimum(least_ref[1:2], got_ref[0:1])
+        move.wait()
+
+    anywhere = pl.BlockSpec(memory_space=pl.ANY)
+    return pl.pallas_call(
+        body,
+        in_specs=[scalars()] + [whole()] * 3 + [anywhere],
+        out_specs=[anywhere, whole()],
+        out_shape=[f32(*result.shape), f32(2, result.shape[3])],
+        input_output_aliases={4: 0},
+        scratch_shapes=[pltpu.SemaphoreType.DMA((1,))],
+        compiler_params=compiler_params(),
+        cost_estimate=estimate(),
+        name="finish",
+    )(flags, outer, least, least_got, result)
 
 
 def per_device(value, cost, accel_first, accel_second):
@@ -575,10 +577,12 @@
             maxima = jnp.maximum(maxima, other)
         return maxima
 
-    value_outer = take(flags, value, True, 1)
+    def half_of(array, row, which):
+        return lax.dynamic_slice(array, (row, 0, which * half, 0), (1, cells_v, half, width))[0]
+
+    value_outer = half_of(value, parity, 1 - parity)
+    late = after(parity, value_outer)
     value_outer_got = partner(value_outer)
-    value_inner = after(take(flags, value, False, 1), value_outer)
-    value_inner_got = partner(value_inner)
     push_got = partner(after(accel_first, value_outer))
 
     low_own = from_low_vx(after(value[:, cells_v - 1], value_outer))
@@ -587,21 +591,12 @@
     row_given = lax.dynamic_slice(value, (0, 0, half - 1 + parity, 0), (rows, cells_v, 1, width))[:, :, 0]
     row_got = partner(after(row_given, value_outer))
 
-    def chain_halo(own):
-        given = lax.dynamic_slice(own, (0, (1 - parity) * half, 0), (rows, half, width))
-        mine = lax.dynamic_slice(own, (0, parity * half, 0), (rows, half, width))
-        return mine, given
-
-    low_mine, low_given = chain_halo(low_own)
-    high_mine, high_given = chain_halo(high_own)
-    halo_given = jnp.concatenate([low_given, high_given], axis=0)
-    got = partner(halo_given)
     maxima = first_maxima(value, low_own, high_own, accel_first, accel_second, flags)
     maxima = jnp.maximum(maxima, partner(maxima))
-    ahead = (maxima, got, row_got, push_got)
-    cost_outer = after(take(flags, cost, True, 1), *ahead)
-    cost_outer_got = partner(cost_outer)
-    cost_inner_got = partner(after(take(flags, cost, False, 1), *ahead))
+    ahead = (maxima, row_got, push_got)
+    value_inner_got = partner(after(half_of(value, 1 - late, 1 - late), *ahead))
+    cost_outer_got = partner(after(half_of(cost, late, 1 - late), *ahead))
+    cost_inner_got = partner(after(half_of(cost, 1 - late, 1 - late), *ahead))
     shared_first = share(maxima, partner_done=True)
 
     def pick(x, which):
@@ -610,8 +605,12 @@
     def in_chain(mine, others):
         return jnp.concatenate([pick(mine, parity), pick(mine, 1 - parity), pick(others, parity), pick(others, 1 - parity)], axis=0)
 
-    vx_low = in_chain(low_mine, got[:rows])
-    vx_high = in_chain(high_mine, got[rows:])
+    def halo_chain(own, received):
+        mine = lax.dynamic_slice(own, (0, parity * half, 0), (rows, half, width))
+        return jnp.concatenate([pick(mine, parity), pick(mine, 1 - parity), received], axis=0)
+
+    vx_low = halo_chain(low_own, from_low_vx(jnp.stack([value_inner_got[cells_v - 1], value_outer_got[cells_v - 1]])))
+    vx_high = halo_chain(high_own, from_high_vx(jnp.stack([value_inner_got[0], value_outer_got[0]])))
     vy_next = jnp.concatenate([pick(row_got, 1 - parity), pick(row_got, parity), pick(row_needed, 1 - parity), pick(row_needed, parity)], axis=0)
     push = in_chain(accel_first, push_got)
     positions = (vx * cells_v + jnp.arange(cells_v, dtype=jnp.int32)).astype(jnp.float32)
@@ -621,7 +620,7 @@
 
     chain = [Own(value, True), Own(value, False), Row(value_inner_got), Row(value_outer_got)]
     costs = [Own(cost, True), Own(cost, False), Row(cost_inner_got), Row(cost_outer_got)]
-    halo_rows = (halo_before(value_outer_got), halo_after(after(take(flags, value, True, 0), value_inner)))
+    halo_rows = (halo_before(value_outer_got), halo_after(half_of(value, late, late)))
 
     def advanced(targets, field, bases, halo_rows, vx_low, vx_high, vy_next, stepper):
         some = None if bases is None else [bases[t] for t in targets]
@@ -674,17 +673,14 @@
 
     updates, shared = next_updates(middle, edges, chain, shared_second, halo_rows, False)
     damping = (shared_first, shared_second, shared, 0.5)
-    (inner, near), (least_inner,) = settled((1, 2), updates, damping=damping, with_edges=False)
+    (near,), (least_near,) = settled((2,), updates, damping=damping, with_edges=False)
     inner_got = partner(near)
-    (outer, far), (least_outer,) = settled((0, 3), updates, damping=damping, with_edges=False)
+    (outer, inner, far), (least,) = settled((0, 1, 3), updates, damping=damping, with_edges=False)
     outer_got = partner(far)
-    least = lax.pmin(jnp.concatenate([least_outer, least_inner], axis=0), "vx")
-    least_got = partner(after(least[1::2][::-1], far))
-    final = place(flags, [(True, outer), (False, inner)], 0, None, value.shape)
-    final = place(flags, [(False, inner_got)], 1, final, value.shape)
-    final = place(flags, [(True, outer_got)], 1, final, value.shape)
-    funnel = jnp.minimum(least[0::2], after(least_got, final)[::-1])
-    return final, jnp.concatenate([pick(funnel, parity), pick(funnel, 1 - parity)], axis=0)
+    least = lax.pmin(jnp.concatenate([least[:2], least_near, least[2:]], axis=0), "vx")
+    least_got = partner(after(least[2:], far))
+    final = place(flags, [(True, outer), (False, inner)], None, value.shape)
+    return finish(flags, outer_got, least, least_got, place(flags, [(False, inner_got)], final, value.shape, 1))
 
 
 def solution(mesh):

time: 290 us -> 282 us (0.972)
  Pallas kernels: 78.1 us -> 70.5 us
  local copies, waits for them, and re-layouts: 19.9 us -> 14.9 us
  waiting for transfers between devices: 105 us -> 108 us
    unnamed x31 -> x17, local copies, waits for them, and re-layouts: 13.8 us -> 2.38 us
    squeeze x1 -> x4, local copies, waits for them, and re-layouts: 1.05 us -> 10 us  [the longest x3 8.97 us: half_of(): lax.dynamic_slice(array, (row, 0, which * half, 0), (1, cells_v, half, wi...]
    ppermute x19, waiting for transfers between devices: 29.2 us -> 36.6 us  [share(): lax.ppermute(maxima, axis, [(i, i ^ apart) for i in range(lax.axis_size(a...]
    ppermute x14 -> x13, waiting for transfers between devices: 73.2 us -> 66.7 us  [partner(): return lax.ppermute(x, 'px', [(i, i ^ 1) for i in range(n_px)])]
    pallas_call x5 -> x1, Pallas kernels: 6.27 us -> 2.15 us  [finish(): pl.pallas_call(body, in_specs=[scalars()] + [whole()] * 3 + [anywhere], o...]
    ppermute x14 -> x13, starting transfers between devices: 19.4 us -> 17.4 us  [partner(): return lax.ppermute(x, 'px', [(i, i ^ 1) for i in range(n_px)])]
    pallas_call x3 -> x2, Pallas kernels: 5.84 us -> 4.27 us  [place(): pl.pallas_call(body, in_specs=[scalars()] + [whole()] * count + [anywhere...]
    ppermute x4 -> x5, starting transfers between devices: 5.34 us -> 6.63 us  [from_high_vx(): return lax.ppermute(x, 'vx', [(i + 1, i) for i in range(n_vx - 1)])]
  transfers between devices with their start and end apart: 49 -> 50, of which waited for: 19 -> 19; matrix products, arithmetic and copies ran while one was open for 2% -> 4% of each run, Pallas kernels for 24% -> 22%
where the time goes in v4:
time: 282 us; the launch traced here: 281 us
  waiting for transfers between devices  108 us (38%)
  starting transfers between devices  79.8 us (28%)
  Pallas kernels  70.5 us (25%)
  local copies, waits for them, and re-layouts  14.9 us (5%)
  blocking collectives  6.26 us (2%)
    ppermute x13, waiting for transfers between devices, partner(): return lax.ppermute(x, 'px', [(i, i ^ 1) for i in range(n_px)])  66.7 us
    pallas_call x12, Pallas kernels, advance(): pl.pallas_call(body, out_shape=[f32(cells_v, half, width)] * n_out, in_sp...  41.9 us
    ppermute x19, waiting for transfers between devices, share(): lax.ppermute(maxima, axis, [(i, i ^ apart) for i in range(lax.axis_size(a...  36.6 us
    ppermute x19, starting transfers between devices, share(): lax.ppermute(maxima, axis, [(i, i ^ apart) for i in range(lax.axis_size(a...  28.7 us
    pallas_call x9, Pallas kernels, settle(): pl.pallas_call(body, out_shape=shapes, in_specs=[scalars()] + [whole()] *...  17.9 us
    ppermute x13, starting transfers between devices, partner(): return lax.ppermute(x, 'px', [(i, i ^ 1) for i in range(n_px)])  17.4 us
    ppermute x4, starting transfers between devices, halo_before(): return lax.ppermute(outermost, 'px', moves)  15.4 us
    squeeze x3, local copies, waits for them, and re-layouts, half_of(): lax.dynamic_slice(array, (row, 0, which * half, 0), (1, cells_v, half, wi...  8.97 us
  transfers between devices with their start and end apart: 50, of which 19 were waited for; matrix products, arithmetic and copies ran while one was open for 4% of the time, Pallas kernels for 22%

profile of v4, /device:TPU:0, one launch (start us, length us, event | category | flops | bytes accessed | tf_op | source)
XLA Modules:
  0.0 281.4 jit_solution(4297178358549216053)
XLA Ops:
  0.7 2.4 dynamic-slice_bitcast_fusion.4
  3.0 2.9 %collective-permute-start.6 = (f32[24,32,384]{2,1,0:T(8,128)}, f32[24,32,384]{2,1,0:T(8,128)S(1)}, u32[]{:S(2)}, u32[]{:S(2)}) collective-permute-start(f32[24,32,384]{2,1,0:T(8,128)} %dynamic-slice_bitcast_fusion.4), channel_id=1, source_target_pairs={{0,4},{4,0},{8,12},{12,8},{16,20},{20,16},{24,28},{28,24},{1,5},{5... | collective-permute-start | bytes 3538952 | tf_op jit(solution)/shard_map/ppermute | solution.py:550
  7.1 2.1 collective-permute-start.4
  14.2 3.4 %dynamic-slice_bitcast_fusion.2 = (f32[24,32,384]{2,1,0:T(8,128)}, f32[24,32,384]{2,1,0:T(8,128)}) fusion(f32[2,24,64,384]{3,2,1,0:T(8,128)} %refs_3_.3, s32[]{:T(128)S(6)} %select_n.88, s32[]{:T(128)S(6)} %select_n.89, s32[]{:T(128)S(6)} %select_n.85, s32[]{:T(128)S(6)} %select_n.86), kind=kLoop, calls=%fused_computation.2 | loop fusion | bytes 4718608 | tf_op jit(solution)/shard_map/squeeze | solution.py:581
  18.9 2.2 first_maxima.1
  21.1 3.8 %collective-permute-start.3 = (f32[8,128]{1,0:T(8,128)S(1)}, f32[8,128]{1,0:T(8,128)S(1)}, u32[]{:S(2)}, u32[]{:S(2)}) collective-permute-start(f32[8,128]{1,0:T(8,128)S(1)} %first_maxima.1), channel_id=1, source_target_pairs={{0,4},{4,0},{8,12},{12,8},{16,20},{20,16},{24,28},{28,24},{1,5},{5... | collective-permute-start | bytes 12296 | tf_op jit(solution)/shard_map/ppermute | solution.py:550
  24.9 8.9 %collective-permute-done.3 = f32[8,128]{1,0:T(8,128)S(1)} collective-permute-done((f32[8,128]{1,0:T(8,128)S(1)}, f32[8,128]{1,0:T(8,128)S(1)}, u32[]{:S(2)}, u32[]{:S(2)}) %collective-permute-start.3) | collective-permute-done | bytes 4128 | tf_op jit(solution)/shard_map/ppermute | solution.py:550
  33.8 1.8 collective-permute-start.5
  35.6 3.2 %dynamic-slice_bitcast_fusion = (f32[24,32,384]{2,1,0:T(8,128)}, f32[24,32,384]{2,1,0:T(8,128)}) fusion(f32[2,24,64,384]{3,2,1,0:T(8,128)} %refs_9_.3, s32[]{:T(128)S(6)} %select_n.85, s32[]{:T(128)S(6)} %select_n.86, s32[]{:T(128)S(6)} %select_n.88), kind=kLoop, calls=%fused_computation | loop fusion | bytes 4718604 | tf_op jit(solution)/shard_map/squeeze | solution.py:581
  40.2 1.5 collective-permute-start.12
  41.7 3.5 %collective-permute-start.7 = (f32[24,32,384]{2,1,0:T(8,128)S(1)}, f32[24,32,384]{2,1,0:T(8,128)S(1)}, u32[]{:S(2)}, u32[]{:S(2)}) collective-permute-start(f32[24,32,384]{2,1,0:T(8,128)S(1)} %collective-permute-done.6.refs_2_.refs_3_), channel_id=1, source_target_pairs={{0,8},{8,16},{16,24},{12,4},{20,12},{28,20},{1,9},{9,17},{17,25},{... | collective-permute-start | bytes 3538952 | tf_op jit(solution)/shard_map/ppermute | solution.py:560
  45.3 1.6 collective-permute-start.13
  46.9 23.6 %collective-permute-done.13 = f32[8,128]{1,0:T(8,128)S(1)} collective-permute-done((f32[8,128]{1,0:T(8,128)S(1)}, f32[8,128]{1,0:T(8,128)S(1)}, u32[]{:S(2)}, u32[]{:S(2)}) %collective-permute-start.13) | collective-permute-done | bytes 4128 | tf_op jit(solution)/shard_map/ppermute | solution.py:574
  70.5 2.6 collective-permute-start.14
  73.1 1.9 collective-permute-done.14
  75.0 1.8 collective-permute-start.17
  80.5 3.3 %collective-permute-done.10 = f32[2,32,384]{2,1,0:T(8,128)S(1)} collective-permute-done((f32[2,32,384]{2,1,0:T(8,128)S(1)}, f32[2,32,384]{2,1,0:T(8,128)S(1)}, u32[]{:S(2)}, u32[]{:S(2)}) %collective-permute-start.10) | collective-permute-done | bytes 98336 | tf_op jit(solution)/shard_map/ppermute | solution.py:556
  83.8 2.3 copy-done.1
  86.1 4.7 %advance_12.1 = (f32[24,32,384]{2,1,0:T(8,128)S(1)}, f32[24,32,384]{2,1,0:T(8,128)S(1)}) custom-call(f32[6,24]{1,0:T(8,128)S(1)} %concatenate.15.table_ref, f32[2,24,64,384]{3,2,1,0:T(8,128)S(1)} %copy-done.1, f32[24,32,384]{2,1,0:T(8,128)S(1)} %collective-permute-done.5.refs_1_.refs_3_, f32[24,32,384]{2,1,0:T(8,128)S(1)} %collective-permute-done.6.refs_2_.refs_3_, ...), custom_call_target="tpu_custom_call" | custom-call | tf_op jit(solution)/shard_map/advance_12/pallas_call | solution.py:262
  90.9 5.5 %advance_03.3 = (f32[24,32,384]{2,1,0:T(8,128)S(1)}, f32[24,32,384]{2,1,0:T(8,128)S(1)}) custom-call(f32[6,24]{1,0:T(8,128)S(1)} %concatenate.15.table_ref, f32[2,24,64,384]{3,2,1,0:T(8,128)S(1)} %copy-done.1, f32[24,32,384]{2,1,0:T(8,128)S(1)} %collective-permute-done.5.refs_1_.refs_3_, f32[24,32,384]{2,1,0:T(8,128)S(1)} %collective-permute-done.6.refs_2_.refs_3_, ...), custom_call_target="tpu_custom_call" | custom-call | tf_op jit(solution)/shard_map/advance_03/pallas_call | solution.py:262
  96.5 1.8 settle_01.1
  99.4 2.6 collective-permute-start.16
  103.4 8.6 %collective-permute-done.17.refs_1_.refs_7_.refs_3_ = f32[24,32,384]{2,1,0:T(8,128)S(1)} collective-permute-done((f32[24,32,384]{2,1,0:T(8,128)}, f32[24,32,384]{2,1,0:T(8,128)S(1)}, u32[]{:S(2)}, u32[]{:S(2)}) %collective-permute-start.17) | collective-permute-done | bytes 1179680 | tf_op jit(solution)/shard_map/ppermute | solution.py:550
  117.1 3.8 %collective-permute-done.20.refs_6_.next_ref = f32[4,24,384]{2,1,0:T(8,128)S(1)} collective-permute-done((f32[4,24,384]{2,1,0:T(8,128)S(1)}, f32[4,24,384]{2,1,0:T(8,128)S(1)}, u32[]{:S(2)}, u32[]{:S(2)}) %collective-permute-start.20) | collective-permute-done | bytes 147488 | tf_op jit(solution)/shard_map/ppermute | solution.py:550
  121.7 3.0 %collective-permute-start.22 = (f32[8,128]{1,0:T(8,128)S(1)}, f32[8,128]{1,0:T(8,128)S(1)}, u32[]{:S(2)}, u32[]{:S(2)}) collective-permute-start(f32[8,128]{1,0:T(8,128)S(1)} %edge_maxima.3), channel_id=1, source_target_pairs={{0,1},{1,0},{2,3},{3,2},{4,5},{5,4},{6,7},{7,6},{8,9},{9,8},{10,11... | collective-permute-start | bytes 12296 | tf_op jit(solution)/shard_map/ppermute | solution.py:574
  125.5 1.8 collective-permute-start.23
  127.3 2.8 advance_1.3
  130.1 1.4 collective-permute-start.24
  131.6 2.8 advance_2.3
  134.4 1.7 collective-permute-start.25
  136.1 2.8 %advance_0.1 = (f32[24,32,384]{2,1,0:T(8,128)S(1)}, f32[24,32,384]{2,1,0:T(8,128)S(1)}, f32[24,32,384]{2,1,0:T(8,128)S(1)}) custom-call(f32[6,24]{1,0:T(8,128)S(1)} %concatenate.15.table_ref, f32[24,32,384]{2,1,0:T(8,128)S(1)} %get-tuple-element.136.refs_0_, f32[24,32,384]{2,1,0:T(8,128)S(1)} %get-tuple-element.137.refs_1_.refs_0_, ...), custom_call_target="tpu_custom_call" | custom-call | tf_op jit(solution)/shard_map/advance_0/pallas_call | solution.py:262
  139.0 2.7 collective-permute-start.26
  141.6 2.8 %advance_3.1 = (f32[24,32,384]{2,1,0:T(8,128)S(1)}, f32[24,32,384]{2,1,0:T(8,128)S(1)}, f32[24,32,384]{2,1,0:T(8,128)S(1)}) custom-call(f32[6,24]{1,0:T(8,128)S(1)} %concatenate.15.table_ref, f32[24,32,384]{2,1,0:T(8,128)S(1)} %get-tuple-element.163.refs_0_.refs_2_.refs_1_, f32[24,32,384]{2,1,0:T(8,128)S(1)} %get-tuple-element.147.refs_1_.refs_2_, ...), custom_call_target="tpu_custom_call" | custom-call | tf_op jit(solution)/shard_map/advance_3/pallas_call | solution.py:262
  144.5 2.1 settle_03.2
  147.9 4.6 %collective-permute-start.27 = (f32[24,32,384]{2,1,0:T(8,128)S(1)}, f32[24,32,384]{2,1,0:T(8,128)S(1)}, u32[]{:S(2)}, u32[]{:S(2)}) collective-permute-start(f32[24,32,384]{2,1,0:T(8,128)S(1)} %get-tuple-element.191.refs_3_.refs_2_.refs_9_.refs_7_), channel_id=1, source_target_pairs={{0,8},{8,16},{16,24},{12,4},{20,12},{28,20},{1,9},{9,17},{17,25},{... | collective-permute-start | bytes 3538952 | tf_op jit(solution)/shard_map/ppermute | solution.py:560
  152.5 2.1 settle_12.2
  157.3 5.6 %collective-permute-done.31.refs_8_.next_ref.refs_5_ = f32[4,24,384]{2,1,0:T(8,128)S(1)} collective-permute-done((f32[4,24,384]{2,1,0:T(8,128)S(1)}, f32[4,24,384]{2,1,0:T(8,128)S(1)}, u32[]{:S(2)}, u32[]{:S(2)}) %collective-permute-start.31) | collective-permute-done | bytes 147488 | tf_op jit(solution)/shard_map/ppermute | solution.py:550
  163.6 1.8 collective-permute-start.32
  166.3 1.8 collective-permute-start.33
  168.1 2.6 advance_1.4
  170.8 2.6 advance_2.4
  175.0 3.0 %collective-permute-done.35 = f32[8,128]{1,0:T(8,128)S(1)} collective-permute-done((f32[8,128]{1,0:T(8,128)S(1)}, f32[8,128]{1,0:T(8,128)S(1)}, u32[]{:S(2)}, u32[]{:S(2)}) %collective-permute-start.35) | collective-permute-done | bytes 4128 | tf_op jit(solution)/shard_map/ppermute | solution.py:574
  178.0 1.6 collective-permute-start.36
  179.7 4.7 %advance_03.4 = (f32[24,32,384]{2,1,0:T(8,128)S(1)}, f32[24,32,384]{2,1,0:T(8,128)S(1)}, f32[24,32,384]{2,1,0:T(8,128)S(1)}, f32[24,32,384]{2,1,0:T(8,128)S(1)},...) custom-call(f32[6,24]{1,0:T(8,128)S(1)} %concatenate.15.table_ref, ...), custom_call_target="tpu_custom_call" | custom-call | tf_op jit(solution)/shard_map/advance_03/pallas_call | solution.py:262
  184.4 2.3 settle_03.3
  188.0 4.6 %collective-permute-start.37 = (f32[24,32,384]{2,1,0:T(8,128)S(1)}, f32[24,32,384]{2,1,0:T(8,128)S(1)}, u32[]{:S(2)}, u32[]{:S(2)}) collective-permute-start(f32[24,32,384]{2,1,0:T(8,128)S(1)} %get-tuple-element.224.refs_3_.refs_2_), channel_id=1, source_target_pairs={{0,8},{8,16},{16,24},{12,4},{20,12},{28,20},{1,9},{9,17},{17,25},{... | collective-permute-start | bytes 3538952 | tf_op jit(solution)/shard_map/ppermute | solution.py:560
  192.6 2.3 settle_12.3
  196.2 1.5 collective-permute-start.40
  197.8 5.4 %collective-permute-done.41.refs_10_.refs_6_.next_ref = f32[4,24,384]{2,1,0:T(8,128)S(1)} collective-permute-done((f32[4,24,384]{2,1,0:T(8,128)S(1)}, f32[4,24,384]{2,1,0:T(8,128)S(1)}, u32[]{:S(2)}, u32[]{:S(2)}) %collective-permute-start.41) | collective-permute-done | bytes 147488 | tf_op jit(solution)/shard_map/ppermute | solution.py:550
  203.9 2.0 collective-permute-start.42
  206.8 2.0 collective-permute-start.43
  208.8 2.7 advance_1.5
  211.6 2.8 advance_2.5
  215.9 3.0 %collective-permute-done.45 = f32[8,128]{1,0:T(8,128)S(1)} collective-permute-done((f32[8,128]{1,0:T(8,128)S(1)}, f32[8,128]{1,0:T(8,128)S(1)}, u32[]{:S(2)}, u32[]{:S(2)}) %collective-permute-start.45) | collective-permute-done | bytes 4128 | tf_op jit(solution)/shard_map/ppermute | solution.py:574
  218.9 1.5 collective-permute-start.46
  220.4 5.0 %advance_03.5 = (f32[24,32,384]{2,1,0:T(8,128)S(1)}, f32[24,32,384]{2,1,0:T(8,128)S(1)}, f32[24,32,384]{2,1,0:T(8,128)S(1)}, f32[24,32,384]{2,1,0:T(8,128)S(1)},...) custom-call(f32[6,24]{1,0:T(8,128)S(1)} %concatenate.15.table_ref, ...), custom_call_target="tpu_custom_call" | custom-call | tf_op jit(solution)/shard_map/advance_03/pallas_call | solution.py:262
  225.4 2.1 settle_2.3
  228.5 2.9 %settle_013.1 = (f32[24,32,384]{2,1,0:T(8,128)S(1)}, f32[24,32,384]{2,1,0:T(8,128)S(1)}, f32[24,32,384]{2,1,0:T(8,128)}, f32[3,384]{1,0:T(4,128)S(1)}) custom-call(s32[5]{0:T(128)S(1)} %stack.45.flags_ref, f32[24,32,384]{2,1,0:T(8,128)S(1)} %get-tuple-element.228.refs_0_, f32[24,32,384]{2,1,0:T(8,128)S(1)} %get-tuple-element.229.refs_1_, ...), custom_call_target="tpu_custom_call" | custom-call | tf_op jit(solution)/shard_map/settle_013/pallas_call | solution.py:385
  233.1 6.3 %pmin.7.least_ref = f32[4,384]{1,0:T(4,128)S(1)} all-reduce(f32[4,384]{1,0:T(4,128)} %pad_maximum_fusion.5), channel_id=1, replica_groups=mesh['px'=8,'vx'=4] {'vx'}, use_global_device_ids=true, to_apply=%region_0.1 | all-reduce | flops 1536 | bytes 12288 | tf_op jit(solution)/shard_map/pmin | solution.py:680
  240.4 2.0 place.2.refs_1_
  242.4 14.3 %collective-permute-done.49.refs_0_ = f32[24,32,384]{2,1,0:T(8,128)} collective-permute-done((f32[24,32,384]{2,1,0:T(8,128)}, f32[24,32,384]{2,1,0:T(8,128)}, u32[]{:S(2)}, u32[]{:S(2)}) %collective-permute-start.49) | collective-permute-done | bytes 1179680 | tf_op jit(solution)/shard_map/ppermute | solution.py:550
  256.7 2.3 place.3._
  259.0 20.1 %collective-permute-done.48.got_ref = f32[2,384]{1,0:T(2,128)S(1)} collective-permute-done((f32[2,384]{1,0:T(2,128)S(1)}, f32[2,384]{1,0:T(2,128)S(1)}, u32[]{:S(2)}, u32[]{:S(2)}) %collective-permute-start.48) | collective-permute-done | bytes 3104 | tf_op jit(solution)/shard_map/ppermute | solution.py:550
  279.1 2.1 finish.1
  (132 shorter events, 38.2 us)
Async XLA Ops:
  0.7 5.3 %copy-start.3 = (f32[2,24]{1,0:T(2,128)S(1)}, f32[2,24]{1,0:T(2,128)}, u32[]{:S(2)}) copy-start(f32[2,24]{1,0:T(2,128)} %first_ref.1) | copy-start | bytes 580
  3.0 38.7 %collective-permute-start.6 = (f32[24,32,384]{2,1,0:T(8,128)}, f32[24,32,384]{2,1,0:T(8,128)S(1)}, u32[]{:S(2)}, u32[]{:S(2)}) collective-permute-start(f32[24,32,384]{2,1,0:T(8,128)} %dynamic-slice_bitcast_fusion.4), channel_id=1, source_target_pairs={{0,4},{4,0},{8,12},{12,8},{16,20},{20,16},{24,28},{28,24},{1,5},{5... | collective-permute-start | bytes 3538952 | tf_op jit(solution)/shard_map/ppermute | solution.py:550
  6.0 27.9 %collective-permute-start = (f32[2,24]{1,0:T(2,128)S(1)}, f32[2,24]{1,0:T(2,128)S(1)}, u32[]{:S(2)}, u32[]{:S(2)}) collective-permute-start(f32[2,24]{1,0:T(2,128)S(1)} %copy-done.3), channel_id=1, source_target_pairs={{0,4},{4,0},{8,12},{12,8},{16,20},{20,16},{24,28},{28,24},{1,5},{5... | collective-permute-start | bytes 584 | tf_op jit(solution)/shard_map/ppermute | solution.py:550
  7.1 26.7 %collective-permute-start.4 = (f32[2,24,384]{2,1,0:T(8,128)S(1)}, f32[2,24,384]{2,1,0:T(8,128)S(1)}, u32[]{:S(2)}, u32[]{:S(2)}) collective-permute-start(f32[2,24,384]{2,1,0:T(8,128)S(1)} %bitcast.36), channel_id=1, source_target_pairs={{0,4},{4,0},{8,12},{12,8},{16,20},{20,16},{24,28},{28,24},{1,5},{5... | collective-permute-start | bytes 221192 | tf_op jit(solution)/shard_map/ppermute | solution.py:550
  10.2 7.3 %collective-permute-start.1 = (f32[2,64,384]{2,1,0:T(8,128)S(1)}, f32[2,64,384]{2,1,0:T(8,128)S(1)}, u32[]{:S(2)}, u32[]{:S(2)}) collective-permute-start(f32[2,64,384]{2,1,0:T(8,128)S(1)} %get-tuple-element.130), channel_id=1, source_target_pairs={{0,1},{1,2},{2,3},{4,5},{5,6},{6,7},{8,9},{9,10},{10,11},{12,13},{... | collective-permute-start | bytes 589832 | tf_op jit(solution)/shard_map/ppermute | solution.py:553
  11.5 7.3 %collective-permute-start.2 = (f32[2,64,384]{2,1,0:T(8,128)S(1)}, f32[2,64,384]{2,1,0:T(8,128)S(1)}, u32[]{:S(2)}, u32[]{:S(2)}) collective-permute-start(f32[2,64,384]{2,1,0:T(8,128)S(1)} %get-tuple-element.131), channel_id=1, source_target_pairs={{1,0},{2,1},{3,2},{5,4},{6,5},{7,6},{9,8},{10,9},{11,10},{13,12},{... | collective-permute-start | bytes 589832 | tf_op jit(solution)/shard_map/ppermute | solution.py:556
  13.0 5.9 %copy-start.2 = (f32[64,384]{1,0:T(8,128)S(1)}, f32[64,384]{1,0:T(8,128)}, u32[]{:S(2)}) copy-start(f32[64,384]{1,0:T(8,128)} %refs_7_.11) | copy-start | bytes 294916
  14.2 4.7 %copy-start = (f32[2,24,64,384]{3,2,1,0:T(8,128)S(1)}, f32[2,24,64,384]{3,2,1,0:T(8,128)}, u32[]{:S(2)}) copy-start(f32[2,24,64,384]{3,2,1,0:T(8,128)} %refs_3_.3) | copy-start | bytes 14155780
  17.6 73.3 %collective-permute-start.8 = (f32[24,32,384]{2,1,0:T(8,128)}, f32[24,32,384]{2,1,0:T(8,128)}, u32[]{:S(2)}, u32[]{:S(2)}) collective-permute-start(f32[24,32,384]{2,1,0:T(8,128)} %get-tuple-element.258), channel_id=1, source_target_pairs={{8,0},{16,8},{24,16},{4,12},{12,20},{20,28},{9,1},{17,9},{25,17},{... | collective-permute-start | bytes 3538952 | tf_op jit(solution)/shard_map/ppermute | solution.py:564
  21.1 12.7 %collective-permute-start.3 = (f32[8,128]{1,0:T(8,128)S(1)}, f32[8,128]{1,0:T(8,128)S(1)}, u32[]{:S(2)}, u32[]{:S(2)}) collective-permute-start(f32[8,128]{1,0:T(8,128)S(1)} %first_maxima.1), channel_id=1, source_target_pairs={{0,4},{4,0},{8,12},{12,8},{16,20},{20,16},{24,28},{28,24},{1,5},{5... | collective-permute-start | bytes 12296 | tf_op jit(solution)/shard_map/ppermute | solution.py:550
  33.8 43.1 %collective-permute-start.5 = (f32[24,32,384]{2,1,0:T(8,128)}, f32[24,32,384]{2,1,0:T(8,128)S(1)}, u32[]{:S(2)}, u32[]{:S(2)}) collective-permute-start(f32[24,32,384]{2,1,0:T(8,128)} %get-tuple-element.133), channel_id=1, source_target_pairs={{0,4},{4,0},{8,12},{12,8},{16,20},{20,16},{24,28},{28,24},{1,5},{5... | collective-permute-start | bytes 3538952 | tf_op jit(solution)/shard_map/ppermute | solution.py:550
  38.9 1.2 collective-permute-start.11
  39.0 59.2 %collective-permute-start.15 = (f32[24,32,384]{2,1,0:T(8,128)}, f32[24,32,384]{2,1,0:T(8,128)S(1)}, u32[]{:S(2)}, u32[]{:S(2)}) collective-permute-start(f32[24,32,384]{2,1,0:T(8,128)} %get-tuple-element.139), channel_id=1, source_target_pairs={{0,4},{4,0},{8,12},{12,8},{16,20},{20,16},{24,28},{28,24},{1,5},{5... | collective-permute-start | bytes 3538952 | tf_op jit(solution)/shard_map/ppermute | solution.py:550
  40.2 5.1 %collective-permute-start.12 = (f32[8,128]{1,0:T(8,128)S(1)}, f32[8,128]{1,0:T(8,128)S(1)}, u32[]{:S(2)}, u32[]{:S(2)}) collective-permute-start(f32[8,128]{1,0:T(8,128)S(1)} %max.61), channel_id=1, source_target_pairs={{0,2},{1,3},{2,0},{3,1},{4,6},{5,7},{6,4},{7,5},{8,10},{9,11},{10,... | collective-permute-start | bytes 12296 | tf_op jit(solution)/shard_map/ppermute | solution.py:574
  41.7 49.2 %collective-permute-start.7 = (f32[24,32,384]{2,1,0:T(8,128)S(1)}, f32[24,32,384]{2,1,0:T(8,128)S(1)}, u32[]{:S(2)}, u32[]{:S(2)}) collective-permute-start(f32[24,32,384]{2,1,0:T(8,128)S(1)} %collective-permute-done.6.refs_2_.refs_3_), channel_id=1, source_target_pairs={{0,8},{8,16},{16,24},{12,4},{20,12},{28,20},{1,9},{9,17},{17,25},{... | collective-permute-start | bytes 3538952 | tf_op jit(solution)/shard_map/ppermute | solution.py:560
  45.3 25.2 %collective-permute-start.13 = (f32[8,128]{1,0:T(8,128)S(1)}, f32[8,128]{1,0:T(8,128)S(1)}, u32[]{:S(2)}, u32[]{:S(2)}) collective-permute-start(f32[8,128]{1,0:T(8,128)S(1)} %max.62), channel_id=1, source_target_pairs={{0,8},{4,12},{8,0},{12,4},{16,24},{20,28},{24,16},{28,20},{1,9},{5... | collective-permute-start | bytes 12296 | tf_op jit(solution)/shard_map/ppermute | solution.py:574
  70.5 4.5 %collective-permute-start.14 = (f32[8,128]{1,0:T(8,128)S(1)}, f32[8,128]{1,0:T(8,128)S(1)}, u32[]{:S(2)}, u32[]{:S(2)}) collective-permute-start(f32[8,128]{1,0:T(8,128)S(1)} %max.63), channel_id=1, source_target_pairs={{0,16},{4,20},{8,24},{12,28},{16,0},{20,4},{24,8},{28,12},{1,17},{... | collective-permute-start | bytes 12296 | tf_op jit(solution)/shard_map/ppermute | solution.py:574
  75.0 36.9 %collective-permute-start.17 = (f32[24,32,384]{2,1,0:T(8,128)}, f32[24,32,384]{2,1,0:T(8,128)S(1)}, u32[]{:S(2)}, u32[]{:S(2)}) collective-permute-start(f32[24,32,384]{2,1,0:T(8,128)} %get-tuple-element.149), channel_id=1, source_target_pairs={{0,4},{4,0},{8,12},{12,8},{16,20},{20,16},{24,28},{28,24},{1,5},{5... | collective-permute-start | bytes 3538952 | tf_op jit(solution)/shard_map/ppermute | solution.py:550
  76.9 2.2 collective-permute-start.9
  79.2 4.6 %collective-permute-start.10 = (f32[2,32,384]{2,1,0:T(8,128)S(1)}, f32[2,32,384]{2,1,0:T(8,128)S(1)}, u32[]{:S(2)}, u32[]{:S(2)}) collective-permute-start(f32[2,32,384]{2,1,0:T(8,128)S(1)} %pad_maximum_fusion.4), channel_id=1, source_target_pairs={{1,0},{2,1},{3,2},{5,4},{6,5},{7,6},{9,8},{10,9},{11,10},{13,12},{... | collective-permute-start | bytes 294920 | tf_op jit(solution)/shard_map/ppermute | solution.py:556
  83.8 2.3 copy-start.1
  86.1 10.3 %slice-start = ((s8[4718592]{0:T(1024)(128)(4,1)}), s8[4194304]{0:T(1024)(128)(4,1)S(1)}, s32[]{:S(2)}) async-start(s8[4718592]{0:T(1024)(128)(4,1)} %bitcast.32), calls=%async_computation | async-start | bytes 8388608
  90.8 5.6 %slice-start.1 = ((s8[4718592]{0:T(1024)(128)(4,1)}), s8[524288]{0:T(1024)(128)(4,1)S(1)}, s32[]{:S(2)}) async-start(s8[4718592]{0:T(1024)(128)(4,1)} %bitcast.32), calls=%async_computation.1 | async-start | bytes 1048576
  96.5 30.9 %slice-start.2 = ((s8[4718592]{0:T(1024)(128)(4,1)}), s8[4194304]{0:T(1024)(128)(4,1)S(1)}, s32[]{:S(2)}) async-start(s8[4718592]{0:T(1024)(128)(4,1)} %bitcast.34), calls=%async_computation.2 | async-start | bytes 8388608
  98.3 29.0 %slice-start.3 = ((s8[4718592]{0:T(1024)(128)(4,1)}), s8[524288]{0:T(1024)(128)(4,1)S(1)}, s32[]{:S(2)}) async-start(s8[4718592]{0:T(1024)(128)(4,1)} %bitcast.34), calls=%async_computation.3 | async-start | bytes 1048576
  99.4 36.7 %collective-permute-start.16 = (f32[24,32,384]{2,1,0:T(8,128)S(1)}, f32[24,32,384]{2,1,0:T(8,128)S(1)}, u32[]{:S(2)}, u32[]{:S(2)}) collective-permute-start(f32[24,32,384]{2,1,0:T(8,128)S(1)} %get-tuple-element.147.refs_1_.refs_2_), channel_id=1, source_target_pairs={{0,8},{8,16},{16,24},{12,4},{20,12},{28,20},{1,9},{9,17},{17,25},{... | collective-permute-start | bytes 3538952 | tf_op jit(solution)/shard_map/ppermute | solution.py:560
  102.1 39.6 %collective-permute-start.21 = (f32[24,32,384]{2,1,0:T(8,128)S(1)}, f32[24,32,384]{2,1,0:T(8,128)S(1)}, u32[]{:S(2)}, u32[]{:S(2)}) collective-permute-start(f32[24,32,384]{2,1,0:T(8,128)S(1)} %get-tuple-element.136.refs_0_), channel_id=1, source_target_pairs={{8,0},{16,8},{24,16},{4,12},{12,20},{20,28},{9,1},{17,9},{25,17},{... | collective-permute-start | bytes 3538952 | tf_op jit(solution)/shard_map/ppermute | solution.py:564
  113.1 7.8 %collective-permute-start.18 = (f32[4,32,384]{2,1,0:T(8,128)S(1)}, f32[4,32,384]{2,1,0:T(8,128)S(1)}, u32[]{:S(2)}, u32[]{:S(2)}) collective-permute-start(f32[4,32,384]{2,1,0:T(8,128)S(1)} %get-tuple-element.157.last_ref), channel_id=1, source_target_pairs={{0,1},{1,2},{2,3},{4,5},{5,6},{6,7},{8,9},{9,10},{10,11},{12,13},{... | collective-permute-start | bytes 589832 | tf_op jit(solution)/shard_map/ppermute | solution.py:553
  114.4 6.5 %collective-permute-start.19 = (f32[4,32,384]{2,1,0:T(8,128)S(1)}, f32[4,32,384]{2,1,0:T(8,128)S(1)}, u32[]{:S(2)}, u32[]{:S(2)}) collective-permute-start(f32[4,32,384]{2,1,0:T(8,128)S(1)} %get-tuple-element.158.first_ref), channel_id=1, source_target_pairs={{1,0},{2,1},{3,2},{5,4},{6,5},{7,6},{9,8},{10,9},{11,10},{13,12},{... | collective-permute-start | bytes 589832 | tf_op jit(solution)/shard_map/ppermute | solution.py:556
  115.7 5.2 %collective-permute-start.20 = (f32[4,24,384]{2,1,0:T(8,128)S(1)}, f32[4,24,384]{2,1,0:T(8,128)S(1)}, u32[]{:S(2)}, u32[]{:S(2)}) collective-permute-start(f32[4,24,384]{2,1,0:T(8,128)S(1)} %get-tuple-element.159), channel_id=1, source_target_pairs={{0,4},{4,0},{8,12},{12,8},{16,20},{20,16},{24,28},{28,24},{1,5},{5... | collective-permute-start | bytes 442376 | tf_op jit(solution)/shard_map/ppermute | solution.py:550
  121.7 3.8 %collective-permute-start.22 = (f32[8,128]{1,0:T(8,128)S(1)}, f32[8,128]{1,0:T(8,128)S(1)}, u32[]{:S(2)}, u32[]{:S(2)}) collective-permute-start(f32[8,128]{1,0:T(8,128)S(1)} %edge_maxima.3), channel_id=1, source_target_pairs={{0,1},{1,0},{2,3},{3,2},{4,5},{5,4},{6,7},{7,6},{8,9},{9,8},{10,11... | collective-permute-start | bytes 12296 | tf_op jit(solution)/shard_map/ppermute | solution.py:574
  125.5 4.6 %collective-permute-start.23 = (f32[8,128]{1,0:T(8,128)S(1)}, f32[8,128]{1,0:T(8,128)S(1)}, u32[]{:S(2)}, u32[]{:S(2)}) collective-permute-start(f32[8,128]{1,0:T(8,128)S(1)} %max.65), channel_id=1, source_target_pairs={{0,2},{1,3},{2,0},{3,1},{4,6},{5,7},{6,4},{7,5},{8,10},{9,11},{10,... | collective-permute-start | bytes 12296 | tf_op jit(solution)/shard_map/ppermute | solution.py:574
  130.1 4.2 %collective-permute-start.24 = (f32[8,128]{1,0:T(8,128)S(1)}, f32[8,128]{1,0:T(8,128)S(1)}, u32[]{:S(2)}, u32[]{:S(2)}) collective-permute-start(f32[8,128]{1,0:T(8,128)S(1)} %max.66), channel_id=1, source_target_pairs={{0,4},{4,0},{8,12},{12,8},{16,20},{20,16},{24,28},{28,24},{1,5},{5... | collective-permute-start | bytes 12296 | tf_op jit(solution)/shard_map/ppermute | solution.py:574
  134.4 4.6 %collective-permute-start.25 = (f32[8,128]{1,0:T(8,128)S(1)}, f32[8,128]{1,0:T(8,128)S(1)}, u32[]{:S(2)}, u32[]{:S(2)}) collective-permute-start(f32[8,128]{1,0:T(8,128)S(1)} %max.67), channel_id=1, source_target_pairs={{0,8},{4,12},{8,0},{12,4},{16,24},{20,28},{24,16},{28,20},{1,9},{5... | collective-permute-start | bytes 12296 | tf_op jit(solution)/shard_map/ppermute | solution.py:574
  139.0 5.5 %collective-permute-start.26 = (f32[8,128]{1,0:T(8,128)S(1)}, f32[8,128]{1,0:T(8,128)S(1)}, u32[]{:S(2)}, u32[]{:S(2)}) collective-permute-start(f32[8,128]{1,0:T(8,128)S(1)} %max.68), channel_id=1, source_target_pairs={{0,16},{4,20},{8,24},{12,28},{16,0},{20,4},{24,8},{28,12},{1,17},{... | collective-permute-start | bytes 12296 | tf_op jit(solution)/shard_map/ppermute | solution.py:574
  146.6 33.1 %collective-permute-start.28 = (f32[24,32,384]{2,1,0:T(8,128)S(1)}, f32[24,32,384]{2,1,0:T(8,128)S(1)}, u32[]{:S(2)}, u32[]{:S(2)}) collective-permute-start(f32[24,32,384]{2,1,0:T(8,128)S(1)} %get-tuple-element.181.refs_0_.refs_8_.refs_6_), channel_id=1, source_target_pairs={{8,0},{16,8},{24,16},{4,12},{12,20},{20,28},{9,1},{17,9},{25,17},{... | collective-permute-start | bytes 3538952 | tf_op jit(solution)/shard_map/ppermute | solution.py:564
  147.9 31.8 %collective-permute-start.27 = (f32[24,32,384]{2,1,0:T(8,128)S(1)}, f32[24,32,384]{2,1,0:T(8,128)S(1)}, u32[]{:S(2)}, u32[]{:S(2)}) collective-permute-start(f32[24,32,384]{2,1,0:T(8,128)S(1)} %get-tuple-element.191.refs_3_.refs_2_.refs_9_.refs_7_), channel_id=1, source_target_pairs={{0,8},{8,16},{16,24},{12,4},{20,12},{28,20},{1,9},{9,17},{17,25},{... | collective-permute-start | bytes 3538952 | tf_op jit(solution)/shard_map/ppermute | solution.py:560
  154.6 8.3 %collective-permute-start.29 = (f32[4,32,384]{2,1,0:T(8,128)S(1)}, f32[4,32,384]{2,1,0:T(8,128)S(1)}, u32[]{:S(2)}, u32[]{:S(2)}) collective-permute-start(f32[4,32,384]{2,1,0:T(8,128)S(1)} %get-tuple-element.192.last_ref), channel_id=1, source_target_pairs={{0,1},{1,2},{2,3},{4,5},{5,6},{6,7},{8,9},{9,10},{10,11},{12,13},{... | collective-permute-start | bytes 589832 | tf_op jit(solution)/shard_map/ppermute | solution.py:553
  155.9 7.0 %collective-permute-start.30 = (f32[4,32,384]{2,1,0:T(8,128)S(1)}, f32[4,32,384]{2,1,0:T(8,128)S(1)}, u32[]{:S(2)}, u32[]{:S(2)}) collective-permute-start(f32[4,32,384]{2,1,0:T(8,128)S(1)} %get-tuple-element.193.first_ref), channel_id=1, source_target_pairs={{1,0},{2,1},{3,2},{5,4},{6,5},{7,6},{9,8},{10,9},{11,10},{13,12},{... | collective-permute-start | bytes 589832 | tf_op jit(solution)/shard_map/ppermute | solution.py:556
  157.2 5.7 %collective-permute-start.31 = (f32[4,24,384]{2,1,0:T(8,128)S(1)}, f32[4,24,384]{2,1,0:T(8,128)S(1)}, u32[]{:S(2)}, u32[]{:S(2)}) collective-permute-start(f32[4,24,384]{2,1,0:T(8,128)S(1)} %get-tuple-element.194), channel_id=1, source_target_pairs={{0,4},{4,0},{8,12},{12,8},{16,20},{20,16},{24,28},{28,24},{1,5},{5... | collective-permute-start | bytes 442376 | tf_op jit(solution)/shard_map/ppermute | solution.py:550
  163.6 2.6 collective-permute-start.32
  166.3 4.4 %collective-permute-start.33 = (f32[8,128]{1,0:T(8,128)S(1)}, f32[8,128]{1,0:T(8,128)S(1)}, u32[]{:S(2)}, u32[]{:S(2)}) collective-permute-start(f32[8,128]{1,0:T(8,128)S(1)} %max.70), channel_id=1, source_target_pairs={{0,2},{1,3},{2,0},{3,1},{4,6},{5,7},{6,4},{7,5},{8,10},{9,11},{10,... | collective-permute-start | bytes 12296 | tf_op jit(solution)/shard_map/ppermute | solution.py:574
  170.7 3.7 %collective-permute-start.34 = (f32[8,128]{1,0:T(8,128)S(1)}, f32[8,128]{1,0:T(8,128)S(1)}, u32[]{:S(2)}, u32[]{:S(2)}) collective-permute-start(f32[8,128]{1,0:T(8,128)S(1)} %max.71), channel_id=1, source_target_pairs={{0,4},{4,0},{8,12},{12,8},{16,20},{20,16},{24,28},{28,24},{1,5},{5... | collective-permute-start | bytes 12296 | tf_op jit(solution)/shard_map/ppermute | solution.py:574
  174.4 3.6 %collective-permute-start.35 = (f32[8,128]{1,0:T(8,128)S(1)}, f32[8,128]{1,0:T(8,128)S(1)}, u32[]{:S(2)}, u32[]{:S(2)}) collective-permute-start(f32[8,128]{1,0:T(8,128)S(1)} %max.72), channel_id=1, source_target_pairs={{0,8},{4,12},{8,0},{12,4},{16,24},{20,28},{24,16},{28,20},{1,9},{5... | collective-permute-start | bytes 12296 | tf_op jit(solution)/shard_map/ppermute | solution.py:574
  178.0 6.3 %collective-permute-start.36 = (f32[8,128]{1,0:T(8,128)S(1)}, f32[8,128]{1,0:T(8,128)S(1)}, u32[]{:S(2)}, u32[]{:S(2)}) collective-permute-start(f32[8,128]{1,0:T(8,128)S(1)} %max.73), channel_id=1, source_target_pairs={{0,16},{4,20},{8,24},{12,28},{16,0},{20,4},{24,8},{28,12},{1,17},{... | collective-permute-start | bytes 12296 | tf_op jit(solution)/shard_map/ppermute | solution.py:574
  186.7 33.7 %collective-permute-start.38 = (f32[24,32,384]{2,1,0:T(8,128)S(1)}, f32[24,32,384]{2,1,0:T(8,128)S(1)}, u32[]{:S(2)}, u32[]{:S(2)}) collective-permute-start(f32[24,32,384]{2,1,0:T(8,128)S(1)} %get-tuple-element.214.refs_0_), channel_id=1, source_target_pairs={{8,0},{16,8},{24,16},{4,12},{12,20},{20,28},{9,1},{17,9},{25,17},{... | collective-permute-start | bytes 3538952 | tf_op jit(solution)/shard_map/ppermute | solution.py:564
  188.0 32.4 %collective-permute-start.37 = (f32[24,32,384]{2,1,0:T(8,128)S(1)}, f32[24,32,384]{2,1,0:T(8,128)S(1)}, u32[]{:S(2)}, u32[]{:S(2)}) collective-permute-start(f32[24,32,384]{2,1,0:T(8,128)S(1)} %get-tuple-element.224.refs_3_.refs_2_), channel_id=1, source_target_pairs={{0,8},{8,16},{16,24},{12,4},{20,12},{28,20},{1,9},{9,17},{17,25},{... | collective-permute-start | bytes 3538952 | tf_op jit(solution)/shard_map/ppermute | solution.py:560
  194.9 8.2 %collective-permute-start.39 = (f32[4,32,384]{2,1,0:T(8,128)S(1)}, f32[4,32,384]{2,1,0:T(8,128)S(1)}, u32[]{:S(2)}, u32[]{:S(2)}) collective-permute-start(f32[4,32,384]{2,1,0:T(8,128)S(1)} %get-tuple-element.225.last_ref), channel_id=1, source_target_pairs={{0,1},{1,2},{2,3},{4,5},{5,6},{6,7},{8,9},{9,10},{10,11},{12,13},{... | collective-permute-start | bytes 589832 | tf_op jit(solution)/shard_map/ppermute | solution.py:553
  196.2 6.9 %collective-permute-start.40 = (f32[4,32,384]{2,1,0:T(8,128)S(1)}, f32[4,32,384]{2,1,0:T(8,128)S(1)}, u32[]{:S(2)}, u32[]{:S(2)}) collective-permute-start(f32[4,32,384]{2,1,0:T(8,128)S(1)} %get-tuple-element.226.first_ref), channel_id=1, source_target_pairs={{1,0},{2,1},{3,2},{5,4},{6,5},{7,6},{9,8},{10,9},{11,10},{13,12},{... | collective-permute-start | bytes 589832 | tf_op jit(solution)/shard_map/ppermute | solution.py:556
  197.7 5.5 %collective-permute-start.41 = (f32[4,24,384]{2,1,0:T(8,128)S(1)}, f32[4,24,384]{2,1,0:T(8,128)S(1)}, u32[]{:S(2)}, u32[]{:S(2)}) collective-permute-start(f32[4,24,384]{2,1,0:T(8,128)S(1)} %get-tuple-element.227), channel_id=1, source_target_pairs={{0,4},{4,0},{8,12},{12,8},{16,20},{20,16},{24,28},{28,24},{1,5},{5... | collective-permute-start | bytes 442376 | tf_op jit(solution)/shard_map/ppermute | solution.py:550
  203.9 2.9 %collective-permute-start.42 = (f32[8,128]{1,0:T(8,128)S(1)}, f32[8,128]{1,0:T(8,128)S(1)}, u32[]{:S(2)}, u32[]{:S(2)}) collective-permute-start(f32[8,128]{1,0:T(8,128)S(1)} %edge_maxima.5), channel_id=1, source_target_pairs={{0,1},{1,0},{2,3},{3,2},{4,5},{5,4},{6,7},{7,6},{8,9},{9,8},{10,11... | collective-permute-start | bytes 12296 | tf_op jit(solution)/shard_map/ppermute | solution.py:574
  206.8 4.8 %collective-permute-start.43 = (f32[8,128]{1,0:T(8,128)S(1)}, f32[8,128]{1,0:T(8,128)S(1)}, u32[]{:S(2)}, u32[]{:S(2)}) collective-permute-start(f32[8,128]{1,0:T(8,128)S(1)} %max.75), channel_id=1, source_target_pairs={{0,2},{1,3},{2,0},{3,1},{4,6},{5,7},{6,4},{7,5},{8,10},{9,11},{10,... | collective-permute-start | bytes 12296 | tf_op jit(solution)/shard_map/ppermute | solution.py:574
  211.6 3.7 %collective-permute-start.44 = (f32[8,128]{1,0:T(8,128)S(1)}, f32[8,128]{1,0:T(8,128)S(1)}, u32[]{:S(2)}, u32[]{:S(2)}) collective-permute-start(f32[8,128]{1,0:T(8,128)S(1)} %max.76), channel_id=1, source_target_pairs={{0,4},{4,0},{8,12},{12,8},{16,20},{20,16},{24,28},{28,24},{1,5},{5... | collective-permute-start | bytes 12296 | tf_op jit(solution)/shard_map/ppermute | solution.py:574
  215.2 3.6 %collective-permute-start.45 = (f32[8,128]{1,0:T(8,128)S(1)}, f32[8,128]{1,0:T(8,128)S(1)}, u32[]{:S(2)}, u32[]{:S(2)}) collective-permute-start(f32[8,128]{1,0:T(8,128)S(1)} %max.77), channel_id=1, source_target_pairs={{0,8},{4,12},{8,0},{12,4},{16,24},{20,28},{24,16},{28,20},{1,9},{5... | collective-permute-start | bytes 12296 | tf_op jit(solution)/shard_map/ppermute | solution.py:574
  218.9 6.5 %collective-permute-start.46 = (f32[8,128]{1,0:T(8,128)S(1)}, f32[8,128]{1,0:T(8,128)S(1)}, u32[]{:S(2)}, u32[]{:S(2)}) collective-permute-start(f32[8,128]{1,0:T(8,128)S(1)} %max.78), channel_id=1, source_target_pairs={{0,16},{4,20},{8,24},{12,28},{16,0},{20,4},{24,8},{28,12},{1,17},{... | collective-permute-start | bytes 12296 | tf_op jit(solution)/shard_map/ppermute | solution.py:574
  227.5 29.2 %collective-permute-start.49 = (f32[24,32,384]{2,1,0:T(8,128)}, f32[24,32,384]{2,1,0:T(8,128)}, u32[]{:S(2)}, u32[]{:S(2)}) collective-permute-start(f32[24,32,384]{2,1,0:T(8,128)} %get-tuple-element.251), channel_id=1, source_target_pairs={{0,4},{4,0},{8,12},{12,8},{16,20},{20,16},{24,28},{28,24},{1,5},{5... | collective-permute-start | bytes 3538952 | tf_op jit(solution)/shard_map/ppermute | solution.py:550
  231.4 47.7 %collective-permute-start.47 = (f32[24,32,384]{2,1,0:T(8,128)}, f32[24,32,384]{2,1,0:T(8,128)S(1)}, u32[]{:S(2)}, u32[]{:S(2)}) collective-permute-start(f32[24,32,384]{2,1,0:T(8,128)} %get-tuple-element.247), channel_id=1, source_target_pairs={{0,4},{4,0},{8,12},{12,8},{16,20},{20,16},{24,28},{28,24},{1,5},{5... | collective-permute-start | bytes 3538952 | tf_op jit(solution)/shard_map/ppermute | solution.py:550
  239.3 39.8 %collective-permute-start.48 = (f32[2,384]{1,0:T(2,128)S(1)}, f32[2,384]{1,0:T(2,128)S(1)}, u32[]{:S(2)}, u32[]{:S(2)}) collective-permute-start(f32[2,384]{1,0:T(2,128)S(1)} %slice.40), channel_id=1, source_target_pairs={{0,4},{4,0},{8,12},{12,8},{16,20},{20,16},{24,28},{28,24},{1,5},{5... | collective-permute-start | bytes 9224 | tf_op jit(solution)/shard_map/ppermute | solution.py:550

commit v5 on v4

--- a/solution.py
+++ b/solution.py
@@ -105,18 +105,21 @@
     return pl.CostEstimate(flops=0, bytes_accessed=0, transcendentals=0)
 
 
-def advance(sizes, targets, rows, bases, halo_rows, vx_low, vx_high, vy_next, maxima, stepper, accel_second, table):
+def advance(sizes, targets, rows, bases, halos, maxima, stepper, accel_second, table):
     cells_v, half, width, total_vx, total_vy = sizes
     count = len(targets)
     heun = bases is not None
     late = stepper is None
-    full = not heun and not late
+    full = halos is not None
     ops = Operands()
     needed = sorted({k for t in targets for k in (t - 1, t, t + 1) if 0 <= k <= 3})
     row_at = {k: ops.add(rows[k].array) for k in needed}
-    halo_at = {k: ops.add(halo_rows[i]) for i, k in enumerate((-1, 4)) if any(abs(t - k) == 1 for t in targets)}
     base_at = [ops.add(b.array) for b in bases] if heun else []
-    low_at, high_at, vy_at, accel_at = ops.add(vx_low), ops.add(vx_high), ops.add(vy_next), ops.add(accel_second)
+    accel_at = ops.add(accel_second)
+    if full:
+        halo_rows, vx_low, vx_high, vy_next = halos
+        halo_at = {k: ops.add(halo_rows[i]) for i, k in enumerate((-1, 4)) if any(abs(t - k) == 1 for t in targets)}
+        low_at, high_at, vy_at = ops.add(vx_low), ops.add(vx_high), ops.add(vy_next)
     maxima_at = [] if late else [ops.add(maxima), ops.add(stepper)]
     n_in = len(ops.arrays)
     n_out = count * (1 if full else 3)
@@ -162,6 +165,7 @@
             accel = ins[accel_at][pl.ds(pl.multiple_of(start + 8 * g, 8), 8), :] * wide(to_3)
             acc_up[here, :] = accel + wide(disturb_3)
             acc_down[here, :] = accel - wide(disturb_3)
+        keep_outer = wide(keep - 2.0 * damp_1)
         keep, damp_1, control_2, control_3 = wide(keep), wide(damp_1), wide(control_2), wide(control_3)
         if full:
             damp_2, damp_3 = wide(damp_2), wide(damp_3)
@@ -190,19 +194,23 @@
             drift = table_ref[t, j] * to_2
             flow_up, flow_down = wide(flow + planner), wide(flow - planner)
             drift_up, drift_down = wide(drift + disturb_2), wide(drift - disturb_2)
-            beyond = ins[vy_at][3 - t, pl.ds(j, 1), :]
-            first = readers[t](j, 0)
-            last = readers[t](j, groups - 1)
-            below = jnp.broadcast_to(jnp.where(is_even, first[0:1], beyond), (8, width))
-            above = jnp.broadcast_to(jnp.where(is_even, beyond, last[7:8]), (8, width))
+            below = readers[t](j, 0)[0:1]
+            above = readers[t](j, groups - 1)[7:8]
+            if full:
+                beyond = ins[vy_at][3 - t, pl.ds(j, 1), :]
+                below, above = jnp.where(is_even, below, beyond), jnp.where(is_even, beyond, above)
+            below, above = jnp.broadcast_to(below, (8, width)), jnp.broadcast_to(above, (8, width))
             ups = [below] + [pltpu.roll(readers[t](j, g), 1, 0) for g in range(groups)]
             downs = [pltpu.roll(readers[t](j, g), 7, 0) for g in range(groups)] + [above]
             for g in range(groups):
                 w = readers[t](j, g)
                 here = pl.ds(8 * g, 8)
-                low_1, high_1 = neighbour(t - 1, j, g, w), neighbour(t + 1, j, g, w)
-                total = keep * w - damp_1 * (low_1 + high_1)
-                total = total + upwind(flow_up, flow_down, high_1 - low_1)
+                if full or t in (1, 2):
+                    low_1, high_1 = neighbour(t - 1, j, g, w), neighbour(t + 1, j, g, w)
+                    total = keep * w - damp_1 * (low_1 + high_1)
+                    total = total + upwind(flow_up, flow_down, high_1 - low_1)
+                else:
+                    total = keep_outer * w
 
                 pieces = lane_pieces(w)
                 right = [pltpu.roll(p, 1, 1) for p in pieces]
@@ -215,11 +223,11 @@
                 total = total + jnp.concatenate(parts, axis=1)
 
                 if low_j is None:
-                    low_2 = jnp.where(vx_first, w, ins[low_at][t, here, :])
+                    low_2 = jnp.where(vx_first, w, ins[low_at][t, here, :]) if full else w
                 else:
                     low_2 = readers[t](low_j, g)
                 if high_j is None:
-                    high_2 = jnp.where(vx_last, w, ins[high_at][t, here, :])
+                    high_2 = jnp.where(vx_last, w, ins[high_at][t, here, :]) if full else w
                 else:
                     high_2 = readers[t](high_j, g)
                 slope = high_2 - low_2
@@ -271,13 +279,131 @@
     )(table, *ops.arrays)
 
 
-def settle(sizes, targets, updates, costs, flags, damping=None, fields=None, prior=None, with_edges=True):
+def outer_terms(sizes, rows, halo_rows, maxima, stepper, heun, table):
+    cells_v, half, width, _, _ = sizes
+    groups = half // 8
+    late = stepper is None
+    arrays = [r.array for r in rows] + list(halo_rows) + ([] if late else [maxima, stepper])
+
+    def body(table_ref, *refs):
+        row_refs, before_ref, after_ref, out_refs = refs[:4], refs[4], refs[5], refs[-2:]
+        edge_low, edge_high = table_ref[5, 1] > 0.5, table_ref[5, 2] > 0.5
+        known = Rates(sizes)
+        if late:
+            scale = jnp.ones((8, LANES), jnp.float32)
+        else:
+            scale = known.time_step(known.rates(refs[6], refs[7])) * (0.5 if heun else 1.0)
+
+        def wide(x):
+            return jnp.concatenate([x] * (width // LANES), axis=1)
+
+        damp = wide(scale * (0.5 * known.rate_1 / known.step_1))
+        planner = scale * (PLANNER_SPEED / (2.0 * known.step_1))
+        to_1 = scale / (2.0 * known.step_1)
+
+        @pl.loop(0, cells_v)
+        def _(j):
+            flow = table_ref[4, j] * to_1
+            up, down = wide(flow + planner), wide(flow - planner)
+            for g in range(groups):
+                here = pl.ds(8 * g, 8)
+                for i in range(2):
+                    w = row_refs[3 * i][j, here, :]
+                    inside = row_refs[1 + i][j, here, :]
+                    if i == 0:
+                        low, high = jnp.where(edge_low, w, before_ref[j, here, :]), inside
+                    else:
+                        low, high = inside, jnp.where(edge_high, w, after_ref[j, here, :])
+                    slope = high - low
+                    out_refs[i][j, here, :] = jnp.maximum(up * slope, down * slope) - damp * (low + high - (w + w))
+
+    return pl.pallas_call(
+        body,
+        out_shape=[f32(cells_v, half, width)] * 2,
+        in_specs=[scalars()] + [whole()] * len(arrays),
+        out_specs=[whole()] * 2,
+        compiler_params=compiler_params(),
+        cost_estimate=estimate(),
+        name="outer_terms",
+    )(table, *arrays)
+
+
+def mend(sizes, edges, vx_low, vx_high, vy_next, maxima, stepper, heun, accel_second, table):
+    cells_v, half, width, _, _ = sizes
+    late = stepper is None
+    first, second, before, last, edge, inner, _ = edges
+    arrays = [first, second, before, last, edge, inner, vx_low, vx_high, vy_next, accel_second] + ([] if late else [maxima, stepper])
+
+    def body(table_ref, *refs):
+        first_ref, second_ref, before_ref, last_ref, edge_ref, inner_ref, low_ref, high_ref, next_ref, accel_ref = refs[:10]
+        update_2, bend_2, update_3, bend_3 = refs[-4:]
+        is_odd, _, _, vx_first, vx_last = (table_ref[5, i] > 0.5 for i in range(5))
+        is_even = jnp.logical_not(is_odd)
+        known = Rates(sizes)
+        if late:
+            scale = jnp.ones((8, LANES), jnp.float32)
+        else:
+            scale = known.time_step(known.rates(refs[10], refs[11])) * (0.5 if heun else 1.0)
+
+        def wide(x):
+            return jnp.concatenate([x] * (width // LANES), axis=1)
+
+        disturb_2 = scale * (DISTURBANCE / (2.0 * known.step_2))
+        disturb_3 = wide(scale * (DISTURBANCE / (2.0 * known.step_3)))
+        control_2 = wide(scale * (1.0 / (8.0 * CONTROL_COST * known.step_2 * known.step_2)))
+        control_3 = wide(scale * (1.0 / (8.0 * CONTROL_COST * known.step_3 * known.step_3)))
+        to_2, to_3 = scale / (2.0 * known.step_2), wide(scale / (2.0 * known.step_3))
+
+        def term(up, down, control, slope):
+            return (jnp.where(slope > 0.0, up, down) - control * slope) * slope
+
+        for t in range(4):
+            for e, j in ((0, 0), (1, cells_v - 1)):
+                drift = table_ref[t, j] * to_2
+                up, down = wide(drift + disturb_2), wide(drift - disturb_2)
+                for start in range(0, half, 8):
+                    here = pl.ds(start, 8)
+                    if e == 0:
+                        own, inside = first_ref[t, here, :], second_ref[t, here, :]
+                        halo = jnp.where(vx_first, own, low_ref[t, here, :])
+                        right, wrong = inside - halo, inside - own
+                    else:
+                        own, inside = last_ref[t, here, :], before_ref[t, here, :]
+                        halo = jnp.where(vx_last, own, high_ref[t, here, :])
+                        right, wrong = halo - inside, own - inside
+                    update_2[t, e, here, :] = term(up, down, control_2, right) - term(up, down, control_2, wrong)
+                    bend_2[t, e, here, :] = halo - own
+        at = jnp.where(is_even, half - 1, half)
+        accel = jnp.broadcast_to(accel_ref[pl.ds(at, 1), :], (8, width)) * to_3
+        up, down = accel + disturb_3, accel - disturb_3
+        for t in range(4):
+            for start in range(0, cells_v, 8):
+                here = pl.ds(start, 8)
+                own, inside, halo = edge_ref[t, here, :], inner_ref[t, here, :], next_ref[3 - t, here, :]
+                right = jnp.where(is_even, halo - inside, inside - halo)
+                wrong = jnp.where(is_even, own - inside, inside - own)
+                update_3[t, here, :] = term(up, down, control_3, right) - term(up, down, control_3, wrong)
+                bend_3[t, here, :] = halo - own
+
+    return pl.pallas_call(
+        body,
+        out_shape=[f32(4, 2, half, width)] * 2 + [f32(4, cells_v, width)] * 2,
+        in_specs=[scalars()] + [whole()] * len(arrays),
+        out_specs=[whole()] * 4,
+        compiler_params=compiler_params(),
+        cost_estimate=estimate(),
+        name="mend",
+    )(table, *arrays)
+
+
+def settle(sizes, targets, updates, costs, flags, damping=None, fields=None, prior=None, with_edges=True, mended=None):
     cells_v, half, width, total_vx, total_vy = sizes
     count = len(targets)
     ops = Operands()
     update_at = [[ops.add(a) for a in u] for u in updates]
     cost_at = [ops.add(c.array) for c in costs]
     field_at = [ops.add(f.array) for f in fields] if fields is not None else []
+    mended_at = [ops.add(m) for m in mended] if mended is not None else []
     maxima_at = [ops.add(m) for m in damping[:3]] if damping is not None else []
     before_targets, before_outs = prior if prior is not None else ((), ())
     prior_at = [ops.add(a) for a in before_outs]
@@ -304,15 +430,32 @@
         field_readers = [f.reader(ins[a], parity, half) for f, a in zip(fields or (), field_at)]
         sublane = lax.broadcasted_iota(jnp.int32, (8, width), 0)
 
-        def tile(i, j):
+        row_low = jnp.where(is_even, -1, 0)
+        row_high = jnp.where(is_even, 7, -1)
+
+        def tile(i, j, end=None):
+            t = targets[i]
             out = []
+            if mended is not None:
+                along_2, twice_2, along_3, twice_3 = (ins[a] for a in mended_at)
+                here = pl.ds(j, 1)
+                beside = jnp.broadcast_to(along_3[t, here, :] - damp_3[0:1] * twice_3[t, here, :], (8, width))
             for g in range(groups):
                 here = pl.ds(8 * g, 8)
                 total = ins[update_at[i][0]][j, here, :]
+                if len(update_at[i]) > 3:
+                    total = total + ins[update_at[i][3]][j, here, :]
                 if damping is not None:
                     total = total - damp_2 * ins[update_at[i][1]][j, here, :] - damp_3 * ins[update_at[i][2]][j, here, :]
-                    if fields is not None:
-                        total = field_readers[i](j, g) + scale * total
+                if mended is not None:
+                    if g == 0:
+                        total = total + jnp.where(sublane == row_low, beside, 0.0)
+                    if g == groups - 1:
+                        total = total + jnp.where(sublane == row_high, beside, 0.0)
+                    if end is not None:
+                        total = total + along_2[t, end, here, :] - damp_2 * twice_2[t, end, here, :]
+                if fields is not None:
+                    total = field_readers[i](j, g) + scale * total
                 y = jnp.maximum(cost_readers[i](j, g), total)
                 fields_out[i][j, here, :] = y
                 out.append(y)
@@ -325,7 +468,8 @@
                 def step(j, least, i=i):
                     return functools.reduce(jnp.minimum, tile(i, j), least)
 
-                least = lax.fori_loop(0, cells_v, step, jnp.full((8, width), jnp.inf, jnp.float32))
+                least = functools.reduce(jnp.minimum, tile(i, 0, 0) + tile(i, cells_v - 1, 1))
+                least = lax.fori_loop(1, cells_v - 1, step, least)
                 least_ref[pl.ds(i, 1), :] = jnp.min(least, axis=0, keepdims=True)
             return
 
@@ -339,9 +483,9 @@
             for ref, at in zip((first_ref, second_ref, before_ref, last_ref, edge_ref, inner_ref), prior_at):
                 ref[slot] = ins[at][position]
 
-        def one(i, j, most_3):
+        def one(i, j, most_3, end=None):
             slot = every.index(targets[i])
-            out = tile(i, j)
+            out = tile(i, j, end)
             edge_ref[slot, pl.ds(j, 1), :] = fields_out[i][j, pl.ds(send_at, 1), :]
             inner_ref[slot, pl.ds(j, 1), :] = fields_out[i][j, pl.ds(inner_at, 1), :]
             wall = jnp.abs(fields_out[i][j, pl.ds(next_at, 1), :] - fields_out[i][j, pl.ds(wall_at, 1), :])
@@ -357,17 +501,18 @@
         if prior is not None:
             most_2, most_3 = ins[prior_at[6]][0], ins[prior_at[6]][1]
         for i in range(count):
-            for j in (0, 1):
-                _, most_3 = one(i, j, most_3)
-
-            def step(j, carry, i=i):
+            _, most_3 = one(i, 0, most_3, 0)
+            _, most_3 = one(i, 1, most_3)
+
+            def step(j, carry, i=i, end=None):
                 most_2, most_3 = carry
-                out, most_3 = one(i, j, most_3)
+                out, most_3 = one(i, j, most_3, end)
                 for g in range(groups):
                     most_2 = jnp.maximum(most_2, jnp.abs(out[g] - fields_out[i][j - 2, pl.ds(8 * g, 8), :]))
                 return most_2, most_3
 
-            most_2, most_3 = lax.fori_loop(2, cells_v, step, (most_2, most_3))
+            most_2, most_3 = lax.fori_loop(2, cells_v - 1, step, (most_2, most_3))
+            most_2, most_3 = step(cells_v - 1, (most_2, most_3), end=1)
             slot = every.index(targets[i])
             first_ref[slot] = fields_out[i][0]
             second_ref[slot] = fields_out[i][1]
@@ -622,30 +767,31 @@
     costs = [Own(cost, True), Own(cost, False), Row(cost_inner_got), Row(cost_outer_got)]
     halo_rows = (halo_before(value_outer_got), halo_after(half_of(value, late, late)))
 
-    def advanced(targets, field, bases, halo_rows, vx_low, vx_high, vy_next, stepper):
-        some = None if bases is None else [bases[t] for t in targets]
-        got = advance(
-            sizes, targets, field, some, halo_rows, vx_low, vx_high, vy_next, shared_first, stepper, accel_second, table
-        )
+    every = (0, 1, 2, 3)
+
+    def advanced(targets, field, bases, halos, stepper):
+        got = advance(sizes, targets, field, bases, halos, shared_first, stepper, accel_second, table)
         each = len(got) // len(targets)
         return {t: got[each * i : each * (i + 1)] for i, t in enumerate(targets)}
 
     def settled(targets, updates, **kw):
         return settle(sizes, targets, [updates[t] for t in targets], [costs[t] for t in targets], flags, **kw)
 
-    def next_updates(field, edges, bases, stepper, halo_rows, halo_early):
+    def next_updates(field, edges, bases, stepper, halo_rows):
         first, _, _, last, edge, _, _ = edges
         low, high, row = from_low_vx(last), from_high_vx(first), partner(edge)
-        maxima = edge_maxima(edges, low, high, row, flags)
-        updates, beside = {}, {}
-        for place_at, t in enumerate((1, 2, 0, 3) if halo_early else (1, 2)):
-            updates.update(advanced((t,), field, bases, halo_rows, low, high, row, stepper))
-            beside[place_at + 1] = updates[t]
-        if not halo_early:
-            updates.update(advanced((0, 3), field, bases, halo_rows, low, high, row, stepper))
-            beside[4] = updates[0] + updates[3]
-        maxima = share(maxima, beside)
-        return updates, maxima
+        def ahead(targets):
+            return advanced(targets, field, None if bases is None else [bases[t] for t in targets], None, stepper)
+
+        updates = ahead((1, 2))
+        low, high, row = lax.optimization_barrier((low, high, row, updates))[:3]
+        heun = bases is not None
+        mended = mend(sizes, edges, low, high, row, shared_first, stepper, heun, accel_second, table)
+        updates.update(ahead((0,)))
+        updates.update(ahead((3,)))
+        outer = outer_terms(sizes, field, halo_rows, shared_first, stepper, heun, table)
+        maxima = share(edge_maxima(edges, low, high, row, flags), {1: mended, 2: updates[0], 3: updates[3], 4: outer})
+        return {**updates, 0: updates[0] + outer[:1], 3: updates[3] + outer[1:]}, mended, maxima
 
     def settled_all(updates, **kw):
         fields = kw.pop("fields", None)
@@ -656,8 +802,9 @@
         (inner, near), edges = settled((1, 2), updates, prior=((0, 3), edges), **some, **kw)
         return [Row(f) for f in (outer, inner, near, far)], edges, halo_rows
 
-    updates = advanced((1, 2), chain, None, halo_rows, vx_low, vx_high, vy_next, shared_first)
-    updates.update(advanced((0, 3), chain, None, halo_rows, vx_low, vx_high, vy_next, shared_first))
+    halos = (halo_rows, vx_low, vx_high, vy_next)
+    updates = advanced((1, 2), chain, None, halos, shared_first)
+    updates.update(advanced((0, 3), chain, None, halos, shared_first))
     (outer, inner), edges = settled((0, 1), updates)
     beyond = halo_after(outer)
     (far,), edges = settled((3,), updates, prior=((0, 1), edges))
@@ -665,17 +812,17 @@
     (near,), edges = settled((2,), updates, prior=((0, 1, 3), edges))
     middle = [Row(f) for f in (outer, inner, near, far)]
 
-    updates, shared = next_updates(middle, edges, chain, shared_first, halo_rows, True)
-    chain, edges, halo_rows = settled_all(updates, damping=(shared_first, shared_first, shared, 0.5))
-
-    updates, shared_second = next_updates(chain, edges, None, None, halo_rows, False)
-    middle, edges, halo_rows = settled_all(updates, damping=(shared_first, shared_second, shared_second, 1.0), fields=chain)
-
-    updates, shared = next_updates(middle, edges, chain, shared_second, halo_rows, False)
+    updates, mended, shared = next_updates(middle, edges, chain, shared_first, halo_rows)
+    chain, edges, halo_rows = settled_all(updates, mended=mended, damping=(shared_first, shared_first, shared, 0.5))
+
+    updates, mended, shared_second = next_updates(chain, edges, None, None, halo_rows)
+    middle, edges, halo_rows = settled_all(updates, mended=mended, damping=(shared_first, shared_second, shared_second, 1.0), fields=chain)
+
+    updates, mended, shared = next_updates(middle, edges, chain, shared_second, halo_rows)
     damping = (shared_first, shared_second, shared, 0.5)
-    (near,), (least_near,) = settled((2,), updates, damping=damping, with_edges=False)
+    (near,), (least_near,) = settled((2,), updates, damping=damping, mended=mended, with_edges=False)
     inner_got = partner(near)
-    (outer, inner, far), (least,) = settled((0, 1, 3), updates, damping=damping, with_edges=False)
+    (outer, inner, far), (least,) = settled((0, 1, 3), updates, damping=damping, mended=mended, with_edges=False)
     outer_got = partner(far)
     least = lax.pmin(jnp.concatenate([least[:2], least_near, least[2:]], axis=0), "vx")
     least_got = partner(after(least[2:], far))

time: 282 us -> 276 us (0.979)
  waiting for transfers between devices: 108 us -> 89.7 us
  local copies, waits for them, and re-layouts: 14.9 us -> 21.8 us
  Pallas kernels: 70.5 us -> 75.6 us
    ppermute x13, waiting for transfers between devices: 66.7 us -> 46 us  [partner(): return lax.ppermute(x, 'px', [(i, i ^ 1) for i in range(n_px)])]
    pallas_call x0 -> x6, Pallas kernels: none -> 7.48 us  [the longest x3 4.74 us: outer_terms(): pl.pallas_call(body, out_shape=[f32(cells_v, half, width)] * 2, in_specs=...]
    ppermute x19, starting transfers between devices: 28.7 us -> 21.5 us  [share(): lax.ppermute(maxima, axis, [(i, i ^ apart) for i in range(lax.axis_size(a...]
    unnamed x17 -> x27, local copies, waits for them, and re-layouts: 2.38 us -> 9.35 us
    ppermute x5, starting transfers between devices: 6.5 us -> 11.9 us  [from_low_vx(): return lax.ppermute(x, 'vx', [(i, i + 1) for i in range(n_vx - 1)])]
    pallas_call x12 -> x11, Pallas kernels: 41.9 us -> 38.2 us  [advance(): pl.pallas_call(body, out_shape=[f32(cells_v, half, width)] * n_out, in_sp...]
    ppermute x19, waiting for transfers between devices: 36.6 us -> 39.5 us  [share(): lax.ppermute(maxima, axis, [(i, i ^ apart) for i in range(lax.axis_size(a...]
  transfers between devices with their start and end apart: 50 -> 50, of which waited for: 19 -> 25; matrix products, arithmetic and copies ran while one was open for 4% -> 4% of each run, Pallas kernels for 22% -> 24%
where the time goes in v5:
time: 276 us; the launch traced here: 275 us
  waiting for transfers between devices  89.7 us (32%)
  starting transfers between devices  79.8 us (29%)
  Pallas kernels  75.6 us (27%)
  local copies, waits for them, and re-layouts  21.8 us (8%)
  blocking collectives  6.15 us (2%)
    ppermute x13, waiting for transfers between devices, partner(): return lax.ppermute(x, 'px', [(i, i ^ 1) for i in range(n_px)])  46 us
    ppermute x19, waiting for transfers between devices, share(): lax.ppermute(maxima, axis, [(i, i ^ apart) for i in range(lax.axis_size(a...  39.5 us
    pallas_call x11, Pallas kernels, advance(): pl.pallas_call(body, out_shape=[f32(cells_v, half, width)] * n_out, in_sp...  38.2 us
    ppermute x19, starting transfers between devices, share(): lax.ppermute(maxima, axis, [(i, i ^ apart) for i in range(lax.axis_size(a...  21.5 us
    pallas_call x9, Pallas kernels, settle(): pl.pallas_call(body, out_shape=shapes, in_specs=[scalars()] + [whole()] *...  19.2 us
    ppermute x4, starting transfers between devices, halo_before(): return lax.ppermute(outermost, 'px', moves)  17.4 us
    ppermute x13, starting transfers between devices, partner(): return lax.ppermute(x, 'px', [(i, i ^ 1) for i in range(n_px)])  17.4 us
    ppermute x5, starting transfers between devices, from_low_vx(): return lax.ppermute(x, 'vx', [(i, i + 1) for i in range(n_vx - 1)])  11.9 us
  transfers between devices with their start and end apart: 50, of which 25 were waited for; matrix products, arithmetic and copies ran while one was open for 4% of the time, Pallas kernels for 24%

profile of v5, /device:TPU:0, one launch (start us, length us, event | category | flops | bytes accessed | tf_op | source)
XLA Modules:
  0.0 274.8 jit_solution(2414089217044286811)
XLA Ops:
  0.7 2.4 dynamic-slice_bitcast_fusion.4
  3.0 2.9 %collective-permute-start.6 = (f32[24,32,384]{2,1,0:T(8,128)}, f32[24,32,384]{2,1,0:T(8,128)S(1)}, u32[]{:S(2)}, u32[]{:S(2)}) collective-permute-start(f32[24,32,384]{2,1,0:T(8,128)} %dynamic-slice_bitcast_fusion.4), channel_id=1, source_target_pairs={{0,4},{4,0},{8,12},{12,8},{16,20},{20,16},{24,28},{28,24},{1,5},{5... | collective-permute-start | bytes 3538952 | tf_op jit(solution)/shard_map/ppermute | solution.py:695
  7.1 2.1 collective-permute-start.4
  10.3 1.3 collective-permute-start.1
  14.2 3.3 %dynamic-slice_bitcast_fusion.2 = (f32[24,32,384]{2,1,0:T(8,128)}, f32[24,32,384]{2,1,0:T(8,128)}) fusion(f32[2,24,64,384]{3,2,1,0:T(8,128)} %refs_4_.2, s32[]{:T(128)S(6)} %select_n.88, s32[]{:T(128)S(6)} %select_n.89, s32[]{:T(128)S(6)} %select_n.85, s32[]{:T(128)S(6)} %select_n.86), kind=kLoop, calls=%fused_computation.2 | loop fusion | bytes 4718608 | tf_op jit(solution)/shard_map/squeeze | solution.py:726
  18.9 2.2 first_maxima.1
  21.1 3.8 %collective-permute-start.3 = (f32[8,128]{1,0:T(8,128)S(1)}, f32[8,128]{1,0:T(8,128)S(1)}, u32[]{:S(2)}, u32[]{:S(2)}) collective-permute-start(f32[8,128]{1,0:T(8,128)S(1)} %first_maxima.1), channel_id=1, source_target_pairs={{0,4},{4,0},{8,12},{12,8},{16,20},{20,16},{24,28},{28,24},{1,5},{5... | collective-permute-start | bytes 12296 | tf_op jit(solution)/shard_map/ppermute | solution.py:695
  24.9 9.0 %collective-permute-done.3 = f32[8,128]{1,0:T(8,128)S(1)} collective-permute-done((f32[8,128]{1,0:T(8,128)S(1)}, f32[8,128]{1,0:T(8,128)S(1)}, u32[]{:S(2)}, u32[]{:S(2)}) %collective-permute-start.3) | collective-permute-done | bytes 4128 | tf_op jit(solution)/shard_map/ppermute | solution.py:695
  33.9 1.8 collective-permute-start.5
  35.7 3.2 %dynamic-slice_bitcast_fusion = (f32[24,32,384]{2,1,0:T(8,128)}, f32[24,32,384]{2,1,0:T(8,128)}) fusion(f32[2,24,64,384]{3,2,1,0:T(8,128)} %refs_11_.1, s32[]{:T(128)S(6)} %select_n.88, s32[]{:T(128)S(6)} %select_n.86, s32[]{:T(128)S(6)} %select_n.85), kind=kLoop, calls=%fused_computation | loop fusion | bytes 4718604 | tf_op jit(solution)/shard_map/squeeze | solution.py:726
  40.2 1.5 collective-permute-start.12
  41.7 3.5 %collective-permute-start.7 = (f32[24,32,384]{2,1,0:T(8,128)S(1)}, f32[24,32,384]{2,1,0:T(8,128)S(1)}, u32[]{:S(2)}, u32[]{:S(2)}) collective-permute-start(f32[24,32,384]{2,1,0:T(8,128)S(1)} %collective-permute-done.6.refs_2_), channel_id=1, source_target_pairs={{0,8},{8,16},{16,24},{12,4},{20,12},{28,20},{1,9},{9,17},{17,25},{... | collective-permute-start | bytes 3538952 | tf_op jit(solution)/shard_map/ppermute | solution.py:705
  45.3 1.6 collective-permute-start.13
  46.9 23.6 %collective-permute-done.13 = f32[8,128]{1,0:T(8,128)S(1)} collective-permute-done((f32[8,128]{1,0:T(8,128)S(1)}, f32[8,128]{1,0:T(8,128)S(1)}, u32[]{:S(2)}, u32[]{:S(2)}) %collective-permute-start.13) | collective-permute-done | bytes 4128 | tf_op jit(solution)/shard_map/ppermute | solution.py:719
  70.5 2.6 collective-permute-start.14
  73.1 1.9 collective-permute-done.14
  75.1 1.8 collective-permute-start.15
  77.0 1.3 collective-permute-start.9
  80.5 3.3 %collective-permute-done.10 = f32[2,32,384]{2,1,0:T(8,128)S(1)} collective-permute-done((f32[2,32,384]{2,1,0:T(8,128)S(1)}, f32[2,32,384]{2,1,0:T(8,128)S(1)}, u32[]{:S(2)}, u32[]{:S(2)}) %collective-permute-start.10) | collective-permute-done | bytes 98336 | tf_op jit(solution)/shard_map/ppermute | solution.py:701
  83.8 2.3 copy-done.1
  86.2 4.8 %advance_12.4 = (f32[24,32,384]{2,1,0:T(8,128)S(1)}, f32[24,32,384]{2,1,0:T(8,128)S(1)}) custom-call(f32[6,24]{1,0:T(8,128)S(1)} %concatenate.15.table_ref, f32[2,24,64,384]{3,2,1,0:T(8,128)S(1)} %copy-done.1, f32[24,32,384]{2,1,0:T(8,128)S(1)} %collective-permute-done.5.refs_1_.refs_5_, f32[24,32,384]{2,1,0:T(8,128)S(1)} %collective-permute-done.6.refs_2_, ...), custom_call_target="tpu_custom_call" | custom-call | tf_op jit(solution)/shard_map/advance_12/pallas_call | solution.py:270
  91.0 2.4 copy-done.2
  93.4 5.7 %advance_03.1 = (f32[24,32,384]{2,1,0:T(8,128)S(1)}, f32[24,32,384]{2,1,0:T(8,128)S(1)}) custom-call(f32[6,24]{1,0:T(8,128)S(1)} %concatenate.15.table_ref, f32[2,24,64,384]{3,2,1,0:T(8,128)S(1)} %copy-done.2, f32[24,32,384]{2,1,0:T(8,128)S(1)} %collective-permute-done.5.refs_1_.refs_5_, f32[24,32,384]{2,1,0:T(8,128)S(1)} %collective-permute-done.6.refs_2_, ...), custom_call_target="tpu_custom_call" | custom-call | tf_op jit(solution)/shard_map/advance_03/pallas_call | solution.py:270
  99.1 1.8 settle_01.1
  103.4 4.6 %collective-permute-start.17 = (f32[24,32,384]{2,1,0:T(8,128)S(1)}, f32[24,32,384]{2,1,0:T(8,128)S(1)}, u32[]{:S(2)}, u32[]{:S(2)}) collective-permute-start(f32[24,32,384]{2,1,0:T(8,128)S(1)} %get-tuple-element.189.refs_3_.refs_1_), channel_id=1, source_target_pairs={{0,8},{8,16},{16,24},{12,4},{20,12},{28,20},{1,9},{9,17},{17,25},{... | collective-permute-start | bytes 3538952 | tf_op jit(solution)/shard_map/ppermute | solution.py:705
  108.1 3.9 %collective-permute-done.15.refs_1_.refs_7_.refs_3_ = f32[24,32,384]{2,1,0:T(8,128)S(1)} collective-permute-done((f32[24,32,384]{2,1,0:T(8,128)}, f32[24,32,384]{2,1,0:T(8,128)S(1)}, u32[]{:S(2)}, u32[]{:S(2)}) %collective-permute-start.15) | collective-permute-done | bytes 1179680 | tf_op jit(solution)/shard_map/ppermute | solution.py:695
  114.4 3.0 %collective-permute-start.19 = (f32[4,32,384]{2,1,0:T(8,128)S(1)}, f32[4,32,384]{2,1,0:T(8,128)S(1)}, u32[]{:S(2)}, u32[]{:S(2)}) collective-permute-start(f32[4,32,384]{2,1,0:T(8,128)S(1)} %get-tuple-element.198.refs_3_.last_ref), channel_id=1, source_target_pairs={{0,1},{1,2},{2,3},{4,5},{5,6},{6,7},{8,9},{9,10},{10,11},{12,13},{... | collective-permute-start | bytes 589832 | tf_op jit(solution)/shard_map/ppermute | solution.py:698
  117.5 1.4 collective-permute-start.21
  118.9 4.8 %advance_12.5 = (f32[24,32,384]{2,1,0:T(8,128)S(1)}, f32[24,32,384]{2,1,0:T(8,128)S(1)}, f32[24,32,384]{2,1,0:T(8,128)S(1)}, f32[24,32,384]{2,1,0:T(8,128)S(1)},...) custom-call(f32[6,24]{1,0:T(8,128)S(1)} %concatenate.15.table_ref, ...), custom_call_target="tpu_custom_call" | custom-call | tf_op jit(solution)/shard_map/advance_12/pallas_call | solution.py:270
  128.1 1.7 collective-permute-done.23
  131.0 2.4 advance_0.3
  133.4 1.7 collective-permute-start.25
  135.1 2.4 advance_3.3
  137.5 2.7 collective-permute-start.26
  140.2 1.6 outer_terms.3
  142.1 2.3 settle_03.2
  145.8 4.6 %collective-permute-start.27 = (f32[24,32,384]{2,1,0:T(8,128)S(1)}, f32[24,32,384]{2,1,0:T(8,128)S(1)}, u32[]{:S(2)}, u32[]{:S(2)}) collective-permute-start(f32[24,32,384]{2,1,0:T(8,128)S(1)} %get-tuple-element.232.refs_3_.refs_1_.refs_11_.refs_2_), channel_id=1, source_target_pairs={{0,8},{8,16},{16,24},{12,4},{20,12},{28,20},{1,9},{9,17},{17,25},{... | collective-permute-start | bytes 3538952 | tf_op jit(solution)/shard_map/ppermute | solution.py:705
  150.4 2.3 settle_12.2
  154.0 3.0 %collective-permute-start.29 = (f32[4,32,384]{2,1,0:T(8,128)S(1)}, f32[4,32,384]{2,1,0:T(8,128)S(1)}, u32[]{:S(2)}, u32[]{:S(2)}) collective-permute-start(f32[4,32,384]{2,1,0:T(8,128)S(1)} %get-tuple-element.241.refs_3_.last_ref), channel_id=1, source_target_pairs={{0,1},{1,2},{2,3},{4,5},{5,6},{6,7},{8,9},{9,10},{10,11},{12,13},{... | collective-permute-start | bytes 589832 | tf_op jit(solution)/shard_map/ppermute | solution.py:698
  157.1 4.5 %advance_12.6 = (f32[24,32,384]{2,1,0:T(8,128)S(1)}, f32[24,32,384]{2,1,0:T(8,128)S(1)}, f32[24,32,384]{2,1,0:T(8,128)S(1)}, f32[24,32,384]{2,1,0:T(8,128)S(1)},...) custom-call(f32[6,24]{1,0:T(8,128)S(1)} %concatenate.15.table_ref, ...), custom_call_target="tpu_custom_call" | custom-call | tf_op jit(solution)/shard_map/advance_12/pallas_call | solution.py:270
  161.6 1.8 collective-permute-done.31.refs_8_.next_ref
  166.3 2.7 collective-permute-done.33
  169.3 2.2 advance_0.4
  173.7 2.2 advance_3.4
  176.2 2.6 collective-permute-start.36
  178.8 1.6 outer_terms.4
  180.7 2.5 settle_03.3
  184.5 4.6 %collective-permute-start.37 = (f32[24,32,384]{2,1,0:T(8,128)S(1)}, f32[24,32,384]{2,1,0:T(8,128)S(1)}, u32[]{:S(2)}, u32[]{:S(2)}) collective-permute-start(f32[24,32,384]{2,1,0:T(8,128)S(1)} %get-tuple-element.275.refs_3_.refs_1_), channel_id=1, source_target_pairs={{0,8},{8,16},{16,24},{12,4},{20,12},{28,20},{1,9},{9,17},{17,25},{... | collective-permute-start | bytes 3538952 | tf_op jit(solution)/shard_map/ppermute | solution.py:705
  189.1 2.5 settle_12.3
  192.9 3.2 %collective-permute-start.39 = (f32[4,32,384]{2,1,0:T(8,128)S(1)}, f32[4,32,384]{2,1,0:T(8,128)S(1)}, u32[]{:S(2)}, u32[]{:S(2)}) collective-permute-start(f32[4,32,384]{2,1,0:T(8,128)S(1)} %get-tuple-element.287.refs_3_.last_ref), channel_id=1, source_target_pairs={{0,1},{1,2},{2,3},{4,5},{5,6},{6,7},{8,9},{9,10},{10,11},{12,13},{... | collective-permute-start | bytes 589832 | tf_op jit(solution)/shard_map/ppermute | solution.py:698
  196.2 4.6 %advance_12.7 = (f32[24,32,384]{2,1,0:T(8,128)S(1)}, f32[24,32,384]{2,1,0:T(8,128)S(1)}, f32[24,32,384]{2,1,0:T(8,128)S(1)}, f32[24,32,384]{2,1,0:T(8,128)S(1)},...) custom-call(f32[6,24]{1,0:T(8,128)S(1)} %concatenate.15.table_ref, ...), custom_call_target="tpu_custom_call" | custom-call | tf_op jit(solution)/shard_map/advance_12/pallas_call | solution.py:270
  204.9 2.7 collective-permute-done.43
  208.5 2.3 advance_0.5
  212.3 2.3 advance_3.5
  214.8 2.6 collective-permute-start.46
  217.4 1.6 outer_terms.5
  219.3 2.0 settle_2.3
  222.3 3.4 %settle_013.1 = (f32[24,32,384]{2,1,0:T(8,128)S(1)}, f32[24,32,384]{2,1,0:T(8,128)S(1)}, f32[24,32,384]{2,1,0:T(8,128)}, f32[3,384]{1,0:T(4,128)S(1)}) custom-call(s32[5]{0:T(128)S(1)} %stack.45.flags_ref, f32[24,32,384]{2,1,0:T(8,128)S(1)} %get-tuple-element.271.refs_0_, f32[24,32,384]{2,1,0:T(8,128)S(1)} %get-tuple-element.272.refs_1_, ...), custom_call_target="tpu_custom_call" | custom-call | tf_op jit(solution)/shard_map/settle_013/pallas_call | solution.py:530
  228.8 6.2 %pmin.7.least_ref = f32[4,384]{1,0:T(4,128)S(1)} all-reduce(f32[4,384]{1,0:T(4,128)S(1)} %pad_maximum_fusion.5), channel_id=1, replica_groups=mesh['px'=8,'vx'=4] {'vx'}, use_global_device_ids=true, to_apply=%region_0.1 | all-reduce | flops 1536 | bytes 12288 | tf_op jit(solution)/shard_map/pmin | solution.py:827
  238.5 2.0 place.2.refs_1_
  240.5 10.1 %collective-permute-done.49.refs_0_ = f32[24,32,384]{2,1,0:T(8,128)} collective-permute-done((f32[24,32,384]{2,1,0:T(8,128)}, f32[24,32,384]{2,1,0:T(8,128)}, u32[]{:S(2)}, u32[]{:S(2)}) %collective-permute-start.49) | collective-permute-done | bytes 1179680 | tf_op jit(solution)/shard_map/ppermute | solution.py:695
  250.6 2.3 place.3._
  252.9 19.6 %collective-permute-done.48.got_ref = f32[2,384]{1,0:T(2,128)S(1)} collective-permute-done((f32[2,384]{1,0:T(2,128)S(1)}, f32[2,384]{1,0:T(2,128)S(1)}, u32[]{:S(2)}, u32[]{:S(2)}) %collective-permute-start.48) | collective-permute-done | bytes 3104 | tf_op jit(solution)/shard_map/ppermute | solution.py:695
  272.5 2.1 finish.1
  (147 shorter events, 46.4 us)
Async XLA Ops:
  0.7 5.3 %copy-start.8 = (f32[2,24]{1,0:T(2,128)S(1)}, f32[2,24]{1,0:T(2,128)}, u32[]{:S(2)}) copy-start(f32[2,24]{1,0:T(2,128)} %first_ref.1) | copy-start | bytes 580
  3.0 38.7 %collective-permute-start.6 = (f32[24,32,384]{2,1,0:T(8,128)}, f32[24,32,384]{2,1,0:T(8,128)S(1)}, u32[]{:S(2)}, u32[]{:S(2)}) collective-permute-start(f32[24,32,384]{2,1,0:T(8,128)} %dynamic-slice_bitcast_fusion.4), channel_id=1, source_target_pairs={{0,4},{4,0},{8,12},{12,8},{16,20},{20,16},{24,28},{28,24},{1,5},{5... | collective-permute-start | bytes 3538952 | tf_op jit(solution)/shard_map/ppermute | solution.py:695
  6.0 27.9 %collective-permute-start = (f32[2,24]{1,0:T(2,128)S(1)}, f32[2,24]{1,0:T(2,128)S(1)}, u32[]{:S(2)}, u32[]{:S(2)}) collective-permute-start(f32[2,24]{1,0:T(2,128)S(1)} %copy-done.8), channel_id=1, source_target_pairs={{0,4},{4,0},{8,12},{12,8},{16,20},{20,16},{24,28},{28,24},{1,5},{5... | collective-permute-start | bytes 584 | tf_op jit(solution)/shard_map/ppermute | solution.py:695
  7.1 26.7 %collective-permute-start.4 = (f32[2,24,384]{2,1,0:T(8,128)S(1)}, f32[2,24,384]{2,1,0:T(8,128)S(1)}, u32[]{:S(2)}, u32[]{:S(2)}) collective-permute-start(f32[2,24,384]{2,1,0:T(8,128)S(1)} %bitcast.36), channel_id=1, source_target_pairs={{0,4},{4,0},{8,12},{12,8},{16,20},{20,16},{24,28},{28,24},{1,5},{5... | collective-permute-start | bytes 221192 | tf_op jit(solution)/shard_map/ppermute | solution.py:695
  10.3 7.3 %collective-permute-start.1 = (f32[2,64,384]{2,1,0:T(8,128)S(1)}, f32[2,64,384]{2,1,0:T(8,128)S(1)}, u32[]{:S(2)}, u32[]{:S(2)}) collective-permute-start(f32[2,64,384]{2,1,0:T(8,128)S(1)} %get-tuple-element.159), channel_id=1, source_target_pairs={{0,1},{1,2},{2,3},{4,5},{5,6},{6,7},{8,9},{9,10},{10,11},{12,13},{... | collective-permute-start | bytes 589832 | tf_op jit(solution)/shard_map/ppermute | solution.py:698
  11.6 7.3 %collective-permute-start.2 = (f32[2,64,384]{2,1,0:T(8,128)S(1)}, f32[2,64,384]{2,1,0:T(8,128)S(1)}, u32[]{:S(2)}, u32[]{:S(2)}) collective-permute-start(f32[2,64,384]{2,1,0:T(8,128)S(1)} %get-tuple-element.160), channel_id=1, source_target_pairs={{1,0},{2,1},{3,2},{5,4},{6,5},{7,6},{9,8},{10,9},{11,10},{13,12},{... | collective-permute-start | bytes 589832 | tf_op jit(solution)/shard_map/ppermute | solution.py:701
  13.0 5.8 %copy-start.3 = (f32[64,384]{1,0:T(8,128)S(1)}, f32[64,384]{1,0:T(8,128)}, u32[]{:S(2)}) copy-start(f32[64,384]{1,0:T(8,128)} %refs_9_.5) | copy-start | bytes 294916
  14.2 4.7 %copy-start = (f32[2,24,64,384]{3,2,1,0:T(8,128)S(1)}, f32[2,24,64,384]{3,2,1,0:T(8,128)}, u32[]{:S(2)}) copy-start(f32[2,24,64,384]{3,2,1,0:T(8,128)} %refs_4_.2) | copy-start | bytes 14155780
  17.6 73.4 %collective-permute-start.8 = (f32[24,32,384]{2,1,0:T(8,128)}, f32[24,32,384]{2,1,0:T(8,128)}, u32[]{:S(2)}, u32[]{:S(2)}) collective-permute-start(f32[24,32,384]{2,1,0:T(8,128)} %get-tuple-element.316), channel_id=1, source_target_pairs={{8,0},{16,8},{24,16},{4,12},{12,20},{20,28},{9,1},{17,9},{25,17},{... | collective-permute-start | bytes 3538952 | tf_op jit(solution)/shard_map/ppermute | solution.py:709
  21.1 12.8 %collective-permute-start.3 = (f32[8,128]{1,0:T(8,128)S(1)}, f32[8,128]{1,0:T(8,128)S(1)}, u32[]{:S(2)}, u32[]{:S(2)}) collective-permute-start(f32[8,128]{1,0:T(8,128)S(1)} %first_maxima.1), channel_id=1, source_target_pairs={{0,4},{4,0},{8,12},{12,8},{16,20},{20,16},{24,28},{28,24},{1,5},{5... | collective-permute-start | bytes 12296 | tf_op jit(solution)/shard_map/ppermute | solution.py:695
  33.9 43.1 %collective-permute-start.5 = (f32[24,32,384]{2,1,0:T(8,128)}, f32[24,32,384]{2,1,0:T(8,128)S(1)}, u32[]{:S(2)}, u32[]{:S(2)}) collective-permute-start(f32[24,32,384]{2,1,0:T(8,128)} %get-tuple-element.162), channel_id=1, source_target_pairs={{0,4},{4,0},{8,12},{12,8},{16,20},{20,16},{24,28},{28,24},{1,5},{5... | collective-permute-start | bytes 3538952 | tf_op jit(solution)/shard_map/ppermute | solution.py:695
  38.9 1.2 collective-permute-start.11
  39.0 63.2 %collective-permute-start.16 = (f32[24,32,384]{2,1,0:T(8,128)}, f32[24,32,384]{2,1,0:T(8,128)S(1)}, u32[]{:S(2)}, u32[]{:S(2)}) collective-permute-start(f32[24,32,384]{2,1,0:T(8,128)} %get-tuple-element.173), channel_id=1, source_target_pairs={{0,4},{4,0},{8,12},{12,8},{16,20},{20,16},{24,28},{28,24},{1,5},{5... | collective-permute-start | bytes 3538952 | tf_op jit(solution)/shard_map/ppermute | solution.py:695
  40.2 5.1 %collective-permute-start.12 = (f32[8,128]{1,0:T(8,128)S(1)}, f32[8,128]{1,0:T(8,128)S(1)}, u32[]{:S(2)}, u32[]{:S(2)}) collective-permute-start(f32[8,128]{1,0:T(8,128)S(1)} %max.61), channel_id=1, source_target_pairs={{0,2},{1,3},{2,0},{3,1},{4,6},{5,7},{6,4},{7,5},{8,10},{9,11},{10,... | collective-permute-start | bytes 12296 | tf_op jit(solution)/shard_map/ppermute | solution.py:719
  41.7 49.3 %collective-permute-start.7 = (f32[24,32,384]{2,1,0:T(8,128)S(1)}, f32[24,32,384]{2,1,0:T(8,128)S(1)}, u32[]{:S(2)}, u32[]{:S(2)}) collective-permute-start(f32[24,32,384]{2,1,0:T(8,128)S(1)} %collective-permute-done.6.refs_2_), channel_id=1, source_target_pairs={{0,8},{8,16},{16,24},{12,4},{20,12},{28,20},{1,9},{9,17},{17,25},{... | collective-permute-start | bytes 3538952 | tf_op jit(solution)/shard_map/ppermute | solution.py:705
  45.3 25.2 %collective-permute-start.13 = (f32[8,128]{1,0:T(8,128)S(1)}, f32[8,128]{1,0:T(8,128)S(1)}, u32[]{:S(2)}, u32[]{:S(2)}) collective-permute-start(f32[8,128]{1,0:T(8,128)S(1)} %max.62), channel_id=1, source_target_pairs={{0,8},{4,12},{8,0},{12,4},{16,24},{20,28},{24,16},{28,20},{1,9},{5... | collective-permute-start | bytes 12296 | tf_op jit(solution)/shard_map/ppermute | solution.py:719
  70.5 4.5 %collective-permute-start.14 = (f32[8,128]{1,0:T(8,128)S(1)}, f32[8,128]{1,0:T(8,128)S(1)}, u32[]{:S(2)}, u32[]{:S(2)}) collective-permute-start(f32[8,128]{1,0:T(8,128)S(1)} %max.63), channel_id=1, source_target_pairs={{0,16},{4,20},{8,24},{12,28},{16,0},{20,4},{24,8},{28,12},{1,17},{... | collective-permute-start | bytes 12296 | tf_op jit(solution)/shard_map/ppermute | solution.py:719
  75.1 36.9 %collective-permute-start.15 = (f32[24,32,384]{2,1,0:T(8,128)}, f32[24,32,384]{2,1,0:T(8,128)S(1)}, u32[]{:S(2)}, u32[]{:S(2)}) collective-permute-start(f32[24,32,384]{2,1,0:T(8,128)} %get-tuple-element.171), channel_id=1, source_target_pairs={{0,4},{4,0},{8,12},{12,8},{16,20},{20,16},{24,28},{28,24},{1,5},{5... | collective-permute-start | bytes 3538952 | tf_op jit(solution)/shard_map/ppermute | solution.py:695
  77.0 2.2 collective-permute-start.9
  79.2 4.6 %collective-permute-start.10 = (f32[2,32,384]{2,1,0:T(8,128)S(1)}, f32[2,32,384]{2,1,0:T(8,128)S(1)}, u32[]{:S(2)}, u32[]{:S(2)}) collective-permute-start(f32[2,32,384]{2,1,0:T(8,128)S(1)} %pad_maximum_fusion.4), channel_id=1, source_target_pairs={{1,0},{2,1},{3,2},{5,4},{6,5},{7,6},{9,8},{10,9},{11,10},{13,12},{... | collective-permute-start | bytes 294920 | tf_op jit(solution)/shard_map/ppermute | solution.py:701
  83.8 2.3 copy-start.1
  86.2 13.0 %slice-start = ((s8[4718592]{0:T(1024)(128)(4,1)}), s8[4194304]{0:T(1024)(128)(4,1)S(1)}, s32[]{:S(2)}) async-start(s8[4718592]{0:T(1024)(128)(4,1)} %bitcast.32), calls=%async_computation | async-start | bytes 8388608
  91.0 8.2 %slice-start.1 = ((s8[4718592]{0:T(1024)(128)(4,1)}), s8[524288]{0:T(1024)(128)(4,1)S(1)}, s32[]{:S(2)}) async-start(s8[4718592]{0:T(1024)(128)(4,1)} %bitcast.32), calls=%async_computation.1 | async-start | bytes 1048576
  91.0 2.4 copy-start.2
  93.4 25.5 %slice-start.2 = ((s8[4718592]{0:T(1024)(128)(4,1)}), s8[4194304]{0:T(1024)(128)(4,1)S(1)}, s32[]{:S(2)}) async-start(s8[4718592]{0:T(1024)(128)(4,1)} %bitcast.34), calls=%async_computation.2 | async-start | bytes 8388608
  99.1 19.7 %slice-start.3 = ((s8[4718592]{0:T(1024)(128)(4,1)}), s8[524288]{0:T(1024)(128)(4,1)S(1)}, s32[]{:S(2)}) async-start(s8[4718592]{0:T(1024)(128)(4,1)} %bitcast.34), calls=%async_computation.3 | async-start | bytes 1048576
  101.0 39.2 %collective-permute-start.18 = (f32[24,32,384]{2,1,0:T(8,128)S(1)}, f32[24,32,384]{2,1,0:T(8,128)S(1)}, u32[]{:S(2)}, u32[]{:S(2)}) collective-permute-start(f32[24,32,384]{2,1,0:T(8,128)S(1)} %get-tuple-element.165.refs_0_), channel_id=1, source_target_pairs={{8,0},{16,8},{24,16},{4,12},{12,20},{20,28},{9,1},{17,9},{25,17},{... | collective-permute-start | bytes 3538952 | tf_op jit(solution)/shard_map/ppermute | solution.py:709
  103.4 36.8 %collective-permute-start.17 = (f32[24,32,384]{2,1,0:T(8,128)S(1)}, f32[24,32,384]{2,1,0:T(8,128)S(1)}, u32[]{:S(2)}, u32[]{:S(2)}) collective-permute-start(f32[24,32,384]{2,1,0:T(8,128)S(1)} %get-tuple-element.189.refs_3_.refs_1_), channel_id=1, source_target_pairs={{0,8},{8,16},{16,24},{12,4},{20,12},{28,20},{1,9},{9,17},{17,25},{... | collective-permute-start | bytes 3538952 | tf_op jit(solution)/shard_map/ppermute | solution.py:705
  113.1 11.0 %collective-permute-start.20 = (f32[4,32,384]{2,1,0:T(8,128)S(1)}, f32[4,32,384]{2,1,0:T(8,128)S(1)}, u32[]{:S(2)}, u32[]{:S(2)}) collective-permute-start(f32[4,32,384]{2,1,0:T(8,128)S(1)} %get-tuple-element.195.refs_0_.first_ref), channel_id=1, source_target_pairs={{1,0},{2,1},{3,2},{5,4},{6,5},{7,6},{9,8},{10,9},{11,10},{13,12},{... | collective-permute-start | bytes 589832 | tf_op jit(solution)/shard_map/ppermute | solution.py:701
  114.4 9.8 %collective-permute-start.19 = (f32[4,32,384]{2,1,0:T(8,128)S(1)}, f32[4,32,384]{2,1,0:T(8,128)S(1)}, u32[]{:S(2)}, u32[]{:S(2)}) collective-permute-start(f32[4,32,384]{2,1,0:T(8,128)S(1)} %get-tuple-element.198.refs_3_.last_ref), channel_id=1, source_target_pairs={{0,1},{1,2},{2,3},{4,5},{5,6},{6,7},{8,9},{9,10},{10,11},{12,13},{... | collective-permute-start | bytes 589832 | tf_op jit(solution)/shard_map/ppermute | solution.py:698
  117.5 6.7 %collective-permute-start.21 = (f32[4,24,384]{2,1,0:T(8,128)S(1)}, f32[4,24,384]{2,1,0:T(8,128)S(1)}, u32[]{:S(2)}, u32[]{:S(2)}) collective-permute-start(f32[4,24,384]{2,1,0:T(8,128)S(1)} %get-tuple-element.199.refs_4_), channel_id=1, source_target_pairs={{0,4},{4,0},{8,12},{12,8},{16,20},{20,16},{24,28},{28,24},{1,5},{5... | collective-permute-start | bytes 442376 | tf_op jit(solution)/shard_map/ppermute | solution.py:695
  124.9 1.2 collective-permute-start.22
  126.2 3.6 %collective-permute-start.23 = (f32[8,128]{1,0:T(8,128)S(1)}, f32[8,128]{1,0:T(8,128)S(1)}, u32[]{:S(2)}, u32[]{:S(2)}) collective-permute-start(f32[8,128]{1,0:T(8,128)S(1)} %max.65), channel_id=1, source_target_pairs={{0,2},{1,3},{2,0},{3,1},{4,6},{5,7},{6,4},{7,5},{8,10},{9,11},{10,... | collective-permute-start | bytes 12296 | tf_op jit(solution)/shard_map/ppermute | solution.py:719
  129.8 3.6 %collective-permute-start.24 = (f32[8,128]{1,0:T(8,128)S(1)}, f32[8,128]{1,0:T(8,128)S(1)}, u32[]{:S(2)}, u32[]{:S(2)}) collective-permute-start(f32[8,128]{1,0:T(8,128)S(1)} %max.66), channel_id=1, source_target_pairs={{0,4},{4,0},{8,12},{12,8},{16,20},{20,16},{24,28},{28,24},{1,5},{5... | collective-permute-start | bytes 12296 | tf_op jit(solution)/shard_map/ppermute | solution.py:719
  133.4 4.1 %collective-permute-start.25 = (f32[8,128]{1,0:T(8,128)S(1)}, f32[8,128]{1,0:T(8,128)S(1)}, u32[]{:S(2)}, u32[]{:S(2)}) collective-permute-start(f32[8,128]{1,0:T(8,128)S(1)} %max.67), channel_id=1, source_target_pairs={{0,8},{4,12},{8,0},{12,4},{16,24},{20,28},{24,16},{28,20},{1,9},{5... | collective-permute-start | bytes 12296 | tf_op jit(solution)/shard_map/ppermute | solution.py:719
  137.5 4.6 %collective-permute-start.26 = (f32[8,128]{1,0:T(8,128)S(1)}, f32[8,128]{1,0:T(8,128)S(1)}, u32[]{:S(2)}, u32[]{:S(2)}) collective-permute-start(f32[8,128]{1,0:T(8,128)S(1)} %max.68), channel_id=1, source_target_pairs={{0,16},{4,20},{8,24},{12,28},{16,0},{20,4},{24,8},{28,12},{1,17},{... | collective-permute-start | bytes 12296 | tf_op jit(solution)/shard_map/ppermute | solution.py:719
  144.5 34.3 %collective-permute-start.28 = (f32[24,32,384]{2,1,0:T(8,128)S(1)}, f32[24,32,384]{2,1,0:T(8,128)S(1)}, u32[]{:S(2)}, u32[]{:S(2)}) collective-permute-start(f32[24,32,384]{2,1,0:T(8,128)S(1)} %get-tuple-element.219.refs_0_.refs_10_.refs_2_), channel_id=1, source_target_pairs={{8,0},{16,8},{24,16},{4,12},{12,20},{20,28},{9,1},{17,9},{25,17},{... | collective-permute-start | bytes 3538952 | tf_op jit(solution)/shard_map/ppermute | solution.py:709
  145.8 33.0 %collective-permute-start.27 = (f32[24,32,384]{2,1,0:T(8,128)S(1)}, f32[24,32,384]{2,1,0:T(8,128)S(1)}, u32[]{:S(2)}, u32[]{:S(2)}) collective-permute-start(f32[24,32,384]{2,1,0:T(8,128)S(1)} %get-tuple-element.232.refs_3_.refs_1_.refs_11_.refs_2_), channel_id=1, source_target_pairs={{0,8},{8,16},{16,24},{12,4},{20,12},{28,20},{1,9},{9,17},{17,25},{... | collective-permute-start | bytes 3538952 | tf_op jit(solution)/shard_map/ppermute | solution.py:705
  152.7 10.7 %collective-permute-start.30 = (f32[4,32,384]{2,1,0:T(8,128)S(1)}, f32[4,32,384]{2,1,0:T(8,128)S(1)}, u32[]{:S(2)}, u32[]{:S(2)}) collective-permute-start(f32[4,32,384]{2,1,0:T(8,128)S(1)} %get-tuple-element.238.refs_0_.first_ref), channel_id=1, source_target_pairs={{1,0},{2,1},{3,2},{5,4},{6,5},{7,6},{9,8},{10,9},{11,10},{13,12},{... | collective-permute-start | bytes 589832 | tf_op jit(solution)/shard_map/ppermute | solution.py:701
  154.0 9.4 %collective-permute-start.29 = (f32[4,32,384]{2,1,0:T(8,128)S(1)}, f32[4,32,384]{2,1,0:T(8,128)S(1)}, u32[]{:S(2)}, u32[]{:S(2)}) collective-permute-start(f32[4,32,384]{2,1,0:T(8,128)S(1)} %get-tuple-element.241.refs_3_.last_ref), channel_id=1, source_target_pairs={{0,1},{1,2},{2,3},{4,5},{5,6},{6,7},{8,9},{9,10},{10,11},{12,13},{... | collective-permute-start | bytes 589832 | tf_op jit(solution)/shard_map/ppermute | solution.py:698
  157.0 6.4 %collective-permute-start.31 = (f32[4,24,384]{2,1,0:T(8,128)S(1)}, f32[4,24,384]{2,1,0:T(8,128)S(1)}, u32[]{:S(2)}, u32[]{:S(2)}) collective-permute-start(f32[4,24,384]{2,1,0:T(8,128)S(1)} %get-tuple-element.242.refs_4_), channel_id=1, source_target_pairs={{0,4},{4,0},{8,12},{12,8},{16,20},{20,16},{24,28},{28,24},{1,5},{5... | collective-permute-start | bytes 442376 | tf_op jit(solution)/shard_map/ppermute | solution.py:695
  164.1 1.2 collective-permute-start.32
  165.4 3.6 %collective-permute-start.33 = (f32[8,128]{1,0:T(8,128)S(1)}, f32[8,128]{1,0:T(8,128)S(1)}, u32[]{:S(2)}, u32[]{:S(2)}) collective-permute-start(f32[8,128]{1,0:T(8,128)S(1)} %max.70), channel_id=1, source_target_pairs={{0,2},{1,3},{2,0},{3,1},{4,6},{5,7},{6,4},{7,5},{8,10},{9,11},{10,... | collective-permute-start | bytes 12296 | tf_op jit(solution)/shard_map/ppermute | solution.py:719
  169.0 3.6 %collective-permute-start.34 = (f32[8,128]{1,0:T(8,128)S(1)}, f32[8,128]{1,0:T(8,128)S(1)}, u32[]{:S(2)}, u32[]{:S(2)}) collective-permute-start(f32[8,128]{1,0:T(8,128)S(1)} %max.71), channel_id=1, source_target_pairs={{0,4},{4,0},{8,12},{12,8},{16,20},{20,16},{24,28},{28,24},{1,5},{5... | collective-permute-start | bytes 12296 | tf_op jit(solution)/shard_map/ppermute | solution.py:719
  172.6 3.6 %collective-permute-start.35 = (f32[8,128]{1,0:T(8,128)S(1)}, f32[8,128]{1,0:T(8,128)S(1)}, u32[]{:S(2)}, u32[]{:S(2)}) collective-permute-start(f32[8,128]{1,0:T(8,128)S(1)} %max.72), channel_id=1, source_target_pairs={{0,8},{4,12},{8,0},{12,4},{16,24},{20,28},{24,16},{28,20},{1,9},{5... | collective-permute-start | bytes 12296 | tf_op jit(solution)/shard_map/ppermute | solution.py:719
  176.2 4.5 %collective-permute-start.36 = (f32[8,128]{1,0:T(8,128)S(1)}, f32[8,128]{1,0:T(8,128)S(1)}, u32[]{:S(2)}, u32[]{:S(2)}) collective-permute-start(f32[8,128]{1,0:T(8,128)S(1)} %max.73), channel_id=1, source_target_pairs={{0,16},{4,20},{8,24},{12,28},{16,0},{20,4},{24,8},{28,12},{1,17},{... | collective-permute-start | bytes 12296 | tf_op jit(solution)/shard_map/ppermute | solution.py:719
  183.2 34.2 %collective-permute-start.38 = (f32[24,32,384]{2,1,0:T(8,128)S(1)}, f32[24,32,384]{2,1,0:T(8,128)S(1)}, u32[]{:S(2)}, u32[]{:S(2)}) collective-permute-start(f32[24,32,384]{2,1,0:T(8,128)S(1)} %get-tuple-element.262.refs_0_), channel_id=1, source_target_pairs={{8,0},{16,8},{24,16},{4,12},{12,20},{20,28},{9,1},{17,9},{25,17},{... | collective-permute-start | bytes 3538952 | tf_op jit(solution)/shard_map/ppermute | solution.py:709
  184.5 32.9 %collective-permute-start.37 = (f32[24,32,384]{2,1,0:T(8,128)S(1)}, f32[24,32,384]{2,1,0:T(8,128)S(1)}, u32[]{:S(2)}, u32[]{:S(2)}) collective-permute-start(f32[24,32,384]{2,1,0:T(8,128)S(1)} %get-tuple-element.275.refs_3_.refs_1_), channel_id=1, source_target_pairs={{0,8},{8,16},{16,24},{12,4},{20,12},{28,20},{1,9},{9,17},{17,25},{... | collective-permute-start | bytes 3538952 | tf_op jit(solution)/shard_map/ppermute | solution.py:705
  191.6 10.4 %collective-permute-start.40 = (f32[4,32,384]{2,1,0:T(8,128)S(1)}, f32[4,32,384]{2,1,0:T(8,128)S(1)}, u32[]{:S(2)}, u32[]{:S(2)}) collective-permute-start(f32[4,32,384]{2,1,0:T(8,128)S(1)} %get-tuple-element.284.refs_0_.first_ref), channel_id=1, source_target_pairs={{1,0},{2,1},{3,2},{5,4},{6,5},{7,6},{9,8},{10,9},{11,10},{13,12},{... | collective-permute-start | bytes 589832 | tf_op jit(solution)/shard_map/ppermute | solution.py:701
  192.9 9.1 %collective-permute-start.39 = (f32[4,32,384]{2,1,0:T(8,128)S(1)}, f32[4,32,384]{2,1,0:T(8,128)S(1)}, u32[]{:S(2)}, u32[]{:S(2)}) collective-permute-start(f32[4,32,384]{2,1,0:T(8,128)S(1)} %get-tuple-element.287.refs_3_.last_ref), channel_id=1, source_target_pairs={{0,1},{1,2},{2,3},{4,5},{5,6},{6,7},{8,9},{9,10},{10,11},{12,13},{... | collective-permute-start | bytes 589832 | tf_op jit(solution)/shard_map/ppermute | solution.py:698
  196.2 5.8 %collective-permute-start.41 = (f32[4,24,384]{2,1,0:T(8,128)S(1)}, f32[4,24,384]{2,1,0:T(8,128)S(1)}, u32[]{:S(2)}, u32[]{:S(2)}) collective-permute-start(f32[4,24,384]{2,1,0:T(8,128)S(1)} %get-tuple-element.288.refs_4_), channel_id=1, source_target_pairs={{0,4},{4,0},{8,12},{12,8},{16,20},{20,16},{24,28},{28,24},{1,5},{5... | collective-permute-start | bytes 442376 | tf_op jit(solution)/shard_map/ppermute | solution.py:695
  202.7 1.2 collective-permute-start.42
  204.0 3.6 %collective-permute-start.43 = (f32[8,128]{1,0:T(8,128)S(1)}, f32[8,128]{1,0:T(8,128)S(1)}, u32[]{:S(2)}, u32[]{:S(2)}) collective-permute-start(f32[8,128]{1,0:T(8,128)S(1)} %max.75), channel_id=1, source_target_pairs={{0,2},{1,3},{2,0},{3,1},{4,6},{5,7},{6,4},{7,5},{8,10},{9,11},{10,... | collective-permute-start | bytes 12296 | tf_op jit(solution)/shard_map/ppermute | solution.py:719
  207.6 3.6 %collective-permute-start.44 = (f32[8,128]{1,0:T(8,128)S(1)}, f32[8,128]{1,0:T(8,128)S(1)}, u32[]{:S(2)}, u32[]{:S(2)}) collective-permute-start(f32[8,128]{1,0:T(8,128)S(1)} %max.76), channel_id=1, source_target_pairs={{0,4},{4,0},{8,12},{12,8},{16,20},{20,16},{24,28},{28,24},{1,5},{5... | collective-permute-start | bytes 12296 | tf_op jit(solution)/shard_map/ppermute | solution.py:719
  211.2 3.6 %collective-permute-start.45 = (f32[8,128]{1,0:T(8,128)S(1)}, f32[8,128]{1,0:T(8,128)S(1)}, u32[]{:S(2)}, u32[]{:S(2)}) collective-permute-start(f32[8,128]{1,0:T(8,128)S(1)} %max.77), channel_id=1, source_target_pairs={{0,8},{4,12},{8,0},{12,4},{16,24},{20,28},{24,16},{28,20},{1,9},{5... | collective-permute-start | bytes 12296 | tf_op jit(solution)/shard_map/ppermute | solution.py:719
  214.8 4.5 %collective-permute-start.46 = (f32[8,128]{1,0:T(8,128)S(1)}, f32[8,128]{1,0:T(8,128)S(1)}, u32[]{:S(2)}, u32[]{:S(2)}) collective-permute-start(f32[8,128]{1,0:T(8,128)S(1)} %max.78), channel_id=1, source_target_pairs={{0,16},{4,20},{8,24},{12,28},{16,0},{20,4},{24,8},{28,12},{1,17},{... | collective-permute-start | bytes 12296 | tf_op jit(solution)/shard_map/ppermute | solution.py:719
  221.3 29.2 %collective-permute-start.49 = (f32[24,32,384]{2,1,0:T(8,128)}, f32[24,32,384]{2,1,0:T(8,128)}, u32[]{:S(2)}, u32[]{:S(2)}) collective-permute-start(f32[24,32,384]{2,1,0:T(8,128)} %get-tuple-element.309), channel_id=1, source_target_pairs={{0,4},{4,0},{8,12},{12,8},{16,20},{20,16},{24,28},{28,24},{1,5},{5... | collective-permute-start | bytes 3538952 | tf_op jit(solution)/shard_map/ppermute | solution.py:695
  225.7 1.0 copy-start.4
  226.7 1.0 copy-start.6
  227.7 44.8 %collective-permute-start.47 = (f32[24,32,384]{2,1,0:T(8,128)}, f32[24,32,384]{2,1,0:T(8,128)S(1)}, u32[]{:S(2)}, u32[]{:S(2)}) collective-permute-start(f32[24,32,384]{2,1,0:T(8,128)} %get-tuple-element.305), channel_id=1, source_target_pairs={{0,4},{4,0},{8,12},{12,8},{16,20},{20,16},{24,28},{28,24},{1,5},{5... | collective-permute-start | bytes 3538952 | tf_op jit(solution)/shard_map/ppermute | solution.py:695
  235.0 37.5 %collective-permute-start.48 = (f32[2,384]{1,0:T(2,128)S(1)}, f32[2,384]{1,0:T(2,128)S(1)}, u32[]{:S(2)}, u32[]{:S(2)}) collective-permute-start(f32[2,384]{1,0:T(2,128)S(1)} %slice.40), channel_id=1, source_target_pairs={{0,4},{4,0},{8,12},{12,8},{16,20},{20,16},{24,28},{28,24},{1,5},{5... | collective-permute-start | bytes 9224 | tf_op jit(solution)/shard_map/ppermute | solution.py:695
  236.0 1.3 copy-start.5
  237.3 1.3 copy-start.7

commit v6 on v5

--- a/solution.py
+++ b/solution.py
@@ -301,12 +301,14 @@
         planner = scale * (PLANNER_SPEED / (2.0 * known.step_1))
         to_1 = scale / (2.0 * known.step_1)
 
-        @pl.loop(0, cells_v)
-        def _(j):
-            flow = table_ref[4, j] * to_1
-            up, down = wide(flow + planner), wide(flow - planner)
-            for g in range(groups):
+        together = 2 if cells_v % 2 == 0 else 1
+
+        @pl.loop(0, cells_v, step=together)
+        def _(start):
+            for j, g in [(start + ahead, g) for ahead in range(together) for g in range(groups)]:
                 here = pl.ds(8 * g, 8)
+                flow = table_ref[4, j] * to_1
+                up, down = wide(flow + planner), wide(flow - planner)
                 for i in range(2):
                     w = row_refs[3 * i][j, here, :]
                     inside = row_refs[1 + i][j, here, :]
@@ -463,14 +465,14 @@
 
         if not with_edges:
             least_ref = outs[count]
+            least = [functools.reduce(jnp.minimum, tile(i, 0, 0) + tile(i, cells_v - 1, 1)) for i in range(count)]
+
+            def lower(j, least):
+                return tuple(jnp.minimum(least[i], functools.reduce(jnp.minimum, tile(i, j))) for i in range(count))
+
+            least = lax.fori_loop(1, cells_v - 1, lower, tuple(least))
             for i in range(count):
-
-                def step(j, least, i=i):
-                    return functools.reduce(jnp.minimum, tile(i, j), least)
-
-                least = functools.reduce(jnp.minimum, tile(i, 0, 0) + tile(i, cells_v - 1, 1))
-                least = lax.fori_loop(1, cells_v - 1, step, least)
-                least_ref[pl.ds(i, 1), :] = jnp.min(least, axis=0, keepdims=True)
+                least_ref[pl.ds(i, 1), :] = jnp.min(least[i], axis=0, keepdims=True)
             return
 
         first_ref, second_ref, before_ref, last_ref, edge_ref, inner_ref, part_ref = outs[count : count + 7]
@@ -483,43 +485,43 @@
             for ref, at in zip((first_ref, second_ref, before_ref, last_ref, edge_ref, inner_ref), prior_at):
                 ref[slot] = ins[at][position]
 
-        def one(i, j, most_3, end=None):
+        def one(i, j, end=None):
             slot = every.index(targets[i])
             out = tile(i, j, end)
             edge_ref[slot, pl.ds(j, 1), :] = fields_out[i][j, pl.ds(send_at, 1), :]
             inner_ref[slot, pl.ds(j, 1), :] = fields_out[i][j, pl.ds(inner_at, 1), :]
             wall = jnp.abs(fields_out[i][j, pl.ds(next_at, 1), :] - fields_out[i][j, pl.ds(wall_at, 1), :])
-            most_3 = jnp.maximum(most_3, wall)
             rolled = [pltpu.roll(y, 2, 0) for y in out]
+            slopes_3 = [jnp.broadcast_to(wall, (8, width))]
             for g in range(groups):
                 apart = jnp.where(sublane < 2, rolled[g - 1] if g > 0 else out[0], rolled[g])
-                most_3 = jnp.maximum(most_3, jnp.abs(out[g] - apart))
-            return out, most_3
-
-        most_2 = jnp.zeros((8, width), jnp.float32)
-        most_3 = most_2
+                slopes_3.append(jnp.abs(out[g] - apart))
+            return out, functools.reduce(jnp.maximum, slopes_3)
+
+        def both(i, j, end=None):
+            out, most_3 = one(i, j, end)
+            slopes_2 = [jnp.abs(out[g] - fields_out[i][j - 2, pl.ds(8 * g, 8), :]) for g in range(groups)]
+            return functools.reduce(jnp.maximum, slopes_2), most_3
+
+        starts = [jnp.maximum(one(i, 0, 0)[1], one(i, 1)[1]) for i in range(count)]
+        zero = jnp.zeros((8, width), jnp.float32)
+
+        def step(j, carry):
+            found = [both(i, j) for i in range(count)]
+            return tuple((jnp.maximum(carry[i][0], found[i][0]), jnp.maximum(carry[i][1], found[i][1])) for i in range(count))
+
+        most = lax.fori_loop(2, cells_v - 1, step, tuple((zero, start) for start in starts))
+        most = list(most) + [both(i, cells_v - 1, 1) for i in range(count)]
         if prior is not None:
-            most_2, most_3 = ins[prior_at[6]][0], ins[prior_at[6]][1]
+            most.append((ins[prior_at[6]][0], ins[prior_at[6]][1]))
+        part_ref[0] = functools.reduce(jnp.maximum, [m[0] for m in most])
+        part_ref[1] = functools.reduce(jnp.maximum, [m[1] for m in most])
         for i in range(count):
-            _, most_3 = one(i, 0, most_3, 0)
-            _, most_3 = one(i, 1, most_3)
-
-            def step(j, carry, i=i, end=None):
-                most_2, most_3 = carry
-                out, most_3 = one(i, j, most_3, end)
-                for g in range(groups):
-                    most_2 = jnp.maximum(most_2, jnp.abs(out[g] - fields_out[i][j - 2, pl.ds(8 * g, 8), :]))
-                return most_2, most_3
-
-            most_2, most_3 = lax.fori_loop(2, cells_v - 1, step, (most_2, most_3))
-            most_2, most_3 = step(cells_v - 1, (most_2, most_3), end=1)
             slot = every.index(targets[i])
             first_ref[slot] = fields_out[i][0]
             second_ref[slot] = fields_out[i][1]
             before_ref[slot] = fields_out[i][cells_v - 2]
             last_ref[slot] = fields_out[i][cells_v - 1]
-        part_ref[0] = most_2
-        part_ref[1] = most_3
 
     n = len(every)
     shapes = [f32(cells_v, half, width)] * count
@@ -769,7 +771,7 @@
 
     every = (0, 1, 2, 3)
 
-    def advanced(targets, field, bases, halos, stepper):
+    def advanced(targets, field, bases, halos, stepper, table=table):
         got = advance(sizes, targets, field, bases, halos, shared_first, stepper, accel_second, table)
         each = len(got) // len(targets)
         return {t: got[each * i : each * (i + 1)] for i, t in enumerate(targets)}
@@ -777,20 +779,33 @@
     def settled(targets, updates, **kw):
         return settle(sizes, targets, [updates[t] for t in targets], [costs[t] for t in targets], flags, **kw)
 
-    def next_updates(field, edges, bases, stepper, halo_rows):
+    def next_updates(field, edges, bases, stepper, halo_rows, outer_later=False):
         first, _, _, last, edge, _, _ = edges
         low, high, row = from_low_vx(last), from_high_vx(first), partner(edge)
-        def ahead(targets):
-            return advanced(targets, field, None if bases is None else [bases[t] for t in targets], None, stepper)
+        heun = bases is not None
+
+        def ahead(targets, table=table):
+            return advanced(targets, field, [bases[t] for t in targets] if heun else None, None, stepper, table)
+
+        def terms(table=table):
+            return outer_terms(sizes, field, halo_rows, shared_first, stepper, heun, table)
 
         updates = ahead((1, 2))
         low, high, row = lax.optimization_barrier((low, high, row, updates))[:3]
-        heun = bases is not None
         mended = mend(sizes, edges, low, high, row, shared_first, stepper, heun, accel_second, table)
+        maxima = edge_maxima(edges, low, high, row, flags)
+        if outer_later:
+
+            def outer_updates(settled):
+                late_table = after(table, settled)
+                got, outer = ahead((0, 3), late_table), terms(late_table)
+                return {0: got[0] + outer[:1], 3: got[3] + outer[1:]}
+
+            return updates, outer_updates, mended, share(maxima, {1: mended})
         updates.update(ahead((0,)))
         updates.update(ahead((3,)))
-        outer = outer_terms(sizes, field, halo_rows, shared_first, stepper, heun, table)
-        maxima = share(edge_maxima(edges, low, high, row, flags), {1: mended, 2: updates[0], 3: updates[3], 4: outer})
+        outer = terms()
+        maxima = share(maxima, {1: mended, 2: updates[0], 3: updates[3], 4: outer})
         return {**updates, 0: updates[0] + outer[:1], 3: updates[3] + outer[1:]}, mended, maxima
 
     def settled_all(updates, **kw):
@@ -818,10 +833,11 @@
     updates, mended, shared_second = next_updates(chain, edges, None, None, halo_rows)
     middle, edges, halo_rows = settled_all(updates, mended=mended, damping=(shared_first, shared_second, shared_second, 1.0), fields=chain)
 
-    updates, mended, shared = next_updates(middle, edges, chain, shared_second, halo_rows)
+    updates, outer_updates, mended, shared = next_updates(middle, edges, chain, shared_second, halo_rows, outer_later=True)
     damping = (shared_first, shared_second, shared, 0.5)
     (near,), (least_near,) = settled((2,), updates, damping=damping, mended=mended, with_edges=False)
     inner_got = partner(near)
+    updates.update(outer_updates(near))
     (outer, inner, far), (least,) = settled((0, 1, 3), updates, damping=damping, mended=mended, with_edges=False)
     outer_got = partner(far)
     least = lax.pmin(jnp.concatenate([least[:2], least_near, least[2:]], axis=0), "vx")

time: 276 us -> 274 us (level)
    ppermute x13, waiting for transfers between devices: 46 us -> 39.4 us  [partner(): return lax.ppermute(x, 'px', [(i, i ^ 1) for i in range(n_px)])]
    ppermute x19, waiting for transfers between devices: 39.5 us -> 45.9 us  [share(): lax.ppermute(maxima, axis, [(i, i ^ apart) for i in range(lax.axis_size(a...]
    pallas_call x11 -> x10, Pallas kernels: 38.2 us -> 37.5 us  [advance(): pl.pallas_call(body, out_shape=[f32(cells_v, half, width)] * n_out, in_sp...]
  transfers between devices with their start and end apart: 50 -> 50, of which waited for: 25 -> 25; matrix products, arithmetic and copies ran while one was open for 4% -> 4% of each run, Pallas kernels for 24% -> 25%
where the time goes in v6:
time: 274 us; the launch traced here: 273 us
  waiting for transfers between devices  89.5 us (33%)
  starting transfers between devices  79.8 us (29%)
  Pallas kernels  73.9 us (27%)
  local copies, waits for them, and re-layouts  21.8 us (8%)
  blocking collectives  6.15 us (2%)
    ppermute x19, waiting for transfers between devices, share(): lax.ppermute(maxima, axis, [(i, i ^ apart) for i in range(lax.axis_size(a...  45.9 us
    ppermute x13, waiting for transfers between devices, partner(): return lax.ppermute(x, 'px', [(i, i ^ 1) for i in range(n_px)])  39.4 us
    pallas_call x10, Pallas kernels, advance(): pl.pallas_call(body, out_shape=[f32(cells_v, half, width)] * n_out, in_sp...  37.5 us
    ppermute x19, starting transfers between devices, share(): lax.ppermute(maxima, axis, [(i, i ^ apart) for i in range(lax.axis_size(a...  21.5 us
    pallas_call x9, Pallas kernels, settle(): pl.pallas_call(body, out_shape=shapes, in_specs=[scalars()] + [whole()] *...  18.3 us
    ppermute x4, starting transfers between devices, halo_before(): return lax.ppermute(outermost, 'px', moves)  17.4 us
    ppermute x13, starting transfers between devices, partner(): return lax.ppermute(x, 'px', [(i, i ^ 1) for i in range(n_px)])  17.4 us
    ppermute x5, starting transfers between devices, from_low_vx(): return lax.ppermute(x, 'vx', [(i, i + 1) for i in range(n_vx - 1)])  11.7 us
  transfers between devices with their start and end apart: 50, of which 25 were waited for; matrix products, arithmetic and copies ran while one was open for 4% of the time, Pallas kernels for 25%

profile of v6, /device:TPU:0, one launch (start us, length us, event | category | flops | bytes accessed | tf_op | source)
XLA Modules:
  0.0 272.9 jit_solution(9854210045374633327)
XLA Ops:
  0.7 2.4 dynamic-slice_bitcast_fusion.4
  3.0 2.9 %collective-permute-start.6 = (f32[24,32,384]{2,1,0:T(8,128)}, f32[24,32,384]{2,1,0:T(8,128)S(1)}, u32[]{:S(2)}, u32[]{:S(2)}) collective-permute-start(f32[24,32,384]{2,1,0:T(8,128)} %dynamic-slice_bitcast_fusion.4), channel_id=1, source_target_pairs={{0,4},{4,0},{8,12},{12,8},{16,20},{20,16},{24,28},{28,24},{1,5},{5... | collective-permute-start | bytes 3538952 | tf_op jit(solution)/shard_map/ppermute | solution.py:697
  7.2 2.1 collective-permute-start.4
  14.2 3.3 %dynamic-slice_bitcast_fusion.2 = (f32[24,32,384]{2,1,0:T(8,128)}, f32[24,32,384]{2,1,0:T(8,128)}) fusion(f32[2,24,64,384]{3,2,1,0:T(8,128)} %refs_4_.2, s32[]{:T(128)S(6)} %select_n.88, s32[]{:T(128)S(6)} %select_n.89, s32[]{:T(128)S(6)} %select_n.85, s32[]{:T(128)S(6)} %select_n.86), kind=kLoop, calls=%fused_computation.2 | loop fusion | bytes 4718608 | tf_op jit(solution)/shard_map/squeeze | solution.py:728
  18.9 2.2 first_maxima.1
  21.1 3.8 %collective-permute-start.3 = (f32[8,128]{1,0:T(8,128)S(1)}, f32[8,128]{1,0:T(8,128)S(1)}, u32[]{:S(2)}, u32[]{:S(2)}) collective-permute-start(f32[8,128]{1,0:T(8,128)S(1)} %first_maxima.1), channel_id=1, source_target_pairs={{0,4},{4,0},{8,12},{12,8},{16,20},{20,16},{24,28},{28,24},{1,5},{5... | collective-permute-start | bytes 12296 | tf_op jit(solution)/shard_map/ppermute | solution.py:697
  24.9 9.0 %collective-permute-done.3 = f32[8,128]{1,0:T(8,128)S(1)} collective-permute-done((f32[8,128]{1,0:T(8,128)S(1)}, f32[8,128]{1,0:T(8,128)S(1)}, u32[]{:S(2)}, u32[]{:S(2)}) %collective-permute-start.3) | collective-permute-done | bytes 4128 | tf_op jit(solution)/shard_map/ppermute | solution.py:697
  33.9 1.8 collective-permute-start.5
  35.7 3.2 %dynamic-slice_bitcast_fusion = (f32[24,32,384]{2,1,0:T(8,128)}, f32[24,32,384]{2,1,0:T(8,128)}) fusion(f32[2,24,64,384]{3,2,1,0:T(8,128)} %refs_11_.1, s32[]{:T(128)S(6)} %select_n.88, s32[]{:T(128)S(6)} %select_n.86, s32[]{:T(128)S(6)} %select_n.85), kind=kLoop, calls=%fused_computation | loop fusion | bytes 4718604 | tf_op jit(solution)/shard_map/squeeze | solution.py:728
  40.2 1.5 collective-permute-start.12
  41.7 3.5 %collective-permute-start.7 = (f32[24,32,384]{2,1,0:T(8,128)S(1)}, f32[24,32,384]{2,1,0:T(8,128)S(1)}, u32[]{:S(2)}, u32[]{:S(2)}) collective-permute-start(f32[24,32,384]{2,1,0:T(8,128)S(1)} %collective-permute-done.6.refs_2_), channel_id=1, source_target_pairs={{0,8},{8,16},{16,24},{12,4},{20,12},{28,20},{1,9},{9,17},{17,25},{... | collective-permute-start | bytes 3538952 | tf_op jit(solution)/shard_map/ppermute | solution.py:707
  45.3 1.6 collective-permute-start.13
  46.9 23.6 %collective-permute-done.13 = f32[8,128]{1,0:T(8,128)S(1)} collective-permute-done((f32[8,128]{1,0:T(8,128)S(1)}, f32[8,128]{1,0:T(8,128)S(1)}, u32[]{:S(2)}, u32[]{:S(2)}) %collective-permute-start.13) | collective-permute-done | bytes 4128 | tf_op jit(solution)/shard_map/ppermute | solution.py:721
  70.5 2.6 collective-permute-start.14
  73.1 1.9 collective-permute-done.14
  75.0 1.8 collective-permute-start.15
  80.5 3.3 %collective-permute-done.10 = f32[2,32,384]{2,1,0:T(8,128)S(1)} collective-permute-done((f32[2,32,384]{2,1,0:T(8,128)S(1)}, f32[2,32,384]{2,1,0:T(8,128)S(1)}, u32[]{:S(2)}, u32[]{:S(2)}) %collective-permute-start.10) | collective-permute-done | bytes 98336 | tf_op jit(solution)/shard_map/ppermute | solution.py:703
  83.8 2.3 copy-done.1
  86.2 4.8 %advance_12.4 = (f32[24,32,384]{2,1,0:T(8,128)S(1)}, f32[24,32,384]{2,1,0:T(8,128)S(1)}) custom-call(f32[6,24]{1,0:T(8,128)S(1)} %concatenate.15.table_ref, f32[2,24,64,384]{3,2,1,0:T(8,128)S(1)} %copy-done.1, f32[24,32,384]{2,1,0:T(8,128)S(1)} %collective-permute-done.5.refs_1_.refs_5_, f32[24,32,384]{2,1,0:T(8,128)S(1)} %collective-permute-done.6.refs_2_, ...), custom_call_target="tpu_custom_call" | custom-call | tf_op jit(solution)/shard_map/advance_12/pallas_call | solution.py:270
  91.0 2.4 copy-done.2
  93.4 5.7 %advance_03.2 = (f32[24,32,384]{2,1,0:T(8,128)S(1)}, f32[24,32,384]{2,1,0:T(8,128)S(1)}) custom-call(f32[6,24]{1,0:T(8,128)S(1)} %concatenate.15.table_ref, f32[2,24,64,384]{3,2,1,0:T(8,128)S(1)} %copy-done.2, f32[24,32,384]{2,1,0:T(8,128)S(1)} %collective-permute-done.5.refs_1_.refs_5_, f32[24,32,384]{2,1,0:T(8,128)S(1)} %collective-permute-done.6.refs_2_, ...), custom_call_target="tpu_custom_call" | custom-call | tf_op jit(solution)/shard_map/advance_03/pallas_call | solution.py:270
  99.1 1.6 settle_01.1
  103.2 4.6 %collective-permute-start.17 = (f32[24,32,384]{2,1,0:T(8,128)S(1)}, f32[24,32,384]{2,1,0:T(8,128)S(1)}, u32[]{:S(2)}, u32[]{:S(2)}) collective-permute-start(f32[24,32,384]{2,1,0:T(8,128)S(1)} %get-tuple-element.187.refs_3_.refs_1_), channel_id=1, source_target_pairs={{0,8},{8,16},{16,24},{12,4},{20,12},{28,20},{1,9},{9,17},{17,25},{... | collective-permute-start | bytes 3538952 | tf_op jit(solution)/shard_map/ppermute | solution.py:707
  107.8 4.2 %collective-permute-done.15.refs_1_.refs_7_.refs_3_ = f32[24,32,384]{2,1,0:T(8,128)S(1)} collective-permute-done((f32[24,32,384]{2,1,0:T(8,128)}, f32[24,32,384]{2,1,0:T(8,128)S(1)}, u32[]{:S(2)}, u32[]{:S(2)}) %collective-permute-start.15) | collective-permute-done | bytes 1179680 | tf_op jit(solution)/shard_map/ppermute | solution.py:697
  114.4 3.0 %collective-permute-start.19 = (f32[4,32,384]{2,1,0:T(8,128)S(1)}, f32[4,32,384]{2,1,0:T(8,128)S(1)}, u32[]{:S(2)}, u32[]{:S(2)}) collective-permute-start(f32[4,32,384]{2,1,0:T(8,128)S(1)} %get-tuple-element.196.refs_3_.last_ref), channel_id=1, source_target_pairs={{0,1},{1,2},{2,3},{4,5},{5,6},{6,7},{8,9},{9,10},{10,11},{12,13},{... | collective-permute-start | bytes 589832 | tf_op jit(solution)/shard_map/ppermute | solution.py:700
  118.8 4.8 %advance_12.5 = (f32[24,32,384]{2,1,0:T(8,128)S(1)}, f32[24,32,384]{2,1,0:T(8,128)S(1)}, f32[24,32,384]{2,1,0:T(8,128)S(1)}, f32[24,32,384]{2,1,0:T(8,128)S(1)},...) custom-call(f32[6,24]{1,0:T(8,128)S(1)} %concatenate.15.table_ref, ...), custom_call_target="tpu_custom_call" | custom-call | tf_op jit(solution)/shard_map/advance_12/pallas_call | solution.py:270
  128.1 1.7 collective-permute-done.23
  131.0 2.4 advance_0.2
  133.4 1.7 collective-permute-start.25
  135.1 2.4 advance_3.2
  137.5 2.7 collective-permute-start.26
  140.2 1.5 outer_terms.3
  142.1 2.2 settle_03.2
  145.6 4.6 %collective-permute-start.27 = (f32[24,32,384]{2,1,0:T(8,128)S(1)}, f32[24,32,384]{2,1,0:T(8,128)S(1)}, u32[]{:S(2)}, u32[]{:S(2)}) collective-permute-start(f32[24,32,384]{2,1,0:T(8,128)S(1)} %get-tuple-element.230.refs_3_.refs_1_.refs_11_.refs_5_), channel_id=1, source_target_pairs={{0,8},{8,16},{16,24},{12,4},{20,12},{28,20},{1,9},{9,17},{17,25},{... | collective-permute-start | bytes 3538952 | tf_op jit(solution)/shard_map/ppermute | solution.py:707
  150.2 2.1 settle_12.2
  153.6 3.0 %collective-permute-start.29 = (f32[4,32,384]{2,1,0:T(8,128)S(1)}, f32[4,32,384]{2,1,0:T(8,128)S(1)}, u32[]{:S(2)}, u32[]{:S(2)}) collective-permute-start(f32[4,32,384]{2,1,0:T(8,128)S(1)} %get-tuple-element.239.refs_3_.last_ref), channel_id=1, source_target_pairs={{0,1},{1,2},{2,3},{4,5},{5,6},{6,7},{8,9},{9,10},{10,11},{12,13},{... | collective-permute-start | bytes 589832 | tf_op jit(solution)/shard_map/ppermute | solution.py:700
  156.8 4.5 %advance_12.6 = (f32[24,32,384]{2,1,0:T(8,128)S(1)}, f32[24,32,384]{2,1,0:T(8,128)S(1)}, f32[24,32,384]{2,1,0:T(8,128)S(1)}, f32[24,32,384]{2,1,0:T(8,128)S(1)},...) custom-call(f32[6,24]{1,0:T(8,128)S(1)} %concatenate.15.table_ref, ...), custom_call_target="tpu_custom_call" | custom-call | tf_op jit(solution)/shard_map/advance_12/pallas_call | solution.py:270
  161.2 1.8 collective-permute-done.31.refs_8_.next_ref
  166.0 2.7 collective-permute-done.33
  169.0 2.2 advance_0.3
  173.4 2.2 advance_3.3
  175.9 2.6 collective-permute-start.36
  178.5 1.5 outer_terms.4
  180.4 2.5 settle_03.3
  184.2 4.6 %collective-permute-start.45 = (f32[24,32,384]{2,1,0:T(8,128)S(1)}, f32[24,32,384]{2,1,0:T(8,128)S(1)}, u32[]{:S(2)}, u32[]{:S(2)}) collective-permute-start(f32[24,32,384]{2,1,0:T(8,128)S(1)} %get-tuple-element.270.refs_3_), channel_id=1, source_target_pairs={{0,8},{8,16},{16,24},{12,4},{20,12},{28,20},{1,9},{9,17},{17,25},{... | collective-permute-start | bytes 3538952 | tf_op jit(solution)/shard_map/ppermute | solution.py:707
  188.8 2.4 settle_12.3
  191.2 1.5 collective-permute-start.38
  192.7 3.0 %collective-permute-start.37 = (f32[4,32,384]{2,1,0:T(8,128)S(1)}, f32[4,32,384]{2,1,0:T(8,128)S(1)}, u32[]{:S(2)}, u32[]{:S(2)}) collective-permute-start(f32[4,32,384]{2,1,0:T(8,128)S(1)} %get-tuple-element.277.refs_3_.last_ref), channel_id=1, source_target_pairs={{0,1},{1,2},{2,3},{4,5},{5,6},{6,7},{8,9},{9,10},{10,11},{12,13},{... | collective-permute-start | bytes 589832 | tf_op jit(solution)/shard_map/ppermute | solution.py:700
  195.8 4.6 %advance_12.7 = (f32[24,32,384]{2,1,0:T(8,128)S(1)}, f32[24,32,384]{2,1,0:T(8,128)S(1)}, f32[24,32,384]{2,1,0:T(8,128)S(1)}, f32[24,32,384]{2,1,0:T(8,128)S(1)},...) custom-call(f32[6,24]{1,0:T(8,128)S(1)} %concatenate.15.table_ref, ...), custom_call_target="tpu_custom_call" | custom-call | tf_op jit(solution)/shard_map/advance_12/pallas_call | solution.py:270
  204.5 2.7 collective-permute-done.41
  208.1 2.7 collective-permute-done.42
  211.9 2.5 collective-permute-done.43
  214.4 2.6 collective-permute-start.44
  217.0 1.9 collective-permute-done.44
  218.9 2.1 settle_2.3
  221.9 4.0 %advance_03.3 = (f32[24,32,384]{2,1,0:T(8,128)S(1)}, f32[24,32,384]{2,1,0:T(8,128)S(1)}, f32[24,32,384]{2,1,0:T(8,128)S(1)}, f32[24,32,384]{2,1,0:T(8,128)S(1)},...) custom-call(f32[6,24]{1,0:T(8,128)S(1)} %concatenate.15.table_ref, ...), custom_call_target="tpu_custom_call" | custom-call | tf_op jit(solution)/shard_map/advance_03/pallas_call | solution.py:270
  225.9 1.5 outer_terms.5
  227.4 3.2 %settle_013.1 = (f32[24,32,384]{2,1,0:T(8,128)S(1)}, f32[24,32,384]{2,1,0:T(8,128)S(1)}, f32[24,32,384]{2,1,0:T(8,128)}, f32[3,384]{1,0:T(4,128)S(1)}) custom-call(s32[5]{0:T(128)S(1)} %stack.45.flags_ref, f32[24,32,384]{2,1,0:T(8,128)S(1)} %get-tuple-element.294.refs_0_, f32[24,32,384]{2,1,0:T(8,128)S(1)} %get-tuple-element.295.refs_1_, ...), custom_call_target="tpu_custom_call" | custom-call | tf_op jit(solution)/shard_map/settle_013/pallas_call | solution.py:532
  233.8 6.2 %pmin.7.least_ref = f32[4,384]{1,0:T(4,128)S(1)} all-reduce(f32[4,384]{1,0:T(4,128)S(1)} %pad_maximum_fusion.5), channel_id=1, replica_groups=mesh['px'=8,'vx'=4] {'vx'}, use_global_device_ids=true, to_apply=%region_0.1 | all-reduce | flops 1536 | bytes 12288 | tf_op jit(solution)/shard_map/pmin | solution.py:843
  243.5 2.0 place.2.refs_1_
  245.4 4.8 %collective-permute-done.49.refs_0_ = f32[24,32,384]{2,1,0:T(8,128)} collective-permute-done((f32[24,32,384]{2,1,0:T(8,128)}, f32[24,32,384]{2,1,0:T(8,128)}, u32[]{:S(2)}, u32[]{:S(2)}) %collective-permute-start.49) | collective-permute-done | bytes 1179680 | tf_op jit(solution)/shard_map/ppermute | solution.py:697
  250.2 2.3 place.3._
  252.5 18.1 %collective-permute-done.48.got_ref = f32[2,384]{1,0:T(2,128)S(1)} collective-permute-done((f32[2,384]{1,0:T(2,128)S(1)}, f32[2,384]{1,0:T(2,128)S(1)}, u32[]{:S(2)}, u32[]{:S(2)}) %collective-permute-start.48) | collective-permute-done | bytes 3104 | tf_op jit(solution)/shard_map/ppermute | solution.py:697
  270.6 2.1 finish.1
  (146 shorter events, 48.4 us)
Async XLA Ops:
  0.7 5.3 %copy-start.8 = (f32[2,24]{1,0:T(2,128)S(1)}, f32[2,24]{1,0:T(2,128)}, u32[]{:S(2)}) copy-start(f32[2,24]{1,0:T(2,128)} %first_ref.1) | copy-start | bytes 580
  3.0 38.7 %collective-permute-start.6 = (f32[24,32,384]{2,1,0:T(8,128)}, f32[24,32,384]{2,1,0:T(8,128)S(1)}, u32[]{:S(2)}, u32[]{:S(2)}) collective-permute-start(f32[24,32,384]{2,1,0:T(8,128)} %dynamic-slice_bitcast_fusion.4), channel_id=1, source_target_pairs={{0,4},{4,0},{8,12},{12,8},{16,20},{20,16},{24,28},{28,24},{1,5},{5... | collective-permute-start | bytes 3538952 | tf_op jit(solution)/shard_map/ppermute | solution.py:697
  6.0 27.9 %collective-permute-start = (f32[2,24]{1,0:T(2,128)S(1)}, f32[2,24]{1,0:T(2,128)S(1)}, u32[]{:S(2)}, u32[]{:S(2)}) collective-permute-start(f32[2,24]{1,0:T(2,128)S(1)} %copy-done.8), channel_id=1, source_target_pairs={{0,4},{4,0},{8,12},{12,8},{16,20},{20,16},{24,28},{28,24},{1,5},{5... | collective-permute-start | bytes 584 | tf_op jit(solution)/shard_map/ppermute | solution.py:697
  7.2 26.7 %collective-permute-start.4 = (f32[2,24,384]{2,1,0:T(8,128)S(1)}, f32[2,24,384]{2,1,0:T(8,128)S(1)}, u32[]{:S(2)}, u32[]{:S(2)}) collective-permute-start(f32[2,24,384]{2,1,0:T(8,128)S(1)} %bitcast.36), channel_id=1, source_target_pairs={{0,4},{4,0},{8,12},{12,8},{16,20},{20,16},{24,28},{28,24},{1,5},{5... | collective-permute-start | bytes 221192 | tf_op jit(solution)/shard_map/ppermute | solution.py:697
  10.3 7.3 %collective-permute-start.1 = (f32[2,64,384]{2,1,0:T(8,128)S(1)}, f32[2,64,384]{2,1,0:T(8,128)S(1)}, u32[]{:S(2)}, u32[]{:S(2)}) collective-permute-start(f32[2,64,384]{2,1,0:T(8,128)S(1)} %get-tuple-element.157), channel_id=1, source_target_pairs={{0,1},{1,2},{2,3},{4,5},{5,6},{6,7},{8,9},{9,10},{10,11},{12,13},{... | collective-permute-start | bytes 589832 | tf_op jit(solution)/shard_map/ppermute | solution.py:700
  11.6 7.3 %collective-permute-start.2 = (f32[2,64,384]{2,1,0:T(8,128)S(1)}, f32[2,64,384]{2,1,0:T(8,128)S(1)}, u32[]{:S(2)}, u32[]{:S(2)}) collective-permute-start(f32[2,64,384]{2,1,0:T(8,128)S(1)} %get-tuple-element.158), channel_id=1, source_target_pairs={{1,0},{2,1},{3,2},{5,4},{6,5},{7,6},{9,8},{10,9},{11,10},{13,12},{... | collective-permute-start | bytes 589832 | tf_op jit(solution)/shard_map/ppermute | solution.py:703
  13.0 5.8 %copy-start.3 = (f32[64,384]{1,0:T(8,128)S(1)}, f32[64,384]{1,0:T(8,128)}, u32[]{:S(2)}) copy-start(f32[64,384]{1,0:T(8,128)} %refs_6_.9) | copy-start | bytes 294916
  14.2 4.7 %copy-start = (f32[2,24,64,384]{3,2,1,0:T(8,128)S(1)}, f32[2,24,64,384]{3,2,1,0:T(8,128)}, u32[]{:S(2)}) copy-start(f32[2,24,64,384]{3,2,1,0:T(8,128)} %refs_4_.2) | copy-start | bytes 14155780
  17.6 73.4 %collective-permute-start.8 = (f32[24,32,384]{2,1,0:T(8,128)}, f32[24,32,384]{2,1,0:T(8,128)}, u32[]{:S(2)}, u32[]{:S(2)}) collective-permute-start(f32[24,32,384]{2,1,0:T(8,128)} %get-tuple-element.312), channel_id=1, source_target_pairs={{8,0},{16,8},{24,16},{4,12},{12,20},{20,28},{9,1},{17,9},{25,17},{... | collective-permute-start | bytes 3538952 | tf_op jit(solution)/shard_map/ppermute | solution.py:711
  21.1 12.8 %collective-permute-start.3 = (f32[8,128]{1,0:T(8,128)S(1)}, f32[8,128]{1,0:T(8,128)S(1)}, u32[]{:S(2)}, u32[]{:S(2)}) collective-permute-start(f32[8,128]{1,0:T(8,128)S(1)} %first_maxima.1), channel_id=1, source_target_pairs={{0,4},{4,0},{8,12},{12,8},{16,20},{20,16},{24,28},{28,24},{1,5},{5... | collective-permute-start | bytes 12296 | tf_op jit(solution)/shard_map/ppermute | solution.py:697
  33.9 43.0 %collective-permute-start.5 = (f32[24,32,384]{2,1,0:T(8,128)}, f32[24,32,384]{2,1,0:T(8,128)S(1)}, u32[]{:S(2)}, u32[]{:S(2)}) collective-permute-start(f32[24,32,384]{2,1,0:T(8,128)} %get-tuple-element.160), channel_id=1, source_target_pairs={{0,4},{4,0},{8,12},{12,8},{16,20},{20,16},{24,28},{28,24},{1,5},{5... | collective-permute-start | bytes 3538952 | tf_op jit(solution)/shard_map/ppermute | solution.py:697
  38.9 1.2 collective-permute-start.11
  39.0 63.0 %collective-permute-start.16 = (f32[24,32,384]{2,1,0:T(8,128)}, f32[24,32,384]{2,1,0:T(8,128)S(1)}, u32[]{:S(2)}, u32[]{:S(2)}) collective-permute-start(f32[24,32,384]{2,1,0:T(8,128)} %get-tuple-element.171), channel_id=1, source_target_pairs={{0,4},{4,0},{8,12},{12,8},{16,20},{20,16},{24,28},{28,24},{1,5},{5... | collective-permute-start | bytes 3538952 | tf_op jit(solution)/shard_map/ppermute | solution.py:697
  40.2 5.1 %collective-permute-start.12 = (f32[8,128]{1,0:T(8,128)S(1)}, f32[8,128]{1,0:T(8,128)S(1)}, u32[]{:S(2)}, u32[]{:S(2)}) collective-permute-start(f32[8,128]{1,0:T(8,128)S(1)} %max.61), channel_id=1, source_target_pairs={{0,2},{1,3},{2,0},{3,1},{4,6},{5,7},{6,4},{7,5},{8,10},{9,11},{10,... | collective-permute-start | bytes 12296 | tf_op jit(solution)/shard_map/ppermute | solution.py:721
  41.7 49.3 %collective-permute-start.7 = (f32[24,32,384]{2,1,0:T(8,128)S(1)}, f32[24,32,384]{2,1,0:T(8,128)S(1)}, u32[]{:S(2)}, u32[]{:S(2)}) collective-permute-start(f32[24,32,384]{2,1,0:T(8,128)S(1)} %collective-permute-done.6.refs_2_), channel_id=1, source_target_pairs={{0,8},{8,16},{16,24},{12,4},{20,12},{28,20},{1,9},{9,17},{17,25},{... | collective-permute-start | bytes 3538952 | tf_op jit(solution)/shard_map/ppermute | solution.py:707
  45.3 25.2 %collective-permute-start.13 = (f32[8,128]{1,0:T(8,128)S(1)}, f32[8,128]{1,0:T(8,128)S(1)}, u32[]{:S(2)}, u32[]{:S(2)}) collective-permute-start(f32[8,128]{1,0:T(8,128)S(1)} %max.62), channel_id=1, source_target_pairs={{0,8},{4,12},{8,0},{12,4},{16,24},{20,28},{24,16},{28,20},{1,9},{5... | collective-permute-start | bytes 12296 | tf_op jit(solution)/shard_map/ppermute | solution.py:721
  70.5 4.5 %collective-permute-start.14 = (f32[8,128]{1,0:T(8,128)S(1)}, f32[8,128]{1,0:T(8,128)S(1)}, u32[]{:S(2)}, u32[]{:S(2)}) collective-permute-start(f32[8,128]{1,0:T(8,128)S(1)} %max.63), channel_id=1, source_target_pairs={{0,16},{4,20},{8,24},{12,28},{16,0},{20,4},{24,8},{28,12},{1,17},{... | collective-permute-start | bytes 12296 | tf_op jit(solution)/shard_map/ppermute | solution.py:721
  75.0 36.9 %collective-permute-start.15 = (f32[24,32,384]{2,1,0:T(8,128)}, f32[24,32,384]{2,1,0:T(8,128)S(1)}, u32[]{:S(2)}, u32[]{:S(2)}) collective-permute-start(f32[24,32,384]{2,1,0:T(8,128)} %get-tuple-element.169), channel_id=1, source_target_pairs={{0,4},{4,0},{8,12},{12,8},{16,20},{20,16},{24,28},{28,24},{1,5},{5... | collective-permute-start | bytes 3538952 | tf_op jit(solution)/shard_map/ppermute | solution.py:697
  76.9 2.2 collective-permute-start.9
  79.2 4.6 %collective-permute-start.10 = (f32[2,32,384]{2,1,0:T(8,128)S(1)}, f32[2,32,384]{2,1,0:T(8,128)S(1)}, u32[]{:S(2)}, u32[]{:S(2)}) collective-permute-start(f32[2,32,384]{2,1,0:T(8,128)S(1)} %pad_maximum_fusion.4), channel_id=1, source_target_pairs={{1,0},{2,1},{3,2},{5,4},{6,5},{7,6},{9,8},{10,9},{11,10},{13,12},{... | collective-permute-start | bytes 294920 | tf_op jit(solution)/shard_map/ppermute | solution.py:703
  83.8 2.3 copy-start.1
  86.1 13.0 %slice-start = ((s8[4718592]{0:T(1024)(128)(4,1)}), s8[4194304]{0:T(1024)(128)(4,1)S(1)}, s32[]{:S(2)}) async-start(s8[4718592]{0:T(1024)(128)(4,1)} %bitcast.32), calls=%async_computation | async-start | bytes 8388608
  90.9 8.2 %slice-start.1 = ((s8[4718592]{0:T(1024)(128)(4,1)}), s8[524288]{0:T(1024)(128)(4,1)S(1)}, s32[]{:S(2)}) async-start(s8[4718592]{0:T(1024)(128)(4,1)} %bitcast.32), calls=%async_computation.1 | async-start | bytes 1048576
  91.0 2.4 copy-start.2
  93.4 25.5 %slice-start.2 = ((s8[4718592]{0:T(1024)(128)(4,1)}), s8[4194304]{0:T(1024)(128)(4,1)S(1)}, s32[]{:S(2)}) async-start(s8[4718592]{0:T(1024)(128)(4,1)} %bitcast.34), calls=%async_computation.2 | async-start | bytes 8388608
  99.1 19.7 %slice-start.3 = ((s8[4718592]{0:T(1024)(128)(4,1)}), s8[524288]{0:T(1024)(128)(4,1)S(1)}, s32[]{:S(2)}) async-start(s8[4718592]{0:T(1024)(128)(4,1)} %bitcast.34), calls=%async_computation.3 | async-start | bytes 1048576
  100.7 39.5 %collective-permute-start.18 = (f32[24,32,384]{2,1,0:T(8,128)S(1)}, f32[24,32,384]{2,1,0:T(8,128)S(1)}, u32[]{:S(2)}, u32[]{:S(2)}) collective-permute-start(f32[24,32,384]{2,1,0:T(8,128)S(1)} %get-tuple-element.163.refs_0_), channel_id=1, source_target_pairs={{8,0},{16,8},{24,16},{4,12},{12,20},{20,28},{9,1},{17,9},{25,17},{... | collective-permute-start | bytes 3538952 | tf_op jit(solution)/shard_map/ppermute | solution.py:711
  103.2 37.0 %collective-permute-start.17 = (f32[24,32,384]{2,1,0:T(8,128)S(1)}, f32[24,32,384]{2,1,0:T(8,128)S(1)}, u32[]{:S(2)}, u32[]{:S(2)}) collective-permute-start(f32[24,32,384]{2,1,0:T(8,128)S(1)} %get-tuple-element.187.refs_3_.refs_1_), channel_id=1, source_target_pairs={{0,8},{8,16},{16,24},{12,4},{20,12},{28,20},{1,9},{9,17},{17,25},{... | collective-permute-start | bytes 3538952 | tf_op jit(solution)/shard_map/ppermute | solution.py:707
  113.1 11.0 %collective-permute-start.20 = (f32[4,32,384]{2,1,0:T(8,128)S(1)}, f32[4,32,384]{2,1,0:T(8,128)S(1)}, u32[]{:S(2)}, u32[]{:S(2)}) collective-permute-start(f32[4,32,384]{2,1,0:T(8,128)S(1)} %get-tuple-element.193.refs_0_.first_ref), channel_id=1, source_target_pairs={{1,0},{2,1},{3,2},{5,4},{6,5},{7,6},{9,8},{10,9},{11,10},{13,12},{... | collective-permute-start | bytes 589832 | tf_op jit(solution)/shard_map/ppermute | solution.py:703
  114.4 9.8 %collective-permute-start.19 = (f32[4,32,384]{2,1,0:T(8,128)S(1)}, f32[4,32,384]{2,1,0:T(8,128)S(1)}, u32[]{:S(2)}, u32[]{:S(2)}) collective-permute-start(f32[4,32,384]{2,1,0:T(8,128)S(1)} %get-tuple-element.196.refs_3_.last_ref), channel_id=1, source_target_pairs={{0,1},{1,2},{2,3},{4,5},{5,6},{6,7},{8,9},{9,10},{10,11},{12,13},{... | collective-permute-start | bytes 589832 | tf_op jit(solution)/shard_map/ppermute | solution.py:700
  117.5 6.7 %collective-permute-start.21 = (f32[4,24,384]{2,1,0:T(8,128)S(1)}, f32[4,24,384]{2,1,0:T(8,128)S(1)}, u32[]{:S(2)}, u32[]{:S(2)}) collective-permute-start(f32[4,24,384]{2,1,0:T(8,128)S(1)} %get-tuple-element.197.refs_4_), channel_id=1, source_target_pairs={{0,4},{4,0},{8,12},{12,8},{16,20},{20,16},{24,28},{28,24},{1,5},{5... | collective-permute-start | bytes 442376 | tf_op jit(solution)/shard_map/ppermute | solution.py:697
  124.9 1.2 collective-permute-start.22
  126.2 3.6 %collective-permute-start.23 = (f32[8,128]{1,0:T(8,128)S(1)}, f32[8,128]{1,0:T(8,128)S(1)}, u32[]{:S(2)}, u32[]{:S(2)}) collective-permute-start(f32[8,128]{1,0:T(8,128)S(1)} %max.65), channel_id=1, source_target_pairs={{0,2},{1,3},{2,0},{3,1},{4,6},{5,7},{6,4},{7,5},{8,10},{9,11},{10,... | collective-permute-start | bytes 12296 | tf_op jit(solution)/shard_map/ppermute | solution.py:721
  129.8 3.6 %collective-permute-start.24 = (f32[8,128]{1,0:T(8,128)S(1)}, f32[8,128]{1,0:T(8,128)S(1)}, u32[]{:S(2)}, u32[]{:S(2)}) collective-permute-start(f32[8,128]{1,0:T(8,128)S(1)} %max.66), channel_id=1, source_target_pairs={{0,4},{4,0},{8,12},{12,8},{16,20},{20,16},{24,28},{28,24},{1,5},{5... | collective-permute-start | bytes 12296 | tf_op jit(solution)/shard_map/ppermute | solution.py:721
  133.4 4.1 %collective-permute-start.25 = (f32[8,128]{1,0:T(8,128)S(1)}, f32[8,128]{1,0:T(8,128)S(1)}, u32[]{:S(2)}, u32[]{:S(2)}) collective-permute-start(f32[8,128]{1,0:T(8,128)S(1)} %max.67), channel_id=1, source_target_pairs={{0,8},{4,12},{8,0},{12,4},{16,24},{20,28},{24,16},{28,20},{1,9},{5... | collective-permute-start | bytes 12296 | tf_op jit(solution)/shard_map/ppermute | solution.py:721
  137.5 4.6 %collective-permute-start.26 = (f32[8,128]{1,0:T(8,128)S(1)}, f32[8,128]{1,0:T(8,128)S(1)}, u32[]{:S(2)}, u32[]{:S(2)}) collective-permute-start(f32[8,128]{1,0:T(8,128)S(1)} %max.68), channel_id=1, source_target_pairs={{0,16},{4,20},{8,24},{12,28},{16,0},{20,4},{24,8},{28,12},{1,17},{... | collective-permute-start | bytes 12296 | tf_op jit(solution)/shard_map/ppermute | solution.py:721
  144.3 34.2 %collective-permute-start.28 = (f32[24,32,384]{2,1,0:T(8,128)S(1)}, f32[24,32,384]{2,1,0:T(8,128)S(1)}, u32[]{:S(2)}, u32[]{:S(2)}) collective-permute-start(f32[24,32,384]{2,1,0:T(8,128)S(1)} %get-tuple-element.217.refs_0_.refs_10_.refs_4_), channel_id=1, source_target_pairs={{8,0},{16,8},{24,16},{4,12},{12,20},{20,28},{9,1},{17,9},{25,17},{... | collective-permute-start | bytes 3538952 | tf_op jit(solution)/shard_map/ppermute | solution.py:711
  145.6 32.9 %collective-permute-start.27 = (f32[24,32,384]{2,1,0:T(8,128)S(1)}, f32[24,32,384]{2,1,0:T(8,128)S(1)}, u32[]{:S(2)}, u32[]{:S(2)}) collective-permute-start(f32[24,32,384]{2,1,0:T(8,128)S(1)} %get-tuple-element.230.refs_3_.refs_1_.refs_11_.refs_5_), channel_id=1, source_target_pairs={{0,8},{8,16},{16,24},{12,4},{20,12},{28,20},{1,9},{9,17},{17,25},{... | collective-permute-start | bytes 3538952 | tf_op jit(solution)/shard_map/ppermute | solution.py:707
  152.3 10.7 %collective-permute-start.30 = (f32[4,32,384]{2,1,0:T(8,128)S(1)}, f32[4,32,384]{2,1,0:T(8,128)S(1)}, u32[]{:S(2)}, u32[]{:S(2)}) collective-permute-start(f32[4,32,384]{2,1,0:T(8,128)S(1)} %get-tuple-element.236.refs_0_.first_ref), channel_id=1, source_target_pairs={{1,0},{2,1},{3,2},{5,4},{6,5},{7,6},{9,8},{10,9},{11,10},{13,12},{... | collective-permute-start | bytes 589832 | tf_op jit(solution)/shard_map/ppermute | solution.py:703
  153.6 9.4 %collective-permute-start.29 = (f32[4,32,384]{2,1,0:T(8,128)S(1)}, f32[4,32,384]{2,1,0:T(8,128)S(1)}, u32[]{:S(2)}, u32[]{:S(2)}) collective-permute-start(f32[4,32,384]{2,1,0:T(8,128)S(1)} %get-tuple-element.239.refs_3_.last_ref), channel_id=1, source_target_pairs={{0,1},{1,2},{2,3},{4,5},{5,6},{6,7},{8,9},{9,10},{10,11},{12,13},{... | collective-permute-start | bytes 589832 | tf_op jit(solution)/shard_map/ppermute | solution.py:700
  156.7 6.4 %collective-permute-start.31 = (f32[4,24,384]{2,1,0:T(8,128)S(1)}, f32[4,24,384]{2,1,0:T(8,128)S(1)}, u32[]{:S(2)}, u32[]{:S(2)}) collective-permute-start(f32[4,24,384]{2,1,0:T(8,128)S(1)} %get-tuple-element.240.refs_4_), channel_id=1, source_target_pairs={{0,4},{4,0},{8,12},{12,8},{16,20},{20,16},{24,28},{28,24},{1,5},{5... | collective-permute-start | bytes 442376 | tf_op jit(solution)/shard_map/ppermute | solution.py:697
  163.8 1.2 collective-permute-start.32
  165.1 3.6 %collective-permute-start.33 = (f32[8,128]{1,0:T(8,128)S(1)}, f32[8,128]{1,0:T(8,128)S(1)}, u32[]{:S(2)}, u32[]{:S(2)}) collective-permute-start(f32[8,128]{1,0:T(8,128)S(1)} %max.70), channel_id=1, source_target_pairs={{0,2},{1,3},{2,0},{3,1},{4,6},{5,7},{6,4},{7,5},{8,10},{9,11},{10,... | collective-permute-start | bytes 12296 | tf_op jit(solution)/shard_map/ppermute | solution.py:721
  168.7 3.6 %collective-permute-start.34 = (f32[8,128]{1,0:T(8,128)S(1)}, f32[8,128]{1,0:T(8,128)S(1)}, u32[]{:S(2)}, u32[]{:S(2)}) collective-permute-start(f32[8,128]{1,0:T(8,128)S(1)} %max.71), channel_id=1, source_target_pairs={{0,4},{4,0},{8,12},{12,8},{16,20},{20,16},{24,28},{28,24},{1,5},{5... | collective-permute-start | bytes 12296 | tf_op jit(solution)/shard_map/ppermute | solution.py:721
  172.3 3.6 %collective-permute-start.35 = (f32[8,128]{1,0:T(8,128)S(1)}, f32[8,128]{1,0:T(8,128)S(1)}, u32[]{:S(2)}, u32[]{:S(2)}) collective-permute-start(f32[8,128]{1,0:T(8,128)S(1)} %max.72), channel_id=1, source_target_pairs={{0,8},{4,12},{8,0},{12,4},{16,24},{20,28},{24,16},{28,20},{1,9},{5... | collective-permute-start | bytes 12296 | tf_op jit(solution)/shard_map/ppermute | solution.py:721
  175.9 4.5 %collective-permute-start.36 = (f32[8,128]{1,0:T(8,128)S(1)}, f32[8,128]{1,0:T(8,128)S(1)}, u32[]{:S(2)}, u32[]{:S(2)}) collective-permute-start(f32[8,128]{1,0:T(8,128)S(1)} %max.73), channel_id=1, source_target_pairs={{0,16},{4,20},{8,24},{12,28},{16,0},{20,4},{24,8},{28,12},{1,17},{... | collective-permute-start | bytes 12296 | tf_op jit(solution)/shard_map/ppermute | solution.py:721
  182.9 43.0 %collective-permute-start.46 = (f32[24,32,384]{2,1,0:T(8,128)S(1)}, f32[24,32,384]{2,1,0:T(8,128)S(1)}, u32[]{:S(2)}, u32[]{:S(2)}) collective-permute-start(f32[24,32,384]{2,1,0:T(8,128)S(1)} %get-tuple-element.260.refs_0_), channel_id=1, source_target_pairs={{8,0},{16,8},{24,16},{4,12},{12,20},{20,28},{9,1},{17,9},{25,17},{... | collective-permute-start | bytes 3538952 | tf_op jit(solution)/shard_map/ppermute | solution.py:711
  184.2 41.7 %collective-permute-start.45 = (f32[24,32,384]{2,1,0:T(8,128)S(1)}, f32[24,32,384]{2,1,0:T(8,128)S(1)}, u32[]{:S(2)}, u32[]{:S(2)}) collective-permute-start(f32[24,32,384]{2,1,0:T(8,128)S(1)} %get-tuple-element.270.refs_3_), channel_id=1, source_target_pairs={{0,8},{8,16},{16,24},{12,4},{20,12},{28,20},{1,9},{9,17},{17,25},{... | collective-permute-start | bytes 3538952 | tf_op jit(solution)/shard_map/ppermute | solution.py:707
  191.2 10.4 %collective-permute-start.38 = (f32[4,32,384]{2,1,0:T(8,128)S(1)}, f32[4,32,384]{2,1,0:T(8,128)S(1)}, u32[]{:S(2)}, u32[]{:S(2)}) collective-permute-start(f32[4,32,384]{2,1,0:T(8,128)S(1)} %get-tuple-element.274.refs_0_.first_ref), channel_id=1, source_target_pairs={{1,0},{2,1},{3,2},{5,4},{6,5},{7,6},{9,8},{10,9},{11,10},{13,12},{... | collective-permute-start | bytes 589832 | tf_op jit(solution)/shard_map/ppermute | solution.py:703
  192.7 8.9 %collective-permute-start.37 = (f32[4,32,384]{2,1,0:T(8,128)S(1)}, f32[4,32,384]{2,1,0:T(8,128)S(1)}, u32[]{:S(2)}, u32[]{:S(2)}) collective-permute-start(f32[4,32,384]{2,1,0:T(8,128)S(1)} %get-tuple-element.277.refs_3_.last_ref), channel_id=1, source_target_pairs={{0,1},{1,2},{2,3},{4,5},{5,6},{6,7},{8,9},{9,10},{10,11},{12,13},{... | collective-permute-start | bytes 589832 | tf_op jit(solution)/shard_map/ppermute | solution.py:700
  195.8 5.8 %collective-permute-start.39 = (f32[4,24,384]{2,1,0:T(8,128)S(1)}, f32[4,24,384]{2,1,0:T(8,128)S(1)}, u32[]{:S(2)}, u32[]{:S(2)}) collective-permute-start(f32[4,24,384]{2,1,0:T(8,128)S(1)} %get-tuple-element.278.refs_4_), channel_id=1, source_target_pairs={{0,4},{4,0},{8,12},{12,8},{16,20},{20,16},{24,28},{28,24},{1,5},{5... | collective-permute-start | bytes 442376 | tf_op jit(solution)/shard_map/ppermute | solution.py:697
  202.3 1.2 collective-permute-start.40
  203.6 3.6 %collective-permute-start.41 = (f32[8,128]{1,0:T(8,128)S(1)}, f32[8,128]{1,0:T(8,128)S(1)}, u32[]{:S(2)}, u32[]{:S(2)}) collective-permute-start(f32[8,128]{1,0:T(8,128)S(1)} %max.75), channel_id=1, source_target_pairs={{0,2},{1,3},{2,0},{3,1},{4,6},{5,7},{6,4},{7,5},{8,10},{9,11},{10,... | collective-permute-start | bytes 12296 | tf_op jit(solution)/shard_map/ppermute | solution.py:721
  207.2 3.6 %collective-permute-start.42 = (f32[8,128]{1,0:T(8,128)S(1)}, f32[8,128]{1,0:T(8,128)S(1)}, u32[]{:S(2)}, u32[]{:S(2)}) collective-permute-start(f32[8,128]{1,0:T(8,128)S(1)} %max.76), channel_id=1, source_target_pairs={{0,4},{4,0},{8,12},{12,8},{16,20},{20,16},{24,28},{28,24},{1,5},{5... | collective-permute-start | bytes 12296 | tf_op jit(solution)/shard_map/ppermute | solution.py:721
  210.8 3.6 %collective-permute-start.43 = (f32[8,128]{1,0:T(8,128)S(1)}, f32[8,128]{1,0:T(8,128)S(1)}, u32[]{:S(2)}, u32[]{:S(2)}) collective-permute-start(f32[8,128]{1,0:T(8,128)S(1)} %max.77), channel_id=1, source_target_pairs={{0,8},{4,12},{8,0},{12,4},{16,24},{20,28},{24,16},{28,20},{1,9},{5... | collective-permute-start | bytes 12296 | tf_op jit(solution)/shard_map/ppermute | solution.py:721
  214.4 4.5 %collective-permute-start.44 = (f32[8,128]{1,0:T(8,128)S(1)}, f32[8,128]{1,0:T(8,128)S(1)}, u32[]{:S(2)}, u32[]{:S(2)}) collective-permute-start(f32[8,128]{1,0:T(8,128)S(1)} %max.78), channel_id=1, source_target_pairs={{0,16},{4,20},{8,24},{12,28},{16,0},{20,4},{24,8},{28,12},{1,17},{... | collective-permute-start | bytes 12296 | tf_op jit(solution)/shard_map/ppermute | solution.py:721
  221.0 29.2 %collective-permute-start.49 = (f32[24,32,384]{2,1,0:T(8,128)}, f32[24,32,384]{2,1,0:T(8,128)}, u32[]{:S(2)}, u32[]{:S(2)}) collective-permute-start(f32[24,32,384]{2,1,0:T(8,128)} %get-tuple-element.292), channel_id=1, source_target_pairs={{0,4},{4,0},{8,12},{12,8},{16,20},{20,16},{24,28},{28,24},{1,5},{5... | collective-permute-start | bytes 3538952 | tf_op jit(solution)/shard_map/ppermute | solution.py:697
  230.6 1.0 copy-start.4
  231.6 1.0 copy-start.6
  232.6 37.9 %collective-permute-start.47 = (f32[24,32,384]{2,1,0:T(8,128)}, f32[24,32,384]{2,1,0:T(8,128)S(1)}, u32[]{:S(2)}, u32[]{:S(2)}) collective-permute-start(f32[24,32,384]{2,1,0:T(8,128)} %get-tuple-element.302), channel_id=1, source_target_pairs={{0,4},{4,0},{8,12},{12,8},{16,20},{20,16},{24,28},{28,24},{1,5},{5... | collective-permute-start | bytes 3538952 | tf_op jit(solution)/shard_map/ppermute | solution.py:697
  239.9 30.6 %collective-permute-start.48 = (f32[2,384]{1,0:T(2,128)S(1)}, f32[2,384]{1,0:T(2,128)S(1)}, u32[]{:S(2)}, u32[]{:S(2)}) collective-permute-start(f32[2,384]{1,0:T(2,128)S(1)} %slice.40), channel_id=1, source_target_pairs={{0,4},{4,0},{8,12},{12,8},{16,20},{20,16},{24,28},{28,24},{1,5},{5... | collective-permute-start | bytes 9224 | tf_op jit(solution)/shard_map/ppermute | solution.py:697
  240.9 1.3 copy-start.5
  242.2 1.3 copy-start.7

commit v7 on v6

--- a/solution.py
+++ b/solution.py
@@ -840,7 +840,9 @@
     updates.update(outer_updates(near))
     (outer, inner, far), (least,) = settled((0, 1, 3), updates, damping=damping, mended=mended, with_edges=False)
     outer_got = partner(far)
-    least = lax.pmin(jnp.concatenate([least[:2], least_near, least[2:]], axis=0), "vx")
+    least = jnp.concatenate([least[:2], least_near, least[2:]], axis=0)
+    for k in range((n_vx - 1).bit_length()):
+        least = jnp.minimum(least, lax.ppermute(least, "vx", [(i, i ^ (1 << k)) for i in range(n_vx)]))
     least_got = partner(after(least[2:], far))
     final = place(flags, [(True, outer), (False, inner)], None, value.shape)
     return finish(flags, outer_got, least, least_got, place(flags, [(False, inner_got)], final, value.shape, 1))

time: 274 us -> 272 us (level)
  waiting for transfers between devices: 89.5 us -> 102 us
  blocking collectives: 6.15 us -> 0 us
  local copies, waits for them, and re-layouts: 21.8 us -> 17.2 us
  Pallas kernels: 73.9 us -> 71.1 us
    ppermute x13, waiting for transfers between devices: 39.4 us -> 46.8 us  [partner(): return lax.ppermute(x, 'px', [(i, i ^ 1) for i in range(n_px)])]
    pmin x1 -> x0, blocking collectives: 6.15 us -> none  [per_device(): lax.pmin(jnp.concatenate([least[:2], least_near, least[2:]], axis=0), 'vx')]
    ppermute x0 -> x2, waiting for transfers between devices: none -> 4.77 us  [per_device(): lax.ppermute(least, 'vx', [(i, i ^ 1 << k) for i in range(n_vx)])]
    unnamed x27 -> x19, local copies, waits for them, and re-layouts: 9.36 us -> 4.76 us
  transfers between devices with their start and end apart: 50 -> 52, of which waited for: 25 -> 27; matrix products, arithmetic and copies ran while one was open for 4% -> 4% of each run, Pallas kernels for 25% -> 24%
where the time goes in v7:
time: 272 us
  waiting for transfers between devices  102 us (38%)
  starting transfers between devices  80 us (29%)
  Pallas kernels  71.1 us (26%)
  local copies, waits for them, and re-layouts  17.2 us (6%)
    ppermute x13, waiting for transfers between devices, partner(): return lax.ppermute(x, 'px', [(i, i ^ 1) for i in range(n_px)])  46.8 us
    ppermute x19, waiting for transfers between devices, share(): lax.ppermute(maxima, axis, [(i, i ^ apart) for i in range(lax.axis_size(a...  45.9 us
    pallas_call x10, Pallas kernels, advance(): pl.pallas_call(body, out_shape=[f32(cells_v, half, width)] * n_out, in_sp...  37.5 us
    ppermute x19, starting transfers between devices, share(): lax.ppermute(maxima, axis, [(i, i ^ apart) for i in range(lax.axis_size(a...  21.5 us
    ppermute x13, starting transfers between devices, partner(): return lax.ppermute(x, 'px', [(i, i ^ 1) for i in range(n_px)])  17.5 us
    ppermute x4, starting transfers between devices, halo_before(): return lax.ppermute(outermost, 'px', moves)  17.4 us
    pallas_call x9, Pallas kernels, settle(): pl.pallas_call(body, out_shape=shapes, in_specs=[scalars()] + [whole()] *...  16.2 us
    ppermute x5, starting transfers between devices, from_low_vx(): return lax.ppermute(x, 'vx', [(i, i + 1) for i in range(n_vx - 1)])  11.7 us
  transfers between devices with their start and end apart: 52, of which 27 were waited for; matrix products, arithmetic and copies ran while one was open for 4% of the time, Pallas kernels for 24%

profile of v7, /device:TPU:0, one launch (start us, length us, event | category | flops | bytes accessed | tf_op | source)
XLA Modules:
  0.0 271.7 jit_solution(1979541365496943748)
XLA Ops:
  0.7 2.4 dynamic-slice_bitcast_fusion.4
  3.0 2.9 %collective-permute-start.6 = (f32[24,32,384]{2,1,0:T(8,128)}, f32[24,32,384]{2,1,0:T(8,128)S(1)}, u32[]{:S(2)}, u32[]{:S(2)}) collective-permute-start(f32[24,32,384]{2,1,0:T(8,128)} %dynamic-slice_bitcast_fusion.4), channel_id=1, source_target_pairs={{0,4},{4,0},{8,12},{12,8},{16,20},{20,16},{24,28},{28,24},{1,5},{5... | collective-permute-start | bytes 3538952 | tf_op jit(solution)/shard_map/ppermute | solution.py:697
  7.2 2.1 collective-permute-start.4
  14.2 3.3 %dynamic-slice_bitcast_fusion.2 = (f32[24,32,384]{2,1,0:T(8,128)}, f32[24,32,384]{2,1,0:T(8,128)}) fusion(f32[2,24,64,384]{3,2,1,0:T(8,128)} %refs_4_.2, s32[]{:T(128)S(6)} %select_n.88, s32[]{:T(128)S(6)} %select_n.89, s32[]{:T(128)S(6)} %select_n.85, s32[]{:T(128)S(6)} %select_n.86), kind=kLoop, calls=%fused_computation.2 | loop fusion | bytes 4718608 | tf_op jit(solution)/shard_map/squeeze | solution.py:728
  18.9 2.2 first_maxima.1
  21.1 3.8 %collective-permute-start.3 = (f32[8,128]{1,0:T(8,128)S(1)}, f32[8,128]{1,0:T(8,128)S(1)}, u32[]{:S(2)}, u32[]{:S(2)}) collective-permute-start(f32[8,128]{1,0:T(8,128)S(1)} %first_maxima.1), channel_id=1, source_target_pairs={{0,4},{4,0},{8,12},{12,8},{16,20},{20,16},{24,28},{28,24},{1,5},{5... | collective-permute-start | bytes 12296 | tf_op jit(solution)/shard_map/ppermute | solution.py:697
  24.9 9.0 %collective-permute-done.3 = f32[8,128]{1,0:T(8,128)S(1)} collective-permute-done((f32[8,128]{1,0:T(8,128)S(1)}, f32[8,128]{1,0:T(8,128)S(1)}, u32[]{:S(2)}, u32[]{:S(2)}) %collective-permute-start.3) | collective-permute-done | bytes 4128 | tf_op jit(solution)/shard_map/ppermute | solution.py:697
  33.9 1.8 collective-permute-start.5
  35.7 3.2 %dynamic-slice_bitcast_fusion = (f32[24,32,384]{2,1,0:T(8,128)}, f32[24,32,384]{2,1,0:T(8,128)}) fusion(f32[2,24,64,384]{3,2,1,0:T(8,128)} %refs_11_.1, s32[]{:T(128)S(6)} %select_n.88, s32[]{:T(128)S(6)} %select_n.86, s32[]{:T(128)S(6)} %select_n.85), kind=kLoop, calls=%fused_computation | loop fusion | bytes 4718604 | tf_op jit(solution)/shard_map/squeeze | solution.py:728
  40.2 1.5 collective-permute-start.12
  41.7 3.5 %collective-permute-start.7 = (f32[24,32,384]{2,1,0:T(8,128)S(1)}, f32[24,32,384]{2,1,0:T(8,128)S(1)}, u32[]{:S(2)}, u32[]{:S(2)}) collective-permute-start(f32[24,32,384]{2,1,0:T(8,128)S(1)} %collective-permute-done.6.refs_2_), channel_id=1, source_target_pairs={{0,8},{8,16},{16,24},{12,4},{20,12},{28,20},{1,9},{9,17},{17,25},{... | collective-permute-start | bytes 3538952 | tf_op jit(solution)/shard_map/ppermute | solution.py:707
  45.3 1.6 collective-permute-start.13
  46.9 23.6 %collective-permute-done.13 = f32[8,128]{1,0:T(8,128)S(1)} collective-permute-done((f32[8,128]{1,0:T(8,128)S(1)}, f32[8,128]{1,0:T(8,128)S(1)}, u32[]{:S(2)}, u32[]{:S(2)}) %collective-permute-start.13) | collective-permute-done | bytes 4128 | tf_op jit(solution)/shard_map/ppermute | solution.py:721
  70.5 2.6 collective-permute-start.14
  73.1 1.9 collective-permute-done.14
  75.0 1.8 collective-permute-start.15
  80.5 3.3 %collective-permute-done.10 = f32[2,32,384]{2,1,0:T(8,128)S(1)} collective-permute-done((f32[2,32,384]{2,1,0:T(8,128)S(1)}, f32[2,32,384]{2,1,0:T(8,128)S(1)}, u32[]{:S(2)}, u32[]{:S(2)}) %collective-permute-start.10) | collective-permute-done | bytes 98336 | tf_op jit(solution)/shard_map/ppermute | solution.py:703
  83.8 2.3 copy-done.1
  86.2 4.8 %advance_12.4 = (f32[24,32,384]{2,1,0:T(8,128)S(1)}, f32[24,32,384]{2,1,0:T(8,128)S(1)}) custom-call(f32[6,24]{1,0:T(8,128)S(1)} %concatenate.15.table_ref, f32[2,24,64,384]{3,2,1,0:T(8,128)S(1)} %copy-done.1, f32[24,32,384]{2,1,0:T(8,128)S(1)} %collective-permute-done.5.refs_1_.refs_5_, f32[24,32,384]{2,1,0:T(8,128)S(1)} %collective-permute-done.6.refs_2_, ...), custom_call_target="tpu_custom_call" | custom-call | tf_op jit(solution)/shard_map/advance_12/pallas_call | solution.py:270
  91.0 2.4 copy-done.2
  93.4 5.7 %advance_03.2 = (f32[24,32,384]{2,1,0:T(8,128)S(1)}, f32[24,32,384]{2,1,0:T(8,128)S(1)}) custom-call(f32[6,24]{1,0:T(8,128)S(1)} %concatenate.15.table_ref, f32[2,24,64,384]{3,2,1,0:T(8,128)S(1)} %copy-done.2, f32[24,32,384]{2,1,0:T(8,128)S(1)} %collective-permute-done.5.refs_1_.refs_5_, f32[24,32,384]{2,1,0:T(8,128)S(1)} %collective-permute-done.6.refs_2_, ...), custom_call_target="tpu_custom_call" | custom-call | tf_op jit(solution)/shard_map/advance_03/pallas_call | solution.py:270
  99.1 1.6 settle_01.1
  103.2 4.6 %collective-permute-start.17 = (f32[24,32,384]{2,1,0:T(8,128)S(1)}, f32[24,32,384]{2,1,0:T(8,128)S(1)}, u32[]{:S(2)}, u32[]{:S(2)}) collective-permute-start(f32[24,32,384]{2,1,0:T(8,128)S(1)} %get-tuple-element.187.refs_3_.refs_1_), channel_id=1, source_target_pairs={{0,8},{8,16},{16,24},{12,4},{20,12},{28,20},{1,9},{9,17},{17,25},{... | collective-permute-start | bytes 3538952 | tf_op jit(solution)/shard_map/ppermute | solution.py:707
  107.8 4.2 %collective-permute-done.15.refs_1_.refs_7_.refs_3_ = f32[24,32,384]{2,1,0:T(8,128)S(1)} collective-permute-done((f32[24,32,384]{2,1,0:T(8,128)}, f32[24,32,384]{2,1,0:T(8,128)S(1)}, u32[]{:S(2)}, u32[]{:S(2)}) %collective-permute-start.15) | collective-permute-done | bytes 1179680 | tf_op jit(solution)/shard_map/ppermute | solution.py:697
  114.4 3.0 %collective-permute-start.19 = (f32[4,32,384]{2,1,0:T(8,128)S(1)}, f32[4,32,384]{2,1,0:T(8,128)S(1)}, u32[]{:S(2)}, u32[]{:S(2)}) collective-permute-start(f32[4,32,384]{2,1,0:T(8,128)S(1)} %get-tuple-element.196.refs_3_.last_ref), channel_id=1, source_target_pairs={{0,1},{1,2},{2,3},{4,5},{5,6},{6,7},{8,9},{9,10},{10,11},{12,13},{... | collective-permute-start | bytes 589832 | tf_op jit(solution)/shard_map/ppermute | solution.py:700
  117.5 1.4 collective-permute-start.21
  118.8 4.8 %advance_12.5 = (f32[24,32,384]{2,1,0:T(8,128)S(1)}, f32[24,32,384]{2,1,0:T(8,128)S(1)}, f32[24,32,384]{2,1,0:T(8,128)S(1)}, f32[24,32,384]{2,1,0:T(8,128)S(1)},...) custom-call(f32[6,24]{1,0:T(8,128)S(1)} %concatenate.15.table_ref, ...), custom_call_target="tpu_custom_call" | custom-call | tf_op jit(solution)/shard_map/advance_12/pallas_call | solution.py:270
  128.1 1.7 collective-permute-done.23
  131.0 2.4 advance_0.2
  133.4 1.7 collective-permute-start.25
  135.1 2.4 advance_3.2
  137.5 2.7 collective-permute-start.26
  140.2 1.5 outer_terms.3
  142.1 2.2 settle_03.2
  145.6 4.6 %collective-permute-start.27 = (f32[24,32,384]{2,1,0:T(8,128)S(1)}, f32[24,32,384]{2,1,0:T(8,128)S(1)}, u32[]{:S(2)}, u32[]{:S(2)}) collective-permute-start(f32[24,32,384]{2,1,0:T(8,128)S(1)} %get-tuple-element.230.refs_3_.refs_1_.refs_11_.refs_5_), channel_id=1, source_target_pairs={{0,8},{8,16},{16,24},{12,4},{20,12},{28,20},{1,9},{9,17},{17,25},{... | collective-permute-start | bytes 3538952 | tf_op jit(solution)/shard_map/ppermute | solution.py:707
  150.2 2.1 settle_12.2
  153.6 3.0 %collective-permute-start.29 = (f32[4,32,384]{2,1,0:T(8,128)S(1)}, f32[4,32,384]{2,1,0:T(8,128)S(1)}, u32[]{:S(2)}, u32[]{:S(2)}) collective-permute-start(f32[4,32,384]{2,1,0:T(8,128)S(1)} %get-tuple-element.239.refs_3_.last_ref), channel_id=1, source_target_pairs={{0,1},{1,2},{2,3},{4,5},{5,6},{6,7},{8,9},{9,10},{10,11},{12,13},{... | collective-permute-start | bytes 589832 | tf_op jit(solution)/shard_map/ppermute | solution.py:700
  156.8 4.5 %advance_12.6 = (f32[24,32,384]{2,1,0:T(8,128)S(1)}, f32[24,32,384]{2,1,0:T(8,128)S(1)}, f32[24,32,384]{2,1,0:T(8,128)S(1)}, f32[24,32,384]{2,1,0:T(8,128)S(1)},...) custom-call(f32[6,24]{1,0:T(8,128)S(1)} %concatenate.15.table_ref, ...), custom_call_target="tpu_custom_call" | custom-call | tf_op jit(solution)/shard_map/advance_12/pallas_call | solution.py:270
  161.2 1.8 collective-permute-done.31.refs_8_.next_ref
  166.0 2.7 collective-permute-done.33
  169.0 2.2 advance_0.3
  173.4 2.2 advance_3.3
  175.9 2.6 collective-permute-start.36
  178.5 1.5 outer_terms.4
  180.4 2.5 settle_03.3
  184.2 4.6 %collective-permute-start.45 = (f32[24,32,384]{2,1,0:T(8,128)S(1)}, f32[24,32,384]{2,1,0:T(8,128)S(1)}, u32[]{:S(2)}, u32[]{:S(2)}) collective-permute-start(f32[24,32,384]{2,1,0:T(8,128)S(1)} %get-tuple-element.270.refs_3_), channel_id=1, source_target_pairs={{0,8},{8,16},{16,24},{12,4},{20,12},{28,20},{1,9},{9,17},{17,25},{... | collective-permute-start | bytes 3538952 | tf_op jit(solution)/shard_map/ppermute | solution.py:707
  188.8 2.4 settle_12.3
  191.2 1.5 collective-permute-start.38
  192.7 3.0 %collective-permute-start.37 = (f32[4,32,384]{2,1,0:T(8,128)S(1)}, f32[4,32,384]{2,1,0:T(8,128)S(1)}, u32[]{:S(2)}, u32[]{:S(2)}) collective-permute-start(f32[4,32,384]{2,1,0:T(8,128)S(1)} %get-tuple-element.277.refs_3_.last_ref), channel_id=1, source_target_pairs={{0,1},{1,2},{2,3},{4,5},{5,6},{6,7},{8,9},{9,10},{10,11},{12,13},{... | collective-permute-start | bytes 589832 | tf_op jit(solution)/shard_map/ppermute | solution.py:700
  195.8 4.6 %advance_12.7 = (f32[24,32,384]{2,1,0:T(8,128)S(1)}, f32[24,32,384]{2,1,0:T(8,128)S(1)}, f32[24,32,384]{2,1,0:T(8,128)S(1)}, f32[24,32,384]{2,1,0:T(8,128)S(1)},...) custom-call(f32[6,24]{1,0:T(8,128)S(1)} %concatenate.15.table_ref, ...), custom_call_target="tpu_custom_call" | custom-call | tf_op jit(solution)/shard_map/advance_12/pallas_call | solution.py:270
  204.5 2.7 collective-permute-done.41
  208.1 2.7 collective-permute-done.42
  211.9 2.5 collective-permute-done.43
  214.4 2.6 collective-permute-start.44
  217.0 1.9 collective-permute-done.44
  221.0 4.0 %advance_03.3 = (f32[24,32,384]{2,1,0:T(8,128)S(1)}, f32[24,32,384]{2,1,0:T(8,128)S(1)}, f32[24,32,384]{2,1,0:T(8,128)S(1)}, f32[24,32,384]{2,1,0:T(8,128)S(1)},...) custom-call(f32[6,24]{1,0:T(8,128)S(1)} %concatenate.15.table_ref, ...), custom_call_target="tpu_custom_call" | custom-call | tf_op jit(solution)/shard_map/advance_03/pallas_call | solution.py:270
  225.0 1.5 outer_terms.5
  226.5 2.1 settle_013.1
  231.1 3.6 %collective-permute-done.49 = f32[4,384]{1,0:T(4,128)S(1)} collective-permute-done((f32[4,384]{1,0:T(4,128)S(1)}, f32[4,384]{1,0:T(4,128)S(1)}, u32[]{:S(2)}, u32[]{:S(2)}) %collective-permute-start.49) | collective-permute-done | bytes 6176 | tf_op jit(solution)/shard_map/ppermute | solution.py:845
  235.7 2.0 place.2.refs_1_
  237.7 11.3 %collective-permute-done.51.refs_0_ = f32[24,32,384]{2,1,0:T(8,128)S(1)} collective-permute-done((f32[24,32,384]{2,1,0:T(8,128)S(1)}, f32[24,32,384]{2,1,0:T(8,128)S(1)}, u32[]{:S(2)}, u32[]{:S(2)}) %collective-permute-start.51) | collective-permute-done | bytes 1179680 | tf_op jit(solution)/shard_map/ppermute | solution.py:697
  249.0 1.6 place.3._
  250.5 18.9 %collective-permute-done.50.got_ref = f32[2,384]{1,0:T(2,128)S(1)} collective-permute-done((f32[2,384]{1,0:T(2,128)S(1)}, f32[2,384]{1,0:T(2,128)S(1)}, u32[]{:S(2)}, u32[]{:S(2)}) %collective-permute-start.50) | collective-permute-done | bytes 3104 | tf_op jit(solution)/shard_map/ppermute | solution.py:697
  269.4 2.1 finish.1
  (143 shorter events, 44.9 us)
Async XLA Ops:
  0.7 5.3 %copy-start.4 = (f32[2,24]{1,0:T(2,128)S(1)}, f32[2,24]{1,0:T(2,128)}, u32[]{:S(2)}) copy-start(f32[2,24]{1,0:T(2,128)} %first_ref.1) | copy-start | bytes 580
  3.0 38.7 %collective-permute-start.6 = (f32[24,32,384]{2,1,0:T(8,128)}, f32[24,32,384]{2,1,0:T(8,128)S(1)}, u32[]{:S(2)}, u32[]{:S(2)}) collective-permute-start(f32[24,32,384]{2,1,0:T(8,128)} %dynamic-slice_bitcast_fusion.4), channel_id=1, source_target_pairs={{0,4},{4,0},{8,12},{12,8},{16,20},{20,16},{24,28},{28,24},{1,5},{5... | collective-permute-start | bytes 3538952 | tf_op jit(solution)/shard_map/ppermute | solution.py:697
  6.0 27.9 %collective-permute-start = (f32[2,24]{1,0:T(2,128)S(1)}, f32[2,24]{1,0:T(2,128)S(1)}, u32[]{:S(2)}, u32[]{:S(2)}) collective-permute-start(f32[2,24]{1,0:T(2,128)S(1)} %copy-done.4), channel_id=1, source_target_pairs={{0,4},{4,0},{8,12},{12,8},{16,20},{20,16},{24,28},{28,24},{1,5},{5... | collective-permute-start | bytes 584 | tf_op jit(solution)/shard_map/ppermute | solution.py:697
  7.2 26.7 %collective-permute-start.4 = (f32[2,24,384]{2,1,0:T(8,128)S(1)}, f32[2,24,384]{2,1,0:T(8,128)S(1)}, u32[]{:S(2)}, u32[]{:S(2)}) collective-permute-start(f32[2,24,384]{2,1,0:T(8,128)S(1)} %bitcast.36), channel_id=1, source_target_pairs={{0,4},{4,0},{8,12},{12,8},{16,20},{20,16},{24,28},{28,24},{1,5},{5... | collective-permute-start | bytes 221192 | tf_op jit(solution)/shard_map/ppermute | solution.py:697
  10.3 7.3 %collective-permute-start.1 = (f32[2,64,384]{2,1,0:T(8,128)S(1)}, f32[2,64,384]{2,1,0:T(8,128)S(1)}, u32[]{:S(2)}, u32[]{:S(2)}) collective-permute-start(f32[2,64,384]{2,1,0:T(8,128)S(1)} %get-tuple-element.157), channel_id=1, source_target_pairs={{0,1},{1,2},{2,3},{4,5},{5,6},{6,7},{8,9},{9,10},{10,11},{12,13},{... | collective-permute-start | bytes 589832 | tf_op jit(solution)/shard_map/ppermute | solution.py:700
  11.6 7.3 %collective-permute-start.2 = (f32[2,64,384]{2,1,0:T(8,128)S(1)}, f32[2,64,384]{2,1,0:T(8,128)S(1)}, u32[]{:S(2)}, u32[]{:S(2)}) collective-permute-start(f32[2,64,384]{2,1,0:T(8,128)S(1)} %get-tuple-element.158), channel_id=1, source_target_pairs={{1,0},{2,1},{3,2},{5,4},{6,5},{7,6},{9,8},{10,9},{11,10},{13,12},{... | collective-permute-start | bytes 589832 | tf_op jit(solution)/shard_map/ppermute | solution.py:703
  13.0 5.8 %copy-start.3 = (f32[64,384]{1,0:T(8,128)S(1)}, f32[64,384]{1,0:T(8,128)}, u32[]{:S(2)}) copy-start(f32[64,384]{1,0:T(8,128)} %refs_6_.9) | copy-start | bytes 294916
  14.2 4.7 %copy-start = (f32[2,24,64,384]{3,2,1,0:T(8,128)S(1)}, f32[2,24,64,384]{3,2,1,0:T(8,128)}, u32[]{:S(2)}) copy-start(f32[2,24,64,384]{3,2,1,0:T(8,128)} %refs_4_.2) | copy-start | bytes 14155780
  17.6 73.4 %collective-permute-start.8 = (f32[24,32,384]{2,1,0:T(8,128)}, f32[24,32,384]{2,1,0:T(8,128)}, u32[]{:S(2)}, u32[]{:S(2)}) collective-permute-start(f32[24,32,384]{2,1,0:T(8,128)} %get-tuple-element.312), channel_id=1, source_target_pairs={{8,0},{16,8},{24,16},{4,12},{12,20},{20,28},{9,1},{17,9},{25,17},{... | collective-permute-start | bytes 3538952 | tf_op jit(solution)/shard_map/ppermute | solution.py:711
  21.1 12.8 %collective-permute-start.3 = (f32[8,128]{1,0:T(8,128)S(1)}, f32[8,128]{1,0:T(8,128)S(1)}, u32[]{:S(2)}, u32[]{:S(2)}) collective-permute-start(f32[8,128]{1,0:T(8,128)S(1)} %first_maxima.1), channel_id=1, source_target_pairs={{0,4},{4,0},{8,12},{12,8},{16,20},{20,16},{24,28},{28,24},{1,5},{5... | collective-permute-start | bytes 12296 | tf_op jit(solution)/shard_map/ppermute | solution.py:697
  33.9 43.0 %collective-permute-start.5 = (f32[24,32,384]{2,1,0:T(8,128)}, f32[24,32,384]{2,1,0:T(8,128)S(1)}, u32[]{:S(2)}, u32[]{:S(2)}) collective-permute-start(f32[24,32,384]{2,1,0:T(8,128)} %get-tuple-element.160), channel_id=1, source_target_pairs={{0,4},{4,0},{8,12},{12,8},{16,20},{20,16},{24,28},{28,24},{1,5},{5... | collective-permute-start | bytes 3538952 | tf_op jit(solution)/shard_map/ppermute | solution.py:697
  38.9 1.2 collective-permute-start.11
  39.0 63.0 %collective-permute-start.16 = (f32[24,32,384]{2,1,0:T(8,128)}, f32[24,32,384]{2,1,0:T(8,128)S(1)}, u32[]{:S(2)}, u32[]{:S(2)}) collective-permute-start(f32[24,32,384]{2,1,0:T(8,128)} %get-tuple-element.171), channel_id=1, source_target_pairs={{0,4},{4,0},{8,12},{12,8},{16,20},{20,16},{24,28},{28,24},{1,5},{5... | collective-permute-start | bytes 3538952 | tf_op jit(solution)/shard_map/ppermute | solution.py:697
  40.2 5.1 %collective-permute-start.12 = (f32[8,128]{1,0:T(8,128)S(1)}, f32[8,128]{1,0:T(8,128)S(1)}, u32[]{:S(2)}, u32[]{:S(2)}) collective-permute-start(f32[8,128]{1,0:T(8,128)S(1)} %max.61), channel_id=1, source_target_pairs={{0,2},{1,3},{2,0},{3,1},{4,6},{5,7},{6,4},{7,5},{8,10},{9,11},{10,... | collective-permute-start | bytes 12296 | tf_op jit(solution)/shard_map/ppermute | solution.py:721
  41.7 49.3 %collective-permute-start.7 = (f32[24,32,384]{2,1,0:T(8,128)S(1)}, f32[24,32,384]{2,1,0:T(8,128)S(1)}, u32[]{:S(2)}, u32[]{:S(2)}) collective-permute-start(f32[24,32,384]{2,1,0:T(8,128)S(1)} %collective-permute-done.6.refs_2_), channel_id=1, source_target_pairs={{0,8},{8,16},{16,24},{12,4},{20,12},{28,20},{1,9},{9,17},{17,25},{... | collective-permute-start | bytes 3538952 | tf_op jit(solution)/shard_map/ppermute | solution.py:707
  45.3 25.2 %collective-permute-start.13 = (f32[8,128]{1,0:T(8,128)S(1)}, f32[8,128]{1,0:T(8,128)S(1)}, u32[]{:S(2)}, u32[]{:S(2)}) collective-permute-start(f32[8,128]{1,0:T(8,128)S(1)} %max.62), channel_id=1, source_target_pairs={{0,8},{4,12},{8,0},{12,4},{16,24},{20,28},{24,16},{28,20},{1,9},{5... | collective-permute-start | bytes 12296 | tf_op jit(solution)/shard_map/ppermute | solution.py:721
  70.5 4.5 %collective-permute-start.14 = (f32[8,128]{1,0:T(8,128)S(1)}, f32[8,128]{1,0:T(8,128)S(1)}, u32[]{:S(2)}, u32[]{:S(2)}) collective-permute-start(f32[8,128]{1,0:T(8,128)S(1)} %max.63), channel_id=1, source_target_pairs={{0,16},{4,20},{8,24},{12,28},{16,0},{20,4},{24,8},{28,12},{1,17},{... | collective-permute-start | bytes 12296 | tf_op jit(solution)/shard_map/ppermute | solution.py:721
  75.0 36.9 %collective-permute-start.15 = (f32[24,32,384]{2,1,0:T(8,128)}, f32[24,32,384]{2,1,0:T(8,128)S(1)}, u32[]{:S(2)}, u32[]{:S(2)}) collective-permute-start(f32[24,32,384]{2,1,0:T(8,128)} %get-tuple-element.169), channel_id=1, source_target_pairs={{0,4},{4,0},{8,12},{12,8},{16,20},{20,16},{24,28},{28,24},{1,5},{5... | collective-permute-start | bytes 3538952 | tf_op jit(solution)/shard_map/ppermute | solution.py:697
  76.9 2.2 collective-permute-start.9
  79.2 4.6 %collective-permute-start.10 = (f32[2,32,384]{2,1,0:T(8,128)S(1)}, f32[2,32,384]{2,1,0:T(8,128)S(1)}, u32[]{:S(2)}, u32[]{:S(2)}) collective-permute-start(f32[2,32,384]{2,1,0:T(8,128)S(1)} %pad_maximum_fusion.4), channel_id=1, source_target_pairs={{1,0},{2,1},{3,2},{5,4},{6,5},{7,6},{9,8},{10,9},{11,10},{13,12},{... | collective-permute-start | bytes 294920 | tf_op jit(solution)/shard_map/ppermute | solution.py:703
  83.8 2.3 copy-start.1
  86.1 13.0 %slice-start = ((s8[4718592]{0:T(1024)(128)(4,1)}), s8[4194304]{0:T(1024)(128)(4,1)S(1)}, s32[]{:S(2)}) async-start(s8[4718592]{0:T(1024)(128)(4,1)} %bitcast.32), calls=%async_computation | async-start | bytes 8388608
  90.9 8.2 %slice-start.1 = ((s8[4718592]{0:T(1024)(128)(4,1)}), s8[524288]{0:T(1024)(128)(4,1)S(1)}, s32[]{:S(2)}) async-start(s8[4718592]{0:T(1024)(128)(4,1)} %bitcast.32), calls=%async_computation.1 | async-start | bytes 1048576
  91.0 2.4 copy-start.2
  93.4 25.5 %slice-start.2 = ((s8[4718592]{0:T(1024)(128)(4,1)}), s8[4194304]{0:T(1024)(128)(4,1)S(1)}, s32[]{:S(2)}) async-start(s8[4718592]{0:T(1024)(128)(4,1)} %bitcast.34), calls=%async_computation.2 | async-start | bytes 8388608
  99.1 19.7 %slice-start.3 = ((s8[4718592]{0:T(1024)(128)(4,1)}), s8[524288]{0:T(1024)(128)(4,1)S(1)}, s32[]{:S(2)}) async-start(s8[4718592]{0:T(1024)(128)(4,1)} %bitcast.34), calls=%async_computation.3 | async-start | bytes 1048576
  100.7 39.5 %collective-permute-start.18 = (f32[24,32,384]{2,1,0:T(8,128)S(1)}, f32[24,32,384]{2,1,0:T(8,128)S(1)}, u32[]{:S(2)}, u32[]{:S(2)}) collective-permute-start(f32[24,32,384]{2,1,0:T(8,128)S(1)} %get-tuple-element.163.refs_0_), channel_id=1, source_target_pairs={{8,0},{16,8},{24,16},{4,12},{12,20},{20,28},{9,1},{17,9},{25,17},{... | collective-permute-start | bytes 3538952 | tf_op jit(solution)/shard_map/ppermute | solution.py:711
  103.2 37.0 %collective-permute-start.17 = (f32[24,32,384]{2,1,0:T(8,128)S(1)}, f32[24,32,384]{2,1,0:T(8,128)S(1)}, u32[]{:S(2)}, u32[]{:S(2)}) collective-permute-start(f32[24,32,384]{2,1,0:T(8,128)S(1)} %get-tuple-element.187.refs_3_.refs_1_), channel_id=1, source_target_pairs={{0,8},{8,16},{16,24},{12,4},{20,12},{28,20},{1,9},{9,17},{17,25},{... | collective-permute-start | bytes 3538952 | tf_op jit(solution)/shard_map/ppermute | solution.py:707
  113.1 11.0 %collective-permute-start.20 = (f32[4,32,384]{2,1,0:T(8,128)S(1)}, f32[4,32,384]{2,1,0:T(8,128)S(1)}, u32[]{:S(2)}, u32[]{:S(2)}) collective-permute-start(f32[4,32,384]{2,1,0:T(8,128)S(1)} %get-tuple-element.193.refs_0_.first_ref), channel_id=1, source_target_pairs={{1,0},{2,1},{3,2},{5,4},{6,5},{7,6},{9,8},{10,9},{11,10},{13,12},{... | collective-permute-start | bytes 589832 | tf_op jit(solution)/shard_map/ppermute | solution.py:703
  114.4 9.8 %collective-permute-start.19 = (f32[4,32,384]{2,1,0:T(8,128)S(1)}, f32[4,32,384]{2,1,0:T(8,128)S(1)}, u32[]{:S(2)}, u32[]{:S(2)}) collective-permute-start(f32[4,32,384]{2,1,0:T(8,128)S(1)} %get-tuple-element.196.refs_3_.last_ref), channel_id=1, source_target_pairs={{0,1},{1,2},{2,3},{4,5},{5,6},{6,7},{8,9},{9,10},{10,11},{12,13},{... | collective-permute-start | bytes 589832 | tf_op jit(solution)/shard_map/ppermute | solution.py:700
  117.5 6.7 %collective-permute-start.21 = (f32[4,24,384]{2,1,0:T(8,128)S(1)}, f32[4,24,384]{2,1,0:T(8,128)S(1)}, u32[]{:S(2)}, u32[]{:S(2)}) collective-permute-start(f32[4,24,384]{2,1,0:T(8,128)S(1)} %get-tuple-element.197.refs_4_), channel_id=1, source_target_pairs={{0,4},{4,0},{8,12},{12,8},{16,20},{20,16},{24,28},{28,24},{1,5},{5... | collective-permute-start | bytes 442376 | tf_op jit(solution)/shard_map/ppermute | solution.py:697
  124.9 1.2 collective-permute-start.22
  126.2 3.6 %collective-permute-start.23 = (f32[8,128]{1,0:T(8,128)S(1)}, f32[8,128]{1,0:T(8,128)S(1)}, u32[]{:S(2)}, u32[]{:S(2)}) collective-permute-start(f32[8,128]{1,0:T(8,128)S(1)} %max.65), channel_id=1, source_target_pairs={{0,2},{1,3},{2,0},{3,1},{4,6},{5,7},{6,4},{7,5},{8,10},{9,11},{10,... | collective-permute-start | bytes 12296 | tf_op jit(solution)/shard_map/ppermute | solution.py:721
  129.8 3.6 %collective-permute-start.24 = (f32[8,128]{1,0:T(8,128)S(1)}, f32[8,128]{1,0:T(8,128)S(1)}, u32[]{:S(2)}, u32[]{:S(2)}) collective-permute-start(f32[8,128]{1,0:T(8,128)S(1)} %max.66), channel_id=1, source_target_pairs={{0,4},{4,0},{8,12},{12,8},{16,20},{20,16},{24,28},{28,24},{1,5},{5... | collective-permute-start | bytes 12296 | tf_op jit(solution)/shard_map/ppermute | solution.py:721
  133.4 4.1 %collective-permute-start.25 = (f32[8,128]{1,0:T(8,128)S(1)}, f32[8,128]{1,0:T(8,128)S(1)}, u32[]{:S(2)}, u32[]{:S(2)}) collective-permute-start(f32[8,128]{1,0:T(8,128)S(1)} %max.67), channel_id=1, source_target_pairs={{0,8},{4,12},{8,0},{12,4},{16,24},{20,28},{24,16},{28,20},{1,9},{5... | collective-permute-start | bytes 12296 | tf_op jit(solution)/shard_map/ppermute | solution.py:721
  137.5 4.6 %collective-permute-start.26 = (f32[8,128]{1,0:T(8,128)S(1)}, f32[8,128]{1,0:T(8,128)S(1)}, u32[]{:S(2)}, u32[]{:S(2)}) collective-permute-start(f32[8,128]{1,0:T(8,128)S(1)} %max.68), channel_id=1, source_target_pairs={{0,16},{4,20},{8,24},{12,28},{16,0},{20,4},{24,8},{28,12},{1,17},{... | collective-permute-start | bytes 12296 | tf_op jit(solution)/shard_map/ppermute | solution.py:721
  144.3 34.2 %collective-permute-start.28 = (f32[24,32,384]{2,1,0:T(8,128)S(1)}, f32[24,32,384]{2,1,0:T(8,128)S(1)}, u32[]{:S(2)}, u32[]{:S(2)}) collective-permute-start(f32[24,32,384]{2,1,0:T(8,128)S(1)} %get-tuple-element.217.refs_0_.refs_10_.refs_4_), channel_id=1, source_target_pairs={{8,0},{16,8},{24,16},{4,12},{12,20},{20,28},{9,1},{17,9},{25,17},{... | collective-permute-start | bytes 3538952 | tf_op jit(solution)/shard_map/ppermute | solution.py:711
  145.6 32.9 %collective-permute-start.27 = (f32[24,32,384]{2,1,0:T(8,128)S(1)}, f32[24,32,384]{2,1,0:T(8,128)S(1)}, u32[]{:S(2)}, u32[]{:S(2)}) collective-permute-start(f32[24,32,384]{2,1,0:T(8,128)S(1)} %get-tuple-element.230.refs_3_.refs_1_.refs_11_.refs_5_), channel_id=1, source_target_pairs={{0,8},{8,16},{16,24},{12,4},{20,12},{28,20},{1,9},{9,17},{17,25},{... | collective-permute-start | bytes 3538952 | tf_op jit(solution)/shard_map/ppermute | solution.py:707
  152.3 10.7 %collective-permute-start.30 = (f32[4,32,384]{2,1,0:T(8,128)S(1)}, f32[4,32,384]{2,1,0:T(8,128)S(1)}, u32[]{:S(2)}, u32[]{:S(2)}) collective-permute-start(f32[4,32,384]{2,1,0:T(8,128)S(1)} %get-tuple-element.236.refs_0_.first_ref), channel_id=1, source_target_pairs={{1,0},{2,1},{3,2},{5,4},{6,5},{7,6},{9,8},{10,9},{11,10},{13,12},{... | collective-permute-start | bytes 589832 | tf_op jit(solution)/shard_map/ppermute | solution.py:703
  153.6 9.4 %collective-permute-start.29 = (f32[4,32,384]{2,1,0:T(8,128)S(1)}, f32[4,32,384]{2,1,0:T(8,128)S(1)}, u32[]{:S(2)}, u32[]{:S(2)}) collective-permute-start(f32[4,32,384]{2,1,0:T(8,128)S(1)} %get-tuple-element.239.refs_3_.last_ref), channel_id=1, source_target_pairs={{0,1},{1,2},{2,3},{4,5},{5,6},{6,7},{8,9},{9,10},{10,11},{12,13},{... | collective-permute-start | bytes 589832 | tf_op jit(solution)/shard_map/ppermute | solution.py:700
  156.7 6.4 %collective-permute-start.31 = (f32[4,24,384]{2,1,0:T(8,128)S(1)}, f32[4,24,384]{2,1,0:T(8,128)S(1)}, u32[]{:S(2)}, u32[]{:S(2)}) collective-permute-start(f32[4,24,384]{2,1,0:T(8,128)S(1)} %get-tuple-element.240.refs_4_), channel_id=1, source_target_pairs={{0,4},{4,0},{8,12},{12,8},{16,20},{20,16},{24,28},{28,24},{1,5},{5... | collective-permute-start | bytes 442376 | tf_op jit(solution)/shard_map/ppermute | solution.py:697
  163.8 1.2 collective-permute-start.32
  165.1 3.6 %collective-permute-start.33 = (f32[8,128]{1,0:T(8,128)S(1)}, f32[8,128]{1,0:T(8,128)S(1)}, u32[]{:S(2)}, u32[]{:S(2)}) collective-permute-start(f32[8,128]{1,0:T(8,128)S(1)} %max.70), channel_id=1, source_target_pairs={{0,2},{1,3},{2,0},{3,1},{4,6},{5,7},{6,4},{7,5},{8,10},{9,11},{10,... | collective-permute-start | bytes 12296 | tf_op jit(solution)/shard_map/ppermute | solution.py:721
  168.7 3.6 %collective-permute-start.34 = (f32[8,128]{1,0:T(8,128)S(1)}, f32[8,128]{1,0:T(8,128)S(1)}, u32[]{:S(2)}, u32[]{:S(2)}) collective-permute-start(f32[8,128]{1,0:T(8,128)S(1)} %max.71), channel_id=1, source_target_pairs={{0,4},{4,0},{8,12},{12,8},{16,20},{20,16},{24,28},{28,24},{1,5},{5... | collective-permute-start | bytes 12296 | tf_op jit(solution)/shard_map/ppermute | solution.py:721
  172.3 3.6 %collective-permute-start.35 = (f32[8,128]{1,0:T(8,128)S(1)}, f32[8,128]{1,0:T(8,128)S(1)}, u32[]{:S(2)}, u32[]{:S(2)}) collective-permute-start(f32[8,128]{1,0:T(8,128)S(1)} %max.72), channel_id=1, source_target_pairs={{0,8},{4,12},{8,0},{12,4},{16,24},{20,28},{24,16},{28,20},{1,9},{5... | collective-permute-start | bytes 12296 | tf_op jit(solution)/shard_map/ppermute | solution.py:721
  175.9 4.5 %collective-permute-start.36 = (f32[8,128]{1,0:T(8,128)S(1)}, f32[8,128]{1,0:T(8,128)S(1)}, u32[]{:S(2)}, u32[]{:S(2)}) collective-permute-start(f32[8,128]{1,0:T(8,128)S(1)} %max.73), channel_id=1, source_target_pairs={{0,16},{4,20},{8,24},{12,28},{16,0},{20,4},{24,8},{28,12},{1,17},{... | collective-permute-start | bytes 12296 | tf_op jit(solution)/shard_map/ppermute | solution.py:721
  182.9 42.1 %collective-permute-start.46 = (f32[24,32,384]{2,1,0:T(8,128)S(1)}, f32[24,32,384]{2,1,0:T(8,128)S(1)}, u32[]{:S(2)}, u32[]{:S(2)}) collective-permute-start(f32[24,32,384]{2,1,0:T(8,128)S(1)} %get-tuple-element.260.refs_0_), channel_id=1, source_target_pairs={{8,0},{16,8},{24,16},{4,12},{12,20},{20,28},{9,1},{17,9},{25,17},{... | collective-permute-start | bytes 3538952 | tf_op jit(solution)/shard_map/ppermute | solution.py:711
  184.2 40.8 %collective-permute-start.45 = (f32[24,32,384]{2,1,0:T(8,128)S(1)}, f32[24,32,384]{2,1,0:T(8,128)S(1)}, u32[]{:S(2)}, u32[]{:S(2)}) collective-permute-start(f32[24,32,384]{2,1,0:T(8,128)S(1)} %get-tuple-element.270.refs_3_), channel_id=1, source_target_pairs={{0,8},{8,16},{16,24},{12,4},{20,12},{28,20},{1,9},{9,17},{17,25},{... | collective-permute-start | bytes 3538952 | tf_op jit(solution)/shard_map/ppermute | solution.py:707
  191.2 10.4 %collective-permute-start.38 = (f32[4,32,384]{2,1,0:T(8,128)S(1)}, f32[4,32,384]{2,1,0:T(8,128)S(1)}, u32[]{:S(2)}, u32[]{:S(2)}) collective-permute-start(f32[4,32,384]{2,1,0:T(8,128)S(1)} %get-tuple-element.274.refs_0_.first_ref), channel_id=1, source_target_pairs={{1,0},{2,1},{3,2},{5,4},{6,5},{7,6},{9,8},{10,9},{11,10},{13,12},{... | collective-permute-start | bytes 589832 | tf_op jit(solution)/shard_map/ppermute | solution.py:703
  192.7 8.9 %collective-permute-start.37 = (f32[4,32,384]{2,1,0:T(8,128)S(1)}, f32[4,32,384]{2,1,0:T(8,128)S(1)}, u32[]{:S(2)}, u32[]{:S(2)}) collective-permute-start(f32[4,32,384]{2,1,0:T(8,128)S(1)} %get-tuple-element.277.refs_3_.last_ref), channel_id=1, source_target_pairs={{0,1},{1,2},{2,3},{4,5},{5,6},{6,7},{8,9},{9,10},{10,11},{12,13},{... | collective-permute-start | bytes 589832 | tf_op jit(solution)/shard_map/ppermute | solution.py:700
  195.8 5.8 %collective-permute-start.39 = (f32[4,24,384]{2,1,0:T(8,128)S(1)}, f32[4,24,384]{2,1,0:T(8,128)S(1)}, u32[]{:S(2)}, u32[]{:S(2)}) collective-permute-start(f32[4,24,384]{2,1,0:T(8,128)S(1)} %get-tuple-element.278.refs_4_), channel_id=1, source_target_pairs={{0,4},{4,0},{8,12},{12,8},{16,20},{20,16},{24,28},{28,24},{1,5},{5... | collective-permute-start | bytes 442376 | tf_op jit(solution)/shard_map/ppermute | solution.py:697
  202.3 1.2 collective-permute-start.40
  203.6 3.6 %collective-permute-start.41 = (f32[8,128]{1,0:T(8,128)S(1)}, f32[8,128]{1,0:T(8,128)S(1)}, u32[]{:S(2)}, u32[]{:S(2)}) collective-permute-start(f32[8,128]{1,0:T(8,128)S(1)} %max.75), channel_id=1, source_target_pairs={{0,2},{1,3},{2,0},{3,1},{4,6},{5,7},{6,4},{7,5},{8,10},{9,11},{10,... | collective-permute-start | bytes 12296 | tf_op jit(solution)/shard_map/ppermute | solution.py:721
  207.2 3.6 %collective-permute-start.42 = (f32[8,128]{1,0:T(8,128)S(1)}, f32[8,128]{1,0:T(8,128)S(1)}, u32[]{:S(2)}, u32[]{:S(2)}) collective-permute-start(f32[8,128]{1,0:T(8,128)S(1)} %max.76), channel_id=1, source_target_pairs={{0,4},{4,0},{8,12},{12,8},{16,20},{20,16},{24,28},{28,24},{1,5},{5... | collective-permute-start | bytes 12296 | tf_op jit(solution)/shard_map/ppermute | solution.py:721
  210.8 3.6 %collective-permute-start.43 = (f32[8,128]{1,0:T(8,128)S(1)}, f32[8,128]{1,0:T(8,128)S(1)}, u32[]{:S(2)}, u32[]{:S(2)}) collective-permute-start(f32[8,128]{1,0:T(8,128)S(1)} %max.77), channel_id=1, source_target_pairs={{0,8},{4,12},{8,0},{12,4},{16,24},{20,28},{24,16},{28,20},{1,9},{5... | collective-permute-start | bytes 12296 | tf_op jit(solution)/shard_map/ppermute | solution.py:721
  214.4 4.5 %collective-permute-start.44 = (f32[8,128]{1,0:T(8,128)S(1)}, f32[8,128]{1,0:T(8,128)S(1)}, u32[]{:S(2)}, u32[]{:S(2)}) collective-permute-start(f32[8,128]{1,0:T(8,128)S(1)} %max.78), channel_id=1, source_target_pairs={{0,16},{4,20},{8,24},{12,28},{16,0},{20,4},{24,8},{28,12},{1,17},{... | collective-permute-start | bytes 12296 | tf_op jit(solution)/shard_map/ppermute | solution.py:721
  220.0 29.0 %collective-permute-start.51 = (f32[24,32,384]{2,1,0:T(8,128)S(1)}, f32[24,32,384]{2,1,0:T(8,128)S(1)}, u32[]{:S(2)}, u32[]{:S(2)}) collective-permute-start(f32[24,32,384]{2,1,0:T(8,128)S(1)} %get-tuple-element.292), channel_id=1, source_target_pairs={{0,4},{4,0},{8,12},{12,8},{16,20},{20,16},{24,28},{28,24},{1,5},{5... | collective-permute-start | bytes 3538952 | tf_op jit(solution)/shard_map/ppermute | solution.py:697
  228.5 40.9 %collective-permute-start.47 = (f32[24,32,384]{2,1,0:T(8,128)S(1)}, f32[24,32,384]{2,1,0:T(8,128)S(1)}, u32[]{:S(2)}, u32[]{:S(2)}) collective-permute-start(f32[24,32,384]{2,1,0:T(8,128)S(1)} %get-tuple-element.302), channel_id=1, source_target_pairs={{0,4},{4,0},{8,12},{12,8},{16,20},{20,16},{24,28},{28,24},{1,5},{5... | collective-permute-start | bytes 3538952 | tf_op jit(solution)/shard_map/ppermute | solution.py:697
  229.7 1.2 collective-permute-start.48
  231.0 3.7 %collective-permute-start.49 = (f32[4,384]{1,0:T(4,128)S(1)}, f32[4,384]{1,0:T(4,128)S(1)}, u32[]{:S(2)}, u32[]{:S(2)}) collective-permute-start(f32[4,384]{1,0:T(4,128)S(1)} %fusion), channel_id=1, source_target_pairs={{0,2},{1,3},{2,0},{3,1},{4,6},{5,7},{6,4},{7,5},{8,10},{9,11},{10,... | collective-permute-start | bytes 18440 | tf_op jit(solution)/shard_map/ppermute | solution.py:845
  234.7 34.7 %collective-permute-start.50 = (f32[2,384]{1,0:T(2,128)S(1)}, f32[2,384]{1,0:T(2,128)S(1)}, u32[]{:S(2)}, u32[]{:S(2)}) collective-permute-start(f32[2,384]{1,0:T(2,128)S(1)} %slice.40), channel_id=1, source_target_pairs={{0,4},{4,0},{8,12},{12,8},{16,20},{20,16},{24,28},{28,24},{1,5},{5... | collective-permute-start | bytes 9224 | tf_op jit(solution)/shard_map/ppermute | solution.py:697

commit v8 on v7

--- a/solution.py
+++ b/solution.py
@@ -279,20 +279,20 @@
     )(table, *ops.arrays)
 
 
-def outer_terms(sizes, rows, halo_rows, maxima, stepper, heun, table):
+def outer_terms(sizes, rows, halo_rows, parts, maxima, stepper, heun, table):
     cells_v, half, width, _, _ = sizes
     groups = half // 8
     late = stepper is None
-    arrays = [r.array for r in rows] + list(halo_rows) + ([] if late else [maxima, stepper])
+    arrays = [r.array for r in rows] + list(halo_rows) + list(parts) + ([] if late else [maxima, stepper])
 
     def body(table_ref, *refs):
-        row_refs, before_ref, after_ref, out_refs = refs[:4], refs[4], refs[5], refs[-2:]
+        row_refs, before_ref, after_ref, part_refs, out_refs = refs[:4], refs[4], refs[5], refs[6:8], refs[-2:]
         edge_low, edge_high = table_ref[5, 1] > 0.5, table_ref[5, 2] > 0.5
         known = Rates(sizes)
         if late:
             scale = jnp.ones((8, LANES), jnp.float32)
         else:
-            scale = known.time_step(known.rates(refs[6], refs[7])) * (0.5 if heun else 1.0)
+            scale = known.time_step(known.rates(refs[8], refs[9])) * (0.5 if heun else 1.0)
 
         def wide(x):
             return jnp.concatenate([x] * (width // LANES), axis=1)
@@ -317,7 +317,8 @@
                     else:
                         low, high = inside, jnp.where(edge_high, w, after_ref[j, here, :])
                     slope = high - low
-                    out_refs[i][j, here, :] = jnp.maximum(up * slope, down * slope) - damp * (low + high - (w + w))
+                    total = part_refs[i][j, here, :] + jnp.maximum(up * slope, down * slope)
+                    out_refs[i][j, here, :] = total - damp * (low + high - (w + w))
 
     return pl.pallas_call(
         body,
@@ -445,8 +446,6 @@
             for g in range(groups):
                 here = pl.ds(8 * g, 8)
                 total = ins[update_at[i][0]][j, here, :]
-                if len(update_at[i]) > 3:
-                    total = total + ins[update_at[i][3]][j, here, :]
                 if damping is not None:
                     total = total - damp_2 * ins[update_at[i][1]][j, here, :] - damp_3 * ins[update_at[i][2]][j, here, :]
                 if mended is not None:
@@ -787,8 +786,10 @@
         def ahead(targets, table=table):
             return advanced(targets, field, [bases[t] for t in targets] if heun else None, None, stepper, table)
 
-        def terms(table=table):
-            return outer_terms(sizes, field, halo_rows, shared_first, stepper, heun, table)
+        def with_terms(some, table=table):
+            parts = (some[0][0], some[3][0])
+            outer = outer_terms(sizes, field, halo_rows, parts, shared_first, stepper, heun, table)
+            return {0: [outer[0], *some[0][1:]], 3: [outer[1], *some[3][1:]]}
 
         updates = ahead((1, 2))
         low, high, row = lax.optimization_barrier((low, high, row, updates))[:3]
@@ -798,23 +799,18 @@
 
             def outer_updates(settled):
                 late_table = after(table, settled)
-                got, outer = ahead((0, 3), late_table), terms(late_table)
-                return {0: got[0] + outer[:1], 3: got[3] + outer[1:]}
+                return with_terms(ahead((0, 3), late_table), late_table)
 
             return updates, outer_updates, mended, share(maxima, {1: mended})
         updates.update(ahead((0,)))
         updates.update(ahead((3,)))
-        outer = terms()
-        maxima = share(maxima, {1: mended, 2: updates[0], 3: updates[3], 4: outer})
-        return {**updates, 0: updates[0] + outer[:1], 3: updates[3] + outer[1:]}, mended, maxima
+        outer = with_terms(updates)
+        maxima = share(maxima, {1: mended, 2: updates[0], 3: updates[3], 4: (outer[0][0], outer[3][0])})
+        return {**updates, **outer}, mended, maxima
 
     def settled_all(updates, **kw):
-        fields = kw.pop("fields", None)
-        some = {} if fields is None else {"fields": [fields[0], fields[3]]}
-        (outer, far), edges = settled((0, 3), updates, **some, **kw)
+        (outer, inner, near, far), edges = settled(every, updates, **kw)
         halo_rows = (halo_before(far), halo_after(outer))
-        some = {} if fields is None else {"fields": [fields[1], fields[2]]}
-        (inner, near), edges = settled((1, 2), updates, prior=((0, 3), edges), **some, **kw)
         return [Row(f) for f in (outer, inner, near, far)], edges, halo_rows
 
     halos = (halo_rows, vx_low, vx_high, vy_next)

time: 272 us -> 272 us (level)
    pallas_call x9 -> x7, Pallas kernels: 16.2 us -> 14.6 us  [settle(): pl.pallas_call(body, out_shape=shapes, in_specs=[scalars()] + [whole()] *...]
  transfers between devices with their start and end apart: 52 -> 52, of which waited for: 27 -> 27; matrix products, arithmetic and copies ran while one was open for 4% -> 4% of each run, Pallas kernels for 24% -> 22%
where the time goes in v8:
time: 272 us; the launch traced here: 271 us
  waiting for transfers between devices  103 us (38%)
  starting transfers between devices  81.6 us (30%)
  Pallas kernels  69.7 us (26%)
  local copies, waits for them, and re-layouts  14.8 us (5%)
    ppermute x13, waiting for transfers between devices, partner(): return lax.ppermute(x, 'px', [(i, i ^ 1) for i in range(n_px)])  49.1 us
    ppermute x19, waiting for transfers between devices, share(): lax.ppermute(maxima, axis, [(i, i ^ apart) for i in range(lax.axis_size(a...  45.3 us
    pallas_call x10, Pallas kernels, advance(): pl.pallas_call(body, out_shape=[f32(cells_v, half, width)] * n_out, in_sp...  37.5 us
    ppermute x19, starting transfers between devices, share(): lax.ppermute(maxima, axis, [(i, i ^ apart) for i in range(lax.axis_size(a...  21.9 us
    ppermute x13, starting transfers between devices, partner(): return lax.ppermute(x, 'px', [(i, i ^ 1) for i in range(n_px)])  18.4 us
    ppermute x4, starting transfers between devices, halo_before(): return lax.ppermute(outermost, 'px', moves)  17.5 us
    pallas_call x7, Pallas kernels, settle(): pl.pallas_call(body, out_shape=shapes, in_specs=[scalars()] + [whole()] *...  14.6 us
    ppermute x5, starting transfers between devices, from_low_vx(): return lax.ppermute(x, 'vx', [(i, i + 1) for i in range(n_vx - 1)])  11.9 us
  transfers between devices with their start and end apart: 52, of which 27 were waited for; matrix products, arithmetic and copies ran while one was open for 4% of the time, Pallas kernels for 22%

profile of v8, /device:TPU:0, one launch (start us, length us, event | category | flops | bytes accessed | tf_op | source)
XLA Modules:
  0.0 271.1 jit_solution(17614958980995268755)
XLA Ops:
  0.7 2.4 dynamic-slice_bitcast_fusion.4
  3.0 2.9 %collective-permute-start.6 = (f32[24,32,384]{2,1,0:T(8,128)}, f32[24,32,384]{2,1,0:T(8,128)S(1)}, u32[]{:S(2)}, u32[]{:S(2)}) collective-permute-start(f32[24,32,384]{2,1,0:T(8,128)} %dynamic-slice_bitcast_fusion.4), channel_id=1, source_target_pairs={{0,4},{4,0},{8,12},{12,8},{16,20},{20,16},{24,28},{28,24},{1,5},{5... | collective-permute-start | bytes 3538952 | tf_op jit(solution)/shard_map/ppermute | solution.py:696
  7.2 2.1 collective-permute-start.4
  10.3 1.3 collective-permute-start.1
  14.2 3.4 %dynamic-slice_bitcast_fusion.2 = (f32[24,32,384]{2,1,0:T(8,128)}, f32[24,32,384]{2,1,0:T(8,128)}) fusion(f32[2,24,64,384]{3,2,1,0:T(8,128)} %refs_4_.2, s32[]{:T(128)S(6)} %select_n.88, s32[]{:T(128)S(6)} %select_n.89, s32[]{:T(128)S(6)} %select_n.85, s32[]{:T(128)S(6)} %select_n.86), kind=kLoop, calls=%fused_computation.2 | loop fusion | bytes 4718608 | tf_op jit(solution)/shard_map/squeeze | solution.py:727
  18.9 2.2 first_maxima.1
  21.1 3.8 %collective-permute-start.3 = (f32[8,128]{1,0:T(8,128)S(1)}, f32[8,128]{1,0:T(8,128)S(1)}, u32[]{:S(2)}, u32[]{:S(2)}) collective-permute-start(f32[8,128]{1,0:T(8,128)S(1)} %first_maxima.1), channel_id=1, source_target_pairs={{0,4},{4,0},{8,12},{12,8},{16,20},{20,16},{24,28},{28,24},{1,5},{5... | collective-permute-start | bytes 12296 | tf_op jit(solution)/shard_map/ppermute | solution.py:696
  24.9 8.9 %collective-permute-done.3 = f32[8,128]{1,0:T(8,128)S(1)} collective-permute-done((f32[8,128]{1,0:T(8,128)S(1)}, f32[8,128]{1,0:T(8,128)S(1)}, u32[]{:S(2)}, u32[]{:S(2)}) %collective-permute-start.3) | collective-permute-done | bytes 4128 | tf_op jit(solution)/shard_map/ppermute | solution.py:696
  33.9 1.8 collective-permute-start.5
  35.7 3.2 %dynamic-slice_bitcast_fusion = (f32[24,32,384]{2,1,0:T(8,128)}, f32[24,32,384]{2,1,0:T(8,128)}) fusion(f32[2,24,64,384]{3,2,1,0:T(8,128)} %refs_9_.7, s32[]{:T(128)S(6)} %select_n.88, s32[]{:T(128)S(6)} %select_n.86, s32[]{:T(128)S(6)} %select_n.85), kind=kLoop, calls=%fused_computation | loop fusion | bytes 4718604 | tf_op jit(solution)/shard_map/squeeze | solution.py:727
  40.2 1.5 collective-permute-start.12
  41.7 3.5 %collective-permute-start.7 = (f32[24,32,384]{2,1,0:T(8,128)S(1)}, f32[24,32,384]{2,1,0:T(8,128)S(1)}, u32[]{:S(2)}, u32[]{:S(2)}) collective-permute-start(f32[24,32,384]{2,1,0:T(8,128)S(1)} %collective-permute-done.6.refs_2_), channel_id=1, source_target_pairs={{0,8},{8,16},{16,24},{12,4},{20,12},{28,20},{1,9},{9,17},{17,25},{... | collective-permute-start | bytes 3538952 | tf_op jit(solution)/shard_map/ppermute | solution.py:706
  45.3 1.6 collective-permute-start.13
  46.9 23.6 %collective-permute-done.13 = f32[8,128]{1,0:T(8,128)S(1)} collective-permute-done((f32[8,128]{1,0:T(8,128)S(1)}, f32[8,128]{1,0:T(8,128)S(1)}, u32[]{:S(2)}, u32[]{:S(2)}) %collective-permute-start.13) | collective-permute-done | bytes 4128 | tf_op jit(solution)/shard_map/ppermute | solution.py:720
  70.5 2.6 collective-permute-start.14
  73.1 1.9 collective-permute-done.14
  75.0 1.8 collective-permute-start.15
  80.5 3.3 %collective-permute-done.10 = f32[2,32,384]{2,1,0:T(8,128)S(1)} collective-permute-done((f32[2,32,384]{2,1,0:T(8,128)S(1)}, f32[2,32,384]{2,1,0:T(8,128)S(1)}, u32[]{:S(2)}, u32[]{:S(2)}) %collective-permute-start.10) | collective-permute-done | bytes 98336 | tf_op jit(solution)/shard_map/ppermute | solution.py:702
  83.8 2.3 copy-done.1
  86.1 4.8 %advance_12.4 = (f32[24,32,384]{2,1,0:T(8,128)S(1)}, f32[24,32,384]{2,1,0:T(8,128)S(1)}) custom-call(f32[6,24]{1,0:T(8,128)S(1)} %concatenate.15.table_ref, f32[2,24,64,384]{3,2,1,0:T(8,128)S(1)} %copy-done.1, f32[24,32,384]{2,1,0:T(8,128)S(1)} %collective-permute-done.5.refs_1_.refs_5_, f32[24,32,384]{2,1,0:T(8,128)S(1)} %collective-permute-done.6.refs_2_, ...), custom_call_target="tpu_custom_call" | custom-call | tf_op jit(solution)/shard_map/advance_12/pallas_call | solution.py:270
  91.0 5.7 %advance_03.2 = (f32[24,32,384]{2,1,0:T(8,128)S(1)}, f32[24,32,384]{2,1,0:T(8,128)S(1)}) custom-call(f32[6,24]{1,0:T(8,128)S(1)} %concatenate.15.table_ref, f32[2,24,64,384]{3,2,1,0:T(8,128)S(1)} %copy-done.1, f32[24,32,384]{2,1,0:T(8,128)S(1)} %collective-permute-done.5.refs_1_.refs_5_, f32[24,32,384]{2,1,0:T(8,128)S(1)} %collective-permute-done.6.refs_2_, ...), custom_call_target="tpu_custom_call" | custom-call | tf_op jit(solution)/shard_map/advance_03/pallas_call | solution.py:270
  96.7 1.6 settle_01.1
  100.8 4.6 %collective-permute-start.17 = (f32[24,32,384]{2,1,0:T(8,128)S(1)}, f32[24,32,384]{2,1,0:T(8,128)S(1)}, u32[]{:S(2)}, u32[]{:S(2)}) collective-permute-start(f32[24,32,384]{2,1,0:T(8,128)S(1)} %get-tuple-element.170.refs_1_.refs_3_), channel_id=1, source_target_pairs={{0,8},{8,16},{16,24},{12,4},{20,12},{28,20},{1,9},{9,17},{17,25},{... | collective-permute-start | bytes 3538952 | tf_op jit(solution)/shard_map/ppermute | solution.py:706
  105.4 6.6 %collective-permute-done.15.refs_1_.refs_13_.refs_3_ = f32[24,32,384]{2,1,0:T(8,128)S(1)} collective-permute-done((f32[24,32,384]{2,1,0:T(8,128)}, f32[24,32,384]{2,1,0:T(8,128)S(1)}, u32[]{:S(2)}, u32[]{:S(2)}) %collective-permute-start.15) | collective-permute-done | bytes 1179680 | tf_op jit(solution)/shard_map/ppermute | solution.py:696
  114.4 3.0 %collective-permute-start.19 = (f32[4,32,384]{2,1,0:T(8,128)S(1)}, f32[4,32,384]{2,1,0:T(8,128)S(1)}, u32[]{:S(2)}, u32[]{:S(2)}) collective-permute-start(f32[4,32,384]{2,1,0:T(8,128)S(1)} %get-tuple-element.188.refs_3_.last_ref), channel_id=1, source_target_pairs={{0,1},{1,2},{2,3},{4,5},{5,6},{6,7},{8,9},{9,10},{10,11},{12,13},{... | collective-permute-start | bytes 589832 | tf_op jit(solution)/shard_map/ppermute | solution.py:699
  117.5 1.4 collective-permute-start.21
  118.8 4.8 %advance_12.5 = (f32[24,32,384]{2,1,0:T(8,128)S(1)}, f32[24,32,384]{2,1,0:T(8,128)S(1)}, f32[24,32,384]{2,1,0:T(8,128)S(1)}, f32[24,32,384]{2,1,0:T(8,128)S(1)},...) custom-call(f32[6,24]{1,0:T(8,128)S(1)} %concatenate.15.table_ref, ...), custom_call_target="tpu_custom_call" | custom-call | tf_op jit(solution)/shard_map/advance_12/pallas_call | solution.py:270
  128.1 1.7 collective-permute-done.23
  131.0 2.4 advance_0.2
  133.4 1.7 collective-permute-start.25
  135.1 2.4 advance_3.2
  137.5 2.7 collective-permute-start.26
  140.2 1.6 outer_terms.3
  142.1 3.6 %settle_0123.2 = (f32[24,32,384]{2,1,0:T(8,128)S(1)}, f32[24,32,384]{2,1,0:T(8,128)S(1)}, f32[24,32,384]{2,1,0:T(8,128)S(1)}, f32[24,32,384]{2,1,0:T(8,128)S(1)}...) custom-call(s32[5]{0:T(128)S(1)} %stack.45.flags_ref, ...), custom_call_target="tpu_custom_call" | custom-call | tf_op jit(solution)/shard_map/settle_0123/pallas_call | solution.py:531
  147.0 4.6 %collective-permute-start.27 = (f32[24,32,384]{2,1,0:T(8,128)S(1)}, f32[24,32,384]{2,1,0:T(8,128)S(1)}, u32[]{:S(2)}, u32[]{:S(2)}) collective-permute-start(f32[24,32,384]{2,1,0:T(8,128)S(1)} %get-tuple-element.206.refs_1_.refs_3_.refs_18_.refs_5_), channel_id=1, source_target_pairs={{0,8},{8,16},{16,24},{12,4},{20,12},{28,20},{1,9},{9,17},{17,25},{... | collective-permute-start | bytes 3538952 | tf_op jit(solution)/shard_map/ppermute | solution.py:706
  152.9 3.0 %collective-permute-start.29 = (f32[4,32,384]{2,1,0:T(8,128)S(1)}, f32[4,32,384]{2,1,0:T(8,128)S(1)}, u32[]{:S(2)}, u32[]{:S(2)}) collective-permute-start(f32[4,32,384]{2,1,0:T(8,128)S(1)} %get-tuple-element.224.refs_3_.last_ref), channel_id=1, source_target_pairs={{0,1},{1,2},{2,3},{4,5},{5,6},{6,7},{8,9},{9,10},{10,11},{12,13},{... | collective-permute-start | bytes 589832 | tf_op jit(solution)/shard_map/ppermute | solution.py:699
  156.0 4.5 %advance_12.6 = (f32[24,32,384]{2,1,0:T(8,128)S(1)}, f32[24,32,384]{2,1,0:T(8,128)S(1)}, f32[24,32,384]{2,1,0:T(8,128)S(1)}, f32[24,32,384]{2,1,0:T(8,128)S(1)},...) custom-call(f32[6,24]{1,0:T(8,128)S(1)} %concatenate.15.table_ref, ...), custom_call_target="tpu_custom_call" | custom-call | tf_op jit(solution)/shard_map/advance_12/pallas_call | solution.py:270
  160.5 1.8 collective-permute-done.31.refs_8_.next_ref
  165.2 2.7 collective-permute-done.33
  168.2 2.2 advance_0.3
  172.6 2.2 advance_3.3
  175.2 2.6 collective-permute-start.36
  177.8 1.6 outer_terms.4
  179.7 4.1 %settle_0123.3 = (f32[24,32,384]{2,1,0:T(8,128)S(1)}, f32[24,32,384]{2,1,0:T(8,128)S(1)}, f32[24,32,384]{2,1,0:T(8,128)S(1)}, f32[24,32,384]{2,1,0:T(8,128)S(1)}...) custom-call(s32[5]{0:T(128)S(1)} %stack.45.flags_ref, ...), custom_call_target="tpu_custom_call" | custom-call | tf_op jit(solution)/shard_map/settle_0123/pallas_call | solution.py:531
  185.1 4.7 %collective-permute-start.45 = (f32[24,32,384]{2,1,0:T(8,128)S(1)}, f32[24,32,384]{2,1,0:T(8,128)S(1)}, u32[]{:S(2)}, u32[]{:S(2)}) collective-permute-start(f32[24,32,384]{2,1,0:T(8,128)S(1)} %get-tuple-element.242.refs_3_), channel_id=1, source_target_pairs={{0,8},{8,16},{16,24},{12,4},{20,12},{28,20},{1,9},{9,17},{17,25},{... | collective-permute-start | bytes 3538952 | tf_op jit(solution)/shard_map/ppermute | solution.py:706
  191.1 3.2 %collective-permute-start.37 = (f32[4,32,384]{2,1,0:T(8,128)S(1)}, f32[4,32,384]{2,1,0:T(8,128)S(1)}, u32[]{:S(2)}, u32[]{:S(2)}) collective-permute-start(f32[4,32,384]{2,1,0:T(8,128)S(1)} %get-tuple-element.249.refs_3_.last_ref), channel_id=1, source_target_pairs={{0,1},{1,2},{2,3},{4,5},{5,6},{6,7},{8,9},{9,10},{10,11},{12,13},{... | collective-permute-start | bytes 589832 | tf_op jit(solution)/shard_map/ppermute | solution.py:699
  194.4 4.6 %advance_12.7 = (f32[24,32,384]{2,1,0:T(8,128)S(1)}, f32[24,32,384]{2,1,0:T(8,128)S(1)}, f32[24,32,384]{2,1,0:T(8,128)S(1)}, f32[24,32,384]{2,1,0:T(8,128)S(1)},...) custom-call(f32[6,24]{1,0:T(8,128)S(1)} %concatenate.15.table_ref, ...), custom_call_target="tpu_custom_call" | custom-call | tf_op jit(solution)/shard_map/advance_12/pallas_call | solution.py:270
  203.3 2.7 collective-permute-done.41
  206.7 2.9 %collective-permute-done.42 = f32[8,128]{1,0:T(8,128)S(1)} collective-permute-done((f32[8,128]{1,0:T(8,128)S(1)}, f32[8,128]{1,0:T(8,128)S(1)}, u32[]{:S(2)}, u32[]{:S(2)}) %collective-permute-start.42) | collective-permute-done | bytes 4128 | tf_op jit(solution)/shard_map/ppermute | solution.py:720
  209.6 1.9 collective-permute-start.43
  211.5 1.7 collective-permute-done.43
  213.2 2.3 collective-permute-start.44
  215.5 2.2 collective-permute-done.44
  218.8 1.9 collective-permute-start.51
  220.7 4.0 %advance_03.3 = (f32[24,32,384]{2,1,0:T(8,128)S(1)}, f32[24,32,384]{2,1,0:T(8,128)S(1)}, f32[24,32,384]{2,1,0:T(8,128)S(1)}, f32[24,32,384]{2,1,0:T(8,128)S(1)},...) custom-call(f32[6,24]{1,0:T(8,128)S(1)} %concatenate.15.table_ref, ...), custom_call_target="tpu_custom_call" | custom-call | tf_op jit(solution)/shard_map/advance_03/pallas_call | solution.py:270
  224.7 1.6 outer_terms.5
  226.3 1.9 settle_013.1
  229.9 3.5 %collective-permute-done.49 = f32[4,384]{1,0:T(4,128)S(1)} collective-permute-done((f32[4,384]{1,0:T(4,128)S(1)}, f32[4,384]{1,0:T(4,128)S(1)}, u32[]{:S(2)}, u32[]{:S(2)}) %collective-permute-start.49) | collective-permute-done | bytes 6176 | tf_op jit(solution)/shard_map/ppermute | solution.py:841
  233.4 1.9 collective-permute-start.50
  235.3 2.0 place.2.refs_1_
  237.3 10.4 %collective-permute-done.51.refs_0_ = f32[24,32,384]{2,1,0:T(8,128)S(1)} collective-permute-done((f32[24,32,384]{2,1,0:T(8,128)S(1)}, f32[24,32,384]{2,1,0:T(8,128)S(1)}, u32[]{:S(2)}, u32[]{:S(2)}) %collective-permute-start.51) | collective-permute-done | bytes 1179680 | tf_op jit(solution)/shard_map/ppermute | solution.py:696
  247.7 1.6 place.3._
  249.3 19.5 %collective-permute-done.50.got_ref = f32[2,384]{1,0:T(2,128)S(1)} collective-permute-done((f32[2,384]{1,0:T(2,128)S(1)}, f32[2,384]{1,0:T(2,128)S(1)}, u32[]{:S(2)}, u32[]{:S(2)}) %collective-permute-start.50) | collective-permute-done | bytes 3104 | tf_op jit(solution)/shard_map/ppermute | solution.py:696
  268.8 2.1 finish.1
  (139 shorter events, 40.9 us)
Async XLA Ops:
  0.7 5.3 %copy-start.3 = (f32[2,24]{1,0:T(2,128)S(1)}, f32[2,24]{1,0:T(2,128)}, u32[]{:S(2)}) copy-start(f32[2,24]{1,0:T(2,128)} %first_ref.1) | copy-start | bytes 580
  3.0 38.6 %collective-permute-start.6 = (f32[24,32,384]{2,1,0:T(8,128)}, f32[24,32,384]{2,1,0:T(8,128)S(1)}, u32[]{:S(2)}, u32[]{:S(2)}) collective-permute-start(f32[24,32,384]{2,1,0:T(8,128)} %dynamic-slice_bitcast_fusion.4), channel_id=1, source_target_pairs={{0,4},{4,0},{8,12},{12,8},{16,20},{20,16},{24,28},{28,24},{1,5},{5... | collective-permute-start | bytes 3538952 | tf_op jit(solution)/shard_map/ppermute | solution.py:696
  6.0 27.9 %collective-permute-start = (f32[2,24]{1,0:T(2,128)S(1)}, f32[2,24]{1,0:T(2,128)S(1)}, u32[]{:S(2)}, u32[]{:S(2)}) collective-permute-start(f32[2,24]{1,0:T(2,128)S(1)} %copy-done.3), channel_id=1, source_target_pairs={{0,4},{4,0},{8,12},{12,8},{16,20},{20,16},{24,28},{28,24},{1,5},{5... | collective-permute-start | bytes 584 | tf_op jit(solution)/shard_map/ppermute | solution.py:696
  7.2 26.7 %collective-permute-start.4 = (f32[2,24,384]{2,1,0:T(8,128)S(1)}, f32[2,24,384]{2,1,0:T(8,128)S(1)}, u32[]{:S(2)}, u32[]{:S(2)}) collective-permute-start(f32[2,24,384]{2,1,0:T(8,128)S(1)} %bitcast.36), channel_id=1, source_target_pairs={{0,4},{4,0},{8,12},{12,8},{16,20},{20,16},{24,28},{28,24},{1,5},{5... | collective-permute-start | bytes 221192 | tf_op jit(solution)/shard_map/ppermute | solution.py:696
  10.3 7.3 %collective-permute-start.1 = (f32[2,64,384]{2,1,0:T(8,128)S(1)}, f32[2,64,384]{2,1,0:T(8,128)S(1)}, u32[]{:S(2)}, u32[]{:S(2)}) collective-permute-start(f32[2,64,384]{2,1,0:T(8,128)S(1)} %get-tuple-element.143), channel_id=1, source_target_pairs={{0,1},{1,2},{2,3},{4,5},{5,6},{6,7},{8,9},{9,10},{10,11},{12,13},{... | collective-permute-start | bytes 589832 | tf_op jit(solution)/shard_map/ppermute | solution.py:699
  11.6 7.3 %collective-permute-start.2 = (f32[2,64,384]{2,1,0:T(8,128)S(1)}, f32[2,64,384]{2,1,0:T(8,128)S(1)}, u32[]{:S(2)}, u32[]{:S(2)}) collective-permute-start(f32[2,64,384]{2,1,0:T(8,128)S(1)} %get-tuple-element.144), channel_id=1, source_target_pairs={{1,0},{2,1},{3,2},{5,4},{6,5},{7,6},{9,8},{10,9},{11,10},{13,12},{... | collective-permute-start | bytes 589832 | tf_op jit(solution)/shard_map/ppermute | solution.py:702
  13.0 5.9 %copy-start.2 = (f32[64,384]{1,0:T(8,128)S(1)}, f32[64,384]{1,0:T(8,128)}, u32[]{:S(2)}) copy-start(f32[64,384]{1,0:T(8,128)} %refs_6_.5) | copy-start | bytes 294916
  14.2 4.7 %copy-start = (f32[2,24,64,384]{3,2,1,0:T(8,128)S(1)}, f32[2,24,64,384]{3,2,1,0:T(8,128)}, u32[]{:S(2)}) copy-start(f32[2,24,64,384]{3,2,1,0:T(8,128)} %refs_4_.2) | copy-start | bytes 14155780
  17.6 73.4 %collective-permute-start.8 = (f32[24,32,384]{2,1,0:T(8,128)}, f32[24,32,384]{2,1,0:T(8,128)}, u32[]{:S(2)}, u32[]{:S(2)}) collective-permute-start(f32[24,32,384]{2,1,0:T(8,128)} %get-tuple-element.284), channel_id=1, source_target_pairs={{8,0},{16,8},{24,16},{4,12},{12,20},{20,28},{9,1},{17,9},{25,17},{... | collective-permute-start | bytes 3538952 | tf_op jit(solution)/shard_map/ppermute | solution.py:710
  21.1 12.8 %collective-permute-start.3 = (f32[8,128]{1,0:T(8,128)S(1)}, f32[8,128]{1,0:T(8,128)S(1)}, u32[]{:S(2)}, u32[]{:S(2)}) collective-permute-start(f32[8,128]{1,0:T(8,128)S(1)} %first_maxima.1), channel_id=1, source_target_pairs={{0,4},{4,0},{8,12},{12,8},{16,20},{20,16},{24,28},{28,24},{1,5},{5... | collective-permute-start | bytes 12296 | tf_op jit(solution)/shard_map/ppermute | solution.py:696
  33.9 43.0 %collective-permute-start.5 = (f32[24,32,384]{2,1,0:T(8,128)}, f32[24,32,384]{2,1,0:T(8,128)S(1)}, u32[]{:S(2)}, u32[]{:S(2)}) collective-permute-start(f32[24,32,384]{2,1,0:T(8,128)} %get-tuple-element.146), channel_id=1, source_target_pairs={{0,4},{4,0},{8,12},{12,8},{16,20},{20,16},{24,28},{28,24},{1,5},{5... | collective-permute-start | bytes 3538952 | tf_op jit(solution)/shard_map/ppermute | solution.py:696
  38.9 1.2 collective-permute-start.11
  39.0 60.6 %collective-permute-start.16 = (f32[24,32,384]{2,1,0:T(8,128)}, f32[24,32,384]{2,1,0:T(8,128)S(1)}, u32[]{:S(2)}, u32[]{:S(2)}) collective-permute-start(f32[24,32,384]{2,1,0:T(8,128)} %get-tuple-element.154), channel_id=1, source_target_pairs={{0,4},{4,0},{8,12},{12,8},{16,20},{20,16},{24,28},{28,24},{1,5},{5... | collective-permute-start | bytes 3538952 | tf_op jit(solution)/shard_map/ppermute | solution.py:696
  40.2 5.1 %collective-permute-start.12 = (f32[8,128]{1,0:T(8,128)S(1)}, f32[8,128]{1,0:T(8,128)S(1)}, u32[]{:S(2)}, u32[]{:S(2)}) collective-permute-start(f32[8,128]{1,0:T(8,128)S(1)} %max.61), channel_id=1, source_target_pairs={{0,2},{1,3},{2,0},{3,1},{4,6},{5,7},{6,4},{7,5},{8,10},{9,11},{10,... | collective-permute-start | bytes 12296 | tf_op jit(solution)/shard_map/ppermute | solution.py:720
  41.7 49.3 %collective-permute-start.7 = (f32[24,32,384]{2,1,0:T(8,128)S(1)}, f32[24,32,384]{2,1,0:T(8,128)S(1)}, u32[]{:S(2)}, u32[]{:S(2)}) collective-permute-start(f32[24,32,384]{2,1,0:T(8,128)S(1)} %collective-permute-done.6.refs_2_), channel_id=1, source_target_pairs={{0,8},{8,16},{16,24},{12,4},{20,12},{28,20},{1,9},{9,17},{17,25},{... | collective-permute-start | bytes 3538952 | tf_op jit(solution)/shard_map/ppermute | solution.py:706
  45.3 25.2 %collective-permute-start.13 = (f32[8,128]{1,0:T(8,128)S(1)}, f32[8,128]{1,0:T(8,128)S(1)}, u32[]{:S(2)}, u32[]{:S(2)}) collective-permute-start(f32[8,128]{1,0:T(8,128)S(1)} %max.62), channel_id=1, source_target_pairs={{0,8},{4,12},{8,0},{12,4},{16,24},{20,28},{24,16},{28,20},{1,9},{5... | collective-permute-start | bytes 12296 | tf_op jit(solution)/shard_map/ppermute | solution.py:720
  70.5 4.5 %collective-permute-start.14 = (f32[8,128]{1,0:T(8,128)S(1)}, f32[8,128]{1,0:T(8,128)S(1)}, u32[]{:S(2)}, u32[]{:S(2)}) collective-permute-start(f32[8,128]{1,0:T(8,128)S(1)} %max.63), channel_id=1, source_target_pairs={{0,16},{4,20},{8,24},{12,28},{16,0},{20,4},{24,8},{28,12},{1,17},{... | collective-permute-start | bytes 12296 | tf_op jit(solution)/shard_map/ppermute | solution.py:720
  75.0 36.9 %collective-permute-start.15 = (f32[24,32,384]{2,1,0:T(8,128)}, f32[24,32,384]{2,1,0:T(8,128)S(1)}, u32[]{:S(2)}, u32[]{:S(2)}) collective-permute-start(f32[24,32,384]{2,1,0:T(8,128)} %get-tuple-element.152), channel_id=1, source_target_pairs={{0,4},{4,0},{8,12},{12,8},{16,20},{20,16},{24,28},{28,24},{1,5},{5... | collective-permute-start | bytes 3538952 | tf_op jit(solution)/shard_map/ppermute | solution.py:696
  76.9 2.2 collective-permute-start.9
  79.2 4.6 %collective-permute-start.10 = (f32[2,32,384]{2,1,0:T(8,128)S(1)}, f32[2,32,384]{2,1,0:T(8,128)S(1)}, u32[]{:S(2)}, u32[]{:S(2)}) collective-permute-start(f32[2,32,384]{2,1,0:T(8,128)S(1)} %pad_maximum_fusion.4), channel_id=1, source_target_pairs={{1,0},{2,1},{3,2},{5,4},{6,5},{7,6},{9,8},{10,9},{11,10},{13,12},{... | collective-permute-start | bytes 294920 | tf_op jit(solution)/shard_map/ppermute | solution.py:702
  83.8 2.3 copy-start.1
  86.1 10.6 %slice-start.2 = ((s8[4718592]{0:T(1024)(128)(4,1)}), s8[4194304]{0:T(1024)(128)(4,1)S(1)}, s32[]{:S(2)}) async-start(s8[4718592]{0:T(1024)(128)(4,1)} %bitcast.34), calls=%async_computation.2 | async-start | bytes 8388608
  90.9 5.8 %slice-start.3 = ((s8[4718592]{0:T(1024)(128)(4,1)}), s8[524288]{0:T(1024)(128)(4,1)S(1)}, s32[]{:S(2)}) async-start(s8[4718592]{0:T(1024)(128)(4,1)} %bitcast.34), calls=%async_computation.3 | async-start | bytes 1048576
  91.0 27.9 %slice-start = ((s8[4718592]{0:T(1024)(128)(4,1)}), s8[4194304]{0:T(1024)(128)(4,1)S(1)}, s32[]{:S(2)}) async-start(s8[4718592]{0:T(1024)(128)(4,1)} %bitcast.32), calls=%async_computation | async-start | bytes 8388608
  96.7 22.1 %slice-start.1 = ((s8[4718592]{0:T(1024)(128)(4,1)}), s8[524288]{0:T(1024)(128)(4,1)S(1)}, s32[]{:S(2)}) async-start(s8[4718592]{0:T(1024)(128)(4,1)} %bitcast.32), calls=%async_computation.1 | async-start | bytes 1048576
  98.3 41.9 %collective-permute-start.18 = (f32[24,32,384]{2,1,0:T(8,128)S(1)}, f32[24,32,384]{2,1,0:T(8,128)S(1)}, u32[]{:S(2)}, u32[]{:S(2)}) collective-permute-start(f32[24,32,384]{2,1,0:T(8,128)S(1)} %get-tuple-element.149.refs_0_), channel_id=1, source_target_pairs={{8,0},{16,8},{24,16},{4,12},{12,20},{20,28},{9,1},{17,9},{25,17},{... | collective-permute-start | bytes 3538952 | tf_op jit(solution)/shard_map/ppermute | solution.py:710
  100.8 39.4 %collective-permute-start.17 = (f32[24,32,384]{2,1,0:T(8,128)S(1)}, f32[24,32,384]{2,1,0:T(8,128)S(1)}, u32[]{:S(2)}, u32[]{:S(2)}) collective-permute-start(f32[24,32,384]{2,1,0:T(8,128)S(1)} %get-tuple-element.170.refs_1_.refs_3_), channel_id=1, source_target_pairs={{0,8},{8,16},{16,24},{12,4},{20,12},{28,20},{1,9},{9,17},{17,25},{... | collective-permute-start | bytes 3538952 | tf_op jit(solution)/shard_map/ppermute | solution.py:706
  113.1 11.0 %collective-permute-start.20 = (f32[4,32,384]{2,1,0:T(8,128)S(1)}, f32[4,32,384]{2,1,0:T(8,128)S(1)}, u32[]{:S(2)}, u32[]{:S(2)}) collective-permute-start(f32[4,32,384]{2,1,0:T(8,128)S(1)} %get-tuple-element.185.refs_0_.first_ref), channel_id=1, source_target_pairs={{1,0},{2,1},{3,2},{5,4},{6,5},{7,6},{9,8},{10,9},{11,10},{13,12},{... | collective-permute-start | bytes 589832 | tf_op jit(solution)/shard_map/ppermute | solution.py:702
  114.4 9.8 %collective-permute-start.19 = (f32[4,32,384]{2,1,0:T(8,128)S(1)}, f32[4,32,384]{2,1,0:T(8,128)S(1)}, u32[]{:S(2)}, u32[]{:S(2)}) collective-permute-start(f32[4,32,384]{2,1,0:T(8,128)S(1)} %get-tuple-element.188.refs_3_.last_ref), channel_id=1, source_target_pairs={{0,1},{1,2},{2,3},{4,5},{5,6},{6,7},{8,9},{9,10},{10,11},{12,13},{... | collective-permute-start | bytes 589832 | tf_op jit(solution)/shard_map/ppermute | solution.py:699
  117.5 6.7 %collective-permute-start.21 = (f32[4,24,384]{2,1,0:T(8,128)S(1)}, f32[4,24,384]{2,1,0:T(8,128)S(1)}, u32[]{:S(2)}, u32[]{:S(2)}) collective-permute-start(f32[4,24,384]{2,1,0:T(8,128)S(1)} %get-tuple-element.189.refs_4_), channel_id=1, source_target_pairs={{0,4},{4,0},{8,12},{12,8},{16,20},{20,16},{24,28},{28,24},{1,5},{5... | collective-permute-start | bytes 442376 | tf_op jit(solution)/shard_map/ppermute | solution.py:696
  124.9 1.2 collective-permute-start.22
  126.2 3.6 %collective-permute-start.23 = (f32[8,128]{1,0:T(8,128)S(1)}, f32[8,128]{1,0:T(8,128)S(1)}, u32[]{:S(2)}, u32[]{:S(2)}) collective-permute-start(f32[8,128]{1,0:T(8,128)S(1)} %max.65), channel_id=1, source_target_pairs={{0,2},{1,3},{2,0},{3,1},{4,6},{5,7},{6,4},{7,5},{8,10},{9,11},{10,... | collective-permute-start | bytes 12296 | tf_op jit(solution)/shard_map/ppermute | solution.py:720
  129.8 3.6 %collective-permute-start.24 = (f32[8,128]{1,0:T(8,128)S(1)}, f32[8,128]{1,0:T(8,128)S(1)}, u32[]{:S(2)}, u32[]{:S(2)}) collective-permute-start(f32[8,128]{1,0:T(8,128)S(1)} %max.66), channel_id=1, source_target_pairs={{0,4},{4,0},{8,12},{12,8},{16,20},{20,16},{24,28},{28,24},{1,5},{5... | collective-permute-start | bytes 12296 | tf_op jit(solution)/shard_map/ppermute | solution.py:720
  133.4 4.1 %collective-permute-start.25 = (f32[8,128]{1,0:T(8,128)S(1)}, f32[8,128]{1,0:T(8,128)S(1)}, u32[]{:S(2)}, u32[]{:S(2)}) collective-permute-start(f32[8,128]{1,0:T(8,128)S(1)} %max.67), channel_id=1, source_target_pairs={{0,8},{4,12},{8,0},{12,4},{16,24},{20,28},{24,16},{28,20},{1,9},{5... | collective-permute-start | bytes 12296 | tf_op jit(solution)/shard_map/ppermute | solution.py:720
  137.5 4.6 %collective-permute-start.26 = (f32[8,128]{1,0:T(8,128)S(1)}, f32[8,128]{1,0:T(8,128)S(1)}, u32[]{:S(2)}, u32[]{:S(2)}) collective-permute-start(f32[8,128]{1,0:T(8,128)S(1)} %max.68), channel_id=1, source_target_pairs={{0,16},{4,20},{8,24},{12,28},{16,0},{20,4},{24,8},{28,12},{1,17},{... | collective-permute-start | bytes 12296 | tf_op jit(solution)/shard_map/ppermute | solution.py:720
  145.7 32.1 %collective-permute-start.28 = (f32[24,32,384]{2,1,0:T(8,128)S(1)}, f32[24,32,384]{2,1,0:T(8,128)S(1)}, u32[]{:S(2)}, u32[]{:S(2)}) collective-permute-start(f32[24,32,384]{2,1,0:T(8,128)S(1)} %get-tuple-element.203.refs_0_.refs_15_.refs_4_), channel_id=1, source_target_pairs={{8,0},{16,8},{24,16},{4,12},{12,20},{20,28},{9,1},{17,9},{25,17},{... | collective-permute-start | bytes 3538952 | tf_op jit(solution)/shard_map/ppermute | solution.py:710
  147.0 30.8 %collective-permute-start.27 = (f32[24,32,384]{2,1,0:T(8,128)S(1)}, f32[24,32,384]{2,1,0:T(8,128)S(1)}, u32[]{:S(2)}, u32[]{:S(2)}) collective-permute-start(f32[24,32,384]{2,1,0:T(8,128)S(1)} %get-tuple-element.206.refs_1_.refs_3_.refs_18_.refs_5_), channel_id=1, source_target_pairs={{0,8},{8,16},{16,24},{12,4},{20,12},{28,20},{1,9},{9,17},{17,25},{... | collective-permute-start | bytes 3538952 | tf_op jit(solution)/shard_map/ppermute | solution.py:706
  151.6 10.7 %collective-permute-start.30 = (f32[4,32,384]{2,1,0:T(8,128)S(1)}, f32[4,32,384]{2,1,0:T(8,128)S(1)}, u32[]{:S(2)}, u32[]{:S(2)}) collective-permute-start(f32[4,32,384]{2,1,0:T(8,128)S(1)} %get-tuple-element.221.refs_0_.first_ref), channel_id=1, source_target_pairs={{1,0},{2,1},{3,2},{5,4},{6,5},{7,6},{9,8},{10,9},{11,10},{13,12},{... | collective-permute-start | bytes 589832 | tf_op jit(solution)/shard_map/ppermute | solution.py:702
  152.9 9.4 %collective-permute-start.29 = (f32[4,32,384]{2,1,0:T(8,128)S(1)}, f32[4,32,384]{2,1,0:T(8,128)S(1)}, u32[]{:S(2)}, u32[]{:S(2)}) collective-permute-start(f32[4,32,384]{2,1,0:T(8,128)S(1)} %get-tuple-element.224.refs_3_.last_ref), channel_id=1, source_target_pairs={{0,1},{1,2},{2,3},{4,5},{5,6},{6,7},{8,9},{9,10},{10,11},{12,13},{... | collective-permute-start | bytes 589832 | tf_op jit(solution)/shard_map/ppermute | solution.py:699
  156.0 6.4 %collective-permute-start.31 = (f32[4,24,384]{2,1,0:T(8,128)S(1)}, f32[4,24,384]{2,1,0:T(8,128)S(1)}, u32[]{:S(2)}, u32[]{:S(2)}) collective-permute-start(f32[4,24,384]{2,1,0:T(8,128)S(1)} %get-tuple-element.225.refs_4_), channel_id=1, source_target_pairs={{0,4},{4,0},{8,12},{12,8},{16,20},{20,16},{24,28},{28,24},{1,5},{5... | collective-permute-start | bytes 442376 | tf_op jit(solution)/shard_map/ppermute | solution.py:696
  163.1 1.2 collective-permute-start.32
  164.3 3.6 %collective-permute-start.33 = (f32[8,128]{1,0:T(8,128)S(1)}, f32[8,128]{1,0:T(8,128)S(1)}, u32[]{:S(2)}, u32[]{:S(2)}) collective-permute-start(f32[8,128]{1,0:T(8,128)S(1)} %max.70), channel_id=1, source_target_pairs={{0,2},{1,3},{2,0},{3,1},{4,6},{5,7},{6,4},{7,5},{8,10},{9,11},{10,... | collective-permute-start | bytes 12296 | tf_op jit(solution)/shard_map/ppermute | solution.py:720
  167.9 3.6 %collective-permute-start.34 = (f32[8,128]{1,0:T(8,128)S(1)}, f32[8,128]{1,0:T(8,128)S(1)}, u32[]{:S(2)}, u32[]{:S(2)}) collective-permute-start(f32[8,128]{1,0:T(8,128)S(1)} %max.71), channel_id=1, source_target_pairs={{0,4},{4,0},{8,12},{12,8},{16,20},{20,16},{24,28},{28,24},{1,5},{5... | collective-permute-start | bytes 12296 | tf_op jit(solution)/shard_map/ppermute | solution.py:720
  171.6 3.6 %collective-permute-start.35 = (f32[8,128]{1,0:T(8,128)S(1)}, f32[8,128]{1,0:T(8,128)S(1)}, u32[]{:S(2)}, u32[]{:S(2)}) collective-permute-start(f32[8,128]{1,0:T(8,128)S(1)} %max.72), channel_id=1, source_target_pairs={{0,8},{4,12},{8,0},{12,4},{16,24},{20,28},{24,16},{28,20},{1,9},{5... | collective-permute-start | bytes 12296 | tf_op jit(solution)/shard_map/ppermute | solution.py:720
  175.2 4.5 %collective-permute-start.36 = (f32[8,128]{1,0:T(8,128)S(1)}, f32[8,128]{1,0:T(8,128)S(1)}, u32[]{:S(2)}, u32[]{:S(2)}) collective-permute-start(f32[8,128]{1,0:T(8,128)S(1)} %max.73), channel_id=1, source_target_pairs={{0,16},{4,20},{8,24},{12,28},{16,0},{20,4},{24,8},{28,12},{1,17},{... | collective-permute-start | bytes 12296 | tf_op jit(solution)/shard_map/ppermute | solution.py:720
  183.8 40.8 %collective-permute-start.46 = (f32[24,32,384]{2,1,0:T(8,128)S(1)}, f32[24,32,384]{2,1,0:T(8,128)S(1)}, u32[]{:S(2)}, u32[]{:S(2)}) collective-permute-start(f32[24,32,384]{2,1,0:T(8,128)S(1)} %get-tuple-element.239.refs_0_), channel_id=1, source_target_pairs={{8,0},{16,8},{24,16},{4,12},{12,20},{20,28},{9,1},{17,9},{25,17},{... | collective-permute-start | bytes 3538952 | tf_op jit(solution)/shard_map/ppermute | solution.py:710
  185.1 39.5 %collective-permute-start.45 = (f32[24,32,384]{2,1,0:T(8,128)S(1)}, f32[24,32,384]{2,1,0:T(8,128)S(1)}, u32[]{:S(2)}, u32[]{:S(2)}) collective-permute-start(f32[24,32,384]{2,1,0:T(8,128)S(1)} %get-tuple-element.242.refs_3_), channel_id=1, source_target_pairs={{0,8},{8,16},{16,24},{12,4},{20,12},{28,20},{1,9},{9,17},{17,25},{... | collective-permute-start | bytes 3538952 | tf_op jit(solution)/shard_map/ppermute | solution.py:706
  189.8 10.5 %collective-permute-start.38 = (f32[4,32,384]{2,1,0:T(8,128)S(1)}, f32[4,32,384]{2,1,0:T(8,128)S(1)}, u32[]{:S(2)}, u32[]{:S(2)}) collective-permute-start(f32[4,32,384]{2,1,0:T(8,128)S(1)} %get-tuple-element.246.refs_0_.first_ref), channel_id=1, source_target_pairs={{1,0},{2,1},{3,2},{5,4},{6,5},{7,6},{9,8},{10,9},{11,10},{13,12},{... | collective-permute-start | bytes 589832 | tf_op jit(solution)/shard_map/ppermute | solution.py:702
  191.1 9.2 %collective-permute-start.37 = (f32[4,32,384]{2,1,0:T(8,128)S(1)}, f32[4,32,384]{2,1,0:T(8,128)S(1)}, u32[]{:S(2)}, u32[]{:S(2)}) collective-permute-start(f32[4,32,384]{2,1,0:T(8,128)S(1)} %get-tuple-element.249.refs_3_.last_ref), channel_id=1, source_target_pairs={{0,1},{1,2},{2,3},{4,5},{5,6},{6,7},{8,9},{9,10},{10,11},{12,13},{... | collective-permute-start | bytes 589832 | tf_op jit(solution)/shard_map/ppermute | solution.py:699
  194.4 6.0 %collective-permute-start.39 = (f32[4,24,384]{2,1,0:T(8,128)S(1)}, f32[4,24,384]{2,1,0:T(8,128)S(1)}, u32[]{:S(2)}, u32[]{:S(2)}) collective-permute-start(f32[4,24,384]{2,1,0:T(8,128)S(1)} %get-tuple-element.250.refs_4_), channel_id=1, source_target_pairs={{0,4},{4,0},{8,12},{12,8},{16,20},{20,16},{24,28},{28,24},{1,5},{5... | collective-permute-start | bytes 442376 | tf_op jit(solution)/shard_map/ppermute | solution.py:696
  201.1 1.2 collective-permute-start.40
  202.3 3.6 %collective-permute-start.41 = (f32[8,128]{1,0:T(8,128)S(1)}, f32[8,128]{1,0:T(8,128)S(1)}, u32[]{:S(2)}, u32[]{:S(2)}) collective-permute-start(f32[8,128]{1,0:T(8,128)S(1)} %max.75), channel_id=1, source_target_pairs={{0,2},{1,3},{2,0},{3,1},{4,6},{5,7},{6,4},{7,5},{8,10},{9,11},{10,... | collective-permute-start | bytes 12296 | tf_op jit(solution)/shard_map/ppermute | solution.py:720
  206.0 3.6 %collective-permute-start.42 = (f32[8,128]{1,0:T(8,128)S(1)}, f32[8,128]{1,0:T(8,128)S(1)}, u32[]{:S(2)}, u32[]{:S(2)}) collective-permute-start(f32[8,128]{1,0:T(8,128)S(1)} %max.76), channel_id=1, source_target_pairs={{0,4},{4,0},{8,12},{12,8},{16,20},{20,16},{24,28},{28,24},{1,5},{5... | collective-permute-start | bytes 12296 | tf_op jit(solution)/shard_map/ppermute | solution.py:720
  209.6 3.6 %collective-permute-start.43 = (f32[8,128]{1,0:T(8,128)S(1)}, f32[8,128]{1,0:T(8,128)S(1)}, u32[]{:S(2)}, u32[]{:S(2)}) collective-permute-start(f32[8,128]{1,0:T(8,128)S(1)} %max.77), channel_id=1, source_target_pairs={{0,8},{4,12},{8,0},{12,4},{16,24},{20,28},{24,16},{28,20},{1,9},{5... | collective-permute-start | bytes 12296 | tf_op jit(solution)/shard_map/ppermute | solution.py:720
  213.2 4.5 %collective-permute-start.44 = (f32[8,128]{1,0:T(8,128)S(1)}, f32[8,128]{1,0:T(8,128)S(1)}, u32[]{:S(2)}, u32[]{:S(2)}) collective-permute-start(f32[8,128]{1,0:T(8,128)S(1)} %max.78), channel_id=1, source_target_pairs={{0,16},{4,20},{8,24},{12,28},{16,0},{20,4},{24,8},{28,12},{1,17},{... | collective-permute-start | bytes 12296 | tf_op jit(solution)/shard_map/ppermute | solution.py:720
  218.8 29.0 %collective-permute-start.51 = (f32[24,32,384]{2,1,0:T(8,128)S(1)}, f32[24,32,384]{2,1,0:T(8,128)S(1)}, u32[]{:S(2)}, u32[]{:S(2)}) collective-permute-start(f32[24,32,384]{2,1,0:T(8,128)S(1)} %get-tuple-element.264), channel_id=1, source_target_pairs={{0,4},{4,0},{8,12},{12,8},{16,20},{20,16},{24,28},{28,24},{1,5},{5... | collective-permute-start | bytes 3538952 | tf_op jit(solution)/shard_map/ppermute | solution.py:696
  228.2 40.6 %collective-permute-start.47 = (f32[24,32,384]{2,1,0:T(8,128)S(1)}, f32[24,32,384]{2,1,0:T(8,128)S(1)}, u32[]{:S(2)}, u32[]{:S(2)}) collective-permute-start(f32[24,32,384]{2,1,0:T(8,128)S(1)} %get-tuple-element.274), channel_id=1, source_target_pairs={{0,4},{4,0},{8,12},{12,8},{16,20},{20,16},{24,28},{28,24},{1,5},{5... | collective-permute-start | bytes 3538952 | tf_op jit(solution)/shard_map/ppermute | solution.py:696
  228.5 1.2 collective-permute-start.48
  229.7 3.7 %collective-permute-start.49 = (f32[4,384]{1,0:T(4,128)S(1)}, f32[4,384]{1,0:T(4,128)S(1)}, u32[]{:S(2)}, u32[]{:S(2)}) collective-permute-start(f32[4,384]{1,0:T(4,128)S(1)} %fusion), channel_id=1, source_target_pairs={{0,2},{1,3},{2,0},{3,1},{4,6},{5,7},{6,4},{7,5},{8,10},{9,11},{10,... | collective-permute-start | bytes 18440 | tf_op jit(solution)/shard_map/ppermute | solution.py:841
  233.4 35.4 %collective-permute-start.50 = (f32[2,384]{1,0:T(2,128)S(1)}, f32[2,384]{1,0:T(2,128)S(1)}, u32[]{:S(2)}, u32[]{:S(2)}) collective-permute-start(f32[2,384]{1,0:T(2,128)S(1)} %slice.40), channel_id=1, source_target_pairs={{0,4},{4,0},{8,12},{12,8},{16,20},{20,16},{24,28},{28,24},{1,5},{5... | collective-permute-start | bytes 9224 | tf_op jit(solution)/shard_map/ppermute | solution.py:696
